TPU v7x, 32 devices: a whole 2x2x4 slice. The times are simulated.
32 devices in a mesh: batch: 8 (over z, core), seq: 4 (over y, x).
Axes of the slice: x: 2, y: 2, z: 4, core: 2. Of those that a mesh axis runs over, the one named last changes fastest.
Arguments:
- image_tokens: bfloat16 [16, 1024, 1536], P('batch', 'seq'), may hold values from -6 to 6
- text_tokens: bfloat16 [16, 160, 1536], P('batch', 'seq'), may hold values from -6 to 6
- conditioning: bfloat16 [16, 1536], P('batch'), may hold values from -6 to 6
- key_mask: int32 [16, 1184], P('batch'), may hold values from 0 to 1, as said below
- mod_weight: bfloat16 [2, 1536, 9216], P(None, None, ('batch', 'seq')), may hold values from -0.21875 to 0.21875
- mod_bias: bfloat16 [2, 9216], P(None, ('batch', 'seq')), may hold values from -3 to 3
- qkv_weight: bfloat16 [2, 1536, 4608], P(None, None, ('batch', 'seq')), may hold values from -0.15625 to 0.15625
- qv_bias: bfloat16 [2, 3072], P(None, ('batch', 'seq')), may hold values from -3 to 3
- out_weight: bfloat16 [2, 1536, 1536], P(None, None, ('batch', 'seq')), may hold values from -2.5 to 2.5
- out_bias: bfloat16 [2, 1536], P(None, ('batch', 'seq')), may hold values from -3 to 3
- up_weight: bfloat16 [2, 1536, 6144], P(None, None, ('batch', 'seq')), may hold values from -0.15625 to 0.15625
- up_bias: bfloat16 [2, 6144], P(None, ('batch', 'seq')), may hold values from -3 to 3
- down_weight: bfloat16 [2, 1536, 6144], P(None, None, ('batch', 'seq')), may hold values from -0.078125 to 0.078125
- down_bias: bfloat16 [2, 1536], P(None, ('batch', 'seq')), may hold values from -3 to 3
- image_cotangent: bfloat16 [16, 1024, 1536], P('batch', 'seq'), may hold values from -6 to 6
- text_cotangent: bfloat16 [16, 160, 1536], P('batch', 'seq'), may hold values from -6 to 6
Outputs:
- image_out: bfloat16 [16, 1024, 1536], P('batch', 'seq')
- text_out: bfloat16 [16, 160, 1536], P('batch', 'seq')
- image_grad: float32 [16, 1024, 1536], P('batch', 'seq')
- text_grad: float32 [16, 160, 1536], P('batch', 'seq')
- cond_grad: float32 [16, 1536], P('batch')
- mod_weight_grad: float32 [2, 1536, 9216], P(None, None, ('batch', 'seq'))
- mod_bias_grad: float32 [2, 9216], P(None, ('batch', 'seq'))
- qkv_weight_grad: float32 [2, 1536, 4608], P(None, None, ('batch', 'seq'))
- qv_bias_grad: float32 [2, 3072], P(None, ('batch', 'seq'))
- out_weight_grad: float32 [2, 1536, 1536], P(None, None, ('batch', 'seq'))
- out_bias_grad: float32 [2, 1536], P(None, ('batch', 'seq'))
- up_weight_grad: float32 [2, 1536, 6144], P(None, None, ('batch', 'seq'))
- up_bias_grad: float32 [2, 6144], P(None, ('batch', 'seq'))
- down_weight_grad: float32 [2, 1536, 6144], P(None, None, ('batch', 'seq'))
- down_bias_grad: float32 [2, 1536], P(None, ('batch', 'seq'))
Inputs may be any that keep to these rules, and one draw needn't show every extreme that they name: `key_mask`: in each sequence all 1024 image keys are live, and of its 160 text slots the first n are live and the rest masked, n drawn for each sequence between 40 and (24640) // 160; at least one sequence that is not masked has n = 154. Exactly one of the 16 sequences, drawn from the seed, has every key masked.
All inputs are finite; a program needn't handle non-finite values.
Results may differ from a plain program's by a relative error of at most 0.015.
The roundings to bfloat16 on the way count: a program that leaves them out, or rounds other values in their place, can miss the bound.
Values may be sent and summed in bfloat16 or wider, within the bound.
No kernel may reach another device: no remote copies, remote signals or barrier semaphores. Data moves between devices by JAX's collectives and lax.ppermute only.
A program may use at most 704 MiB of HBM per device.

v0:
```python
import math

import jax
import jax.numpy as jnp
from jax import lax
from jax.sharding import PartitionSpec as P

HEADS = 24


NORM_EPSILON = 1e-06
FLOOR_SCORE = -10000.0


def modulate(tokens, shift_vec, scale_vec):
    row_mean = jnp.mean(tokens, axis=-1, keepdims=True)
    centered = tokens - row_mean
    row_var = jnp.mean(centered * centered, axis=-1, keepdims=True)
    return (
        centered * lax.rsqrt(row_var + NORM_EPSILON) * (1.0 + scale_vec[:, None, :])
        + shift_vec[:, None, :]
    )


def gelu_tanh(values):
    return jax.nn.gelu(values, approximate=True)


def unmix_columns(values, seq_devices, batch_devices):
    array_shape = values.shape
    piece_width = array_shape[-1] // (seq_devices * batch_devices)
    grid_view = values.reshape(array_shape[:-1] + (seq_devices, batch_devices, piece_width))
    return jnp.swapaxes(grid_view, -3, -2).reshape(array_shape)


def remix_columns(values, seq_devices, batch_devices):
    array_shape = values.shape
    piece_width = array_shape[-1] // (seq_devices * batch_devices)
    grid_view = values.reshape(array_shape[:-1] + (batch_devices, seq_devices, piece_width))
    return jnp.swapaxes(grid_view, -3, -2).reshape(array_shape)


def fetch_columns(
    up_weight,
    down_weight,
    mod_weight,
    qkv_weight,
    out_weight,
    up_bias,
    mod_bias,
    qv_bias,
    out_bias,
    down_bias,
):
    return (
        lax.all_gather(up_weight, "batch", axis=2, tiled=True),
        lax.all_gather(down_weight, "batch", axis=2, tiled=True),
        lax.all_gather(mod_weight, "batch", axis=2, tiled=True),
        lax.all_gather(qkv_weight, "batch", axis=2, tiled=True),
        lax.all_gather(out_weight, "batch", axis=2, tiled=True),
        lax.all_gather(up_bias, "batch", axis=1, tiled=True),
        lax.all_gather(mod_bias, "batch", axis=1, tiled=True),
        lax.all_gather(qv_bias, "batch", axis=1, tiled=True),
        lax.all_gather(out_bias, "batch", axis=1, tiled=True),
        lax.all_gather(down_bias, "batch", axis=1, tiled=True),
    )


def fetch_modulation(mod_part, mod_bias_part):
    return (
        lax.all_gather(mod_part, "seq", axis=2, tiled=True),
        lax.all_gather(mod_bias_part, "seq", axis=1, tiled=True),
    )


def gather_rows(first, second):
    return (
        lax.all_gather(first, "seq", axis=1, tiled=True),
        lax.all_gather(second, "seq", axis=1, tiled=True),
    )


def sum_rows(first, second, seq_devices):
    local_seqs, first_rows, width = first.shape
    first_local = first_rows // seq_devices
    second_local = second.shape[1] // seq_devices
    joined = jnp.concatenate(
        [
            first.reshape(local_seqs, seq_devices, first_local, width),
            second.reshape(local_seqs, seq_devices, second_local, width),
        ],
        axis=2,
    )
    joined = joined.reshape(local_seqs, seq_devices * (first_local + second_local), width)
    total = lax.psum_scatter(joined, "seq", scatter_dimension=1, tiled=True)
    return (total[:, :first_local], total[:, first_local:])


def to_rows(first, second):
    return (
        lax.all_to_all(first, "seq", split_axis=1, concat_axis=2, tiled=True),
        lax.all_to_all(second, "seq", split_axis=1, concat_axis=2, tiled=True),
    )


def to_columns(first, second):
    return (
        lax.all_to_all(first, "seq", split_axis=2, concat_axis=1, tiled=True),
        lax.all_to_all(second, "seq", split_axis=2, concat_axis=1, tiled=True),
    )


def own_block(values, seq_index, seq_devices):
    width = values.shape[1] // seq_devices
    return lax.dynamic_slice_in_dim(values, seq_index * width, width, 1)


def on_device(
    image_tokens,
    text_tokens,
    conditioning,
    key_mask,
    mod_weight,
    mod_bias,
    qkv_weight,
    qv_bias,
    out_weight,
    out_bias,
    up_weight,
    up_bias,
    down_weight,
    down_bias,
    image_cotangent,
    text_cotangent,
):
    seq_devices = lax.axis_size("seq")
    batch_devices = lax.axis_size("batch")
    seq_index = lax.axis_index("seq")
    local_seqs, image_count, model_width = image_tokens.shape
    text_count = text_tokens.shape[1]
    block_rows = image_count + text_count
    key_count = block_rows * seq_devices
    head_size = model_width // HEADS
    factor = 1.0 / math.sqrt(head_size)
    inputs = (image_tokens.astype(jnp.float32), text_tokens.astype(jnp.float32))
    cotangents = (image_cotangent.astype(jnp.float32), text_cotangent.astype(jnp.float32))
    row_spans = ((0, image_count), (image_count, block_rows))
    image_keys = key_mask[:, : image_count * seq_devices].reshape(
        local_seqs, seq_devices, image_count
    )
    text_keys = key_mask[:, image_count * seq_devices :].reshape(
        local_seqs, seq_devices, text_count
    )
    key_live = (
        jnp.concatenate([image_keys, text_keys], axis=2).reshape(local_seqs, key_count) > 0
    )[:, None, None, :]
    cond_float = conditioning.astype(jnp.float32)
    smooth = jax.nn.silu(cond_float).astype(jnp.bfloat16)
    fetched = fetch_columns(
        up_weight,
        down_weight,
        mod_weight,
        qkv_weight,
        out_weight,
        up_bias,
        mod_bias,
        qv_bias,
        out_bias,
        down_bias,
    )
    (
        up_part,
        down_part,
        mod_part,
        qkv_part,
        out_part,
        up_bias_part,
        mod_bias_part,
        qv_part,
        out_bias_part,
        down_bias_part,
    ) = fetched
    mod_full, mod_bias_full = fetch_modulation(mod_part, mod_bias_part)
    mixed_mod = (
        jnp.einsum("sd,tdf->tsf", smooth, mod_full, preferred_element_type=jnp.float32)
        + mod_bias_full.astype(jnp.float32)[:, None, :]
    )
    modulation = unmix_columns(mixed_mod, seq_devices, batch_devices).reshape(
        2, local_seqs, 6, model_width
    )
    first_norms = []
    for modality in range(2):
        pieces = modulation[modality]
        first_norms.append(
            modulate(inputs[modality], pieces[:, 0], pieces[:, 1]).astype(jnp.bfloat16)
        )
    norm_image_all, norm_text_all, qv_seq, out_bias_seq, down_bias_seq = (
        lax.all_gather(first_norms[0], "seq", axis=1, tiled=True),
        lax.all_gather(first_norms[1], "seq", axis=1, tiled=True),
        lax.all_gather(qv_part, "seq", axis=1, tiled=True),
        lax.all_gather(out_bias_part, "seq", axis=1, tiled=True),
        lax.all_gather(down_bias_part, "seq", axis=1, tiled=True),
    )
    first_all = (norm_image_all, norm_text_all)
    qv_full = unmix_columns(qv_seq, seq_devices, batch_devices).astype(jnp.float32)
    out_bias_full = unmix_columns(out_bias_seq, seq_devices, batch_devices).astype(jnp.float32)
    down_bias_full = unmix_columns(down_bias_seq, seq_devices, batch_devices).astype(jnp.float32)
    qkv_cols = [
        jnp.einsum(
            "srd,df->srf",
            first_all[modality],
            qkv_part[modality],
            preferred_element_type=jnp.float32,
        )
        for modality in range(2)
    ]
    qkv_rows = to_rows(qkv_cols[0], qkv_cols[1])
    queries, keyvals = ([], [])
    for modality in range(2):
        projected = unmix_columns(qkv_rows[modality], seq_devices, batch_devices)
        qv_vector = qv_full[modality]
        queries.append(
            (projected[..., :model_width] + qv_vector[:model_width]).astype(jnp.bfloat16)
        )
        value_shift = jnp.concatenate(
            [jnp.zeros((model_width,), jnp.float32), qv_vector[model_width:]]
        )
        keyvals.append((projected[..., model_width:] + value_shift).astype(jnp.bfloat16))
    joined_query = jnp.concatenate(queries, axis=1)
    joined_keyval = jnp.concatenate(keyvals, axis=1)
    all_keyval = lax.all_gather(joined_keyval, "seq", axis=1, tiled=True)
    query_heads = joined_query.reshape(local_seqs, block_rows, HEADS, head_size)
    key_heads = all_keyval[..., :model_width].reshape(local_seqs, key_count, HEADS, head_size)
    value_heads = all_keyval[..., model_width:].reshape(local_seqs, key_count, HEADS, head_size)
    scores = (
        jnp.einsum("sqhe,skhe->shqk", query_heads, key_heads, preferred_element_type=jnp.float32)
        * factor
    )
    row_max = jnp.max(jnp.where(key_live, scores, FLOOR_SCORE), axis=-1, keepdims=True)
    exp_terms = jnp.exp(jnp.where(key_live, scores - row_max, FLOOR_SCORE))
    denominator = jnp.maximum(jnp.sum(exp_terms, axis=-1, keepdims=True), 1.0)
    prob_low = (exp_terms / denominator).astype(jnp.bfloat16)
    logsum = row_max + jnp.log(denominator)
    attended = jnp.einsum(
        "shqk,skhe->sqhe", prob_low, value_heads, preferred_element_type=jnp.float32
    )
    attended = attended.reshape(local_seqs, block_rows, model_width).astype(jnp.bfloat16)
    attended_all = gather_rows(attended[:, :image_count], attended[:, image_count:])
    out_cols = [
        jnp.einsum(
            "srd,df->srf",
            attended_all[modality],
            out_part[modality],
            preferred_element_type=jnp.float32,
        )
        for modality in range(2)
    ]
    out_rows = to_rows(out_cols[0], out_cols[1])
    projections, middles, second_norms = ([], [], [])
    for modality in range(2):
        pieces = modulation[modality]
        projection = (
            unmix_columns(out_rows[modality], seq_devices, batch_devices) + out_bias_full[modality]
        )
        middle = inputs[modality] + pieces[:, 2][:, None, :] * projection
        second_norms.append(modulate(middle, pieces[:, 3], pieces[:, 4]).astype(jnp.bfloat16))
        projections.append(projection)
        middles.append(middle)
    group_rows = gather_rows(second_norms[0], second_norms[1])
    hidden_pre, hidden_act, partials = ([], [], [])
    for modality in range(2):
        pre_values = jnp.einsum(
            "srd,df->srf",
            group_rows[modality],
            up_part[modality],
            preferred_element_type=jnp.float32,
        ) + up_bias_part[modality].astype(jnp.float32)
        act_values = gelu_tanh(pre_values).astype(jnp.bfloat16)
        partials.append(
            jnp.einsum(
                "srf,df->srd", act_values, down_part[modality], preferred_element_type=jnp.float32
            )
        )
        hidden_pre.append(pre_values)
        hidden_act.append(act_values)
    mlp_rows = sum_rows(partials[0], partials[1], seq_devices)
    mlp_outs, results = ([], [])
    for modality in range(2):
        pieces = modulation[modality]
        mlp_value = mlp_rows[modality] + down_bias_full[modality]
        results.append(
            (middles[modality] + pieces[:, 5][:, None, :] * mlp_value).astype(jnp.bfloat16)
        )
        mlp_outs.append(mlp_value)
    fetched_back = fetch_columns(
        up_weight,
        down_weight,
        mod_weight,
        qkv_weight,
        out_weight,
        up_bias,
        mod_bias,
        qv_bias,
        out_bias,
        down_bias,
    )
    up_back, down_back, mod_back, qkv_back, out_back = (
        fetched_back[0],
        fetched_back[1],
        fetched_back[2],
        fetched_back[3],
        fetched_back[4],
    )
    mod_bias_back = fetched_back[6]
    mlp_grads, gate_twos, down_bias_grads = ([], [], [])
    for modality in range(2):
        pieces = modulation[modality]
        mlp_grad = (pieces[:, 5][:, None, :] * cotangents[modality]).astype(jnp.bfloat16)
        gate_twos.append(jnp.sum(cotangents[modality] * mlp_outs[modality], axis=1))
        down_bias_grads.append(jnp.sum(mlp_grad.astype(jnp.float32), axis=(0, 1)))
        mlp_grads.append(mlp_grad)
    group_grads = gather_rows(mlp_grads[0], mlp_grads[1])
    down_grads, up_grads, up_bias_grads, norm_partials = ([], [], [], [])
    for modality in range(2):
        down_grads.append(
            jnp.einsum(
                "srd,srf->df",
                group_grads[modality],
                hidden_act[modality],
                preferred_element_type=jnp.float32,
            )
        )
        act_grad = jnp.einsum(
            "srd,df->srf",
            group_grads[modality],
            down_back[modality],
            preferred_element_type=jnp.float32,
        )
        pullback = jax.vjp(gelu_tanh, hidden_pre[modality])[1]
        pre_grad = pullback(act_grad)[0].astype(jnp.bfloat16)
        up_grads.append(
            jnp.einsum(
                "srd,srf->df", group_rows[modality], pre_grad, preferred_element_type=jnp.float32
            )
        )
        up_bias_grads.append(jnp.sum(pre_grad.astype(jnp.float32), axis=(0, 1)))
        norm_partials.append(
            jnp.einsum(
                "srf,df->srd", pre_grad, up_back[modality], preferred_element_type=jnp.float32
            )
        )
    norm_grads = sum_rows(norm_partials[0], norm_partials[1], seq_devices)
    middle_grads, shift_twos, scale_twos, gate_ones, out_bias_grads, proj_grads = (
        [],
        [],
        [],
        [],
        [],
        [],
    )
    for modality in range(2):
        pieces = modulation[modality]
        pullback = jax.vjp(modulate, middles[modality], pieces[:, 3], pieces[:, 4])[1]
        middle_part, shift_two, scale_two = pullback(norm_grads[modality])
        middle_grad = cotangents[modality] + middle_part
        proj_grad = (pieces[:, 2][:, None, :] * middle_grad).astype(jnp.bfloat16)
        gate_ones.append(jnp.sum(middle_grad * projections[modality], axis=1))
        out_bias_grads.append(jnp.sum(proj_grad.astype(jnp.float32), axis=(0, 1)))
        proj_grads.append(remix_columns(proj_grad, seq_devices, batch_devices))
        middle_grads.append(middle_grad)
        shift_twos.append(shift_two)
        scale_twos.append(scale_two)
    proj_cols = to_columns(proj_grads[0], proj_grads[1])
    out_grads, attended_partials = ([], [])
    for modality in range(2):
        out_grads.append(
            jnp.einsum(
                "srd,srf->df",
                attended_all[modality],
                proj_cols[modality],
                preferred_element_type=jnp.float32,
            )
        )
        attended_partials.append(
            jnp.einsum(
                "srf,df->srd",
                proj_cols[modality],
                out_back[modality],
                preferred_element_type=jnp.float32,
            )
        )
    attended_sums = sum_rows(attended_partials[0], attended_partials[1], seq_devices)
    attended_grad = jnp.concatenate([attended_sums[0], attended_sums[1]], axis=1).astype(
        jnp.bfloat16
    )
    grad_heads = attended_grad.reshape(local_seqs, block_rows, HEADS, head_size)
    scores_again = (
        jnp.einsum("sqhe,skhe->shqk", query_heads, key_heads, preferred_element_type=jnp.float32)
        * factor
    )
    probs_again = jnp.exp(jnp.where(key_live, scores_again - logsum, FLOOR_SCORE))
    probs_again_low = probs_again.astype(jnp.bfloat16)
    prob_grad = jnp.einsum(
        "sqhe,skhe->shqk", grad_heads, value_heads, preferred_element_type=jnp.float32
    )
    inner_sum = jnp.sum(probs_again * prob_grad, axis=-1, keepdims=True)
    score_grad = (probs_again * (prob_grad - inner_sum)).astype(jnp.bfloat16)
    query_grad = (
        jnp.einsum("shqk,skhe->sqhe", score_grad, key_heads, preferred_element_type=jnp.float32)
        * factor
    )
    query_grad = query_grad.reshape(local_seqs, block_rows, model_width).astype(jnp.bfloat16)
    key_grad = (
        jnp.einsum("shqk,sqhe->skhe", score_grad, query_heads, preferred_element_type=jnp.float32)
        * factor
    )
    value_grad = jnp.einsum(
        "shqk,sqhe->skhe", probs_again_low, grad_heads, preferred_element_type=jnp.float32
    )
    key_rows, value_rows = (
        lax.psum_scatter(
            key_grad.reshape(local_seqs, key_count, model_width),
            "seq",
            scatter_dimension=1,
            tiled=True,
        ),
        lax.psum_scatter(
            value_grad.reshape(local_seqs, key_count, model_width),
            "seq",
            scatter_dimension=1,
            tiled=True,
        ),
    )
    key_rows = key_rows.astype(jnp.bfloat16)
    value_rows = value_rows.astype(jnp.bfloat16)
    qv_bias_grads, joined_grads = ([], [])
    for modality in range(2):
        row_start, row_stop = row_spans[modality]
        query_part = query_grad[:, row_start:row_stop]
        value_part = value_rows[:, row_start:row_stop]
        joined_grad = jnp.concatenate(
            [query_part, key_rows[:, row_start:row_stop], value_part], axis=-1
        )
        qv_bias_grads.append(
            jnp.concatenate(
                [
                    jnp.sum(query_part.astype(jnp.float32), axis=(0, 1)),
                    jnp.sum(value_part.astype(jnp.float32), axis=(0, 1)),
                ]
            )
        )
        joined_grads.append(remix_columns(joined_grad, seq_devices, batch_devices))
    qkv_grad_cols = to_columns(joined_grads[0], joined_grads[1])
    qkv_grads, first_partials = ([], [])
    for modality in range(2):
        qkv_grads.append(
            jnp.einsum(
                "srd,srf->df",
                first_all[modality],
                qkv_grad_cols[modality],
                preferred_element_type=jnp.float32,
            )
        )
        first_partials.append(
            jnp.einsum(
                "srf,df->srd",
                qkv_grad_cols[modality],
                qkv_back[modality],
                preferred_element_type=jnp.float32,
            )
        )
    first_grads = sum_rows(first_partials[0], first_partials[1], seq_devices)
    input_grads, mod_partials = ([], [])
    for modality in range(2):
        pieces = modulation[modality]
        pullback = jax.vjp(modulate, inputs[modality], pieces[:, 0], pieces[:, 1])[1]
        input_part, shift_one, scale_one = pullback(first_grads[modality])
        input_grads.append(middle_grads[modality] + input_part)
        stacked = jnp.stack(
            [
                shift_one,
                scale_one,
                gate_ones[modality],
                shift_twos[modality],
                scale_twos[modality],
                gate_twos[modality],
            ],
            axis=1,
        )
        mod_partials.append(stacked.reshape(local_seqs, 6 * model_width))
    qv_mixed = remix_columns(jnp.stack(qv_bias_grads), seq_devices, batch_devices)
    out_bias_mixed = remix_columns(jnp.stack(out_bias_grads), seq_devices, batch_devices)
    down_bias_mixed = remix_columns(jnp.stack(down_bias_grads), seq_devices, batch_devices)
    mod_sum, qv_summed, out_bias_summed, down_bias_summed = lax.psum(
        (jnp.stack(mod_partials), qv_mixed, out_bias_mixed, down_bias_mixed), "seq"
    )
    mod_low = mod_sum.astype(jnp.bfloat16)
    mod_mixed = remix_columns(mod_low, seq_devices, batch_devices)
    columns = mod_part.shape[2]
    own_columns = lax.dynamic_slice_in_dim(mod_mixed, seq_index * columns, columns, 2)
    mod_grad = jnp.einsum("sd,tsf->tdf", smooth, own_columns, preferred_element_type=jnp.float32)
    mod_bias_grad = jnp.sum(own_columns.astype(jnp.float32), axis=1)
    mod_again = fetch_modulation(mod_back, mod_bias_back)[0]
    smooth_grad = jnp.einsum(
        "tsf,tdf->sd", mod_mixed, mod_again, preferred_element_type=jnp.float32
    )
    cond_pullback = jax.vjp(jax.nn.silu, cond_float)[1]
    cond_grad = cond_pullback(smooth_grad)[0]
    qv_own = own_block(qv_summed, seq_index, seq_devices)
    out_bias_own = own_block(out_bias_summed, seq_index, seq_devices)
    down_bias_own = own_block(down_bias_summed, seq_index, seq_devices)
    column_grads = (
        lax.psum_scatter(jnp.stack(up_grads), "batch", scatter_dimension=2, tiled=True),
        lax.psum_scatter(jnp.stack(down_grads), "batch", scatter_dimension=2, tiled=True),
        lax.psum_scatter(mod_grad, "batch", scatter_dimension=2, tiled=True),
        lax.psum_scatter(jnp.stack(qkv_grads), "batch", scatter_dimension=2, tiled=True),
        lax.psum_scatter(jnp.stack(out_grads), "batch", scatter_dimension=2, tiled=True),
        lax.psum_scatter(jnp.stack(up_bias_grads), "batch", scatter_dimension=1, tiled=True),
        lax.psum_scatter(mod_bias_grad, "batch", scatter_dimension=1, tiled=True),
        lax.psum_scatter(qv_own, "batch", scatter_dimension=1, tiled=True),
        lax.psum_scatter(out_bias_own, "batch", scatter_dimension=1, tiled=True),
        lax.psum_scatter(down_bias_own, "batch", scatter_dimension=1, tiled=True),
    )
    return (
        results[0],
        results[1],
        input_grads[0],
        input_grads[1],
        cond_grad,
        column_grads[2],
        column_grads[6],
        column_grads[3],
        column_grads[7],
        column_grads[4],
        column_grads[8],
        column_grads[0],
        column_grads[5],
        column_grads[1],
        column_grads[9],
    )


def solution(mesh):
    return jax.shard_map(
        on_device,
        mesh=mesh,
        in_specs=(
            P("batch", "seq", None),
            P("batch", "seq", None),
            P("batch", None),
            P("batch", None),
            P(None, None, ("batch", "seq")),
            P(None, ("batch", "seq")),
            P(None, None, ("batch", "seq")),
            P(None, ("batch", "seq")),
            P(None, None, ("batch", "seq")),
            P(None, ("batch", "seq")),
            P(None, None, ("batch", "seq")),
            P(None, ("batch", "seq")),
            P(None, None, ("batch", "seq")),
            P(None, ("batch", "seq")),
            P("batch", "seq", None),
            P("batch", "seq", None),
        ),
        out_specs=(
            P("batch", "seq", None),
            P("batch", "seq", None),
            P("batch", "seq", None),
            P("batch", "seq", None),
            P("batch", None),
            P(None, None, ("batch", "seq")),
            P(None, ("batch", "seq")),
            P(None, None, ("batch", "seq")),
            P(None, ("batch", "seq")),
            P(None, None, ("batch", "seq")),
            P(None, ("batch", "seq")),
            P(None, None, ("batch", "seq")),
            P(None, ("batch", "seq")),
            P(None, None, ("batch", "seq")),
            P(None, ("batch", "seq")),
        ),
        check_vma=False,
    )
```

profile of v0, /device:TPU:16, one launch (start us, length us, event | category | flops | bytes accessed | tf_op | source)
XLA Modules:
  0.0 5310.7 jit_solution(5333170870355353146)
XLA Ops:
  11.8 129.0 %all-gather.17.cloned.1.call-done = bf16[2,1536,2304]{1,0,2:T(2,128)(2,1)} async-done(((bf16[2,1536,288]{1,0,2:T(2,128)(2,1)}), bf16[2,1536,2304]{1,0,2:T(2,128)(2,1)}) %all-gather.17.cloned.1.call-update) | async-done | bytes 14155792 | tf_op jit(solution)/shard_map/all_gather | solution.py:58
  140.8 35.0 copy.213
  200.9 465.0 %all-gather.19.cloned.1.call-done = bf16[2,1536,9216]{2,1,0:T(8,128)(2,1)} async-done(((bf16[2,1536,2304]{2,1,0:T(8,128)(2,1)}), bf16[2,1536,9216]{2,1,0:T(8,128)(2,1)}) %all-gather.19.cloned.1.call-update) | async-done | bytes 56623120 | tf_op jit(solution)/shard_map/all_gather | solution.py:71
  691.2 47.0 all-gather.23.cloned.1.call-done
  854.2 96.9 %all_gather.85 = bf16[2,3072]{1,0:T(2,128)(2,1)S(1)} all-gather(bf16[2,768]{1,0:T(2,128)(2,1)S(1)} %bitcast.448), channel_id=1, replica_groups=mesh['batch'=8,'seq'=4] {'seq'}, dimensions={1}, use_global_device_ids=true | all-gather | bytes 15360 | tf_op jit(solution)/shard_map/all_gather | solution.py:200
  1008.4 133.5 %all-gather.25.cloned.1.call-done = bf16[2,1184,3072]{2,0,1:T(2,128)(2,1)} async-done(((bf16[2,296,3072]{2,0,1:T(2,128)(2,1)}), bf16[2,1184,3072]{2,0,1:T(2,128)(2,1)}) %all-gather.25.cloned.1.call-update) | async-done | bytes 14549008 | tf_op jit(solution)/shard_map/all_gather | solution.py:231
  1194.7 28.9 select_reduce_fusion
  1247.4 29.6 fusion.57
  1295.1 55.4 %all-gather.27.cloned.1.call-done = bf16[2,1024,1536]{2,1,0:T(8,128)(2,1)} async-done(((bf16[2,256,1536]{2,1,0:T(8,128)(2,1)}), bf16[2,1024,1536]{2,1,0:T(8,128)(2,1)}) %all-gather.27.cloned.1.call-update) | async-done | bytes 6291472 | tf_op jit(solution)/shard_map/all_gather | solution.py:78
  1373.3 30.1 all_gather.91
  1508.7 24.2 all-gather.33.cloned.1.call-done
  1708.1 25.8 convert_reduce_fusion
  1751.7 136.5 %reduce-scatter.23.cloned.1.call-done = f32[2,296,1536]{2,1,0:T(8,128)} async-done(((f32[2,1184,1536]{2,1,0:T(8,128)}), f32[2,296,1536]{2,1,0:T(8,128)}) %reduce-scatter.23.cloned.1.call-update) | async-done | bytes 3637264 | tf_op jit(solution)/shard_map/reduce_scatter | solution.py:95
  1971.5 135.1 %reduce-scatter.25.cloned.1.call-done = f32[2,296,1536]{2,1,0:T(8,128)} async-done(((f32[2,1184,1536]{2,1,0:T(8,128)}), f32[2,296,1536]{2,1,0:T(8,128)}) %reduce-scatter.25.cloned.1.call-update) | async-done | bytes 3637264 | tf_op jit(solution)/shard_map/reduce_scatter | solution.py:95
  2113.0 31.2 fusion.2
  2144.2 50.5 multiply_reduce_fusion
  2194.7 57.1 %multiply_convert_fusion = bf16[2,24,296,1184]{3,2,1,0:T(8,128)(2,1)} fusion(f32[2,24,296,1184]{3,2,1,0:T(8,128)} %get-tuple-element.177, f32[2,24,296,1184]{3,2,1,0:T(8,128)} %get-tuple-element.171, f32[2,24,296]{2,1,0:T(8,128)S(1)} %get-tuple-element.176, f32[2,24,296]{2,1,0:T(8,128)S(1)} %copy-done.38, pred[2,1184]{1,0:T(4,128)(4,1)S(1)} %copy-done.49), kind=kLoop, calls=%fused_computation | loop fusion | flops 100933632 | bytes 168338752 | tf_op jit(solution)/shard_map/convert_element_type | solution.py:407
  2291.9 23.8 copy.267
  2315.6 23.8 copy.265
  2339.4 960.5 %all-reduce.22 = (bf16[2,1184,1536]{2,0,1:T(2,128)(2,1)}, bf16[2,1184,1536]{2,0,1:T(2,128)(2,1)}) all-reduce(f32[2,1184,1536]{2,0,1:T(2,128)} %copy.267, f32[2,1184,1536]{2,0,1:T(2,128)} %copy.265), channel_id=6, replica_groups=mesh['batch'=8,'seq'=4] {'seq'}, use_global_device_ids=true, to_apply=%region_19.20.clone | all-reduce | flops 7274496 | bytes 43646976
  3349.7 30.5 copy.270
  3397.2 39.7 all-to-all-done.6
  3525.0 28.7 copy.288
  3580.0 28.6 copy.290
  3706.4 35.9 reduce-scatter.21.cloned.1.call-done
  3799.3 350.3 %all-reduce.17.cloned.1.call-done = f32[2,1536,1536]{1,0,2:T(2,128)} async-done(((f32[2,1536,1536]{1,0,2:T(2,128)}), f32[2,1536,1536]{1,0,2:T(2,128)}) %all-reduce.17.cloned.1.call-update) | async-done | bytes 18874384
  4153.9 370.6 %all-reduce.19.cloned.1.call-done = f32[2,1536,1536]{1,0,2:T(2,128)} async-done(((f32[2,1536,1536]{1,0,2:T(2,128)}), f32[2,1536,1536]{1,0,2:T(2,128)}) %all-reduce.19.cloned.1.call-update) | async-done | bytes 18874384
  4528.8 371.6 %all-reduce.21.cloned.1.call-done = (f32[2,1536,1152]{1,0,2:T(2,128)}, f32[2,1536,384]{1,0,2:T(2,128)}) async-done(((f32[2,1536,1152]{1,0,2:T(2,128)}, f32[2,1536,384]{1,0,2:T(2,128)}), (f32[2,1536,1152]{1,0,2:T(2,128)}, f32[2,1536,384]{1,0,2:T(2,128)})) %all-reduce.21.cloned.1.call-update) | async-done | bytes 18874384
  4930.0 27.9 reduce-scatter.35.cloned.1.call-done
  4959.3 29.8 reduce-scatter.33.cloned.1.call-done
  4990.5 31.5 reduce-scatter.31.cloned.1.call-done
  5023.6 280.1 %reduce-scatter.29.cloned.1.call-done = f32[2,1536,288]{1,2,0:T(8,128)} async-done(((f32[2,1536,2304]{1,2,0:T(8,128)}), f32[2,1536,288]{1,2,0:T(8,128)}) %reduce-scatter.29.cloned.1.call-update) | async-done | bytes 3538960 | tf_op jit(solution)/shard_map/reduce_scatter | solution.py:515
  (632 shorter events, 1147.0 us)
Async XLA Ops:
  7.2 133.7 %all-gather.17.cloned.1.call-start = ((), (), s32[]{:S(2)}) async-start(), calls=%async_computation.18 | async-start | bytes 15925248 | tf_op jit(solution)/shard_map/all_gather | solution.py:58
  11.8 654.2 %all-gather.19.cloned.1.call-start = ((), (), s32[]{:S(2)}) async-start(), calls=%async_computation.19 | async-start | bytes 70778880 | tf_op jit(solution)/shard_map/all_gather | solution.py:71
  175.9 562.2 %all-gather.23.cloned.1.call-start = ((), (), s32[]{:S(2)}) async-start(), calls=%async_computation.21 | async-start | bytes 7962624 | tf_op jit(solution)/shard_map/all_gather | solution.py:59
  178.8 641.4 %all-gather.21.cloned.1.call-start = ((), (), s32[]{:S(2)}) async-start(), calls=%async_computation.20 | async-start | bytes 7864320 | tf_op jit(solution)/shard_map/all_gather | solution.py:198
  816.7 23.6 all-to-all-start.1
  840.2 121.1 %all-to-all-start = ((f32[2,1024,1152]{2,0,1:T(2,128)}), f32[2,1024,1152]{2,0,1:T(2,128)}, u32[]{:S(2)}, u32[]{:S(2)}) async-start(f32[2,1024,1152]{2,0,1:T(2,128)} %copy.218), calls=%async_computation | async-start | bytes 18874368 | tf_op jit(solution)/shard_map/all_to_all | solution.py:101
  846.2 295.7 %all-gather.25.cloned.1.call-start = ((), (), s32[]{:S(2)}) async-start(), calls=%async_computation.22 | async-start | bytes 18186240 | tf_op jit(solution)/shard_map/all_gather | solution.py:231
  1002.4 282.6 %all-gather.29.cloned.1.call-start = ((), (), s32[]{:S(2)}) async-start(), calls=%async_computation.24 | async-start | bytes 2654208 | tf_op jit(solution)/shard_map/all_gather | solution.py:60
  1003.5 347.0 %all-gather.27.cloned.1.call-start = ((), (), s32[]{:S(2)}) async-start(), calls=%async_computation.23 | async-start | bytes 7864320 | tf_op jit(solution)/shard_map/all_gather | solution.py:78
  1280.2 161.8 %all-gather.35.cloned.1.call-start = ((), (), s32[]{:S(2)}) async-start(), calls=%async_computation.27 | async-start | bytes 10616832 | tf_op jit(solution)/shard_map/all_gather | solution.py:57
  1282.7 250.2 %all-gather.33.cloned.1.call-start = ((), (), s32[]{:S(2)}) async-start(), calls=%async_computation.26 | async-start | bytes 10616832 | tf_op jit(solution)/shard_map/all_gather | solution.py:56
  1360.1 43.6 all-to-all-start.2
  1364.2 324.4 %all-gather.31.cloned.1.call-start = ((), (), s32[]{:S(2)}) async-start(), calls=%async_computation.25 | async-start | bytes 7864320 | tf_op jit(solution)/shard_map/all_gather | solution.py:78
  1419.6 288.5 %all-gather.37.cloned.1.call-start = ((), (), s32[]{:S(2)}) async-start(), calls=%async_computation.29 | async-start | bytes 7864320 | tf_op jit(solution)/shard_map/all_gather | solution.py:78
  1639.1 11.6 all-to-all-start.3
  1642.7 245.5 %reduce-scatter.23.cloned.1.call-start = ((), (), s32[]{:S(2)}) async-start(), calls=%async_computation.30 | async-start | bytes 18186240 | tf_op jit(solution)/shard_map/reduce_scatter | solution.py:95
  1910.2 19.8 all-to-all-start.5
  1930.0 23.9 all-to-all-start.4
  1934.4 172.2 %reduce-scatter.25.cloned.1.call-start = ((), (), s32[]{:S(2)}) async-start(), calls=%async_computation.31 | async-start | bytes 18186240 | tf_op jit(solution)/shard_map/reduce_scatter | solution.py:95
  3343.1 37.2 all-to-all-start.7
  3380.3 56.7 %all-to-all-start.6 = ((bf16[2,256,4608]{1,0,2:T(2,128)(2,1)}), bf16[2,256,4608]{1,0,2:T(2,128)(2,1)}, u32[]{:S(2)}, u32[]{:S(2)}) async-start(bf16[2,256,4608]{1,0,2:T(2,128)(2,1)} %copy.270), calls=%async_computation.9 | async-start | bytes 9437184 | tf_op jit(solution)/shard_map/all_to_all | solution.py:108
  3385.2 318.4 %reduce-scatter.27.cloned.1.call-start = ((), (), s32[]{:S(2)}) async-start(), calls=%async_computation.32 | async-start | bytes 18186240 | tf_op jit(solution)/shard_map/reduce_scatter | solution.py:95
  3465.4 276.9 %reduce-scatter.21.cloned.1.call-start = ((), (), s32[]{:S(2)}) async-start(), calls=%async_computation.28 | async-start | bytes 18186240 | tf_op jit(solution)/shard_map/reduce_scatter | solution.py:95
  3491.0 306.7 %reduce-scatter.37.cloned.1.call-start = ((), (), s32[]{:S(2)}) async-start(), calls=%async_computation.37 | async-start | bytes 884736
  3499.1 650.5 %all-reduce.17.cloned.1.call-start = ((), (), s32[]{:S(2)}) async-start(), calls=%async_computation.39 | async-start | bytes 37748736
  3553.8 970.7 %all-reduce.19.cloned.1.call-start = ((), (), s32[]{:S(2)}) async-start(), calls=%async_computation.40 | async-start | bytes 37748736
  3608.6 1291.9 %all-reduce.21.cloned.1.call-start = ((), (), s32[]{:S(2)}) async-start(), calls=%async_computation.41 | async-start | bytes 37748736
  3678.7 1250.0 %reduce-scatter.39.cloned.1.call-start = ((), (), s32[]{:S(2)}) async-start(), calls=%async_computation.38 | async-start | bytes 221184
  3778.8 1179.1 %reduce-scatter.35.cloned.1.call-start = ((), (), s32[]{:S(2)}) async-start(), calls=%async_computation.36 | async-start | bytes 221184
  3779.7 1209.3 %reduce-scatter.33.cloned.1.call-start = ((), (), s32[]{:S(2)}) async-start(), calls=%async_computation.35 | async-start | bytes 442368
  3780.8 1241.2 %reduce-scatter.31.cloned.1.call-start = ((), (), s32[]{:S(2)}) async-start(), calls=%async_computation.34 | async-start | bytes 1327104
  3782.7 1520.9 %reduce-scatter.29.cloned.1.call-start = ((), (), s32[]{:S(2)}) async-start(), calls=%async_computation.33 | async-start | bytes 31850496 | tf_op jit(solution)/shard_map/reduce_scatter | solution.py:515
  (133 other events, 7118.9 us)
Sparse Core Ops, SparseCore 0:
  11.9 128.9 all-gather.16
  176.0 489.9 all-gather.18
  668.2 69.8 all-gather.22
  740.4 78.0 all-gather.20
  1002.6 139.2 all-gather.24
  1144.0 30.7 all-gather.28
  1280.4 70.1 all-gather.26
  1352.7 89.2 all-gather.34
  1443.7 89.1 all-gather.32
  1535.2 71.5 all-gather.30
  1609.2 89.5 all-gather.36
  1751.8 136.3 reduce-scatter.22
  1969.8 136.8 reduce-scatter.24
  3465.6 136.8 reduce-scatter.26
  3605.5 136.8 reduce-scatter.20
  3745.1 25.3 reduce-scatter.36
  3773.0 376.5 all-reduce.16
  4152.1 372.3 all-reduce.18
  4527.3 373.1 all-reduce.20
  4902.6 24.5 reduce-scatter.38
  4929.4 28.4 reduce-scatter.34
  4960.2 28.7 reduce-scatter.32
  4991.3 30.6 reduce-scatter.30
  5024.8 278.8 reduce-scatter.28
where the time goes:
time: 5330 us; the launch traced here: 5310 us
  waiting for transfers between devices  2690 us (50%)
  blocking collectives  1250 us (23%)
  local copies, waits for them, and re-layouts  676 us (13%)
  matrix products  427 us (8%)
  other arithmetic  203 us (4%)
    unnamed x32, waiting for transfers between devices  1180 us
    unnamed x1, blocking collectives  961 us
    all_gather x1, waiting for transfers between devices, fetch_modulation(): lax.all_gather(mod_part, 'seq', axis=2, tiled=True)  465 us
    reduce_scatter x4, waiting for transfers between devices, sum_rows(): total = lax.psum_scatter(joined, 'seq', scatter_dimension=1, tiled=True)  308 us
    reduce_scatter x1, waiting for transfers between devices, on_device(): lax.psum_scatter(mod_grad, 'batch', scatter_dimension=2, tiled=True)  280 us
    unnamed x314, local copies, waits for them, and re-layouts  213 us
    all_gather x1, waiting for transfers between devices, on_device(): all_keyval = lax.all_gather(joined_keyval, 'seq', axis=1, tiled=True)  133 us
    all_gather x1, waiting for transfers between devices, fetch_columns(): lax.all_gather(mod_weight, 'batch', axis=2, tiled=True)  129 us
  transfers between devices with their start and end apart: 32, of which 20 were waited for; matrix products, arithmetic and copies ran while one was open for 16% of the time, Pallas kernels for 0%

commit v1 on v0

--- a/solution.py
+++ b/solution.py
@@ -1,8 +1,12 @@
+import functools
 import math
 
 import jax
 import jax.numpy as jnp
+import numpy as np
 from jax import lax
+from jax.experimental import pallas as pl
+from jax.experimental.pallas import tpu as pltpu
 from jax.sharding import PartitionSpec as P
 
 HEADS = 24
@@ -115,7 +119,7 @@
     return lax.dynamic_slice_in_dim(values, seq_index * width, width, 1)
 
 
-def on_device(
+def general_layer(
     image_tokens,
     text_tokens,
     conditioning,
@@ -540,9 +544,720 @@
     )
 
 
+LOG2E = 1.4426950408889634
+DEAD = -1e30
+BF16 = jnp.bfloat16
+F32 = jnp.float32
+
+
+def dot_nt(a, b):
+    return lax.dot_general(a, b, (((1,), (1,)), ((), ())), preferred_element_type=F32)
+
+
+def dot_nn(a, b):
+    return lax.dot_general(a, b, (((1,), (0,)), ((), ())), preferred_element_type=F32)
+
+
+def dot_tn(a, b):
+    return lax.dot_general(a, b, (((0,), (0,)), ((), ())), preferred_element_type=F32)
+
+
+def attention_kernel(
+    query_rows, scale, head, bias_ref, floor_ref, qi, qt, ki, kt, vi, vt, oi, ot, keys, values
+):
+    image_rows = qi.shape[0]
+    keys[:image_rows] = ki[...]
+    keys[image_rows:] = kt[...]
+    values[:image_rows] = vi[...]
+    values[image_rows:] = vt[...]
+    bias = bias_ref[...]
+    floor = floor_ref[0, 0]
+    spans = [(qi, oi, start, query_rows) for start in range(0, image_rows, query_rows)]
+    spans.append((qt, ot, 0, qt.shape[0]))
+    for source, target, start, size in spans:
+        sides = []
+        for side in range(2):
+            lanes = slice(side * head, (side + 1) * head)
+            scores = dot_nt(source[start : start + size, lanes], keys[:, lanes]) * scale + bias
+            row_max = jnp.maximum(jnp.max(scores, axis=1, keepdims=True), floor)
+            exps = jnp.exp2(scores - row_max)
+            total = jnp.maximum(jnp.sum(exps, axis=1, keepdims=True), 1.0)
+            probs = (exps * (1.0 / total)).astype(BF16)
+            sides.append(dot_nn(probs, values[:, lanes]))
+        target[start : start + size, :] = jnp.concatenate(sides, axis=1).astype(BF16)
+
+
+def pair_block(rows, lanes, pairs, part):
+    return pl.BlockSpec((rows, lanes), lambda pair: (0, part * pairs + pair))
+
+
+def attention(qkv_image, qkv_text, key_bias, floor, head):
+    image_rows, width = qkv_image.shape
+    text_rows = qkv_text.shape[0]
+    rows = image_rows + text_rows
+    lanes = 2 * head
+    pairs = width // (3 * lanes)
+    columns = [
+        pair_block(count, lanes, pairs, part)
+        for part in range(3)
+        for count in (image_rows, text_rows)
+    ]
+    return pl.pallas_call(
+        functools.partial(attention_kernel, 256, LOG2E / math.sqrt(head), head),
+        grid=(pairs,),
+        in_specs=[
+            pl.BlockSpec((1, rows), lambda pair: (0, 0)),
+            pl.BlockSpec(memory_space=pltpu.SMEM),
+            *columns,
+        ],
+        out_specs=[columns[0], columns[1]],
+        out_shape=[
+            jax.ShapeDtypeStruct((image_rows, width // 3), BF16),
+            jax.ShapeDtypeStruct((text_rows, width // 3), BF16),
+        ],
+        scratch_shapes=[pltpu.VMEM((rows, lanes), BF16), pltpu.VMEM((rows, lanes), BF16)],
+        compiler_params=pltpu.CompilerParams(vmem_limit_bytes=48 << 20),
+        cost_estimate=pl.CostEstimate(
+            flops=16 * rows * rows * width // 3,
+            bytes_accessed=8 * rows * width // 3,
+            transcendentals=rows * rows * width // (3 * head),
+        ),
+        name="attention",
+    )(key_bias[None, :], floor, qkv_image, qkv_text, qkv_image, qkv_text, qkv_image, qkv_text)
+
+
+def attention_back_kernel(
+    query_rows, scale, factor, head, pairs,
+    bias_ref, floor_ref, qi, qt, ki, kt, vi, vt, gi, gt, oi, ot, keys, values, key_sum, value_sum,
+):
+    pair = pl.program_id(0)
+    image_rows = qi.shape[0]
+    width = 2 * head
+    keys[:image_rows] = ki[...]
+    keys[image_rows:] = kt[...]
+    values[:image_rows] = vi[...]
+    values[image_rows:] = vt[...]
+    key_sum[...] = jnp.zeros_like(key_sum)
+    value_sum[...] = jnp.zeros_like(value_sum)
+    bias = bias_ref[...]
+    floor = floor_ref[0, 0]
+    spans = [(qi, gi, oi, start, query_rows) for start in range(0, image_rows, query_rows)]
+    spans.append((qt, gt, ot, 0, qt.shape[0]))
+    query_lanes = pl.ds(pl.multiple_of(pair * width, width), width)
+    key_lanes = pl.ds(pl.multiple_of((pairs + pair) * width, width), width)
+    value_lanes = pl.ds(pl.multiple_of((2 * pairs + pair) * width, width), width)
+    for source, grads, target, start, size in spans:
+        wide_bias = jnp.concatenate([bias] * -(-size // 128), axis=1)[:, :size]
+        dq, dk, dv = ([], [], [])
+        for side in range(2):
+            lanes = slice(side * head, (side + 1) * head)
+            query = source[start : start + size, lanes]
+            grad = grads[start : start + size, lanes]
+            scores = dot_nt(keys[:, lanes], query) * scale + wide_bias
+            top = jnp.maximum(jnp.max(scores, axis=0, keepdims=True), floor)
+            exps = jnp.exp2(scores - top)
+            total = jnp.maximum(jnp.sum(exps, axis=0, keepdims=True), 1.0)
+            probs = exps * (1.0 / total)
+            prob_grad = dot_nt(values[:, lanes], grad)
+            weighted = probs * prob_grad
+            inner = jnp.sum(weighted, axis=0, keepdims=True)
+            score_grad = (weighted - probs * inner).astype(BF16)
+            dv.append(dot_nn(probs.astype(BF16), grad))
+            dk.append(dot_nn(score_grad, query))
+            dq.append(dot_tn(score_grad, keys[:, lanes]))
+        key_sum[...] += jnp.concatenate(dk, axis=1)
+        value_sum[...] += jnp.concatenate(dv, axis=1)
+        target[start : start + size, query_lanes] = (
+            jnp.concatenate(dq, axis=1) * factor
+        ).astype(BF16)
+    oi[:, key_lanes] = (key_sum[:image_rows] * factor).astype(BF16)
+    ot[:, key_lanes] = (key_sum[image_rows:] * factor).astype(BF16)
+    oi[:, value_lanes] = value_sum[:image_rows].astype(BF16)
+    ot[:, value_lanes] = value_sum[image_rows:].astype(BF16)
+
+
+def attention_back(qkv_image, qkv_text, grad_image, grad_text, key_bias, floor, head):
+    image_rows, width = qkv_image.shape
+    text_rows = qkv_text.shape[0]
+    rows = image_rows + text_rows
+    lanes = 2 * head
+    pairs = width // (3 * lanes)
+    columns = [
+        pair_block(count, lanes, pairs, part)
+        for part in range(3)
+        for count in (image_rows, text_rows)
+    ]
+    return pl.pallas_call(
+        functools.partial(
+            attention_back_kernel, 256, LOG2E / math.sqrt(head), 1.0 / math.sqrt(head), head, pairs
+        ),
+        grid=(pairs,),
+        in_specs=[
+            pl.BlockSpec((rows, 128), lambda pair: (0, 0)),
+            pl.BlockSpec(memory_space=pltpu.SMEM),
+            *columns,
+            columns[0],
+            columns[1],
+        ],
+        out_specs=[
+            pl.BlockSpec((image_rows, width), lambda pair: (0, 0)),
+            pl.BlockSpec((text_rows, width), lambda pair: (0, 0)),
+        ],
+        out_shape=[
+            jax.ShapeDtypeStruct((image_rows, width), BF16),
+            jax.ShapeDtypeStruct((text_rows, width), BF16),
+        ],
+        scratch_shapes=[
+            pltpu.VMEM((rows, lanes), BF16),
+            pltpu.VMEM((rows, lanes), BF16),
+            pltpu.VMEM((rows, lanes), F32),
+            pltpu.VMEM((rows, lanes), F32),
+        ],
+        compiler_params=pltpu.CompilerParams(vmem_limit_bytes=48 << 20),
+        cost_estimate=pl.CostEstimate(
+            flops=40 * rows * rows * width // 3,
+            bytes_accessed=16 * rows * width // 3,
+            transcendentals=rows * rows * width // (3 * head),
+        ),
+        name="attention_back",
+    )(
+        jnp.broadcast_to(key_bias[:, None], (rows, 128)),
+        floor,
+        qkv_image, qkv_text, qkv_image, qkv_text, qkv_image, qkv_text,
+        grad_image, grad_text,
+    )
+
+
+def flip(values, bit):
+    return lax.ppermute(values, "seq", [(i, i ^ bit) for i in range(4)])
+
+
+def gather_blocks(own):
+    half = own.shape[1] // 2
+    near_x = flip(own, 1)
+    near_y = flip(own, 2)
+    far_a = flip(near_x[:, :half], 2)
+    far_b = flip(near_y[:, half:], 1)
+    return (own, near_x, near_y, jnp.concatenate([far_a, far_b], axis=1))
+
+
+def add_low(a, b):
+    return (a.astype(F32) + b.astype(F32)).astype(BF16)
+
+
+def scatter_blocks(blocks):
+    own, near_x, near_y, far = blocks
+    half = own.shape[1] // 2
+    for_y = flip(far[:, :half], 1)
+    for_x = flip(far[:, half:], 2)
+    from_x_a = flip(near_x[:, :half], 1)
+    from_y_b = flip(near_y[:, half:], 2)
+    from_x_b = flip(add_low(near_x[:, half:], for_x), 1)
+    from_y_a = flip(add_low(near_y[:, :half], for_y), 2)
+    return (
+        own.astype(F32)
+        + jnp.concatenate([from_x_a, from_x_b], axis=1).astype(F32)
+        + jnp.concatenate([from_y_a, from_y_b], axis=1).astype(F32)
+    )
+
+
+def join_rows(blocks, image_count):
+    return (
+        jnp.concatenate([block[:image_count] for block in blocks], axis=0),
+        jnp.concatenate([block[image_count:] for block in blocks], axis=0),
+    )
+
+
+def split_rows(image, text, image_count, text_count):
+    return [
+        jnp.concatenate(
+            [
+                image[r * image_count : (r + 1) * image_count],
+                text[r * text_count : (r + 1) * text_count],
+            ],
+            axis=0,
+        )
+        for r in range(4)
+    ]
+
+
+def match_units(batch_devices, seq_devices, per_device, group_units):
+    devices = batch_devices * seq_devices
+    total = devices * per_device
+    part_units = total // 3
+    sources, targets = ([], [])
+    for seq_at in range(seq_devices):
+        listed = [
+            part * part_units + seq_at * group_units + k
+            for part in range(3)
+            for k in range(group_units)
+        ]
+        for place, unit in enumerate(listed):
+            sources.append((unit // per_device, unit % per_device))
+            targets.append(
+                ((place // per_device) * seq_devices + seq_at, place % per_device)
+            )
+    edges = list(zip(sources, targets))
+    rounds = []
+    left = list(range(total))
+    for _ in range(per_device):
+        by_source = {}
+        for e in left:
+            by_source.setdefault(edges[e][0][0], []).append(e)
+        taken = {}
+
+        def place_edge(device, seen):
+            for e in by_source[device]:
+                target = edges[e][1][0]
+                if target in seen:
+                    continue
+                seen.add(target)
+                if target not in taken or place_edge(edges[taken[target]][0][0], seen):
+                    taken[target] = e
+                    return True
+            return False
+
+        for device in range(devices):
+            place_edge(device, set())
+        chosen = sorted(taken.values())
+        rounds.append(chosen)
+        left = [e for e in left if e not in chosen]
+    send = np.zeros((per_device, devices), np.int32)
+    land = np.zeros((per_device, devices), np.int32)
+    perms = []
+    for k, chosen in enumerate(rounds):
+        pairs = []
+        for e in chosen:
+            (source, source_slot), (target, target_slot) = edges[e]
+            pairs.append((source, target))
+            send[k, source] = source_slot
+            land[k, target] = target_slot
+        perms.append(sorted(pairs))
+    return perms, send, land
+
+
+def move_units(units, perms, take, put, place):
+    arrived = jnp.zeros_like(units)
+    for k, pairs in enumerate(perms):
+        slot = jnp.asarray(take[k])[place]
+        moved = lax.ppermute(
+            lax.dynamic_index_in_dim(units, slot, 0, keepdims=True), ("batch", "seq"), pairs
+        )
+        arrived = lax.dynamic_update_slice_in_dim(arrived, moved, jnp.asarray(put[k])[place], 0)
+    return arrived
+
+
+def gather_batch(values):
+    return lax.all_gather(values, "batch", axis=0)
+
+
+def scatter_batch(values):
+    return lax.psum_scatter(values, "batch", scatter_dimension=0)
+
+
+def swap(values, axis):
+    return lax.all_to_all(values, axis, 0, 0, tiled=True)
+
+
+def norm_stats(values):
+    mean = jnp.mean(values, axis=-1, keepdims=True)
+    centered = values - mean
+    variance = jnp.mean(centered * centered, axis=-1, keepdims=True)
+    return mean, lax.rsqrt(variance + NORM_EPSILON)
+
+
+def norm_back(norm, inverse, grad, scale):
+    scaled = grad * (1.0 + scale)
+    return inverse * (
+        scaled
+        - jnp.mean(scaled, axis=-1, keepdims=True)
+        - norm * jnp.mean(scaled * norm, axis=-1, keepdims=True)
+    )
+
+
+def swift_layer(
+    image_tokens,
+    text_tokens,
+    conditioning,
+    key_mask,
+    mod_weight,
+    mod_bias,
+    qkv_weight,
+    qv_bias,
+    out_weight,
+    out_bias,
+    up_weight,
+    up_bias,
+    down_weight,
+    down_bias,
+    image_cotangent,
+    text_cotangent,
+):
+    S = lax.axis_size("seq")
+    B = lax.axis_size("batch")
+    seq_index = lax.axis_index("seq")
+    place = lax.axis_index(("batch", "seq"))
+    L, image_count, D = image_tokens.shape
+    text_count = text_tokens.shape[1]
+    head = D // HEADS
+    own_width = D // S
+    spans = (slice(0, image_count), slice(image_count, image_count + text_count))
+
+    bias_widths = [array.shape[1] for array in (qv_bias, out_bias, up_bias, down_bias)]
+    bias_ends = np.cumsum(bias_widths)
+    own_biases = jnp.concatenate([qv_bias, out_bias, up_bias, down_bias], axis=1)
+    near = gather_batch(jnp.concatenate([conditioning, own_biases], axis=1))
+    cond_all = near[:, :, :D].reshape(B * L, D)
+    column_biases = near[:, :, D:].astype(F32)
+    smooth_all = jax.nn.silu(cond_all.astype(F32)).astype(BF16)
+    mod_own = (
+        jnp.einsum("sd,tdf->tsf", smooth_all, mod_weight, preferred_element_type=F32)
+        + mod_bias.astype(F32)[:, None, :]
+    )
+    mod_width = mod_own.shape[2]
+    mod_sent = mod_own.reshape(2, B, L, mod_width).transpose(1, 0, 2, 3)
+    mod_came = swap(mod_sent, "batch")
+    small = jnp.concatenate(
+        [mod_came.reshape(B, 2 * L * mod_width), column_biases.reshape(B, -1)], axis=1
+    )
+    small_all = lax.all_gather(small, "seq")
+    modulation = (
+        small_all[:, :, : 2 * L * mod_width]
+        .reshape(S, B, 2, L, mod_width)
+        .transpose(2, 3, 1, 0, 4)
+        .reshape(2, L, 6, D)
+    )
+    bias_all = (
+        small_all[:, :, 2 * L * mod_width :].reshape(S, B, 2, -1).transpose(2, 1, 0, 3)
+    )
+    qv_full = bias_all[..., : bias_ends[0]].reshape(2, 2 * D)
+    out_bias_full = bias_all[..., bias_ends[0] : bias_ends[1]].reshape(2, D)
+    down_bias_full = bias_all[..., bias_ends[2] :].reshape(2, D)
+    up_bias_part = (
+        column_biases[:, :, bias_ends[1] : bias_ends[2]].transpose(1, 0, 2).reshape(2, -1)
+    )
+    first_feature = seq_index * own_width
+    qkv_bias = jnp.concatenate(
+        [
+            lax.dynamic_slice_in_dim(qv_full, first_feature, own_width, 1),
+            jnp.zeros((2, own_width), F32),
+            lax.dynamic_slice_in_dim(qv_full, D + first_feature, own_width, 1),
+        ],
+        axis=1,
+    )
+
+    unit = math.gcd(qkv_weight.shape[2], own_width)
+    per_device = qkv_weight.shape[2] // unit
+    perms, send, land = match_units(B, S, per_device, own_width // unit)
+    back_perms = [[(target, source) for source, target in pairs] for pairs in perms]
+    qkv_units = jnp.swapaxes(qkv_weight, 1, 2).reshape(2, per_device, unit, D).swapaxes(0, 1)
+    qkv_mine = move_units(qkv_units, perms, send, land, place)
+    out_units = jnp.swapaxes(out_weight, 1, 2).reshape(2, -1, S, own_width).transpose(2, 0, 1, 3)
+    out_mine = swap(out_units, "seq")
+    out_columns = out_mine.shape[2]
+    heads_all = gather_batch(
+        jnp.concatenate([qkv_mine.reshape(-1, D), out_mine.reshape(-1, D)], axis=0)
+    )
+    qkv_rows = 2 * per_device * unit
+    qkv_all = heads_all[:, :qkv_rows].reshape(B, per_device, 2, unit, D)
+    out_all = heads_all[:, qkv_rows:].reshape(B, S, 2, out_columns, own_width)
+    hidden_all = gather_batch(
+        jnp.stack([jnp.swapaxes(up_weight, 1, 2), jnp.swapaxes(down_weight, 1, 2)])
+    )
+    qkv_part = [qkv_all[:, :, t].reshape(-1, D) for t in range(2)]
+    out_part = [out_all[:, :, t].reshape(D, own_width) for t in range(2)]
+    up_part = [hidden_all[:, 0, t].reshape(-1, D) for t in range(2)]
+    down_part = [hidden_all[:, 1, t].reshape(-1, D) for t in range(2)]
+    hidden_columns = up_weight.shape[2]
+
+    order = jnp.bitwise_xor(seq_index, jnp.arange(S))
+    image_keys = jnp.take(
+        key_mask[:, : S * image_count].reshape(L, S, image_count), order, axis=1
+    ).reshape(L, -1)
+    text_keys = jnp.take(
+        key_mask[:, S * image_count :].reshape(L, S, text_count), order, axis=1
+    ).reshape(L, -1)
+    live = jnp.concatenate([image_keys, text_keys], axis=1) > 0
+    key_bias = jnp.where(live, 0.0, DEAD).astype(F32)
+    floors = jnp.where(jnp.all(live, axis=1), -3e38, FLOOR_SCORE * LOG2E).astype(F32)
+    floors = floors.reshape(L, 1, 1)
+
+    token_blocks, grad_blocks = ([], [])
+    for s in range(L):
+        token_blocks.append(
+            gather_blocks(jnp.concatenate([image_tokens[s], text_tokens[s]], axis=0))
+        )
+    for s in range(L):
+        grad_blocks.append(
+            gather_blocks(jnp.concatenate([image_cotangent[s], text_cotangent[s]], axis=0))
+        )
+    tokens_all = [join_rows(blocks, image_count) for blocks in token_blocks]
+    grads_all = [join_rows(blocks, image_count) for blocks in grad_blocks]
+    own_tokens = [[image_tokens[s].astype(F32), text_tokens[s].astype(F32)] for s in range(L)]
+    own_grads = [
+        [image_cotangent[s].astype(F32), text_cotangent[s].astype(F32)] for s in range(L)
+    ]
+
+    first_norms, first_stats, qkvs, attended, projections, middles, middle_stats = (
+        [], [], [], [], [], [], [],
+    )
+    second_all = []
+    for s in range(L):
+        norms, stats, rows = ([], [], [])
+        for t in range(2):
+            pieces = modulation[t, s]
+            values = tokens_all[s][t].astype(F32)
+            mean, inverse = norm_stats(values)
+            norm = (
+                (values - mean) * inverse * (1.0 + pieces[1][None, :]) + pieces[0][None, :]
+            ).astype(BF16)
+            rows.append((dot_nt(norm, qkv_part[t]) + qkv_bias[t][None, :]).astype(BF16))
+            norms.append(norm)
+            stats.append((mean, inverse))
+        first_norms.append(norms)
+        first_stats.append(stats)
+        qkvs.append(rows)
+        attended.append(attention(rows[0], rows[1], key_bias[s], floors[s], head))
+    for s in range(L):
+        partial = [dot_nt(attended[s][t], out_part[t]).astype(BF16) for t in range(2)]
+        summed = scatter_blocks(split_rows(partial[0], partial[1], image_count, text_count))
+        seconds = []
+        kept_projection, kept_middle, kept_stats = ([], [], [])
+        for t in range(2):
+            pieces = modulation[t, s]
+            projection = summed[spans[t]] + out_bias_full[t][None, :]
+            middle = own_tokens[s][t] + pieces[2][None, :] * projection
+            mean, inverse = norm_stats(middle)
+            second = (middle - mean) * inverse * (1.0 + pieces[4][None, :]) + pieces[3][None, :]
+            seconds.append(second.astype(BF16))
+            kept_projection.append(projection)
+            kept_middle.append(middle)
+            kept_stats.append((mean, inverse))
+        projections.append(kept_projection)
+        middles.append(kept_middle)
+        middle_stats.append(kept_stats)
+        blocks = gather_blocks(jnp.concatenate(seconds, axis=0))
+        second_all.append(join_rows(blocks, image_count))
+    hidden_acts, hidden_pres, mlp_grads, pre_grads = ([], [], [], [])
+    norm2_sums, mlp_sums = ([], [])
+    for s in range(L):
+        acts, pres, partial, grads, pre_low, back = ([], [], [], [], [], [])
+        for t in range(2):
+            pre = dot_nt(second_all[s][t], up_part[t]) + up_bias_part[t][None, :]
+            act = gelu_tanh(pre).astype(BF16)
+            acts.append(act)
+            pres.append(pre)
+            grad = (modulation[t, s][5][None, :] * grads_all[s][t].astype(F32)).astype(BF16)
+            act_grad = dot_nt(grad, down_part[t])
+            pre_grad = jax.vjp(gelu_tanh, pre)[1](act_grad)[0].astype(BF16)
+            grads.append(grad)
+            pre_low.append(pre_grad)
+            back.append(dot_nn(pre_grad, up_part[t]).astype(BF16))
+            partial.append(dot_nn(act, down_part[t]).astype(BF16))
+        hidden_acts.append(acts)
+        hidden_pres.append(pres)
+        mlp_grads.append(grads)
+        pre_grads.append(pre_low)
+        norm2_sums.append(
+            scatter_blocks(split_rows(back[0], back[1], image_count, text_count))
+        )
+        mlp_sums.append(
+            scatter_blocks(split_rows(partial[0], partial[1], image_count, text_count))
+        )
+
+    def both(left, right, t):
+        total = dot_tn(left[0][t], right[0][t])
+        for s in range(1, L):
+            total = total + dot_tn(left[s][t], right[s][t])
+        return total.astype(BF16)
+
+    up_sum = [both(pre_grads, second_all, t) for t in range(2)]
+    down_sum = [both(hidden_acts, mlp_grads, t) for t in range(2)]
+    hidden_grads = scatter_batch(
+        jnp.stack(
+            [
+                jnp.stack([value.reshape(B, hidden_columns, D) for value in values], axis=1)
+                for values in (up_sum, down_sum)
+            ],
+            axis=1,
+        )
+    )
+    up_bias_sum = jnp.stack(
+        [
+            sum(jnp.sum(pre_grads[s][t].astype(F32), axis=0) for s in range(L))
+            for t in range(2)
+        ]
+    )
+
+    results = [[], []]
+    mod_grads = [[[None] * 6 for _ in range(L)] for _ in range(2)]
+    middle_grads, proj_all = ([], [])
+    out_bias_sum = [0.0, 0.0]
+    down_bias_sum = [0.0, 0.0]
+    for s in range(L):
+        kept, lows = ([], [])
+        for t in range(2):
+            pieces = modulation[t, s]
+            grad = own_grads[s][t]
+            mlp_value = mlp_sums[s][spans[t]] + down_bias_full[t][None, :]
+            results[t].append(
+                (middles[s][t] + pieces[5][None, :] * mlp_value).astype(BF16)
+            )
+            mod_grads[t][s][5] = jnp.sum(grad * mlp_value, axis=0)
+            own_low = (pieces[5][None, :] * grad).astype(BF16)
+            down_bias_sum[t] = down_bias_sum[t] + jnp.sum(own_low.astype(F32), axis=0)
+            norm_grad = norm2_sums[s][spans[t]]
+            mean, inverse = middle_stats[s][t]
+            norm = (middles[s][t] - mean) * inverse
+            mod_grads[t][s][3] = jnp.sum(norm_grad, axis=0)
+            mod_grads[t][s][4] = jnp.sum(norm_grad * norm, axis=0)
+            middle_grad = grad + norm_back(norm, inverse, norm_grad, pieces[4][None, :])
+            mod_grads[t][s][2] = jnp.sum(middle_grad * projections[s][t], axis=0)
+            low = (pieces[2][None, :] * middle_grad).astype(BF16)
+            out_bias_sum[t] = out_bias_sum[t] + jnp.sum(low.astype(F32), axis=0)
+            kept.append(middle_grad)
+            lows.append(low)
+        middle_grads.append(kept)
+        proj_all.append(join_rows(gather_blocks(jnp.concatenate(lows, axis=0)), image_count))
+
+    qkv_grads, norm1_sums = ([], [])
+    for s in range(L):
+        attended_grad = [dot_nn(proj_all[s][t], out_part[t]).astype(BF16) for t in range(2)]
+        grads = attention_back(
+            qkvs[s][0], qkvs[s][1], attended_grad[0], attended_grad[1], key_bias[s], floors[s], head
+        )
+        qkv_grads.append(grads)
+        back = [dot_nn(grads[t], qkv_part[t]).astype(BF16) for t in range(2)]
+        for t in range(2):
+            wide = back[t].astype(F32)
+            mean, inverse = first_stats[s][t]
+            norm = (tokens_all[s][t].astype(F32) - mean) * inverse
+            mod_grads[t][s][0] = jnp.sum(wide, axis=0)
+            mod_grads[t][s][1] = jnp.sum(wide * norm, axis=0)
+        norm1_sums.append(
+            scatter_blocks(split_rows(back[0], back[1], image_count, text_count))
+        )
+    out_sum = [both(proj_all, attended, t) for t in range(2)]
+    qkv_sum = [both(qkv_grads, first_norms, t) for t in range(2)]
+    qkv_sent = jnp.stack(
+        [value.reshape(B, per_device, unit, D) for value in qkv_sum], axis=2
+    ).reshape(B, qkv_rows, D)
+    out_sent = jnp.stack(
+        [value.reshape(B, S, out_columns, own_width) for value in out_sum], axis=2
+    ).reshape(B, -1, D)
+    head_grads = scatter_batch(jnp.concatenate([qkv_sent, out_sent], axis=1))
+    qkv_home = move_units(
+        head_grads[:qkv_rows].reshape(per_device, 2, unit, D), back_perms, land, send, place
+    )
+    out_home = swap(head_grads[qkv_rows:].reshape(S, 2, out_columns, own_width), "seq")
+    qkv_weight_grad = qkv_home.swapaxes(0, 1).reshape(2, -1, D).swapaxes(1, 2).astype(F32)
+    out_weight_grad = (
+        out_home.transpose(1, 2, 0, 3).reshape(2, out_columns, D).swapaxes(1, 2).astype(F32)
+    )
+    up_weight_grad = hidden_grads[0].swapaxes(1, 2).astype(F32)
+    down_weight_grad = hidden_grads[1].swapaxes(1, 2).astype(F32)
+
+    input_grads = [[], []]
+    for s in range(L):
+        for t in range(2):
+            mean, inverse = norm_stats(own_tokens[s][t])
+            norm = (own_tokens[s][t] - mean) * inverse
+            input_grads[t].append(
+                middle_grads[s][t]
+                + norm_back(
+                    norm, inverse, norm1_sums[s][spans[t]], modulation[t, s][1][None, :]
+                )
+            )
+
+    mod_rows = jnp.stack(
+        [jnp.stack([jnp.concatenate(mod_grads[t][s]) for s in range(L)]) for t in range(2)]
+    )
+    mod_rows = mod_rows.reshape(2, L, B, S, mod_width).transpose(3, 2, 0, 1, 4)
+    qv_bias_sum = jnp.zeros((2, 2 * D), F32)
+    for part, column in ((0, 0), (1, 2 * own_width)):
+        sums = jnp.stack(
+            [
+                sum(
+                    jnp.sum(
+                        qkv_grads[s][t][:, column : column + own_width].astype(F32), axis=0
+                    )
+                    for s in range(L)
+                )
+                for t in range(2)
+            ]
+        )
+        qv_bias_sum = lax.dynamic_update_slice_in_dim(
+            qv_bias_sum, sums, part * D + first_feature, 1
+        )
+    up_bias_rows = lax.dynamic_update_slice_in_dim(
+        jnp.zeros((2, B, S, hidden_columns), F32),
+        up_bias_sum.reshape(2, B, 1, hidden_columns),
+        seq_index,
+        2,
+    )
+    bias_rows = jnp.concatenate(
+        [
+            qv_bias_sum.reshape(2, B, S, -1),
+            jnp.stack(out_bias_sum).reshape(2, B, S, -1),
+            up_bias_rows,
+            jnp.stack(down_bias_sum).reshape(2, B, S, -1),
+        ],
+        axis=3,
+    ).transpose(2, 1, 0, 3)
+    packed = jnp.concatenate(
+        [mod_rows.reshape(S, B, -1), bias_rows.reshape(S, B, -1)], axis=2
+    )
+    packed = jnp.sum(swap(packed, "seq"), axis=0)
+    packed = swap(packed, "batch")
+    mod_mine = (
+        packed[:, : 2 * L * mod_width]
+        .reshape(B, 2, L, mod_width)
+        .transpose(1, 0, 2, 3)
+        .reshape(2, B * L, mod_width)
+        .astype(BF16)
+    )
+    bias_mine = jnp.sum(packed[:, 2 * L * mod_width :], axis=0).reshape(2, -1)
+    qv_bias_grad, out_bias_grad, up_bias_grad, down_bias_grad = jnp.split(
+        bias_mine, bias_ends[:3], axis=1
+    )
+    mod_weight_grad = jnp.einsum(
+        "sd,tsf->tdf", smooth_all, mod_mine, preferred_element_type=F32
+    )
+    mod_bias_grad = jnp.sum(mod_mine.astype(F32), axis=1)
+    smooth_part = jnp.einsum("tsf,tdf->sd", mod_mine, mod_weight, preferred_element_type=F32)
+    smooth_grad = jnp.sum(swap(smooth_part.reshape(B, L, D), "batch"), axis=0)
+    smooth_grad = smooth_grad + flip(smooth_grad, 1)
+    smooth_grad = smooth_grad + flip(smooth_grad, 2)
+    cond_grad = jax.vjp(jax.nn.silu, conditioning.astype(F32))[1](smooth_grad)[0]
+    return (
+        jnp.stack(results[0]),
+        jnp.stack(results[1]),
+        jnp.stack(input_grads[0]),
+        jnp.stack(input_grads[1]),
+        cond_grad,
+        mod_weight_grad,
+        mod_bias_grad,
+        qkv_weight_grad,
+        qv_bias_grad,
+        out_weight_grad,
+        out_bias_grad,
+        up_weight_grad,
+        up_bias_grad,
+        down_weight_grad,
+        down_bias_grad,
+    )
+
+
+def choose_layer(mesh):
+    if mesh.shape["seq"] == 4 and HEADS % 8 == 0:
+        return swift_layer
+    return general_layer
+
+
 def solution(mesh):
+    layer = choose_layer(mesh)
     return jax.shard_map(
-        on_device,
+        layer,
         mesh=mesh,
         in_specs=(
             P("batch", "seq", None),

time: 5330 us -> 1160 us (0.22)
  the two profiles are of different devices: /device:TPU:16 before, /device:TPU:0 now
where the time goes in v1:
time: 1160 us; the launch traced here: 1150 us
  waiting for transfers between devices  263 us (23%)
  matrix products  222 us (19%)
  local copies, waits for them, and re-layouts  189 us (16%)
  other arithmetic  153 us (13%)
  Pallas kernels  141 us (12%)
  starting transfers between devices  124 us (11%)
  blocking collectives  32.9 us (3%)
  between operations  25.8 us (2%)
    ppermute x82, waiting for transfers between devices, flip(): return lax.ppermute(values, 'seq', [(i, i ^ bit) for i in range(4)])  198 us
    pallas_call x2, Pallas kernels, attention_back(): pl.pallas_call(functools.partial(attention_back_kernel, 256, LOG2E / math...  93.2 us
    ppermute x82, starting transfers between devices, flip(): return lax.ppermute(values, 'seq', [(i, i ^ bit) for i in range(4)])  86.5 us
    dot_general x16, matrix products, dot_tn(): lax.dot_general(a, b, (((0,), (0,)), ((), ())), preferred_element_type=F32)  81.3 us
    dot_general x16, matrix products, dot_nt(): lax.dot_general(a, b, (((1,), (1,)), ((), ())), preferred_element_type=F32)  70.4 us
    dot_general x16, matrix products, dot_nn(): lax.dot_general(a, b, (((1,), (0,)), ((), ())), preferred_element_type=F32)  64.9 us
    reduce_scatter x2, waiting for transfers between devices, scatter_batch(): return lax.psum_scatter(values, 'batch', scatter_dimension=0)  58.3 us
    pallas_call x2, Pallas kernels, attention(): pl.pallas_call(functools.partial(attention_kernel, 256, LOG2E / math.sqrt...  48.2 us
  transfers between devices with their start and end apart: 98, of which 40 were waited for; matrix products, arithmetic and copies ran while one was open for 37% of the time, Pallas kernels for 4%

profile of v1, /device:TPU:0, one launch (start us, length us, event | category | flops | bytes accessed | tf_op | source)
XLA Modules:
  0.0 1151.1 jit_solution(1031046514662359291)
XLA Ops:
  40.1 7.1 collective-permute-start.24
  52.0 15.1 %all-gather.4 = bf16[8,2,1920]{2,1,0:T(2,128)(2,1)S(1)} all-gather(bf16[1,2,1920]{2,1,0:T(2,128)(2,1)S(1)} %bitcast.386), channel_id=2, replica_groups=mesh['batch'=8,'seq'=4] {'batch'}, dimensions={0}, use_global_device_ids=true | all-gather | bytes 69120 | tf_op jit(solution)/shard_map/all_gather | solution.py:851
  96.0 17.9 %all-gather.1 = f32[32,1920]{1,0:T(8,128)S(1)} all-gather(f32[8,1920]{1,0:T(8,128)S(1)} %pad_maximum_fusion.84), channel_id=3, replica_groups=mesh['batch'=8,'seq'=4] {'seq'}, dimensions={0}, use_global_device_ids=true | all-gather | bytes 307200 | tf_op jit(solution)/shard_map/all_gather | solution.py:923
  190.4 7.5 add_convert_fusion.3.qi.ki.vi
  197.9 24.2 %attention.2 = (bf16[1024,384]{1,0:T(8,128)(2,1)S(1)}, bf16[160,384]{1,0:T(8,128)(2,1)S(1)}) custom-call(f32[1,1184]{1,0:T(1,128)S(1)} %get-tuple-element.297.bias_ref, f32[1,1]{1,0:T(1,128)} %bitcast.12.floor_ref, bf16[1024,1152]{1,0:T(8,128)(2,1)S(1)} %add_convert_fusion.3.qi.ki.vi, bf16[160,1152]{1,0:T(8,128)(2,1)S(1)} %fusion.34.qt.kt.vt, ...), custom_call_target="tpu_custom_call" | custom-call | flops 8613003264 | bytes 3637248 | tf_op jit(solution)/shard_map/attention/pallas_call | solution.py:605
  231.5 7.6 add_convert_fusion.2.qi.ki.vi
  239.1 24.1 %attention.3 = (bf16[1024,384]{1,0:T(8,128)(2,1)S(1)}, bf16[160,384]{1,0:T(8,128)(2,1)S(1)}) custom-call(f32[1,1184]{1,0:T(1,128)S(1)} %get-tuple-element.296.bias_ref, f32[1,1]{1,0:T(1,128)} %bitcast.45.floor_ref, bf16[1024,1152]{1,0:T(8,128)(2,1)S(1)} %add_convert_fusion.2.qi.ki.vi, bf16[160,1152]{1,0:T(8,128)(2,1)S(1)} %fusion.35.qt.kt.vt, ...), custom_call_target="tpu_custom_call" | custom-call | flops 8613003264 | bytes 3637248 | tf_op jit(solution)/shard_map/attention/pallas_call | solution.py:605
  315.9 7.7 collective-permute-done.31
  353.9 14.8 %collective-permute-done.33 = bf16[296,1536]{1,0:T(8,128)(2,1)S(1)} collective-permute-done((bf16[296,1536]{1,0:T(8,128)(2,1)}, bf16[296,1536]{1,0:T(8,128)(2,1)S(1)}, u32[]{:S(2)}, u32[]{:S(2)}) %collective-permute-start.33) | collective-permute-done | bytes 909344 | tf_op jit(solution)/shard_map/ppermute | solution.py:732
  391.1 10.5 collective-permute-done.65
  424.2 7.7 fusion.219
  469.2 14.5 %convert_reduce_fusion.5 = (f32[1536]{0:T(1024)}, bf16[1024,1536]{1,0:T(8,128)(2,1)}) fusion(f32[1024,1536]{1,0:T(8,128)} %copy-done.372, f32[1536]{0:T(1024)S(1)} %add.919, bf16[1536,1536]{1,0:T(8,128)(2,1)S(1)} %bitcast.340, bf16[256,1536]{1,0:T(8,128)(2,1)S(1)} %copy-done.177, bf16[256,1536]{1,0:T(8,128)(2,1)S(1)} %copy-done.172, ...), kind=kOutput, calls=%fused_computation.58 | convolution fusion | flops 4883741184 | bytes 17319936 | tf_op jit(solution)/shard_map/dot_general | solution.py:554
  483.7 7.1 convolution_convert_fusion.1
  504.0 14.0 %convert_reduce_fusion.4 = (f32[1536]{0:T(1024)}, bf16[1024,1536]{1,0:T(8,128)(2,1)}) fusion(f32[1024,1536]{1,0:T(8,128)} %copy-done.373, f32[1536]{0:T(1024)S(1)} %add.919, bf16[1536,1536]{1,0:T(8,128)(2,1)S(1)} %bitcast.342, bf16[256,1536]{1,0:T(8,128)(2,1)} %slice.1400, bf16[256,1536]{1,0:T(8,128)(2,1)} %slice.1397, bf16[256,1536]{1,0:T(8,128)(2,1)} %slice.1396, ...), kind=kOutput, calls=%fused_computation.57 | convolution fusion | flops 4883741184 | bytes 17319936 | tf_op jit(solution)/shard_map/dot_general | solution.py:554
  518.0 7.5 convolution_convert_fusion
  543.0 10.8 collective-permute-done.40
  572.0 8.4 collective-permute-done.21
  582.4 7.7 collective-permute-done.41
  639.4 18.8 %collective-permute-done.53 = bf16[296,1536]{1,0:T(8,128)(2,1)S(1)} collective-permute-done((bf16[296,1536]{1,0:T(8,128)(2,1)S(1)}, bf16[296,1536]{1,0:T(8,128)(2,1)S(1)}, u32[]{:S(2)}, u32[]{:S(2)}) %collective-permute-start.53) | collective-permute-done | bytes 909344 | tf_op jit(solution)/shard_map/ppermute | solution.py:732
  660.3 13.4 %collective-permute-done.73 = bf16[296,1536]{1,0:T(8,128)(2,1)S(1)} collective-permute-done((bf16[296,1536]{1,0:T(8,128)(2,1)S(1)}, bf16[296,1536]{1,0:T(8,128)(2,1)S(1)}, u32[]{:S(2)}, u32[]{:S(2)}) %collective-permute-start.73) | collective-permute-done | bytes 909344 | tf_op jit(solution)/shard_map/ppermute | solution.py:732
  707.3 46.0 %attention_back.2 = (bf16[1024,1152]{1,0:T(8,128)(2,1)S(1)}, bf16[160,1152]{1,0:T(8,128)(2,1)S(1)}) custom-call(f32[1184,128]{1,0:T(8,128)S(1)} %broadcast_in_dim.122.bias_ref, f32[1,1]{1,0:T(1,128)} %bitcast.12.floor_ref, bf16[1024,1152]{1,0:T(8,128)(2,1)} %copy-done.17, bf16[160,1152]{1,0:T(8,128)(2,1)S(1)} %copy-done.14, bf16[1024,1152]{1,0:T(8,128)(2,1)} %copy-done.17, ...), custom_call_target="tpu_custom_call" | custom-call | flops 21532508160 | bytes 7274496 | tf_op jit(solution)/shard_map/attention_back/pallas_call | solution.py:690
  762.2 47.1 %attention_back.3 = (bf16[1024,1152]{1,0:T(8,128)(2,1)S(1)}, bf16[160,1152]{1,0:T(8,128)(2,1)S(1)}) custom-call(f32[1184,128]{1,0:T(8,128)S(1)} %broadcast_in_dim.124.bias_ref, f32[1,1]{1,0:T(1,128)} %bitcast.45.floor_ref, bf16[1024,1152]{1,0:T(8,128)(2,1)} %copy-done.18, bf16[160,1152]{1,0:T(8,128)(2,1)S(1)} %copy-done.16, bf16[1024,1152]{1,0:T(8,128)(2,1)} %copy-done.18, ...), custom_call_target="tpu_custom_call" | custom-call | flops 21532508160 | bytes 7274496 | tf_op jit(solution)/shard_map/attention_back/pallas_call | solution.py:690
  809.5 10.2 fusion
  840.5 7.9 fusion.96
  848.4 9.7 add_convert_fusion.1
  858.2 13.3 %fusion.148 = f32[1536,1536]{1,0:T(8,128)} fusion(bf16[256,1536]{1,0:T(8,128)(2,1)S(1)} %copy-done.178, bf16[256,1536]{1,0:T(8,128)(2,1)S(1)} %copy-done.173, bf16[256,1536]{1,0:T(8,128)(2,1)S(1)} %copy-done.176, bf16[256,1536]{1,0:T(8,128)(2,1)S(1)} %copy-done.87, f32[1536]{0:T(1024)S(1)} %copy-done.279, f32[1024,1536]{1,0:T(8,128)} %copy-done.372, ...), kind=kOutput, calls=%fused_computation.459 | convolution fusion | flops 4863295488 | bytes 18886656 | tf_op jit(solution)/shard_map/dot_general | solution.py:562
  871.6 15.1 %add_convert_fusion = bf16[1536,1536]{1,0:T(8,128)(2,1)} fusion(f32[1536,1536]{1,0:T(8,128)} %fusion.148, bf16[256,1536]{1,0:T(8,128)(2,1)} %slice.1400, bf16[256,1536]{1,0:T(8,128)(2,1)S(1)} %copy-done.171, bf16[256,1536]{1,0:T(8,128)(2,1)S(1)} %copy-done.174, bf16[256,1536]{1,0:T(8,128)(2,1)S(1)} %copy-done.84, f32[1536]{0:T(1024)S(1)} %copy-done.277, ...), kind=kOutput, calls=%fused_computation.9 | convolution fusion | flops 4868014080 | bytes 23605248 | tf_op jit(solution)/shard_map/dot_general | solution.py:562
  893.6 8.0 pad_maximum_fusion
  943.0 8.8 fusion.16
  952.0 8.8 fusion.17
  1042.0 8.5 collective-permute-done.77
  1081.4 58.3 %reduce-scatter.5.cloned.1.call-done = bf16[1,2,2,192,1536]{4,3,2,1,0:T(8,128)(2,1)} async-done(((bf16[8,2,2,192,1536]{4,3,2,1,0:T(8,128)(2,1)}), bf16[1,2,2,192,1536]{4,3,2,1,0:T(8,128)(2,1)}) %reduce-scatter.5.cloned.1.call-update) | async-done | bytes 2359312 | tf_op jit(solution)/shard_map/reduce_scatter | solution.py:855
  (1396 shorter events, 637.0 us)
Async XLA Ops:
  17.9 146.8 %all-gather.8.cloned.1.call-start = ((), (), s32[]{:S(2)}) async-start(), calls=%async_computation.10 | async-start | bytes 10616832 | tf_op jit(solution)/shard_map/all_gather | solution.py:851
  33.6 390.6 %all-gather.10.cloned.1.call-start = ((), (), s32[]{:S(2)}) async-start(), calls=%async_computation.11 | async-start | bytes 21233664 | tf_op jit(solution)/shard_map/all_gather | solution.py:851
  40.1 88.6 %collective-permute-start.24 = (bf16[296,1536]{1,0:T(8,128)(2,1)}, bf16[296,1536]{1,0:T(8,128)(2,1)}, u32[]{:S(2)}, u32[]{:S(2)}) collective-permute-start(bf16[296,1536]{1,0:T(8,128)(2,1)} %pad_maximum_fusion.16), channel_id=1, source_target_pairs={{0,2},{1,3},{2,0},{3,1},{4,6},{5,7},{6,4},{7,5},{8,10},{9,11},{10,... | collective-permute-start | bytes 2727944 | tf_op jit(solution)/shard_map/ppermute | solution.py:732
  47.3 70.4 %collective-permute-start.23 = (bf16[296,1536]{1,0:T(8,128)(2,1)}, bf16[296,1536]{1,0:T(8,128)(2,1)}, u32[]{:S(2)}, u32[]{:S(2)}) collective-permute-start(bf16[296,1536]{1,0:T(8,128)(2,1)} %pad_maximum_fusion.16), channel_id=1, source_target_pairs={{0,1},{1,0},{2,3},{3,2},{4,5},{5,4},{6,7},{7,6},{8,9},{9,8},{10,11... | collective-permute-start | bytes 2727944 | tf_op jit(solution)/shard_map/ppermute | solution.py:732
  51.8 85.5 %collective-permute-start.1 = (bf16[296,1536]{1,0:T(8,128)(2,1)}, bf16[296,1536]{1,0:T(8,128)(2,1)}, u32[]{:S(2)}, u32[]{:S(2)}) collective-permute-start(bf16[296,1536]{1,0:T(8,128)(2,1)} %pad_maximum_fusion.14), channel_id=1, source_target_pairs={{0,2},{1,3},{2,0},{3,1},{4,6},{5,7},{6,4},{7,5},{8,10},{9,11},{10,... | collective-permute-start | bytes 2727944 | tf_op jit(solution)/shard_map/ppermute | solution.py:732
  51.8 80.9 %collective-permute-start = (bf16[296,1536]{1,0:T(8,128)(2,1)}, bf16[296,1536]{1,0:T(8,128)(2,1)}, u32[]{:S(2)}, u32[]{:S(2)}) collective-permute-start(bf16[296,1536]{1,0:T(8,128)(2,1)} %pad_maximum_fusion.14), channel_id=1, source_target_pairs={{0,1},{1,0},{2,3},{3,2},{4,5},{5,4},{6,7},{7,6},{8,9},{9,8},{10,11... | collective-permute-start | bytes 2727944 | tf_op jit(solution)/shard_map/ppermute | solution.py:732
  80.1 986.3 %reduce-scatter.3.cloned.1.call-start = ((), (), s32[]{:S(2)}) async-start(), calls=%async_computation.8 | async-start | bytes 10616832 | tf_op jit(solution)/shard_map/reduce_scatter | solution.py:855
  86.2 198.5 %collective-permute-start.44 = (bf16[296,1536]{1,0:T(8,128)(2,1)}, bf16[296,1536]{1,0:T(8,128)(2,1)}, u32[]{:S(2)}, u32[]{:S(2)}) collective-permute-start(bf16[296,1536]{1,0:T(8,128)(2,1)} %pad_maximum_fusion.18), channel_id=1, source_target_pairs={{0,2},{1,3},{2,0},{3,1},{4,6},{5,7},{6,4},{7,5},{8,10},{9,11},{10,... | collective-permute-start | bytes 2727944 | tf_op jit(solution)/shard_map/ppermute | solution.py:732
  149.8 135.5 %collective-permute-start.43 = (bf16[296,1536]{1,0:T(8,128)(2,1)}, bf16[296,1536]{1,0:T(8,128)(2,1)}, u32[]{:S(2)}, u32[]{:S(2)}) collective-permute-start(bf16[296,1536]{1,0:T(8,128)(2,1)} %pad_maximum_fusion.18), channel_id=1, source_target_pairs={{0,1},{1,0},{2,3},{3,2},{4,5},{5,4},{6,7},{7,6},{8,9},{9,8},{10,11... | collective-permute-start | bytes 2727944 | tf_op jit(solution)/shard_map/ppermute | solution.py:732
  227.4 41.9 %collective-permute-start.10 = (bf16[296,768]{1,0:T(8,128)(2,1)}, bf16[296,768]{1,0:T(8,128)(2,1)}, u32[]{:S(2)}, u32[]{:S(2)}) collective-permute-start(bf16[296,768]{1,0:T(8,128)(2,1)} %get-tuple-element.231), channel_id=1, source_target_pairs={{0,1},{1,0},{2,3},{3,2},{4,5},{5,4},{6,7},{7,6},{8,9},{9,8},{10,11... | collective-permute-start | bytes 1363976 | tf_op jit(solution)/shard_map/ppermute | solution.py:732
  227.7 44.7 %collective-permute-start.8 = (bf16[296,768]{1,0:T(8,128)(2,1)}, bf16[296,768]{1,0:T(8,128)(2,1)}, u32[]{:S(2)}, u32[]{:S(2)}) collective-permute-start(bf16[296,768]{1,0:T(8,128)(2,1)} %get-tuple-element.232), channel_id=1, source_target_pairs={{0,2},{1,3},{2,0},{3,1},{4,6},{5,7},{6,4},{7,5},{8,10},{9,11},{10,... | collective-permute-start | bytes 1363976 | tf_op jit(solution)/shard_map/ppermute | solution.py:732
  307.9 35.1 %collective-permute-start.64 = (bf16[296,1536]{1,0:T(8,128)(2,1)}, bf16[296,1536]{1,0:T(8,128)(2,1)S(1)}, u32[]{:S(2)}, u32[]{:S(2)}) collective-permute-start(bf16[296,1536]{1,0:T(8,128)(2,1)} %pad_maximum_fusion.20), channel_id=1, source_target_pairs={{0,2},{1,3},{2,0},{3,1},{4,6},{5,7},{6,4},{7,5},{8,10},{9,11},{10,... | collective-permute-start | bytes 2727944 | tf_op jit(solution)/shard_map/ppermute | solution.py:732
  314.1 35.1 %collective-permute-start.46 = (bf16[296,768]{1,0:T(8,128)(2,1)S(1)}, bf16[296,768]{1,0:T(8,128)(2,1)S(1)}, u32[]{:S(2)}, u32[]{:S(2)}) collective-permute-start(bf16[296,768]{1,0:T(8,128)(2,1)S(1)} %slice.1353), channel_id=1, source_target_pairs={{0,1},{1,0},{2,3},{3,2},{4,5},{5,4},{6,7},{7,6},{8,9},{9,8},{10,11... | collective-permute-start | bytes 1363976 | tf_op jit(solution)/shard_map/ppermute | solution.py:732
  335.3 46.9 %collective-permute-start.34 = (bf16[296,1536]{1,0:T(8,128)(2,1)}, bf16[296,1536]{1,0:T(8,128)(2,1)}, u32[]{:S(2)}, u32[]{:S(2)}) collective-permute-start(bf16[296,1536]{1,0:T(8,128)(2,1)} %pad_maximum_fusion.17), channel_id=1, source_target_pairs={{0,2},{1,3},{2,0},{3,1},{4,6},{5,7},{6,4},{7,5},{8,10},{9,11},{10,... | collective-permute-start | bytes 2727944 | tf_op jit(solution)/shard_map/ppermute | solution.py:732
  344.3 44.0 %collective-permute-start.13 = (bf16[296,1536]{1,0:T(8,128)(2,1)}, bf16[296,1536]{1,0:T(8,128)(2,1)}, u32[]{:S(2)}, u32[]{:S(2)}) collective-permute-start(bf16[296,1536]{1,0:T(8,128)(2,1)} %pad_maximum_fusion.15), channel_id=1, source_target_pairs={{0,1},{1,0},{2,3},{3,2},{4,5},{5,4},{6,7},{7,6},{8,9},{9,8},{10,11... | collective-permute-start | bytes 2727944 | tf_op jit(solution)/shard_map/ppermute | solution.py:732
  349.2 53.7 %collective-permute-start.14 = (bf16[296,1536]{1,0:T(8,128)(2,1)}, bf16[296,1536]{1,0:T(8,128)(2,1)}, u32[]{:S(2)}, u32[]{:S(2)}) collective-permute-start(bf16[296,1536]{1,0:T(8,128)(2,1)} %pad_maximum_fusion.15), channel_id=1, source_target_pairs={{0,2},{1,3},{2,0},{3,1},{4,6},{5,7},{6,4},{7,5},{8,10},{9,11},{10,... | collective-permute-start | bytes 2727944 | tf_op jit(solution)/shard_map/ppermute | solution.py:732
  352.8 48.8 %collective-permute-start.65 = (bf16[296,768]{1,0:T(8,128)(2,1)}, bf16[296,768]{1,0:T(8,128)(2,1)}, u32[]{:S(2)}, u32[]{:S(2)}) collective-permute-start(bf16[296,768]{1,0:T(8,128)(2,1)} %slice.1398), channel_id=1, source_target_pairs={{0,2},{1,3},{2,0},{3,1},{4,6},{5,7},{6,4},{7,5},{8,10},{9,11},{10,... | collective-permute-start | bytes 1363976 | tf_op jit(solution)/shard_map/ppermute | solution.py:732
  369.6 36.1 %collective-permute-start.66 = (bf16[296,768]{1,0:T(8,128)(2,1)}, bf16[296,768]{1,0:T(8,128)(2,1)}, u32[]{:S(2)}, u32[]{:S(2)}) collective-permute-start(bf16[296,768]{1,0:T(8,128)(2,1)} %slice.1399), channel_id=1, source_target_pairs={{0,1},{1,0},{2,3},{3,2},{4,5},{5,4},{6,7},{7,6},{8,9},{9,8},{10,11... | collective-permute-start | bytes 1363976 | tf_op jit(solution)/shard_map/ppermute | solution.py:732
  382.1 38.6 %collective-permute-start.35 = (bf16[296,768]{1,0:T(8,128)(2,1)S(1)}, bf16[296,768]{1,0:T(8,128)(2,1)S(1)}, u32[]{:S(2)}, u32[]{:S(2)}) collective-permute-start(bf16[296,768]{1,0:T(8,128)(2,1)S(1)} %slice.1326), channel_id=1, source_target_pairs={{0,2},{1,3},{2,0},{3,1},{4,6},{5,7},{6,4},{7,5},{8,10},{9,11},{10,... | collective-permute-start | bytes 1363976 | tf_op jit(solution)/shard_map/ppermute | solution.py:732
  388.2 32.6 %collective-permute-start.36 = (bf16[296,768]{1,0:T(8,128)(2,1)S(1)}, bf16[296,768]{1,0:T(8,128)(2,1)S(1)}, u32[]{:S(2)}, u32[]{:S(2)}) collective-permute-start(bf16[296,768]{1,0:T(8,128)(2,1)S(1)} %slice.1327), channel_id=1, source_target_pairs={{0,1},{1,0},{2,3},{3,2},{4,5},{5,4},{6,7},{7,6},{8,9},{9,8},{10,11... | collective-permute-start | bytes 1363976 | tf_op jit(solution)/shard_map/ppermute | solution.py:732
  463.3 71.8 %collective-permute-start.17 = (bf16[296,768]{1,0:T(8,128)(2,1)}, bf16[296,768]{1,0:T(8,128)(2,1)}, u32[]{:S(2)}, u32[]{:S(2)}) collective-permute-start(bf16[296,768]{1,0:T(8,128)(2,1)} %fusion.120), channel_id=1, source_target_pairs={{0,1},{1,0},{2,3},{3,2},{4,5},{5,4},{6,7},{7,6},{8,9},{9,8},{10,11... | collective-permute-start | bytes 1363976 | tf_op jit(solution)/shard_map/ppermute | solution.py:732
  464.4 90.3 %collective-permute-start.22 = (bf16[296,768]{1,0:T(8,128)(2,1)}, bf16[296,768]{1,0:T(8,128)(2,1)}, u32[]{:S(2)}, u32[]{:S(2)}) collective-permute-start(bf16[296,768]{1,0:T(8,128)(2,1)} %pad_maximum_fusion.55), channel_id=1, source_target_pairs={{0,2},{1,3},{2,0},{3,1},{4,6},{5,7},{6,4},{7,5},{8,10},{9,11},{10,... | collective-permute-start | bytes 1363976 | tf_op jit(solution)/shard_map/ppermute | solution.py:732
  467.3 60.5 %collective-permute-start.20 = (bf16[296,768]{1,0:T(8,128)(2,1)}, bf16[296,768]{1,0:T(8,128)(2,1)}, u32[]{:S(2)}, u32[]{:S(2)}) collective-permute-start(bf16[296,768]{1,0:T(8,128)(2,1)} %get-tuple-element.229), channel_id=1, source_target_pairs={{0,1},{1,0},{2,3},{3,2},{4,5},{5,4},{6,7},{7,6},{8,9},{9,8},{10,11... | collective-permute-start | bytes 1363976 | tf_op jit(solution)/shard_map/ppermute | solution.py:732
  467.4 63.3 %collective-permute-start.18 = (bf16[296,768]{1,0:T(8,128)(2,1)}, bf16[296,768]{1,0:T(8,128)(2,1)}, u32[]{:S(2)}, u32[]{:S(2)}) collective-permute-start(bf16[296,768]{1,0:T(8,128)(2,1)} %get-tuple-element.230), channel_id=1, source_target_pairs={{0,2},{1,3},{2,0},{3,1},{4,6},{5,7},{6,4},{7,5},{8,10},{9,11},{10,... | collective-permute-start | bytes 1363976 | tf_op jit(solution)/shard_map/ppermute | solution.py:732
  492.1 40.5 %collective-permute-start.50 = (bf16[296,768]{1,0:T(8,128)(2,1)}, bf16[296,768]{1,0:T(8,128)(2,1)}, u32[]{:S(2)}, u32[]{:S(2)}) collective-permute-start(bf16[296,768]{1,0:T(8,128)(2,1)} %get-tuple-element.227), channel_id=1, source_target_pairs={{0,1},{1,0},{2,3},{3,2},{4,5},{5,4},{6,7},{7,6},{8,9},{9,8},{10,11... | collective-permute-start | bytes 1363976 | tf_op jit(solution)/shard_map/ppermute | solution.py:732
  637.6 36.1 %collective-permute-start.73 = (bf16[296,1536]{1,0:T(8,128)(2,1)S(1)}, bf16[296,1536]{1,0:T(8,128)(2,1)S(1)}, u32[]{:S(2)}, u32[]{:S(2)}) collective-permute-start(bf16[296,1536]{1,0:T(8,128)(2,1)S(1)} %pad_maximum_fusion.21), channel_id=1, source_target_pairs={{0,1},{1,0},{2,3},{3,2},{4,5},{5,4},{6,7},{7,6},{8,9},{9,8},{10,11... | collective-permute-start | bytes 2727944 | tf_op jit(solution)/shard_map/ppermute | solution.py:732
  638.7 36.0 %collective-permute-start.74 = (bf16[296,1536]{1,0:T(8,128)(2,1)S(1)}, bf16[296,1536]{1,0:T(8,128)(2,1)S(1)}, u32[]{:S(2)}, u32[]{:S(2)}) collective-permute-start(bf16[296,1536]{1,0:T(8,128)(2,1)S(1)} %pad_maximum_fusion.21), channel_id=1, source_target_pairs={{0,2},{1,3},{2,0},{3,1},{4,6},{5,7},{6,4},{7,5},{8,10},{9,11},{10,... | collective-permute-start | bytes 2727944 | tf_op jit(solution)/shard_map/ppermute | solution.py:732
  829.4 310.3 %reduce-scatter.5.cloned.1.call-start = ((), (), s32[]{:S(2)}) async-start(), calls=%async_computation.9 | async-start | bytes 21233664 | tf_op jit(solution)/shard_map/reduce_scatter | solution.py:855
  971.5 42.1 %collective-permute-start.80 = (bf16[296,768]{1,0:T(8,128)(2,1)}, bf16[296,768]{1,0:T(8,128)(2,1)}, u32[]{:S(2)}, u32[]{:S(2)}) collective-permute-start(bf16[296,768]{1,0:T(8,128)(2,1)} %get-tuple-element.223), channel_id=1, source_target_pairs={{0,1},{1,0},{2,3},{3,2},{4,5},{5,4},{6,7},{7,6},{8,9},{9,8},{10,11... | collective-permute-start | bytes 1363976 | tf_op jit(solution)/shard_map/ppermute | solution.py:732
  973.5 54.0 %collective-permute-start.78 = (bf16[296,768]{1,0:T(8,128)(2,1)}, bf16[296,768]{1,0:T(8,128)(2,1)}, u32[]{:S(2)}, u32[]{:S(2)}) collective-permute-start(bf16[296,768]{1,0:T(8,128)(2,1)} %get-tuple-element.224), channel_id=1, source_target_pairs={{0,2},{1,3},{2,0},{3,1},{4,6},{5,7},{6,4},{7,5},{8,10},{9,11},{10,... | collective-permute-start | bytes 1363976 | tf_op jit(solution)/shard_map/ppermute | solution.py:732
  978.5 56.3 %collective-permute-start.57 = (bf16[296,768]{1,0:T(8,128)(2,1)}, bf16[296,768]{1,0:T(8,128)(2,1)S(1)}, u32[]{:S(2)}, u32[]{:S(2)}) collective-permute-start(bf16[296,768]{1,0:T(8,128)(2,1)} %fusion.108), channel_id=1, source_target_pairs={{0,1},{1,0},{2,3},{3,2},{4,5},{5,4},{6,7},{7,6},{8,9},{9,8},{10,11... | collective-permute-start | bytes 1363976 | tf_op jit(solution)/shard_map/ppermute | solution.py:732
  979.9 56.6 %collective-permute-start.62 = (bf16[296,768]{1,0:T(8,128)(2,1)}, bf16[296,768]{1,0:T(8,128)(2,1)}, u32[]{:S(2)}, u32[]{:S(2)}) collective-permute-start(bf16[296,768]{1,0:T(8,128)(2,1)} %pad_maximum_fusion.43), channel_id=1, source_target_pairs={{0,2},{1,3},{2,0},{3,1},{4,6},{5,7},{6,4},{7,5},{8,10},{9,11},{10,... | collective-permute-start | bytes 1363976 | tf_op jit(solution)/shard_map/ppermute | solution.py:732
  (443 other events, 6896.3 us)
Sparse Core Ops, SparseCore 0:
  33.7 100.1 all-gather.7
  136.2 166.6 all-gather.9
  829.6 99.9 reduce-scatter.2
  931.8 207.8 reduce-scatter.4

commit v2 on v1

--- a/solution.py
+++ b/solution.py
@@ -733,12 +733,12 @@
 
 
 def gather_blocks(own):
-    half = own.shape[1] // 2
+    half = own.shape[-1] // 2
     near_x = flip(own, 1)
     near_y = flip(own, 2)
-    far_a = flip(near_x[:, :half], 2)
-    far_b = flip(near_y[:, half:], 1)
-    return (own, near_x, near_y, jnp.concatenate([far_a, far_b], axis=1))
+    far_a = flip(near_x[..., :half], 2)
+    far_b = flip(near_y[..., half:], 1)
+    return (own, near_x, near_y, jnp.concatenate([far_a, far_b], axis=-1))
 
 
 def add_low(a, b):
@@ -747,18 +747,16 @@
 
 def scatter_blocks(blocks):
     own, near_x, near_y, far = blocks
-    half = own.shape[1] // 2
-    for_y = flip(far[:, :half], 1)
-    for_x = flip(far[:, half:], 2)
-    from_x_a = flip(near_x[:, :half], 1)
-    from_y_b = flip(near_y[:, half:], 2)
-    from_x_b = flip(add_low(near_x[:, half:], for_x), 1)
-    from_y_a = flip(add_low(near_y[:, :half], for_y), 2)
-    return (
-        own.astype(F32)
-        + jnp.concatenate([from_x_a, from_x_b], axis=1).astype(F32)
-        + jnp.concatenate([from_y_a, from_y_b], axis=1).astype(F32)
-    )
+    half = own.shape[-1] // 2
+    for_y = flip(far[..., :half], 1)
+    for_x = flip(far[..., half:], 2)
+    from_x = flip(
+        jnp.concatenate([near_x[..., :half], add_low(near_x[..., half:], for_x)], axis=-1), 1
+    )
+    from_y = flip(
+        jnp.concatenate([add_low(near_y[..., :half], for_y), near_y[..., half:]], axis=-1), 2
+    )
+    return own.astype(F32) + from_x.astype(F32) + from_y.astype(F32)
 
 
 def join_rows(blocks, image_count):
@@ -898,10 +896,12 @@
     seq_index = lax.axis_index("seq")
     place = lax.axis_index(("batch", "seq"))
     L, image_count, D = image_tokens.shape
-    text_count = text_tokens.shape[1]
+    live_text = text_tokens.shape[1]
+    text_count = -(-live_text // 16) * 16
+    pad = ((0, 0), (0, text_count - live_text), (0, 0))
     head = D // HEADS
     own_width = D // S
-    spans = (slice(0, image_count), slice(image_count, image_count + text_count))
+    is_image = (jnp.arange(image_count + text_count) < image_count)[:, None]
 
     bias_widths = [array.shape[1] for array in (qv_bias, out_bias, up_bias, down_bias)]
     bias_ends = np.cumsum(bias_widths)
@@ -951,57 +951,49 @@
     perms, send, land = match_units(B, S, per_device, own_width // unit)
     back_perms = [[(target, source) for source, target in pairs] for pairs in perms]
     qkv_units = jnp.swapaxes(qkv_weight, 1, 2).reshape(2, per_device, unit, D).swapaxes(0, 1)
-    qkv_mine = move_units(qkv_units, perms, send, land, place)
+    qkv_mine = move_units(qkv_units, perms, send, land, place).swapaxes(0, 1)
     out_units = jnp.swapaxes(out_weight, 1, 2).reshape(2, -1, S, own_width).transpose(2, 0, 1, 3)
     out_mine = swap(out_units, "seq")
     out_columns = out_mine.shape[2]
     heads_all = gather_batch(
         jnp.concatenate([qkv_mine.reshape(-1, D), out_mine.reshape(-1, D)], axis=0)
     )
-    qkv_rows = 2 * per_device * unit
-    qkv_all = heads_all[:, :qkv_rows].reshape(B, per_device, 2, unit, D)
+    up_all = gather_batch(jnp.swapaxes(up_weight, 1, 2))
+    down_all = gather_batch(jnp.swapaxes(down_weight, 1, 2))
+    qkv_width = per_device * unit
+    qkv_rows = 2 * qkv_width
     out_all = heads_all[:, qkv_rows:].reshape(B, S, 2, out_columns, own_width)
-    hidden_all = gather_batch(
-        jnp.stack([jnp.swapaxes(up_weight, 1, 2), jnp.swapaxes(down_weight, 1, 2)])
-    )
-    qkv_part = [qkv_all[:, :, t].reshape(-1, D) for t in range(2)]
+    qkv_part = [
+        heads_all[:, t * qkv_width : (t + 1) * qkv_width].reshape(-1, D) for t in range(2)
+    ]
     out_part = [out_all[:, :, t].reshape(D, own_width) for t in range(2)]
-    up_part = [hidden_all[:, 0, t].reshape(-1, D) for t in range(2)]
-    down_part = [hidden_all[:, 1, t].reshape(-1, D) for t in range(2)]
+    up_part = [up_all[:, t].reshape(-1, D) for t in range(2)]
+    down_part = [down_all[:, t].reshape(-1, D) for t in range(2)]
     hidden_columns = up_weight.shape[2]
 
     order = jnp.bitwise_xor(seq_index, jnp.arange(S))
     image_keys = jnp.take(
         key_mask[:, : S * image_count].reshape(L, S, image_count), order, axis=1
-    ).reshape(L, -1)
+    )
     text_keys = jnp.take(
-        key_mask[:, S * image_count :].reshape(L, S, text_count), order, axis=1
-    ).reshape(L, -1)
-    live = jnp.concatenate([image_keys, text_keys], axis=1) > 0
+        key_mask[:, S * image_count :].reshape(L, S, live_text), order, axis=1
+    )
+    text_keys = jnp.pad(text_keys, ((0, 0), (0, 0), (0, text_count - live_text)))
+    live = jnp.concatenate([image_keys.reshape(L, -1), text_keys.reshape(L, -1)], axis=1) > 0
     key_bias = jnp.where(live, 0.0, DEAD).astype(F32)
-    floors = jnp.where(jnp.all(live, axis=1), -3e38, FLOOR_SCORE * LOG2E).astype(F32)
+    floors = jnp.where(jnp.all(key_mask > 0, axis=1), -3e38, FLOOR_SCORE * LOG2E).astype(F32)
     floors = floors.reshape(L, 1, 1)
 
-    token_blocks, grad_blocks = ([], [])
-    for s in range(L):
-        token_blocks.append(
-            gather_blocks(jnp.concatenate([image_tokens[s], text_tokens[s]], axis=0))
-        )
-    for s in range(L):
-        grad_blocks.append(
-            gather_blocks(jnp.concatenate([image_cotangent[s], text_cotangent[s]], axis=0))
-        )
-    tokens_all = [join_rows(blocks, image_count) for blocks in token_blocks]
-    grads_all = [join_rows(blocks, image_count) for blocks in grad_blocks]
-    own_tokens = [[image_tokens[s].astype(F32), text_tokens[s].astype(F32)] for s in range(L)]
-    own_grads = [
-        [image_cotangent[s].astype(F32), text_cotangent[s].astype(F32)] for s in range(L)
-    ]
-
-    first_norms, first_stats, qkvs, attended, projections, middles, middle_stats = (
-        [], [], [], [], [], [], [],
-    )
-    second_all = []
+    own_tokens = jnp.concatenate([image_tokens, jnp.pad(text_tokens, pad)], axis=1)
+    own_grads = jnp.concatenate([image_cotangent, jnp.pad(text_cotangent, pad)], axis=1)
+    token_blocks = gather_blocks(own_tokens)
+    grad_blocks = gather_blocks(own_grads)
+    tokens_all = [join_rows([block[s] for block in token_blocks], image_count) for s in range(L)]
+
+    def by_row(vectors):
+        return jnp.where(is_image, vectors[0][None, :], vectors[1][None, :])
+
+    first_norms, first_stats, qkvs, attended = ([], [], [], [])
     for s in range(L):
         norms, stats, rows = ([], [], [])
         for t in range(2):
@@ -1014,56 +1006,26 @@
             rows.append((dot_nt(norm, qkv_part[t]) + qkv_bias[t][None, :]).astype(BF16))
             norms.append(norm)
             stats.append((mean, inverse))
+        if s == L - 1:
+            rows, grad_blocks = lax.optimization_barrier((rows, grad_blocks))
         first_norms.append(norms)
         first_stats.append(stats)
         qkvs.append(rows)
         attended.append(attention(rows[0], rows[1], key_bias[s], floors[s], head))
+    grads_all = [join_rows([block[s] for block in grad_blocks], image_count) for s in range(L)]
+    projections, middles, middle_stats, second_all = ([], [], [], [])
     for s in range(L):
         partial = [dot_nt(attended[s][t], out_part[t]).astype(BF16) for t in range(2)]
         summed = scatter_blocks(split_rows(partial[0], partial[1], image_count, text_count))
-        seconds = []
-        kept_projection, kept_middle, kept_stats = ([], [], [])
-        for t in range(2):
-            pieces = modulation[t, s]
-            projection = summed[spans[t]] + out_bias_full[t][None, :]
-            middle = own_tokens[s][t] + pieces[2][None, :] * projection
-            mean, inverse = norm_stats(middle)
-            second = (middle - mean) * inverse * (1.0 + pieces[4][None, :]) + pieces[3][None, :]
-            seconds.append(second.astype(BF16))
-            kept_projection.append(projection)
-            kept_middle.append(middle)
-            kept_stats.append((mean, inverse))
-        projections.append(kept_projection)
-        middles.append(kept_middle)
-        middle_stats.append(kept_stats)
-        blocks = gather_blocks(jnp.concatenate(seconds, axis=0))
-        second_all.append(join_rows(blocks, image_count))
-    hidden_acts, hidden_pres, mlp_grads, pre_grads = ([], [], [], [])
-    norm2_sums, mlp_sums = ([], [])
-    for s in range(L):
-        acts, pres, partial, grads, pre_low, back = ([], [], [], [], [], [])
-        for t in range(2):
-            pre = dot_nt(second_all[s][t], up_part[t]) + up_bias_part[t][None, :]
-            act = gelu_tanh(pre).astype(BF16)
-            acts.append(act)
-            pres.append(pre)
-            grad = (modulation[t, s][5][None, :] * grads_all[s][t].astype(F32)).astype(BF16)
-            act_grad = dot_nt(grad, down_part[t])
-            pre_grad = jax.vjp(gelu_tanh, pre)[1](act_grad)[0].astype(BF16)
-            grads.append(grad)
-            pre_low.append(pre_grad)
-            back.append(dot_nn(pre_grad, up_part[t]).astype(BF16))
-            partial.append(dot_nn(act, down_part[t]).astype(BF16))
-        hidden_acts.append(acts)
-        hidden_pres.append(pres)
-        mlp_grads.append(grads)
-        pre_grads.append(pre_low)
-        norm2_sums.append(
-            scatter_blocks(split_rows(back[0], back[1], image_count, text_count))
-        )
-        mlp_sums.append(
-            scatter_blocks(split_rows(partial[0], partial[1], image_count, text_count))
-        )
+        pieces = [by_row(modulation[:, s, k]) for k in range(6)]
+        projection = summed + by_row(out_bias_full)
+        middle = own_tokens[s].astype(F32) + pieces[2] * projection
+        mean, inverse = norm_stats(middle)
+        second = (middle - mean) * inverse * (1.0 + pieces[4]) + pieces[3]
+        projections.append(projection)
+        middles.append(middle)
+        middle_stats.append((mean, inverse))
+        second_all.append(join_rows(gather_blocks(second.astype(BF16)), image_count))
 
     def both(left, right, t):
         total = dot_tn(left[0][t], right[0][t])
@@ -1071,107 +1033,144 @@
             total = total + dot_tn(left[s][t], right[s][t])
         return total.astype(BF16)
 
-    up_sum = [both(pre_grads, second_all, t) for t in range(2)]
-    down_sum = [both(hidden_acts, mlp_grads, t) for t in range(2)]
-    hidden_grads = scatter_batch(
-        jnp.stack(
-            [
-                jnp.stack([value.reshape(B, hidden_columns, D) for value in values], axis=1)
-                for values in (up_sum, down_sum)
-            ],
-            axis=1,
-        )
-    )
+    def stack_columns(values, width):
+        return jnp.stack([value.reshape(B, width, D) for value in values], axis=1)
+
+    hidden_acts, hidden_pres, mlp_grads = ([], [], [])
+    for s in range(L):
+        acts, pres, grads = ([], [], [])
+        for t in range(2):
+            pre = dot_nt(second_all[s][t], up_part[t]) + up_bias_part[t][None, :]
+            acts.append(gelu_tanh(pre).astype(BF16))
+            pres.append(pre)
+            grads.append(
+                (modulation[t, s][5][None, :] * grads_all[s][t].astype(F32)).astype(BF16)
+            )
+        hidden_acts.append(acts)
+        hidden_pres.append(pres)
+        mlp_grads.append(grads)
+    down_sent = stack_columns([both(hidden_acts, mlp_grads, t) for t in range(2)], hidden_columns)
+    down_came = scatter_batch(down_sent)
+    late_pres, down_sent = lax.optimization_barrier((hidden_pres[-1], down_sent))
+    hidden_pres[-1] = late_pres
+    pre_grads, norm2_sums = ([], [])
+    for s in range(L):
+        pre_low, back = ([], [])
+        for t in range(2):
+            act_grad = dot_nt(mlp_grads[s][t], down_part[t])
+            pre_grad = jax.vjp(gelu_tanh, hidden_pres[s][t])[1](act_grad)[0].astype(BF16)
+            pre_low.append(pre_grad)
+            back.append(dot_nn(pre_grad, up_part[t]).astype(BF16))
+        pre_grads.append(pre_low)
+        norm2_sums.append(
+            scatter_blocks(split_rows(back[0], back[1], image_count, text_count))
+        )
+    up_sent = stack_columns([both(pre_grads, second_all, t) for t in range(2)], hidden_columns)
+    up_came = scatter_batch(up_sent)
     up_bias_sum = jnp.stack(
         [
             sum(jnp.sum(pre_grads[s][t].astype(F32), axis=0) for s in range(L))
             for t in range(2)
         ]
     )
-
-    results = [[], []]
-    mod_grads = [[[None] * 6 for _ in range(L)] for _ in range(2)]
+    mlp_parts = [
+        split_rows(
+            dot_nn(hidden_acts[s][0], down_part[0]).astype(BF16),
+            dot_nn(hidden_acts[s][1], down_part[1]).astype(BF16),
+            image_count,
+            text_count,
+        )
+        for s in range(L)
+    ]
+    mlp_sums = scatter_blocks([jnp.stack([mlp_parts[s][r] for s in range(L)]) for r in range(4)])
+
+    def row_sums(values):
+        return jnp.stack(
+            [jnp.sum(values[:image_count], axis=0), jnp.sum(values[image_count:], axis=0)]
+        )
+
+    mod_grads = [[None] * 6 for _ in range(L)]
     middle_grads, proj_all = ([], [])
-    out_bias_sum = [0.0, 0.0]
-    down_bias_sum = [0.0, 0.0]
+    out_bias_sum = 0.0
     for s in range(L):
-        kept, lows = ([], [])
-        for t in range(2):
-            pieces = modulation[t, s]
-            grad = own_grads[s][t]
-            mlp_value = mlp_sums[s][spans[t]] + down_bias_full[t][None, :]
-            results[t].append(
-                (middles[s][t] + pieces[5][None, :] * mlp_value).astype(BF16)
-            )
-            mod_grads[t][s][5] = jnp.sum(grad * mlp_value, axis=0)
-            own_low = (pieces[5][None, :] * grad).astype(BF16)
-            down_bias_sum[t] = down_bias_sum[t] + jnp.sum(own_low.astype(F32), axis=0)
-            norm_grad = norm2_sums[s][spans[t]]
-            mean, inverse = middle_stats[s][t]
-            norm = (middles[s][t] - mean) * inverse
-            mod_grads[t][s][3] = jnp.sum(norm_grad, axis=0)
-            mod_grads[t][s][4] = jnp.sum(norm_grad * norm, axis=0)
-            middle_grad = grad + norm_back(norm, inverse, norm_grad, pieces[4][None, :])
-            mod_grads[t][s][2] = jnp.sum(middle_grad * projections[s][t], axis=0)
-            low = (pieces[2][None, :] * middle_grad).astype(BF16)
-            out_bias_sum[t] = out_bias_sum[t] + jnp.sum(low.astype(F32), axis=0)
-            kept.append(middle_grad)
-            lows.append(low)
-        middle_grads.append(kept)
-        proj_all.append(join_rows(gather_blocks(jnp.concatenate(lows, axis=0)), image_count))
+        pieces = [by_row(modulation[:, s, k]) for k in range(6)]
+        norm_grad = norm2_sums[s]
+        mean, inverse = middle_stats[s]
+        norm = (middles[s] - mean) * inverse
+        middle_grad = own_grads[s].astype(F32) + norm_back(norm, inverse, norm_grad, pieces[4])
+        low = (pieces[2] * middle_grad).astype(BF16)
+        proj_all.append(join_rows(gather_blocks(low), image_count))
+        mod_grads[s][3] = row_sums(norm_grad)
+        mod_grads[s][4] = row_sums(norm_grad * norm)
+        mod_grads[s][2] = row_sums(middle_grad * projections[s])
+        out_bias_sum = out_bias_sum + row_sums(low.astype(F32))
+        middle_grads.append(middle_grad)
 
     qkv_grads, norm1_sums = ([], [])
     for s in range(L):
         attended_grad = [dot_nn(proj_all[s][t], out_part[t]).astype(BF16) for t in range(2)]
+        if s == 0:
+            attended_grad, up_sent = lax.optimization_barrier((attended_grad, up_sent))
+        if s == L - 1:
+            attended_grad, mlp_sums = lax.optimization_barrier((attended_grad, mlp_sums))
         grads = attention_back(
             qkvs[s][0], qkvs[s][1], attended_grad[0], attended_grad[1], key_bias[s], floors[s], head
         )
         qkv_grads.append(grads)
         back = [dot_nn(grads[t], qkv_part[t]).astype(BF16) for t in range(2)]
-        for t in range(2):
-            wide = back[t].astype(F32)
-            mean, inverse = first_stats[s][t]
-            norm = (tokens_all[s][t].astype(F32) - mean) * inverse
-            mod_grads[t][s][0] = jnp.sum(wide, axis=0)
-            mod_grads[t][s][1] = jnp.sum(wide * norm, axis=0)
+        for k in range(2):
+            sums = []
+            for t in range(2):
+                wide = back[t].astype(F32)
+                if k == 1:
+                    mean, inverse = first_stats[s][t]
+                    wide = wide * ((tokens_all[s][t].astype(F32) - mean) * inverse)
+                sums.append(jnp.sum(wide, axis=0))
+            mod_grads[s][k] = jnp.stack(sums)
         norm1_sums.append(
             scatter_blocks(split_rows(back[0], back[1], image_count, text_count))
         )
     out_sum = [both(proj_all, attended, t) for t in range(2)]
     qkv_sum = [both(qkv_grads, first_norms, t) for t in range(2)]
-    qkv_sent = jnp.stack(
-        [value.reshape(B, per_device, unit, D) for value in qkv_sum], axis=2
-    ).reshape(B, qkv_rows, D)
+    qkv_sent = stack_columns(qkv_sum, qkv_width).reshape(B, qkv_rows, D)
     out_sent = jnp.stack(
         [value.reshape(B, S, out_columns, own_width) for value in out_sum], axis=2
     ).reshape(B, -1, D)
     head_grads = scatter_batch(jnp.concatenate([qkv_sent, out_sent], axis=1))
     qkv_home = move_units(
-        head_grads[:qkv_rows].reshape(per_device, 2, unit, D), back_perms, land, send, place
+        head_grads[:qkv_rows].reshape(2, per_device, unit, D).swapaxes(0, 1),
+        back_perms,
+        land,
+        send,
+        place,
     )
     out_home = swap(head_grads[qkv_rows:].reshape(S, 2, out_columns, own_width), "seq")
     qkv_weight_grad = qkv_home.swapaxes(0, 1).reshape(2, -1, D).swapaxes(1, 2).astype(F32)
     out_weight_grad = (
         out_home.transpose(1, 2, 0, 3).reshape(2, out_columns, D).swapaxes(1, 2).astype(F32)
     )
-    up_weight_grad = hidden_grads[0].swapaxes(1, 2).astype(F32)
-    down_weight_grad = hidden_grads[1].swapaxes(1, 2).astype(F32)
-
-    input_grads = [[], []]
+    up_weight_grad = up_came.swapaxes(1, 2).astype(F32)
+    down_weight_grad = down_came.swapaxes(1, 2).astype(F32)
+
+    results, input_grads = ([], [])
+    down_bias_sum = 0.0
     for s in range(L):
-        for t in range(2):
-            mean, inverse = norm_stats(own_tokens[s][t])
-            norm = (own_tokens[s][t] - mean) * inverse
-            input_grads[t].append(
-                middle_grads[s][t]
-                + norm_back(
-                    norm, inverse, norm1_sums[s][spans[t]], modulation[t, s][1][None, :]
-                )
-            )
-
-    mod_rows = jnp.stack(
-        [jnp.stack([jnp.concatenate(mod_grads[t][s]) for s in range(L)]) for t in range(2)]
-    )
+        pieces = [by_row(modulation[:, s, k]) for k in range(6)]
+        grad = own_grads[s].astype(F32)
+        mlp_value = mlp_sums[s] + by_row(down_bias_full)
+        results.append((middles[s] + pieces[5] * mlp_value).astype(BF16))
+        mod_grads[s][5] = row_sums(grad * mlp_value)
+        own_low = (pieces[5] * grad).astype(BF16)
+        down_bias_sum = down_bias_sum + row_sums(own_low.astype(F32))
+        values = own_tokens[s].astype(F32)
+        mean, inverse = norm_stats(values)
+        norm = (values - mean) * inverse
+        input_grads.append(
+            middle_grads[s] + norm_back(norm, inverse, norm1_sums[s], pieces[1])
+        )
+    text_rows = slice(image_count, image_count + live_text)
+
+    mod_rows = jnp.stack([jnp.concatenate(mod_grads[s], axis=1) for s in range(L)], axis=1)
     mod_rows = mod_rows.reshape(2, L, B, S, mod_width).transpose(3, 2, 0, 1, 4)
     qv_bias_sum = jnp.zeros((2, 2 * D), F32)
     for part, column in ((0, 0), (1, 2 * own_width)):
@@ -1198,9 +1197,9 @@
     bias_rows = jnp.concatenate(
         [
             qv_bias_sum.reshape(2, B, S, -1),
-            jnp.stack(out_bias_sum).reshape(2, B, S, -1),
+            out_bias_sum.reshape(2, B, S, -1),
             up_bias_rows,
-            jnp.stack(down_bias_sum).reshape(2, B, S, -1),
+            down_bias_sum.reshape(2, B, S, -1),
         ],
         axis=3,
     ).transpose(2, 1, 0, 3)
@@ -1230,10 +1229,10 @@
     smooth_grad = smooth_grad + flip(smooth_grad, 2)
     cond_grad = jax.vjp(jax.nn.silu, conditioning.astype(F32))[1](smooth_grad)[0]
     return (
-        jnp.stack(results[0]),
-        jnp.stack(results[1]),
-        jnp.stack(input_grads[0]),
-        jnp.stack(input_grads[1]),
+        jnp.stack([values[:image_count] for values in results]),
+        jnp.stack([values[text_rows] for values in results]),
+        jnp.stack([values[:image_count] for values in input_grads]),
+        jnp.stack([values[text_rows] for values in input_grads]),
         cond_grad,
         mod_weight_grad,
         mod_bias_grad,

time: 1160 us -> 1350 us (1.16)
  the two profiles are of different devices: /device:TPU:0 before, /device:TPU:16 now
where the time goes in v2:
time: 1350 us; the launch traced here: 1330 us
  waiting for transfers between devices  414 us (31%)
  matrix products  235 us (17%)
  other arithmetic  171 us (13%)
  local copies, waits for them, and re-layouts  169 us (13%)
  Pallas kernels  143 us (11%)
  starting transfers between devices  114 us (8%)
  blocking collectives  56.3 us (4%)
  between operations  25.6 us (2%)
    ppermute x54, waiting for transfers between devices, flip(): return lax.ppermute(values, 'seq', [(i, i ^ bit) for i in range(4)])  262 us
    pallas_call x2, Pallas kernels, attention_back(): pl.pallas_call(functools.partial(attention_back_kernel, 256, LOG2E / math...  94.4 us
    dot_general x16, matrix products, dot_tn(): lax.dot_general(a, b, (((0,), (0,)), ((), ())), preferred_element_type=F32)  87.2 us
    dot_general x16, matrix products, dot_nt(): lax.dot_general(a, b, (((1,), (1,)), ((), ())), preferred_element_type=F32)  71.7 us
    dot_general x16, matrix products, dot_nn(): lax.dot_general(a, b, (((1,), (0,)), ((), ())), preferred_element_type=F32)  71.6 us
    all_gather x3, waiting for transfers between devices, gather_batch(): return lax.all_gather(values, 'batch', axis=0)  67.6 us
    ppermute x54, starting transfers between devices, flip(): return lax.ppermute(values, 'seq', [(i, i ^ bit) for i in range(4)])  62.1 us
    reduce_scatter x3, waiting for transfers between devices, scatter_batch(): return lax.psum_scatter(values, 'batch', scatter_dimension=0)  53.6 us
  transfers between devices with their start and end apart: 72, of which 31 were waited for; matrix products, arithmetic and copies ran while one was open for 30% of the time, Pallas kernels for 7%

profile of v2, /device:TPU:16, one launch (start us, length us, event | category | flops | bytes accessed | tf_op | source)
XLA Modules:
  0.0 1327.9 jit_solution(7642586023072995255)
XLA Ops:
  33.8 21.8 %collective-permute-done.5 = bf16[1,2,48,1536]{3,2,1,0:T(8,128)(2,1)} collective-permute-done((bf16[1,2,48,1536]{3,2,1,0:T(8,128)(2,1)S(1)}, bf16[1,2,48,1536]{3,2,1,0:T(8,128)(2,1)}, u32[]{:S(2)}, u32[]{:S(2)}) %collective-permute-start.5) | collective-permute-done | bytes 294944 | tf_op jit(solution)/shard_map/ppermute | solution.py:841
  68.6 17.2 %all-gather.5 = bf16[8,2,1920]{2,1,0:T(2,128)(2,1)S(1)} all-gather(bf16[1,2,1920]{2,1,0:T(2,128)(2,1)S(1)} %bitcast.478), channel_id=2, replica_groups=mesh['batch'=8,'seq'=4] {'batch'}, dimensions={0}, use_global_device_ids=true | all-gather | bytes 69120 | tf_op jit(solution)/shard_map/all_gather | solution.py:849
  106.9 39.2 %all-gather.1 = f32[32,1920]{1,0:T(8,128)S(1)} all-gather(f32[8,1920]{1,0:T(8,128)S(1)} %pad_maximum_fusion.65), channel_id=3, replica_groups=mesh['batch'=8,'seq'=4] {'seq'}, dimensions={0}, use_global_device_ids=true | all-gather | bytes 307200 | tf_op jit(solution)/shard_map/all_gather | solution.py:923
  180.3 10.0 collective-permute-done.2
  205.0 8.8 fusion.251
  213.8 8.3 fusion.250
  222.2 67.5 %all-gather.10.cloned.1.call-done = bf16[3072,1536]{1,0:T(8,128)(2,1)} async-done(((bf16[384,1536]{1,0:T(8,128)(2,1)}), bf16[3072,1536]{1,0:T(8,128)(2,1)}) %all-gather.10.cloned.1.call-update) | async-done | bytes 9437200 | tf_op jit(solution)/shard_map/all_gather | solution.py:849
  318.5 24.5 %attention.2 = (bf16[1024,384]{1,0:T(8,128)(2,1)S(1)}, bf16[192,384]{1,0:T(8,128)(2,1)S(1)}) custom-call(f32[1,1216]{1,0:T(1,128)S(1)} %get-tuple-element.279.bias_ref, f32[1,1]{1,0:T(1,128)} %bitcast.12.floor_ref, bf16[1024,1152]{1,0:T(8,128)(2,1)S(1)} %add_convert_fusion.3.qi.ki.vi, bf16[192,1152]{1,0:T(8,128)(2,1)S(1)} %fusion.45.qt.kt.vt, ...), custom_call_target="tpu_custom_call" | custom-call | flops 9084862464 | bytes 3735552 | tf_op jit(solution)/shard_map/attention/pallas_call | solution.py:605
  362.4 24.1 %attention.3 = (bf16[1024,384]{1,0:T(8,128)(2,1)S(1)}, bf16[192,384]{1,0:T(8,128)(2,1)S(1)}) custom-call(f32[1,1216]{1,0:T(1,128)S(1)} %get-tuple-element.280.bias_ref, f32[1,1]{1,0:T(1,128)} %bitcast.45.floor_ref, bf16[1024,1152]{1,0:T(8,128)(2,1)S(1)} %add_convert_fusion.2.qi.ki.vi, bf16[192,1152]{1,0:T(8,128)(2,1)S(1)} %fusion.46.qt.kt.vt, ...), custom_call_target="tpu_custom_call" | custom-call | flops 9084862464 | bytes 3735552 | tf_op jit(solution)/shard_map/attention/pallas_call | solution.py:605
  398.9 10.1 fusion.178
  419.5 15.9 %collective-permute-done.18 = bf16[304,1536]{1,0:T(8,128)(2,1)S(1)} collective-permute-done((bf16[304,1536]{1,0:T(8,128)(2,1)S(1)}, bf16[304,1536]{1,0:T(8,128)(2,1)S(1)}, u32[]{:S(2)}, u32[]{:S(2)}) %collective-permute-start.18) | collective-permute-done | bytes 933920 | tf_op jit(solution)/shard_map/ppermute | solution.py:732
  439.8 14.9 %collective-permute-done.10 = bf16[304,1536]{1,0:T(8,128)(2,1)S(1)} collective-permute-done((bf16[304,1536]{1,0:T(8,128)(2,1)S(1)}, bf16[304,1536]{1,0:T(8,128)(2,1)S(1)}, u32[]{:S(2)}, u32[]{:S(2)}) %collective-permute-start.10) | collective-permute-done | bytes 933920 | tf_op jit(solution)/shard_map/ppermute | solution.py:732
  468.4 15.5 %collective-permute-done.24 = bf16[304,1536]{1,0:T(8,128)(2,1)S(1)} collective-permute-done((bf16[304,1536]{1,0:T(8,128)(2,1)S(1)}, bf16[304,1536]{1,0:T(8,128)(2,1)S(1)}, u32[]{:S(2)}, u32[]{:S(2)}) %collective-permute-start.24) | collective-permute-done | bytes 933920 | tf_op jit(solution)/shard_map/ppermute | solution.py:732
  489.6 14.3 %collective-permute-done.20 = bf16[304,1536]{1,0:T(8,128)(2,1)S(1)} collective-permute-done((bf16[304,1536]{1,0:T(8,128)(2,1)S(1)}, bf16[304,1536]{1,0:T(8,128)(2,1)S(1)}, u32[]{:S(2)}, u32[]{:S(2)}) %collective-permute-start.20) | collective-permute-done | bytes 933920 | tf_op jit(solution)/shard_map/ppermute | solution.py:732
  536.5 14.9 %convert_reduce_fusion.5 = (f32[1536]{0:T(1024)}, bf16[1024,1536]{1,0:T(8,128)(2,1)}) fusion(f32[1024,1536]{1,0:T(8,128)} %copy-done.347, f32[1536]{0:T(1024)S(1)} %copy-done.322, bf16[1536,1536]{1,0:T(8,128)(2,1)S(1)} %bitcast.431, bf16[256,1536]{1,0:T(8,128)(2,1)S(1)} %copy-done.182, bf16[256,1536]{1,0:T(8,128)(2,1)S(1)} %copy-done.181, ...), kind=kOutput, calls=%fused_computation.66 | convolution fusion | flops 4883741184 | bytes 17319936 | tf_op jit(solution)/shard_map/dot_general | solution.py:554
  551.5 13.2 fusion.180
  591.9 9.1 convolution_convert_fusion.1
  601.0 15.2 %add_convert_fusion.1 = bf16[1536,1536]{1,0:T(8,128)(2,1)} fusion(f32[1536,1536]{1,0:T(8,128)} %fusion.180, bf16[256,1536]{1,0:T(8,128)(2,1)} %get-tuple-element.191, bf16[256,1536]{1,0:T(8,128)(2,1)} %get-tuple-element.189, bf16[256,1536]{1,0:T(8,128)(2,1)} %copy-done.176, bf16[256,1536]{1,0:T(8,128)(2,1)} %copy-done.179, f32[1536]{0:T(1024)} %get-tuple-element.81, ...), kind=kOutput, calls=%fused_computation.10 | convolution fusion | flops 4866441216 | bytes 23599104 | tf_op jit(solution)/shard_map/dot_general | solution.py:562
  679.9 10.4 add_convert_fusion
  707.3 8.4 pad_maximum_fusion.1
  745.8 24.0 %collective-permute-done.27 = bf16[304,768]{1,0:T(8,128)(2,1)S(1)} collective-permute-done((bf16[304,768]{1,0:T(8,128)(2,1)S(1)}, bf16[304,768]{1,0:T(8,128)(2,1)S(1)}, u32[]{:S(2)}, u32[]{:S(2)}) %collective-permute-start.27) | collective-permute-done | bytes 466976 | tf_op jit(solution)/shard_map/ppermute | solution.py:732
  777.9 21.3 %collective-permute-done.45 = bf16[304,768]{1,0:T(8,128)(2,1)S(1)} collective-permute-done((bf16[304,768]{1,0:T(8,128)(2,1)S(1)}, bf16[304,768]{1,0:T(8,128)(2,1)S(1)}, u32[]{:S(2)}, u32[]{:S(2)}) %collective-permute-start.45) | collective-permute-done | bytes 466976 | tf_op jit(solution)/shard_map/ppermute | solution.py:732
  805.1 47.2 %attention_back.2 = (bf16[1024,1152]{1,0:T(8,128)(2,1)S(1)}, bf16[192,1152]{1,0:T(8,128)(2,1)S(1)}) custom-call(f32[1216,128]{1,0:T(8,128)S(1)} %broadcast_in_dim.419.bias_ref, f32[1,1]{1,0:T(1,128)} %bitcast.12.floor_ref, bf16[1024,1152]{1,0:T(8,128)(2,1)} %copy-done.17, bf16[192,1152]{1,0:T(8,128)(2,1)S(1)} %copy-done.15, bf16[1024,1152]{1,0:T(8,128)(2,1)} %copy-done.17, ...), custom_call_target="tpu_custom_call" | custom-call | flops 22712156160 | bytes 7471104 | tf_op jit(solution)/shard_map/attention_back/pallas_call | solution.py:690
  852.4 10.0 fusion.16
  875.9 45.6 %collective-permute-done.47 = bf16[304,768]{1,0:T(8,128)(2,1)S(1)} collective-permute-done((bf16[304,768]{1,0:T(8,128)(2,1)S(1)}, bf16[304,768]{1,0:T(8,128)(2,1)S(1)}, u32[]{:S(2)}, u32[]{:S(2)}) %collective-permute-start.47) | collective-permute-done | bytes 466976 | tf_op jit(solution)/shard_map/ppermute | solution.py:732
  927.5 8.4 collective-permute-done.50
  935.9 9.5 collective-permute-done.48
  965.6 32.8 %collective-permute-done.31 = bf16[304,1536]{1,0:T(8,128)(2,1)S(1)} collective-permute-done((bf16[304,1536]{1,0:T(8,128)(2,1)S(1)}, bf16[304,1536]{1,0:T(8,128)(2,1)S(1)}, u32[]{:S(2)}, u32[]{:S(2)}) %collective-permute-start.31) | collective-permute-done | bytes 933920 | tf_op jit(solution)/shard_map/ppermute | solution.py:732
  1030.9 47.2 %attention_back.3 = (bf16[1024,1152]{1,0:T(8,128)(2,1)S(1)}, bf16[192,1152]{1,0:T(8,128)(2,1)S(1)}) custom-call(f32[1216,128]{1,0:T(8,128)S(1)} %broadcast_in_dim.423.bias_ref, f32[1,1]{1,0:T(1,128)} %bitcast.45.floor_ref, bf16[1024,1152]{1,0:T(8,128)(2,1)} %copy-done.16, bf16[192,1152]{1,0:T(8,128)(2,1)S(1)} %copy-done.13, bf16[1024,1152]{1,0:T(8,128)(2,1)} %copy-done.16, ...), custom_call_target="tpu_custom_call" | custom-call | flops 22712156160 | bytes 7471104 | tf_op jit(solution)/shard_map/attention_back/pallas_call | solution.py:690
  1134.4 10.7 fusion.17
  1207.5 15.9 %collective-permute-done.55 = f32[2,1536]{1,0:T(2,128)S(1)} collective-permute-done((f32[2,1536]{1,0:T(2,128)S(1)}, f32[2,1536]{1,0:T(2,128)S(1)}, u32[]{:S(2)}, u32[]{:S(2)}) %collective-permute-start.55) | collective-permute-done | bytes 12320 | tf_op jit(solution)/shard_map/ppermute | solution.py:732
  1252.2 53.6 %reduce-scatter.6.cloned.1.call-done = bf16[1,2,192,1536]{3,2,1,0:T(8,128)(2,1)} async-done(((bf16[8,2,192,1536]{3,2,1,0:T(8,128)(2,1)}), bf16[1,2,192,1536]{3,2,1,0:T(8,128)(2,1)}) %reduce-scatter.6.cloned.1.call-update) | async-done | bytes 1179664 | tf_op jit(solution)/shard_map/reduce_scatter | solution.py:853
  (1337 shorter events, 613.1 us)
Async XLA Ops:
  7.2 197.8 %all-gather.14.cloned.1.call-start = ((), (), s32[]{:S(2)}) async-start(), calls=%async_computation.14 | async-start | bytes 10616832 | tf_op jit(solution)/shard_map/all_gather | solution.py:849
  7.9 205.9 %all-gather.12.cloned.1.call-start = ((), (), s32[]{:S(2)}) async-start(), calls=%async_computation.13 | async-start | bytes 10616832 | tf_op jit(solution)/shard_map/all_gather | solution.py:849
  17.3 272.5 %all-gather.10.cloned.1.call-start = ((), (), s32[]{:S(2)}) async-start(), calls=%async_computation.12 | async-start | bytes 10616832 | tf_op jit(solution)/shard_map/all_gather | solution.py:849
  17.3 39.3 %collective-permute-start.6 = (bf16[1,2,48,1536]{3,2,1,0:T(8,128)(2,1)S(1)}, bf16[1,2,48,1536]{3,2,1,0:T(8,128)(2,1)S(1)}, u32[]{:S(2)}, u32[]{:S(2)}) collective-permute-start(bf16[1,2,48,1536]{3,2,1,0:T(8,128)(2,1)S(1)} %get-tuple-element.234), channel_id=1, source_target_pairs={{0,0},{1,4},{2,1},{3,5},{4,9},{5,2},{6,6},{7,10},{8,3},{9,7},{10,8... | collective-permute-start | bytes 884744 | tf_op jit(solution)/shard_map/ppermute | solution.py:841
  20.6 34.9 %collective-permute-start.5 = (bf16[1,2,48,1536]{3,2,1,0:T(8,128)(2,1)S(1)}, bf16[1,2,48,1536]{3,2,1,0:T(8,128)(2,1)}, u32[]{:S(2)}, u32[]{:S(2)}) collective-permute-start(bf16[1,2,48,1536]{3,2,1,0:T(8,128)(2,1)S(1)} %get-tuple-element.235), channel_id=1, source_target_pairs={{0,0},{1,4},{2,8},{3,1},{4,5},{5,2},{6,6},{7,10},{8,3},{9,7},{10,1... | collective-permute-start | bytes 884744 | tf_op jit(solution)/shard_map/ppermute | solution.py:841
  60.2 105.1 %collective-permute-start = (bf16[2,304,1536]{2,1,0:T(8,128)(2,1)}, bf16[2,304,1536]{2,1,0:T(8,128)(2,1)}, u32[]{:S(2)}, u32[]{:S(2)}) collective-permute-start(bf16[2,304,1536]{2,1,0:T(8,128)(2,1)} %pad_maximum_fusion.11), channel_id=1, source_target_pairs={{0,1},{1,0},{2,3},{3,2},{4,5},{5,4},{6,7},{7,6},{8,9},{9,8},{10,11... | collective-permute-start | bytes 5603336 | tf_op jit(solution)/shard_map/ppermute | solution.py:732
  60.3 107.0 %collective-permute-start.1 = (bf16[2,304,1536]{2,1,0:T(8,128)(2,1)}, bf16[2,304,1536]{2,1,0:T(8,128)(2,1)}, u32[]{:S(2)}, u32[]{:S(2)}) collective-permute-start(bf16[2,304,1536]{2,1,0:T(8,128)(2,1)} %pad_maximum_fusion.11), channel_id=1, source_target_pairs={{0,2},{1,3},{2,0},{3,1},{4,6},{5,7},{6,4},{7,5},{8,10},{9,11},{10,... | collective-permute-start | bytes 5603336 | tf_op jit(solution)/shard_map/ppermute | solution.py:732
  67.6 102.5 %collective-permute-start.12 = (bf16[2,304,1536]{2,1,0:T(8,128)(2,1)}, bf16[2,304,1536]{2,1,0:T(8,128)(2,1)}, u32[]{:S(2)}, u32[]{:S(2)}) collective-permute-start(bf16[2,304,1536]{2,1,0:T(8,128)(2,1)} %fusion.77), channel_id=1, source_target_pairs={{0,2},{1,3},{2,0},{3,1},{4,6},{5,7},{6,4},{7,5},{8,10},{9,11},{10,... | collective-permute-start | bytes 5603336 | tf_op jit(solution)/shard_map/ppermute | solution.py:732
  67.6 104.3 %collective-permute-start.11 = (bf16[2,304,1536]{2,1,0:T(8,128)(2,1)}, bf16[2,304,1536]{2,1,0:T(8,128)(2,1)}, u32[]{:S(2)}, u32[]{:S(2)}) collective-permute-start(bf16[2,304,1536]{2,1,0:T(8,128)(2,1)} %fusion.77), channel_id=1, source_target_pairs={{0,1},{1,0},{2,3},{3,2},{4,5},{5,4},{6,7},{7,6},{8,9},{9,8},{10,11... | collective-permute-start | bytes 5603336 | tf_op jit(solution)/shard_map/ppermute | solution.py:732
  93.4 1142.6 %reduce-scatter.8.cloned.1.call-start = ((), (), s32[]{:S(2)}) async-start(), calls=%async_computation.11 | async-start | bytes 10616832 | tf_op jit(solution)/shard_map/reduce_scatter | solution.py:853
  171.3 32.4 %collective-permute-start.14 = (bf16[2,304,768]{2,1,0:T(8,128)(2,1)S(1)}, bf16[2,304,768]{2,1,0:T(8,128)(2,1)S(1)}, u32[]{:S(2)}, u32[]{:S(2)}) collective-permute-start(bf16[2,304,768]{2,1,0:T(8,128)(2,1)S(1)} %slice.1540), channel_id=1, source_target_pairs={{0,1},{1,0},{2,3},{3,2},{4,5},{5,4},{6,7},{7,6},{8,9},{9,8},{10,11... | collective-permute-start | bytes 2801672 | tf_op jit(solution)/shard_map/ppermute | solution.py:732
  417.1 37.6 %collective-permute-start.10 = (bf16[304,1536]{1,0:T(8,128)(2,1)S(1)}, bf16[304,1536]{1,0:T(8,128)(2,1)S(1)}, u32[]{:S(2)}, u32[]{:S(2)}) collective-permute-start(bf16[304,1536]{1,0:T(8,128)(2,1)S(1)} %fusion.143), channel_id=1, source_target_pairs={{0,2},{1,3},{2,0},{3,1},{4,6},{5,7},{6,4},{7,5},{8,10},{9,11},{10,... | collective-permute-start | bytes 2801672 | tf_op jit(solution)/shard_map/ppermute | solution.py:732
  417.9 38.0 %collective-permute-start.8 = (bf16[304,1536]{1,0:T(8,128)(2,1)S(1)}, bf16[304,1536]{1,0:T(8,128)(2,1)S(1)}, u32[]{:S(2)}, u32[]{:S(2)}) collective-permute-start(bf16[304,1536]{1,0:T(8,128)(2,1)S(1)} %pad_maximum_fusion.20), channel_id=1, source_target_pairs={{0,1},{1,0},{2,3},{3,2},{4,5},{5,4},{6,7},{7,6},{8,9},{9,8},{10,11... | collective-permute-start | bytes 2801672 | tf_op jit(solution)/shard_map/ppermute | solution.py:732
  463.9 40.0 %collective-permute-start.20 = (bf16[304,1536]{1,0:T(8,128)(2,1)S(1)}, bf16[304,1536]{1,0:T(8,128)(2,1)S(1)}, u32[]{:S(2)}, u32[]{:S(2)}) collective-permute-start(bf16[304,1536]{1,0:T(8,128)(2,1)S(1)} %get-tuple-element.283), channel_id=1, source_target_pairs={{0,2},{1,3},{2,0},{3,1},{4,6},{5,7},{6,4},{7,5},{8,10},{9,11},{10,... | collective-permute-start | bytes 2801672 | tf_op jit(solution)/shard_map/ppermute | solution.py:732
  465.4 40.1 %collective-permute-start.19 = (bf16[304,1536]{1,0:T(8,128)(2,1)S(1)}, bf16[304,1536]{1,0:T(8,128)(2,1)S(1)}, u32[]{:S(2)}, u32[]{:S(2)}) collective-permute-start(bf16[304,1536]{1,0:T(8,128)(2,1)S(1)} %get-tuple-element.283), channel_id=1, source_target_pairs={{0,1},{1,0},{2,3},{3,2},{4,5},{5,4},{6,7},{7,6},{8,9},{9,8},{10,11... | collective-permute-start | bytes 2801672 | tf_op jit(solution)/shard_map/ppermute | solution.py:732
  629.1 609.8 %reduce-scatter.4.cloned.1.call-start = ((), (), s32[]{:S(2)}) async-start(), calls=%async_computation.9 | async-start | bytes 10616832 | tf_op jit(solution)/shard_map/reduce_scatter | solution.py:853
  663.5 205.0 %collective-permute-start.35 = (bf16[2,304,768]{2,1,0:T(8,128)(2,1)}, bf16[2,304,768]{2,1,0:T(8,128)(2,1)}, u32[]{:S(2)}, u32[]{:S(2)}) collective-permute-start(bf16[2,304,768]{2,1,0:T(8,128)(2,1)} %get-tuple-element.183), channel_id=1, source_target_pairs={{0,2},{1,3},{2,0},{3,1},{4,6},{5,7},{6,4},{7,5},{8,10},{9,11},{10,... | collective-permute-start | bytes 2801672 | tf_op jit(solution)/shard_map/ppermute | solution.py:732
  664.9 109.8 %collective-permute-start.37 = (bf16[2,304,768]{2,1,0:T(8,128)(2,1)}, bf16[2,304,768]{2,1,0:T(8,128)(2,1)}, u32[]{:S(2)}, u32[]{:S(2)}) collective-permute-start(bf16[2,304,768]{2,1,0:T(8,128)(2,1)} %get-tuple-element.184), channel_id=1, source_target_pairs={{0,1},{1,0},{2,3},{3,2},{4,5},{5,4},{6,7},{7,6},{8,9},{9,8},{10,11... | collective-permute-start | bytes 2801672 | tf_op jit(solution)/shard_map/ppermute | solution.py:732
  678.7 63.6 %collective-permute-start.29 = (bf16[304,768]{1,0:T(8,128)(2,1)}, bf16[304,768]{1,0:T(8,128)(2,1)}, u32[]{:S(2)}, u32[]{:S(2)}) collective-permute-start(bf16[304,768]{1,0:T(8,128)(2,1)} %get-tuple-element.221), channel_id=1, source_target_pairs={{0,1},{1,0},{2,3},{3,2},{4,5},{5,4},{6,7},{7,6},{8,9},{9,8},{10,11... | collective-permute-start | bytes 1400840 | tf_op jit(solution)/shard_map/ppermute | solution.py:732
  739.8 32.4 %collective-permute-start.43 = (bf16[304,1536]{1,0:T(8,128)(2,1)S(1)}, bf16[304,1536]{1,0:T(8,128)(2,1)S(1)}, u32[]{:S(2)}, u32[]{:S(2)}) collective-permute-start(bf16[304,1536]{1,0:T(8,128)(2,1)S(1)} %get-tuple-element.124), channel_id=1, source_target_pairs={{0,1},{1,0},{2,3},{3,2},{4,5},{5,4},{6,7},{7,6},{8,9},{9,8},{10,11... | collective-permute-start | bytes 2801672 | tf_op jit(solution)/shard_map/ppermute | solution.py:732
  769.8 153.1 %collective-permute-start.30 = (bf16[304,1536]{1,0:T(8,128)(2,1)}, bf16[304,1536]{1,0:T(8,128)(2,1)}, u32[]{:S(2)}, u32[]{:S(2)}) collective-permute-start(bf16[304,1536]{1,0:T(8,128)(2,1)} %fusion.147), channel_id=1, source_target_pairs={{0,2},{1,3},{2,0},{3,1},{4,6},{5,7},{6,4},{7,5},{8,10},{9,11},{10,... | collective-permute-start | bytes 2801672 | tf_op jit(solution)/shard_map/ppermute | solution.py:732
  774.7 149.4 %collective-permute-start.28 = (bf16[304,1536]{1,0:T(8,128)(2,1)}, bf16[304,1536]{1,0:T(8,128)(2,1)}, u32[]{:S(2)}, u32[]{:S(2)}) collective-permute-start(bf16[304,1536]{1,0:T(8,128)(2,1)} %pad_maximum_fusion.23), channel_id=1, source_target_pairs={{0,1},{1,0},{2,3},{3,2},{4,5},{5,4},{6,7},{7,6},{8,9},{9,8},{10,11... | collective-permute-start | bytes 2801672 | tf_op jit(solution)/shard_map/ppermute | solution.py:732
  867.7 131.5 %collective-permute-start.38 = (bf16[2,304,1536]{2,1,0:T(8,128)(2,1)S(1)}, bf16[2,304,1536]{2,1,0:T(8,128)(2,1)S(1)}, u32[]{:S(2)}, u32[]{:S(2)}) collective-permute-start(bf16[2,304,1536]{2,1,0:T(8,128)(2,1)S(1)} %fusion.79), channel_id=1, source_target_pairs={{0,2},{1,3},{2,0},{3,1},{4,6},{5,7},{6,4},{7,5},{8,10},{9,11},{10,... | collective-permute-start | bytes 5603336 | tf_op jit(solution)/shard_map/ppermute | solution.py:732
  869.9 51.5 %collective-permute-start.47 = (bf16[304,768]{1,0:T(8,128)(2,1)S(1)}, bf16[304,768]{1,0:T(8,128)(2,1)S(1)}, u32[]{:S(2)}, u32[]{:S(2)}) collective-permute-start(bf16[304,768]{1,0:T(8,128)(2,1)S(1)} %get-tuple-element.223), channel_id=1, source_target_pairs={{0,2},{1,3},{2,0},{3,1},{4,6},{5,7},{6,4},{7,5},{8,10},{9,11},{10,... | collective-permute-start | bytes 1400840 | tf_op jit(solution)/shard_map/ppermute | solution.py:732
  875.1 60.8 %collective-permute-start.50 = (bf16[304,1536]{1,0:T(8,128)(2,1)S(1)}, bf16[304,1536]{1,0:T(8,128)(2,1)S(1)}, u32[]{:S(2)}, u32[]{:S(2)}) collective-permute-start(bf16[304,1536]{1,0:T(8,128)(2,1)S(1)} %fusion.151), channel_id=1, source_target_pairs={{0,2},{1,3},{2,0},{3,1},{4,6},{5,7},{6,4},{7,5},{8,10},{9,11},{10,... | collective-permute-start | bytes 2801672 | tf_op jit(solution)/shard_map/ppermute | solution.py:732
  922.9 76.3 %collective-permute-start.36 = (bf16[2,304,1536]{2,1,0:T(8,128)(2,1)S(1)}, bf16[2,304,1536]{2,1,0:T(8,128)(2,1)S(1)}, u32[]{:S(2)}, u32[]{:S(2)}) collective-permute-start(bf16[2,304,1536]{2,1,0:T(8,128)(2,1)S(1)} %pad_maximum_fusion.14), channel_id=1, source_target_pairs={{0,1},{1,0},{2,3},{3,2},{4,5},{5,4},{6,7},{7,6},{8,9},{9,8},{10,11... | collective-permute-start | bytes 5603336 | tf_op jit(solution)/shard_map/ppermute | solution.py:732
  956.8 44.9 %collective-permute-start.32 = (bf16[304,1536]{1,0:T(8,128)(2,1)S(1)}, bf16[304,1536]{1,0:T(8,128)(2,1)S(1)}, u32[]{:S(2)}, u32[]{:S(2)}) collective-permute-start(bf16[304,1536]{1,0:T(8,128)(2,1)S(1)} %get-tuple-element.122), channel_id=1, source_target_pairs={{0,2},{1,3},{2,0},{3,1},{4,6},{5,7},{6,4},{7,5},{8,10},{9,11},{10,... | collective-permute-start | bytes 2801672 | tf_op jit(solution)/shard_map/ppermute | solution.py:732
  957.6 40.8 %collective-permute-start.31 = (bf16[304,1536]{1,0:T(8,128)(2,1)S(1)}, bf16[304,1536]{1,0:T(8,128)(2,1)S(1)}, u32[]{:S(2)}, u32[]{:S(2)}) collective-permute-start(bf16[304,1536]{1,0:T(8,128)(2,1)S(1)} %get-tuple-element.122), channel_id=1, source_target_pairs={{0,1},{1,0},{2,3},{3,2},{4,5},{5,4},{6,7},{7,6},{8,9},{9,8},{10,11... | collective-permute-start | bytes 2801672 | tf_op jit(solution)/shard_map/ppermute | solution.py:732
  1099.8 205.9 %reduce-scatter.6.cloned.1.call-start = ((), (), s32[]{:S(2)}) async-start(), calls=%async_computation.10 | async-start | bytes 10616832 | tf_op jit(solution)/shard_map/reduce_scatter | solution.py:853
  1240.9 71.7 %all-to-all-start.5 = ((bf16[4,2,48,384]{3,2,1,0:T(8,128)(2,1)}), bf16[4,2,48,384]{3,2,1,0:T(8,128)(2,1)S(1)}, u32[]{:S(2)}, u32[]{:S(2)}) async-start(bf16[4,2,48,384]{3,2,1,0:T(8,128)(2,1)} %reshape.582), calls=%async_computation.6 | async-start | bytes 589824 | tf_op jit(solution)/shard_map/all_to_all | solution.py:857
  1245.2 68.4 %collective-permute-start.58 = (bf16[1,2,48,1536]{3,2,0,1:T(8,128)(2,1)S(1)}, bf16[1,2,48,1536]{3,2,0,1:T(8,128)(2,1)S(1)}, u32[]{:S(2)}, u32[]{:S(2)}) collective-permute-start(bf16[1,2,48,1536]{3,2,0,1:T(8,128)(2,1)S(1)} %get-tuple-element.232), channel_id=1, source_target_pairs={{0,0},{4,1},{8,2},{1,3},{5,4},{2,5},{6,6},{10,7},{3,8},{7,9},{11,1... | collective-permute-start | bytes 884744 | tf_op jit(solution)/shard_map/ppermute | solution.py:841
  1247.1 66.4 %collective-permute-start.57 = (bf16[1,2,48,1536]{3,2,0,1:T(8,128)(2,1)}, bf16[1,2,48,1536]{3,2,0,1:T(8,128)(2,1)S(1)}, u32[]{:S(2)}, u32[]{:S(2)}) collective-permute-start(bf16[1,2,48,1536]{3,2,0,1:T(8,128)(2,1)} %get-tuple-element.233), channel_id=1, source_target_pairs={{0,0},{4,1},{8,2},{1,3},{5,4},{9,5},{2,6},{6,7},{3,8},{7,9},{11,10... | collective-permute-start | bytes 884744 | tf_op jit(solution)/shard_map/ppermute | solution.py:841
  (407 other events, 6904.6 us)
Sparse Core Ops, SparseCore 0:
  9.7 94.9 all-gather.13
  106.3 91.9 all-gather.11
  200.5 89.1 all-gather.9
  629.2 96.8 reduce-scatter.7
  1099.9 100.9 reduce-scatter.3
  1203.1 102.5 reduce-scatter.5

commit v3 on v2

--- a/solution.py
+++ b/solution.py
@@ -845,12 +845,27 @@
     return arrived
 
 
-def gather_batch(values):
-    return lax.all_gather(values, "batch", axis=0)
-
-
-def scatter_batch(values):
-    return lax.psum_scatter(values, "batch", scatter_dimension=0)
+def gather_rows_over_batch(values):
+    return lax.all_gather(values, "batch", axis=1, tiled=True)
+
+
+def gather_small(values, axis):
+    count = lax.axis_size(axis)
+    held = values[None]
+    bit = 1
+    while bit < count:
+        pairs = [(i, i ^ bit) for i in range(count)]
+        held = jnp.concatenate([held, lax.ppermute(held, axis, pairs)])
+        bit *= 2
+    return jnp.take(held, jnp.bitwise_xor(lax.axis_index(axis), jnp.arange(count)), axis=0)
+
+
+def after(values, *others):
+    return lax.optimization_barrier((values, others))[0]
+
+
+def scatter_rows_over_batch(values):
+    return lax.psum_scatter(values, "batch", scatter_dimension=1, tiled=True)
 
 
 def swap(values, axis):
@@ -906,7 +921,7 @@
     bias_widths = [array.shape[1] for array in (qv_bias, out_bias, up_bias, down_bias)]
     bias_ends = np.cumsum(bias_widths)
     own_biases = jnp.concatenate([qv_bias, out_bias, up_bias, down_bias], axis=1)
-    near = gather_batch(jnp.concatenate([conditioning, own_biases], axis=1))
+    near = gather_small(jnp.concatenate([conditioning, own_biases], axis=1), "batch")
     cond_all = near[:, :, :D].reshape(B * L, D)
     column_biases = near[:, :, D:].astype(F32)
     smooth_all = jax.nn.silu(cond_all.astype(F32)).astype(BF16)
@@ -920,7 +935,7 @@
     small = jnp.concatenate(
         [mod_came.reshape(B, 2 * L * mod_width), column_biases.reshape(B, -1)], axis=1
     )
-    small_all = lax.all_gather(small, "seq")
+    small_all = gather_small(small, "seq")
     modulation = (
         small_all[:, :, : 2 * L * mod_width]
         .reshape(S, B, 2, L, mod_width)
@@ -953,22 +968,14 @@
     qkv_units = jnp.swapaxes(qkv_weight, 1, 2).reshape(2, per_device, unit, D).swapaxes(0, 1)
     qkv_mine = move_units(qkv_units, perms, send, land, place).swapaxes(0, 1)
     out_units = jnp.swapaxes(out_weight, 1, 2).reshape(2, -1, S, own_width).transpose(2, 0, 1, 3)
-    out_mine = swap(out_units, "seq")
+    out_mine = swap(after(out_units, qkv_mine), "seq")
     out_columns = out_mine.shape[2]
-    heads_all = gather_batch(
-        jnp.concatenate([qkv_mine.reshape(-1, D), out_mine.reshape(-1, D)], axis=0)
-    )
-    up_all = gather_batch(jnp.swapaxes(up_weight, 1, 2))
-    down_all = gather_batch(jnp.swapaxes(down_weight, 1, 2))
     qkv_width = per_device * unit
-    qkv_rows = 2 * qkv_width
-    out_all = heads_all[:, qkv_rows:].reshape(B, S, 2, out_columns, own_width)
-    qkv_part = [
-        heads_all[:, t * qkv_width : (t + 1) * qkv_width].reshape(-1, D) for t in range(2)
-    ]
-    out_part = [out_all[:, :, t].reshape(D, own_width) for t in range(2)]
-    up_part = [up_all[:, t].reshape(-1, D) for t in range(2)]
-    down_part = [down_all[:, t].reshape(-1, D) for t in range(2)]
+    qkv_part = gather_rows_over_batch(qkv_mine.reshape(2, qkv_width, D))
+    out_rows = out_mine.transpose(1, 0, 2, 3).reshape(2, S * out_columns, own_width)
+    out_part = gather_rows_over_batch(after(out_rows, qkv_part))
+    up_part = gather_rows_over_batch(after(jnp.swapaxes(up_weight, 1, 2), out_part))
+    down_part = gather_rows_over_batch(after(jnp.swapaxes(down_weight, 1, 2), up_part))
     hidden_columns = up_weight.shape[2]
 
     order = jnp.bitwise_xor(seq_index, jnp.arange(S))
@@ -986,14 +993,14 @@
 
     own_tokens = jnp.concatenate([image_tokens, jnp.pad(text_tokens, pad)], axis=1)
     own_grads = jnp.concatenate([image_cotangent, jnp.pad(text_cotangent, pad)], axis=1)
-    token_blocks = gather_blocks(own_tokens)
-    grad_blocks = gather_blocks(own_grads)
+    token_blocks = gather_blocks(after(own_tokens, qkv_mine))
+    grad_blocks = gather_blocks(after(own_grads, token_blocks))
     tokens_all = [join_rows([block[s] for block in token_blocks], image_count) for s in range(L)]
 
     def by_row(vectors):
         return jnp.where(is_image, vectors[0][None, :], vectors[1][None, :])
 
-    first_norms, first_stats, qkvs, attended = ([], [], [], [])
+    first_norms, first_stats, qkvs, attended, partials = ([], [], [], [], [])
     for s in range(L):
         norms, stats, rows = ([], [], [])
         for t in range(2):
@@ -1007,16 +1014,16 @@
             norms.append(norm)
             stats.append((mean, inverse))
         if s == L - 1:
-            rows, grad_blocks = lax.optimization_barrier((rows, grad_blocks))
+            rows, grad_blocks, partials = lax.optimization_barrier((rows, grad_blocks, partials))
         first_norms.append(norms)
         first_stats.append(stats)
         qkvs.append(rows)
         attended.append(attention(rows[0], rows[1], key_bias[s], floors[s], head))
+        partials.append([dot_nt(attended[s][t], out_part[t]).astype(BF16) for t in range(2)])
     grads_all = [join_rows([block[s] for block in grad_blocks], image_count) for s in range(L)]
     projections, middles, middle_stats, second_all = ([], [], [], [])
     for s in range(L):
-        partial = [dot_nt(attended[s][t], out_part[t]).astype(BF16) for t in range(2)]
-        summed = scatter_blocks(split_rows(partial[0], partial[1], image_count, text_count))
+        summed = scatter_blocks(split_rows(*partials[s], image_count, text_count))
         pieces = [by_row(modulation[:, s, k]) for k in range(6)]
         projection = summed + by_row(out_bias_full)
         middle = own_tokens[s].astype(F32) + pieces[2] * projection
@@ -1032,9 +1039,6 @@
         for s in range(1, L):
             total = total + dot_tn(left[s][t], right[s][t])
         return total.astype(BF16)
-
-    def stack_columns(values, width):
-        return jnp.stack([value.reshape(B, width, D) for value in values], axis=1)
 
     hidden_acts, hidden_pres, mlp_grads = ([], [], [])
     for s in range(L):
@@ -1049,8 +1053,8 @@
         hidden_acts.append(acts)
         hidden_pres.append(pres)
         mlp_grads.append(grads)
-    down_sent = stack_columns([both(hidden_acts, mlp_grads, t) for t in range(2)], hidden_columns)
-    down_came = scatter_batch(down_sent)
+    down_sent = jnp.stack([both(hidden_acts, mlp_grads, t) for t in range(2)])
+    down_came = scatter_rows_over_batch(down_sent)
     late_pres, down_sent = lax.optimization_barrier((hidden_pres[-1], down_sent))
     hidden_pres[-1] = late_pres
     pre_grads, norm2_sums = ([], [])
@@ -1065,8 +1069,8 @@
         norm2_sums.append(
             scatter_blocks(split_rows(back[0], back[1], image_count, text_count))
         )
-    up_sent = stack_columns([both(pre_grads, second_all, t) for t in range(2)], hidden_columns)
-    up_came = scatter_batch(up_sent)
+    up_sent = jnp.stack([both(pre_grads, second_all, t) for t in range(2)])
+    up_came = scatter_rows_over_batch(up_sent)
     up_bias_sum = jnp.stack(
         [
             sum(jnp.sum(pre_grads[s][t].astype(F32), axis=0) for s in range(L))
@@ -1074,15 +1078,9 @@
         ]
     )
     mlp_parts = [
-        split_rows(
-            dot_nn(hidden_acts[s][0], down_part[0]).astype(BF16),
-            dot_nn(hidden_acts[s][1], down_part[1]).astype(BF16),
-            image_count,
-            text_count,
-        )
+        [dot_nn(hidden_acts[s][t], down_part[t]).astype(BF16) for t in range(2)]
         for s in range(L)
     ]
-    mlp_sums = scatter_blocks([jnp.stack([mlp_parts[s][r] for s in range(L)]) for r in range(4)])
 
     def row_sums(values):
         return jnp.stack(
@@ -1106,13 +1104,17 @@
         out_bias_sum = out_bias_sum + row_sums(low.astype(F32))
         middle_grads.append(middle_grad)
 
-    qkv_grads, norm1_sums = ([], [])
+    mlp_parts = after(mlp_parts, proj_all)
+    mlp_parts = [split_rows(*parts, image_count, text_count) for parts in mlp_parts]
+    mlp_sums = scatter_blocks([jnp.stack([mlp_parts[s][r] for s in range(L)]) for r in range(4)])
+
+    qkv_grads, norm1_parts = ([], [])
     for s in range(L):
         attended_grad = [dot_nn(proj_all[s][t], out_part[t]).astype(BF16) for t in range(2)]
         if s == 0:
-            attended_grad, up_sent = lax.optimization_barrier((attended_grad, up_sent))
+            attended_grad = after(attended_grad, up_sent)
         if s == L - 1:
-            attended_grad, mlp_sums = lax.optimization_barrier((attended_grad, mlp_sums))
+            attended_grad = after(attended_grad, mlp_sums, norm1_parts)
         grads = attention_back(
             qkvs[s][0], qkvs[s][1], attended_grad[0], attended_grad[1], key_bias[s], floors[s], head
         )
@@ -1127,24 +1129,16 @@
                     wide = wide * ((tokens_all[s][t].astype(F32) - mean) * inverse)
                 sums.append(jnp.sum(wide, axis=0))
             mod_grads[s][k] = jnp.stack(sums)
-        norm1_sums.append(
-            scatter_blocks(split_rows(back[0], back[1], image_count, text_count))
-        )
+        norm1_parts.append(split_rows(back[0], back[1], image_count, text_count))
+    norm1_sums = [scatter_blocks(parts) for parts in norm1_parts]
     out_sum = [both(proj_all, attended, t) for t in range(2)]
     qkv_sum = [both(qkv_grads, first_norms, t) for t in range(2)]
-    qkv_sent = stack_columns(qkv_sum, qkv_width).reshape(B, qkv_rows, D)
-    out_sent = jnp.stack(
-        [value.reshape(B, S, out_columns, own_width) for value in out_sum], axis=2
-    ).reshape(B, -1, D)
-    head_grads = scatter_batch(jnp.concatenate([qkv_sent, out_sent], axis=1))
+    out_came = scatter_rows_over_batch(after(jnp.stack(out_sum), up_came))
+    qkv_came = scatter_rows_over_batch(after(jnp.stack(qkv_sum), out_came))
     qkv_home = move_units(
-        head_grads[:qkv_rows].reshape(2, per_device, unit, D).swapaxes(0, 1),
-        back_perms,
-        land,
-        send,
-        place,
-    )
-    out_home = swap(head_grads[qkv_rows:].reshape(S, 2, out_columns, own_width), "seq")
+        qkv_came.reshape(2, per_device, unit, D).swapaxes(0, 1), back_perms, land, send, place
+    )
+    out_home = swap(out_came.reshape(2, S, out_columns, own_width).swapaxes(0, 1), "seq")
     qkv_weight_grad = qkv_home.swapaxes(0, 1).reshape(2, -1, D).swapaxes(1, 2).astype(F32)
     out_weight_grad = (
         out_home.transpose(1, 2, 0, 3).reshape(2, out_columns, D).swapaxes(1, 2).astype(F32)

time: 1350 us -> 1170 us (0.87)
  waiting for transfers between devices: 414 us -> 320 us
  blocking collectives: 56.3 us -> 0 us
  local copies, waits for them, and re-layouts: 169 us -> 147 us
    all_gather x2 -> x0, blocking collectives: 56.3 us -> none  [the longest x1 39.2 us: swift_layer(): small_all = lax.all_gather(small, 'seq')]
    reduce_scatter x3 -> x4, waiting for transfers between devices: 53.6 us -> 9.63 us  [scatter_rows_over_batch(): return lax.psum_scatter(values, 'batch', scatter_dimension=1, tiled=True)]
    all_gather x3 -> x4, waiting for transfers between devices: 67.6 us -> 29.7 us  [gather_rows_over_batch(): return lax.all_gather(values, 'batch', axis=1, tiled=True)]
    slice x9 -> x0, local copies, waits for them, and re-layouts: 31 us -> none  [the longest x1 8.79 us: swift_layer(): up_part = [up_all[:, t].reshape(-1, D) for t in range(2)]]
    ppermute x6, waiting for transfers between devices: 27.5 us -> 8.65 us  [move_units(): lax.ppermute(lax.dynamic_index_in_dim(units, slot, 0, keepdims=True), ('b...]
  transfers between devices with their start and end apart: 72 -> 79, of which waited for: 31 -> 32; matrix products, arithmetic and copies ran while one was open for 30% -> 45% of each run, Pallas kernels for 7% -> 12%
where the time goes in v3:
time: 1170 us; the launch traced here: 1150 us
  waiting for transfers between devices  320 us (27%)
  matrix products  237 us (20%)
  other arithmetic  158 us (14%)
  local copies, waits for them, and re-layouts  147 us (13%)
  Pallas kernels  143 us (12%)
  starting transfers between devices  122 us (10%)
  between operations  25.9 us (2%)
    ppermute x54, waiting for transfers between devices, flip(): return lax.ppermute(values, 'seq', [(i, i ^ bit) for i in range(4)])  254 us
    pallas_call x2, Pallas kernels, attention_back(): pl.pallas_call(functools.partial(attention_back_kernel, 256, LOG2E / math...  94.1 us
    dot_general x16, matrix products, dot_nt(): lax.dot_general(a, b, (((1,), (1,)), ((), ())), preferred_element_type=F32)  84.9 us
    dot_general x16, matrix products, dot_tn(): lax.dot_general(a, b, (((0,), (0,)), ((), ())), preferred_element_type=F32)  75.7 us
    dot_general x16, matrix products, dot_nn(): lax.dot_general(a, b, (((1,), (0,)), ((), ())), preferred_element_type=F32)  72.4 us
    ppermute x54, starting transfers between devices, flip(): return lax.ppermute(values, 'seq', [(i, i ^ bit) for i in range(4)])  57.5 us
    pallas_call x2, Pallas kernels, attention(): pl.pallas_call(functools.partial(attention_kernel, 256, LOG2E / math.sqrt...  48.9 us
    all_to_all x6, starting transfers between devices, swap(): return lax.all_to_all(values, axis, 0, 0, tiled=True)  36.1 us
  transfers between devices with their start and end apart: 79, of which 32 were waited for; matrix products, arithmetic and copies ran while one was open for 45% of the time, Pallas kernels for 12%

profile of v3, /device:TPU:16, one launch (start us, length us, event | category | flops | bytes accessed | tf_op | source)
XLA Modules:
  0.0 1153.0 jit_solution(18212978221028046025)
XLA Ops:
  67.2 8.8 all-to-all-start
  76.8 29.7 %all-gather.5.cloned.1.call-done = bf16[2,1152,1536]{2,1,0:T(8,128)(2,1)} async-done(((bf16[2,144,1536]{2,1,0:T(8,128)(2,1)}), bf16[2,1152,1536]{2,1,0:T(8,128)(2,1)}) %all-gather.5.cloned.1.call-update) | async-done | bytes 7077904 | tf_op jit(solution)/shard_map/all_gather | solution.py:849
  139.2 19.1 %collective-permute-done.9 = bf16[2,304,1536]{2,1,0:T(8,128)(2,1)} collective-permute-done((bf16[2,304,1536]{2,1,0:T(8,128)(2,1)}, bf16[2,304,1536]{2,1,0:T(8,128)(2,1)}, u32[]{:S(2)}, u32[]{:S(2)}) %collective-permute-start.9) | collective-permute-done | bytes 1867808 | tf_op jit(solution)/shard_map/ppermute | solution.py:732
  170.5 14.3 %collective-permute-done.10 = bf16[2,304,768]{2,1,0:T(8,128)(2,1)} collective-permute-done((bf16[2,304,768]{2,1,0:T(8,128)(2,1)}, bf16[2,304,768]{2,1,0:T(8,128)(2,1)}, u32[]{:S(2)}, u32[]{:S(2)}) %collective-permute-start.10) | collective-permute-done | bytes 933920 | tf_op jit(solution)/shard_map/ppermute | solution.py:732
  193.7 34.1 %collective-permute-done.13 = bf16[2,304,1536]{2,1,0:T(8,128)(2,1)S(1)} collective-permute-done((bf16[2,304,1536]{2,1,0:T(8,128)(2,1)S(1)}, bf16[2,304,1536]{2,1,0:T(8,128)(2,1)S(1)}, u32[]{:S(2)}, u32[]{:S(2)}) %collective-permute-start.13) | collective-permute-done | bytes 1867808 | tf_op jit(solution)/shard_map/ppermute | solution.py:732
  233.8 13.2 %collective-permute-done.15 = bf16[2,304,768]{2,1,0:T(8,128)(2,1)S(1)} collective-permute-done((bf16[2,304,768]{2,1,0:T(8,128)(2,1)S(1)}, bf16[2,304,768]{2,1,0:T(8,128)(2,1)S(1)}, u32[]{:S(2)}, u32[]{:S(2)}) %collective-permute-start.15) | collective-permute-done | bytes 933920 | tf_op jit(solution)/shard_map/ppermute | solution.py:732
  255.8 24.6 %attention.2 = (bf16[1024,384]{1,0:T(8,128)(2,1)S(1)}, bf16[192,384]{1,0:T(8,128)(2,1)S(1)}) custom-call(f32[1,1216]{1,0:T(1,128)S(1)} %get-tuple-element.289.bias_ref, f32[1,1]{1,0:T(1,128)} %bitcast.40.floor_ref, bf16[1024,1152]{1,0:T(8,128)(2,1)S(1)} %add_convert_fusion.2.qi.ki.vi, bf16[192,1152]{1,0:T(8,128)(2,1)S(1)} %fusion.72.qt.kt.vt, ...), custom_call_target="tpu_custom_call" | custom-call | flops 9084862464 | bytes 3735552 | tf_op jit(solution)/shard_map/attention/pallas_call | solution.py:605
  294.0 24.4 %attention.3 = (bf16[1024,384]{1,0:T(8,128)(2,1)S(1)}, bf16[192,384]{1,0:T(8,128)(2,1)S(1)}) custom-call(f32[1,1216]{1,0:T(1,128)S(1)} %get-tuple-element.288.bias_ref, f32[1,1]{1,0:T(1,128)} %bitcast.63.floor_ref, bf16[1024,1152]{1,0:T(8,128)(2,1)S(1)} %add_convert_fusion.3.qi.ki.vi, bf16[192,1152]{1,0:T(8,128)(2,1)S(1)} %fusion.71.qt.kt.vt, ...), custom_call_target="tpu_custom_call" | custom-call | flops 9084862464 | bytes 3735552 | tf_op jit(solution)/shard_map/attention/pallas_call | solution.py:605
  343.9 14.8 %collective-permute-done.19 = bf16[304,1536]{1,0:T(8,128)(2,1)S(1)} collective-permute-done((bf16[304,1536]{1,0:T(8,128)(2,1)S(1)}, bf16[304,1536]{1,0:T(8,128)(2,1)S(1)}, u32[]{:S(2)}, u32[]{:S(2)}) %collective-permute-start.19) | collective-permute-done | bytes 933920 | tf_op jit(solution)/shard_map/ppermute | solution.py:732
  359.2 15.7 %collective-permute-done.27 = bf16[304,1536]{1,0:T(8,128)(2,1)S(1)} collective-permute-done((bf16[304,1536]{1,0:T(8,128)(2,1)S(1)}, bf16[304,1536]{1,0:T(8,128)(2,1)S(1)}, u32[]{:S(2)}, u32[]{:S(2)}) %collective-permute-start.27) | collective-permute-done | bytes 933920 | tf_op jit(solution)/shard_map/ppermute | solution.py:732
  388.6 18.3 %collective-permute-done.28 = bf16[304,1536]{1,0:T(8,128)(2,1)S(1)} collective-permute-done((bf16[304,1536]{1,0:T(8,128)(2,1)S(1)}, bf16[304,1536]{1,0:T(8,128)(2,1)S(1)}, u32[]{:S(2)}, u32[]{:S(2)}) %collective-permute-start.28) | collective-permute-done | bytes 933920 | tf_op jit(solution)/shard_map/ppermute | solution.py:732
  409.8 18.6 %collective-permute-done.21 = bf16[304,1536]{1,0:T(8,128)(2,1)S(1)} collective-permute-done((bf16[304,1536]{1,0:T(8,128)(2,1)S(1)}, bf16[304,1536]{1,0:T(8,128)(2,1)S(1)}, u32[]{:S(2)}, u32[]{:S(2)}) %collective-permute-start.21) | collective-permute-done | bytes 933920 | tf_op jit(solution)/shard_map/ppermute | solution.py:732
  462.1 13.6 %convolution_add_fusion.4 = f32[1024,1536]{1,0:T(8,128)} fusion(f32[1536]{0:T(1024)S(1)} %copy-done.290, bf16[2,1536,1536]{2,1,0:T(8,128)(2,1)} %all-gather.9.cloned.1.call-done, bf16[256,1536]{1,0:T(8,128)(2,1)S(1)} %slice.1583, bf16[256,1536]{1,0:T(8,128)(2,1)S(1)} %slice.1580, bf16[256,1536]{1,0:T(8,128)(2,1)S(1)} %slice.1579, ...), kind=kOutput, calls=%fused_computation.83 | convolution fusion | flops 4845993984 | bytes 14161920 | tf_op jit(solution)/shard_map/dot_general | solution.py:554
  475.8 11.0 fusion.200
  486.8 13.8 %fusion.14 = bf16[1,1536,1536]{2,1,0:T(8,128)(2,1)} fusion(f32[1536,1536]{1,0:T(8,128)} %fusion.200, bf16[256,1536]{1,0:T(8,128)(2,1)S(1)} %get-tuple-element.204, bf16[256,1536]{1,0:T(8,128)(2,1)S(1)} %get-tuple-element.202, bf16[256,1536]{1,0:T(8,128)(2,1)S(1)} %copy-done.156, bf16[256,1536]{1,0:T(8,128)(2,1)S(1)} %get-tuple-element.198, ...), kind=kOutput, calls=%fused_computation.40 | convolution fusion | flops 4866441216 | bytes 23599104 | tf_op jit(solution)/shard_map/dot_general | solution.py:562
  500.6 8.2 pad_maximum_fusion
  525.3 14.7 %convert_reduce_fusion.5 = (f32[1536]{0:T(1024)S(1)}, bf16[1024,1536]{1,0:T(8,128)(2,1)S(1)}) fusion(f32[1024,1536]{1,0:T(8,128)} %copy-done.315, f32[1536]{0:T(1024)S(1)} %copy-done.291, bf16[2,1536,1536]{2,1,0:T(8,128)(2,1)} %all-gather.11.cloned.1.call-done, bf16[256,1536]{1,0:T(8,128)(2,1)S(1)} %copy-done.167, bf16[256,1536]{1,0:T(8,128)(2,1)S(1)} %copy-done.165, ...), kind=kOutput, calls=%fused_computation.73 | convolution fusion | flops 4883741184 | bytes 17321984 | tf_op jit(solution)/shard_map/dot_general | solution.py:554
  551.5 15.7 %convert_reduce_fusion.4 = (f32[1536]{0:T(1024)S(1)}, bf16[1024,1536]{1,0:T(8,128)(2,1)}) fusion(f32[1024,1536]{1,0:T(8,128)} %convolution_add_fusion.4, bf16[2,1536,1536]{2,1,0:T(8,128)(2,1)} %all-gather.11.cloned.1.call-done, bf16[256,1536]{1,0:T(8,128)(2,1)S(1)} %copy-done.163, bf16[256,1536]{1,0:T(8,128)(2,1)S(1)} %copy-done.161, ...), kind=kOutput, calls=%fused_computation.72 | convolution fusion | flops 4882168320 | bytes 17315840 | tf_op jit(solution)/shard_map/dot_general | solution.py:554
  577.8 7.8 convolution_convert_fusion
  604.0 7.5 fusion.15
  611.5 8.2 pad_maximum_fusion.1
  625.9 11.1 convolution_convert_fusion.4
  655.5 15.2 %collective-permute-done.35 = bf16[304,1536]{1,0:T(8,128)(2,1)S(1)} collective-permute-done((bf16[304,1536]{1,0:T(8,128)(2,1)S(1)}, bf16[304,1536]{1,0:T(8,128)(2,1)S(1)}, u32[]{:S(2)}, u32[]{:S(2)}) %collective-permute-start.35) | collective-permute-done | bytes 933920 | tf_op jit(solution)/shard_map/ppermute | solution.py:732
  674.4 9.7 collective-permute-done.43
  735.6 14.7 %collective-permute-done.37 = bf16[304,1536]{1,0:T(8,128)(2,1)} collective-permute-done((bf16[304,1536]{1,0:T(8,128)(2,1)S(1)}, bf16[304,1536]{1,0:T(8,128)(2,1)}, u32[]{:S(2)}, u32[]{:S(2)}) %collective-permute-start.37) | collective-permute-done | bytes 933920 | tf_op jit(solution)/shard_map/ppermute | solution.py:732
  792.5 47.1 %attention_back.2 = (bf16[1024,1152]{1,0:T(8,128)(2,1)S(1)}, bf16[192,1152]{1,0:T(8,128)(2,1)S(1)}) custom-call(f32[1216,128]{1,0:T(8,128)S(1)} %broadcast_in_dim.451.bias_ref, f32[1,1]{1,0:T(1,128)} %bitcast.40.floor_ref, bf16[1024,1152]{1,0:T(8,128)(2,1)} %copy-done.16, bf16[192,1152]{1,0:T(8,128)(2,1)S(1)} %copy-done.14, bf16[1024,1152]{1,0:T(8,128)(2,1)} %copy-done.16, ...), custom_call_target="tpu_custom_call" | custom-call | flops 22712156160 | bytes 7471104 | tf_op jit(solution)/shard_map/attention_back/pallas_call | solution.py:690
  901.0 18.3 %collective-permute-done.51 = bf16[2,304,1536]{2,1,0:T(8,128)(2,1)} collective-permute-done((bf16[2,304,1536]{2,1,0:T(8,128)(2,1)}, bf16[2,304,1536]{2,1,0:T(8,128)(2,1)}, u32[]{:S(2)}, u32[]{:S(2)}) %collective-permute-start.51) | collective-permute-done | bytes 1867808 | tf_op jit(solution)/shard_map/ppermute | solution.py:732
  927.6 47.0 %attention_back.3 = (bf16[1024,1152]{1,0:T(8,128)(2,1)S(1)}, bf16[192,1152]{1,0:T(8,128)(2,1)S(1)}) custom-call(f32[1216,128]{1,0:T(8,128)S(1)} %broadcast_in_dim.455.bias_ref, f32[1,1]{1,0:T(1,128)} %bitcast.63.floor_ref, bf16[1024,1152]{1,0:T(8,128)(2,1)} %copy-done.15, bf16[192,1152]{1,0:T(8,128)(2,1)S(1)} %copy-done.12, bf16[1024,1152]{1,0:T(8,128)(2,1)} %copy-done.15, ...), custom_call_target="tpu_custom_call" | custom-call | flops 22712156160 | bytes 7471104 | tf_op jit(solution)/shard_map/attention_back/pallas_call | solution.py:690
  974.6 7.6 fusion.23
  1011.3 9.6 reduce-scatter.7.cloned.1.call-done
  1043.0 10.0 all-to-all-start.3
  1079.0 16.7 %collective-permute-done.60 = f32[2,1536]{1,0:T(2,128)S(1)} collective-permute-done((f32[2,1536]{1,0:T(2,128)S(1)}, f32[2,1536]{1,0:T(2,128)S(1)}, u32[]{:S(2)}, u32[]{:S(2)}) %collective-permute-start.60) | collective-permute-done | bytes 12320 | tf_op jit(solution)/shard_map/ppermute | solution.py:732
  (1275 shorter events, 584.1 us)
Async XLA Ops:
  7.2 99.3 %all-gather.5.cloned.1.call-start = ((), (), s32[]{:S(2)}) async-start(), calls=%async_computation.10 | async-start | bytes 7962624 | tf_op jit(solution)/shard_map/all_gather | solution.py:849
  67.2 39.4 %all-to-all-start = ((f32[8,2,2,288]{3,2,1,0:T(2,128)}), f32[8,2,2,288]{3,2,1,0:T(2,128)S(1)}, u32[]{:S(2)}, u32[]{:S(2)}) async-start(f32[8,2,2,288]{3,2,1,0:T(2,128)} %bitcast.430), calls=%async_computation | async-start | bytes 98304 | tf_op jit(solution)/shard_map/all_to_all | solution.py:872
  76.0 88.5 %all-gather.7.cloned.1.call-start = ((), (), s32[]{:S(2)}) async-start(), calls=%async_computation.11 | async-start | bytes 2654208 | tf_op jit(solution)/shard_map/all_gather | solution.py:849
  106.5 224.8 %all-gather.9.cloned.1.call-start = ((), (), s32[]{:S(2)}) async-start(), calls=%async_computation.12 | async-start | bytes 10616832 | tf_op jit(solution)/shard_map/all_gather | solution.py:849
  116.6 41.7 %collective-permute-start.9 = (bf16[2,304,1536]{2,1,0:T(8,128)(2,1)}, bf16[2,304,1536]{2,1,0:T(8,128)(2,1)}, u32[]{:S(2)}, u32[]{:S(2)}) collective-permute-start(bf16[2,304,1536]{2,1,0:T(8,128)(2,1)} %fusion.103), channel_id=1, source_target_pairs={{0,2},{1,3},{2,0},{3,1},{4,6},{5,7},{6,4},{7,5},{8,10},{9,11},{10,... | collective-permute-start | bytes 5603336 | tf_op jit(solution)/shard_map/ppermute | solution.py:732
  117.2 44.9 %collective-permute-start.8 = (bf16[2,304,1536]{2,1,0:T(8,128)(2,1)}, bf16[2,304,1536]{2,1,0:T(8,128)(2,1)}, u32[]{:S(2)}, u32[]{:S(2)}) collective-permute-start(bf16[2,304,1536]{2,1,0:T(8,128)(2,1)} %fusion.103), channel_id=1, source_target_pairs={{0,1},{1,0},{2,3},{3,2},{4,5},{5,4},{6,7},{7,6},{8,9},{9,8},{10,11... | collective-permute-start | bytes 5603336 | tf_op jit(solution)/shard_map/ppermute | solution.py:732
  164.6 351.5 %all-gather.11.cloned.1.call-start = ((), (), s32[]{:S(2)}) async-start(), calls=%async_computation.13 | async-start | bytes 10616832 | tf_op jit(solution)/shard_map/all_gather | solution.py:849
  187.3 40.5 %collective-permute-start.13 = (bf16[2,304,1536]{2,1,0:T(8,128)(2,1)S(1)}, bf16[2,304,1536]{2,1,0:T(8,128)(2,1)S(1)}, u32[]{:S(2)}, u32[]{:S(2)}) collective-permute-start(bf16[2,304,1536]{2,1,0:T(8,128)(2,1)S(1)} %copy-done.23), channel_id=1, source_target_pairs={{0,2},{1,3},{2,0},{3,1},{4,6},{5,7},{6,4},{7,5},{8,10},{9,11},{10,... | collective-permute-start | bytes 5603336 | tf_op jit(solution)/shard_map/ppermute | solution.py:732
  187.9 40.9 %collective-permute-start.12 = (bf16[2,304,1536]{2,1,0:T(8,128)(2,1)S(1)}, bf16[2,304,1536]{2,1,0:T(8,128)(2,1)S(1)}, u32[]{:S(2)}, u32[]{:S(2)}) collective-permute-start(bf16[2,304,1536]{2,1,0:T(8,128)(2,1)S(1)} %copy-done.23), channel_id=1, source_target_pairs={{0,1},{1,0},{2,3},{3,2},{4,5},{5,4},{6,7},{7,6},{8,9},{9,8},{10,11... | collective-permute-start | bytes 5603336 | tf_op jit(solution)/shard_map/ppermute | solution.py:732
  292.2 42.0 %collective-permute-start.16 = (bf16[304,768]{1,0:T(8,128)(2,1)}, bf16[304,768]{1,0:T(8,128)(2,1)}, u32[]{:S(2)}, u32[]{:S(2)}) collective-permute-start(bf16[304,768]{1,0:T(8,128)(2,1)} %get-tuple-element.238), channel_id=1, source_target_pairs={{0,2},{1,3},{2,0},{3,1},{4,6},{5,7},{6,4},{7,5},{8,10},{9,11},{10,... | collective-permute-start | bytes 1400840 | tf_op jit(solution)/shard_map/ppermute | solution.py:732
  331.3 437.4 %reduce-scatter.11.cloned.1.call-start = ((), (), s32[]{:S(2)}) async-start(), calls=%async_computation.17 | async-start | bytes 10616832 | tf_op jit(solution)/shard_map/reduce_scatter | solution.py:868
  337.4 37.6 %collective-permute-start.27 = (bf16[304,1536]{1,0:T(8,128)(2,1)S(1)}, bf16[304,1536]{1,0:T(8,128)(2,1)S(1)}, u32[]{:S(2)}, u32[]{:S(2)}) collective-permute-start(bf16[304,1536]{1,0:T(8,128)(2,1)S(1)} %fusion.168), channel_id=1, source_target_pairs={{0,2},{1,3},{2,0},{3,1},{4,6},{5,7},{6,4},{7,5},{8,10},{9,11},{10,... | collective-permute-start | bytes 2801672 | tf_op jit(solution)/shard_map/ppermute | solution.py:732
  386.1 42.3 %collective-permute-start.21 = (bf16[304,1536]{1,0:T(8,128)(2,1)S(1)}, bf16[304,1536]{1,0:T(8,128)(2,1)S(1)}, u32[]{:S(2)}, u32[]{:S(2)}) collective-permute-start(bf16[304,1536]{1,0:T(8,128)(2,1)S(1)} %get-tuple-element.295), channel_id=1, source_target_pairs={{0,2},{1,3},{2,0},{3,1},{4,6},{5,7},{6,4},{7,5},{8,10},{9,11},{10,... | collective-permute-start | bytes 2801672 | tf_op jit(solution)/shard_map/ppermute | solution.py:732
  386.7 42.6 %collective-permute-start.20 = (bf16[304,1536]{1,0:T(8,128)(2,1)S(1)}, bf16[304,1536]{1,0:T(8,128)(2,1)S(1)}, u32[]{:S(2)}, u32[]{:S(2)}) collective-permute-start(bf16[304,1536]{1,0:T(8,128)(2,1)S(1)} %get-tuple-element.295), channel_id=1, source_target_pairs={{0,1},{1,0},{2,3},{3,2},{4,5},{5,4},{6,7},{7,6},{8,9},{9,8},{10,11... | collective-permute-start | bytes 2801672 | tf_op jit(solution)/shard_map/ppermute | solution.py:732
  508.9 474.8 %reduce-scatter.5.cloned.1.call-start = ((), (), s32[]{:S(2)}) async-start(), calls=%async_computation.14 | async-start | bytes 10616832 | tf_op jit(solution)/shard_map/reduce_scatter | solution.py:868
  549.1 99.5 %collective-permute-start.32 = (bf16[304,768]{1,0:T(8,128)(2,1)}, bf16[304,768]{1,0:T(8,128)(2,1)}, u32[]{:S(2)}, u32[]{:S(2)}) collective-permute-start(bf16[304,768]{1,0:T(8,128)(2,1)} %get-tuple-element.234), channel_id=1, source_target_pairs={{0,2},{1,3},{2,0},{3,1},{4,6},{5,7},{6,4},{7,5},{8,10},{9,11},{10,... | collective-permute-start | bytes 1400840 | tf_op jit(solution)/shard_map/ppermute | solution.py:732
  550.7 95.0 %collective-permute-start.34 = (bf16[304,768]{1,0:T(8,128)(2,1)}, bf16[304,768]{1,0:T(8,128)(2,1)}, u32[]{:S(2)}, u32[]{:S(2)}) collective-permute-start(bf16[304,768]{1,0:T(8,128)(2,1)} %get-tuple-element.235), channel_id=1, source_target_pairs={{0,1},{1,0},{2,3},{3,2},{4,5},{5,4},{6,7},{7,6},{8,9},{9,8},{10,11... | collective-permute-start | bytes 1400840 | tf_op jit(solution)/shard_map/ppermute | solution.py:732
  588.0 64.9 %collective-permute-start.40 = (bf16[304,768]{1,0:T(8,128)(2,1)}, bf16[304,768]{1,0:T(8,128)(2,1)}, u32[]{:S(2)}, u32[]{:S(2)}) collective-permute-start(bf16[304,768]{1,0:T(8,128)(2,1)} %get-tuple-element.236), channel_id=1, source_target_pairs={{0,2},{1,3},{2,0},{3,1},{4,6},{5,7},{6,4},{7,5},{8,10},{9,11},{10,... | collective-permute-start | bytes 1400840 | tf_op jit(solution)/shard_map/ppermute | solution.py:732
  588.5 62.5 %collective-permute-start.42 = (bf16[304,768]{1,0:T(8,128)(2,1)}, bf16[304,768]{1,0:T(8,128)(2,1)}, u32[]{:S(2)}, u32[]{:S(2)}) collective-permute-start(bf16[304,768]{1,0:T(8,128)(2,1)} %get-tuple-element.237), channel_id=1, source_target_pairs={{0,1},{1,0},{2,3},{3,2},{4,5},{5,4},{6,7},{7,6},{8,9},{9,8},{10,11... | collective-permute-start | bytes 1400840 | tf_op jit(solution)/shard_map/ppermute | solution.py:732
  619.7 401.2 %reduce-scatter.7.cloned.1.call-start = ((), (), s32[]{:S(2)}) async-start(), calls=%async_computation.15 | async-start | bytes 2654208 | tf_op jit(solution)/shard_map/reduce_scatter | solution.py:868
  707.9 42.4 %collective-permute-start.37 = (bf16[304,1536]{1,0:T(8,128)(2,1)S(1)}, bf16[304,1536]{1,0:T(8,128)(2,1)}, u32[]{:S(2)}, u32[]{:S(2)}) collective-permute-start(bf16[304,1536]{1,0:T(8,128)(2,1)S(1)} %get-tuple-element.293), channel_id=1, source_target_pairs={{0,2},{1,3},{2,0},{3,1},{4,6},{5,7},{6,4},{7,5},{8,10},{9,11},{10,... | collective-permute-start | bytes 2801672 | tf_op jit(solution)/shard_map/ppermute | solution.py:732
  709.2 43.8 %collective-permute-start.36 = (bf16[304,1536]{1,0:T(8,128)(2,1)S(1)}, bf16[304,1536]{1,0:T(8,128)(2,1)}, u32[]{:S(2)}, u32[]{:S(2)}) collective-permute-start(bf16[304,1536]{1,0:T(8,128)(2,1)S(1)} %get-tuple-element.293), channel_id=1, source_target_pairs={{0,1},{1,0},{2,3},{3,2},{4,5},{5,4},{6,7},{7,6},{8,9},{9,8},{10,11... | collective-permute-start | bytes 2801672 | tf_op jit(solution)/shard_map/ppermute | solution.py:732
  732.1 40.7 %collective-permute-start.47 = (bf16[304,768]{1,0:T(8,128)(2,1)}, bf16[304,768]{1,0:T(8,128)(2,1)}, u32[]{:S(2)}, u32[]{:S(2)}) collective-permute-start(bf16[304,768]{1,0:T(8,128)(2,1)} %slice.1634), channel_id=1, source_target_pairs={{0,1},{1,0},{2,3},{3,2},{4,5},{5,4},{6,7},{7,6},{8,9},{9,8},{10,11... | collective-permute-start | bytes 1400840 | tf_op jit(solution)/shard_map/ppermute | solution.py:732
  787.2 97.3 %collective-permute-start.48 = (bf16[2,304,768]{2,1,0:T(8,128)(2,1)}, bf16[2,304,768]{2,1,0:T(8,128)(2,1)}, u32[]{:S(2)}, u32[]{:S(2)}) collective-permute-start(bf16[2,304,768]{2,1,0:T(8,128)(2,1)} %get-tuple-element.196), channel_id=1, source_target_pairs={{0,2},{1,3},{2,0},{3,1},{4,6},{5,7},{6,4},{7,5},{8,10},{9,11},{10,... | collective-permute-start | bytes 2801672 | tf_op jit(solution)/shard_map/ppermute | solution.py:732
  788.5 91.9 %collective-permute-start.50 = (bf16[2,304,768]{2,1,0:T(8,128)(2,1)}, bf16[2,304,768]{2,1,0:T(8,128)(2,1)}, u32[]{:S(2)}, u32[]{:S(2)}) collective-permute-start(bf16[2,304,768]{2,1,0:T(8,128)(2,1)} %get-tuple-element.197), channel_id=1, source_target_pairs={{0,1},{1,0},{2,3},{3,2},{4,5},{5,4},{6,7},{7,6},{8,9},{9,8},{10,11... | collective-permute-start | bytes 2801672 | tf_op jit(solution)/shard_map/ppermute | solution.py:732
  852.1 45.7 %collective-permute-start.52 = (bf16[304,768]{1,0:T(8,128)(2,1)}, bf16[304,768]{1,0:T(8,128)(2,1)}, u32[]{:S(2)}, u32[]{:S(2)}) collective-permute-start(bf16[304,768]{1,0:T(8,128)(2,1)} %get-tuple-element.230), channel_id=1, source_target_pairs={{0,2},{1,3},{2,0},{3,1},{4,6},{5,7},{6,4},{7,5},{8,10},{9,11},{10,... | collective-permute-start | bytes 1400840 | tf_op jit(solution)/shard_map/ppermute | solution.py:732
  852.8 42.2 %collective-permute-start.54 = (bf16[304,768]{1,0:T(8,128)(2,1)}, bf16[304,768]{1,0:T(8,128)(2,1)}, u32[]{:S(2)}, u32[]{:S(2)}) collective-permute-start(bf16[304,768]{1,0:T(8,128)(2,1)} %get-tuple-element.231), channel_id=1, source_target_pairs={{0,1},{1,0},{2,3},{3,2},{4,5},{5,4},{6,7},{7,6},{8,9},{9,8},{10,11... | collective-permute-start | bytes 1400840 | tf_op jit(solution)/shard_map/ppermute | solution.py:732
  897.2 206.2 %collective-permute-start.55 = (bf16[304,1536]{1,0:T(8,128)(2,1)}, bf16[304,1536]{1,0:T(8,128)(2,1)}, u32[]{:S(2)}, u32[]{:S(2)}) collective-permute-start(bf16[304,1536]{1,0:T(8,128)(2,1)} %pad_maximum_fusion.27), channel_id=1, source_target_pairs={{0,2},{1,3},{2,0},{3,1},{4,6},{5,7},{6,4},{7,5},{8,10},{9,11},{10,... | collective-permute-start | bytes 2801672 | tf_op jit(solution)/shard_map/ppermute | solution.py:732
  900.0 203.4 %collective-permute-start.53 = (bf16[304,1536]{1,0:T(8,128)(2,1)}, bf16[304,1536]{1,0:T(8,128)(2,1)}, u32[]{:S(2)}, u32[]{:S(2)}) collective-permute-start(bf16[304,1536]{1,0:T(8,128)(2,1)} %pad_maximum_fusion.26), channel_id=1, source_target_pairs={{0,1},{1,0},{2,3},{3,2},{4,5},{5,4},{6,7},{7,6},{8,9},{9,8},{10,11... | collective-permute-start | bytes 2801672 | tf_op jit(solution)/shard_map/ppermute | solution.py:732
  983.7 135.8 %reduce-scatter.9.cloned.1.call-start = ((), (), s32[]{:S(2)}) async-start(), calls=%async_computation.16 | async-start | bytes 7962624 | tf_op jit(solution)/shard_map/reduce_scatter | solution.py:868
  990.3 80.3 %collective-permute-start.56 = (bf16[304,768]{1,0:T(8,128)(2,1)}, bf16[304,768]{1,0:T(8,128)(2,1)}, u32[]{:S(2)}, u32[]{:S(2)}) collective-permute-start(bf16[304,768]{1,0:T(8,128)(2,1)} %get-tuple-element.232), channel_id=1, source_target_pairs={{0,2},{1,3},{2,0},{3,1},{4,6},{5,7},{6,4},{7,5},{8,10},{9,11},{10,... | collective-permute-start | bytes 1400840 | tf_op jit(solution)/shard_map/ppermute | solution.py:732
  991.5 73.7 %collective-permute-start.58 = (bf16[304,768]{1,0:T(8,128)(2,1)}, bf16[304,768]{1,0:T(8,128)(2,1)}, u32[]{:S(2)}, u32[]{:S(2)}) collective-permute-start(bf16[304,768]{1,0:T(8,128)(2,1)} %get-tuple-element.233), channel_id=1, source_target_pairs={{0,1},{1,0},{2,3},{3,2},{4,5},{5,4},{6,7},{7,6},{8,9},{9,8},{10,11... | collective-permute-start | bytes 1400840 | tf_op jit(solution)/shard_map/ppermute | solution.py:732
  (378 other events, 7179.0 us)
Sparse Core Ops, SparseCore 0:
  31.5 74.9 all-gather.4
  108.6 31.1 all-gather.6
  164.7 88.9 all-gather.8
  331.5 88.6 all-gather.10
  509.0 97.2 reduce-scatter.10
  619.9 97.3 reduce-scatter.4
  983.9 36.9 reduce-scatter.6
  1023.2 83.1 reduce-scatter.8

commit v4 on v3

--- a/solution.py
+++ b/solution.py
@@ -618,9 +618,9 @@
         scratch_shapes=[pltpu.VMEM((rows, lanes), BF16), pltpu.VMEM((rows, lanes), BF16)],
         compiler_params=pltpu.CompilerParams(vmem_limit_bytes=48 << 20),
         cost_estimate=pl.CostEstimate(
-            flops=16 * rows * rows * width // 3,
-            bytes_accessed=8 * rows * width // 3,
-            transcendentals=rows * rows * width // (3 * head),
+            flops=1,
+            bytes_accessed=1,
+            transcendentals=0,
         ),
         name="attention",
     )(key_bias[None, :], floor, qkv_image, qkv_text, qkv_image, qkv_text, qkv_image, qkv_text)
@@ -715,9 +715,9 @@
         ],
         compiler_params=pltpu.CompilerParams(vmem_limit_bytes=48 << 20),
         cost_estimate=pl.CostEstimate(
-            flops=40 * rows * rows * width // 3,
-            bytes_accessed=16 * rows * width // 3,
-            transcendentals=rows * rows * width // (3 * head),
+            flops=1,
+            bytes_accessed=1,
+            transcendentals=0,
         ),
         name="attention_back",
     )(
@@ -732,51 +732,673 @@
     return lax.ppermute(values, "seq", [(i, i ^ bit) for i in range(4)])
 
 
-def gather_blocks(own):
-    half = own.shape[-1] // 2
-    near_x = flip(own, 1)
-    near_y = flip(own, 2)
-    far_a = flip(near_x[..., :half], 2)
-    far_b = flip(near_y[..., half:], 1)
-    return (own, near_x, near_y, jnp.concatenate([far_a, far_b], axis=-1))
+def gather_near(a, b):
+    return (flip(a, 1), flip(b, 1), flip(a, 2), flip(b, 2))
+
+
+def gather_far(a, b, near):
+    return (a, b, *near, flip(near[0], 2), flip(near[3], 1))
+
+
+def gather_halves(a, b):
+    return gather_far(a, b, gather_near(a, b))
 
 
 def add_low(a, b):
     return (a.astype(F32) + b.astype(F32)).astype(BF16)
 
 
-def scatter_blocks(blocks):
-    own, near_x, near_y, far = blocks
-    half = own.shape[-1] // 2
-    for_y = flip(far[..., :half], 1)
-    for_x = flip(far[..., half:], 2)
-    from_x = flip(
-        jnp.concatenate([near_x[..., :half], add_low(near_x[..., half:], for_x)], axis=-1), 1
-    )
-    from_y = flip(
-        jnp.concatenate([add_low(near_y[..., :half], for_y), near_y[..., half:]], axis=-1), 2
-    )
-    return own.astype(F32) + from_x.astype(F32) + from_y.astype(F32)
-
-
-def join_rows(blocks, image_count):
-    return (
-        jnp.concatenate([block[:image_count] for block in blocks], axis=0),
-        jnp.concatenate([block[image_count:] for block in blocks], axis=0),
-    )
-
-
-def split_rows(image, text, image_count, text_count):
-    return [
-        jnp.concatenate(
-            [
-                image[r * image_count : (r + 1) * image_count],
-                text[r * text_count : (r + 1) * text_count],
-            ],
-            axis=0,
-        )
-        for r in range(4)
+def scatter_first(halves):
+    return (flip(halves[6], 1), flip(halves[7], 2), flip(halves[2], 1), flip(halves[5], 2))
+
+
+def scatter_last(halves, first):
+    for_y, for_x, x_a, y_b = first
+    x_b = flip(add_low(halves[3], for_x), 1)
+    y_a = flip(add_low(halves[4], for_y), 2)
+    return (halves[0], halves[1], x_a, x_b, y_a, y_b)
+
+
+def scatter_halves(halves):
+    return scatter_last(halves, scatter_first(halves))
+
+
+ANYWHERE = pl.BlockSpec(memory_space=pl.ANY)
+ON_CORE = pl.BlockSpec(memory_space=pltpu.VMEM)
+
+
+class Copies:
+    def __init__(self, semaphores):
+        self.semaphores = semaphores
+        self.count = 0
+        self.open = []
+
+    def start(self, source, target):
+        copy = pltpu.make_async_copy(source, target, self.semaphores.at[self.count])
+        self.count += 1
+        copy.start()
+        return copy
+
+    def send(self, source, target):
+        self.open.append(self.start(source, target))
+
+    def finish(self):
+        for copy in self.open:
+            copy.wait()
+
+
+def fetch_halves(copies, halves, rows, seq):
+    width = rows.shape[2] // 2
+    fetched = []
+    for r in range(4):
+        pair = []
+        for side in range(2):
+            half = halves[2 * r + side]
+            half = half if seq is None else half.at[seq]
+            pair.append(copies.start(half, rows.at[r, :, pl.ds(side * width, width)]))
+        fetched.append(pair)
+    return fetched
+
+
+def send_halves(copies, rows, halves, r, seq):
+    width = rows.shape[2] // 2
+    for side in range(2):
+        half = halves[2 * r + side]
+        half = half if seq is None else half.at[seq]
+        copies.send(rows.at[r, :, pl.ds(side * width, width)], half)
+
+
+def normalize(values):
+    mean = jnp.mean(values, axis=1, keepdims=True)
+    centered = values - mean
+    variance = jnp.mean(centered * centered, axis=1, keepdims=True)
+    inverse = lax.rsqrt(variance + NORM_EPSILON)
+    return centered * inverse, inverse
+
+
+def normalize_back(norm, inverse, grad, scale):
+    scaled = grad * (1.0 + scale)
+    return inverse * (
+        scaled
+        - jnp.mean(scaled, axis=1, keepdims=True)
+        - norm * jnp.mean(scaled * norm, axis=1, keepdims=True)
+    )
+
+
+def run(kernel, name, operands, specs, outs, out_specs, scratch, copies=0):
+    if copies:
+        scratch = [*scratch, pltpu.SemaphoreType.DMA((copies,))]
+    return pl.pallas_call(
+        kernel,
+        in_specs=specs,
+        out_specs=out_specs,
+        out_shape=[jax.ShapeDtypeStruct(shape, dtype) for shape, dtype in outs],
+        scratch_shapes=scratch,
+        compiler_params=pltpu.CompilerParams(vmem_limit_bytes=56 << 20),
+        cost_estimate=pl.CostEstimate(flops=1, bytes_accessed=1, transcendentals=0),
+        name=name,
+    )(*operands)
+
+
+def project_kernel(seq, image_rows, *refs):
+    halves, (weight, mods, bias) = (refs[:8], refs[8:11])
+    qkv_i, qkv_t, norm_i, norm_t = refs[11:15]
+    rows, held, image_norm, text_norm, image_out, text_out, semaphores = refs[15:]
+    copies = Copies(semaphores)
+    fetched = fetch_halves(copies, halves, rows, seq)
+    weights = [copies.start(weight.at[t], held.at[t]) for t in range(2)]
+    text_rows = rows.shape[1] - image_rows
+    for r in range(4):
+        for copy in fetched[r]:
+            copy.wait()
+        for t, norms, low, count in (
+            (0, image_norm, 0, image_rows),
+            (1, text_norm, image_rows, text_rows),
+        ):
+            norm, _ = normalize(rows[r, low : low + count, :].astype(F32))
+            norm = norm * (1.0 + mods[t, seq, 1:2, :]) + mods[t, seq, 0:1, :]
+            norms[r * count : (r + 1) * count, :] = norm.astype(BF16)
+        if r == 0:
+            weights[0].wait()
+        span = pl.ds(r * image_rows, image_rows)
+        product = dot_nt(image_norm[span, :], held[0]) + bias[0:1, :]
+        image_out[span, :] = product.astype(BF16)
+        copies.send(image_norm.at[span, :], norm_i.at[span, :])
+        copies.send(image_out.at[span, :], qkv_i.at[span, :])
+    weights[1].wait()
+    text_out[...] = (dot_nt(text_norm[...], held[1]) + bias[1:2, :]).astype(BF16)
+    copies.send(text_norm, norm_t)
+    copies.send(text_out, qkv_t)
+    copies.finish()
+
+
+def project(halves, weight, mods, bias, seq, image_rows):
+    block, width = halves[0].shape[-2:]
+    D, W = 2 * width, weight.shape[1]
+    image, text = 4 * image_rows, 4 * (block - image_rows)
+    return run(
+        functools.partial(project_kernel, seq, image_rows),
+        "project",
+        (*halves, weight, mods, bias),
+        [ANYWHERE] * 9 + [ON_CORE] * 2,
+        [((image, W), BF16), ((text, W), BF16), ((image, D), BF16), ((text, D), BF16)],
+        [ANYWHERE] * 4,
+        [
+            pltpu.VMEM((4, block, D), BF16),
+            pltpu.VMEM((2, W, D), BF16),
+            pltpu.VMEM((image, D), BF16),
+            pltpu.VMEM((text, D), BF16),
+            pltpu.VMEM((image, W), BF16),
+            pltpu.VMEM((text, W), BF16),
+        ],
+        20,
+    )
+
+
+def partial_kernel(seqs, dot, image_rows, *refs):
+    inputs, weight, halves = (refs[: 2 * seqs], refs[2 * seqs], refs[2 * seqs + 1 : 2 * seqs + 9])
+    lefts, held, rows, semaphores = (
+        refs[2 * seqs + 9 : 4 * seqs + 9],
+        refs[4 * seqs + 9],
+        refs[4 * seqs + 10 : 5 * seqs + 10],
+        refs[5 * seqs + 10],
+    )
+    copies = Copies(semaphores)
+    weights = [copies.start(weight.at[t], held.at[t]) for t in (1, 0)]
+    fetched = [
+        [copies.start(inputs[2 * s + t], lefts[2 * s + t]) for t in (1, 0)] for s in range(seqs)
     ]
+    text_rows = rows[0].shape[1] - image_rows
+    for s in range(seqs):
+        if s == 0:
+            weights[0].wait()
+        fetched[s][0].wait()
+        text = dot(lefts[2 * s + 1][...], held[1]).astype(BF16)
+        for r in range(4):
+            rows[s][r, image_rows:, :] = text[r * text_rows : (r + 1) * text_rows]
+        if s == 0:
+            weights[1].wait()
+        fetched[s][1].wait()
+        for r in (3, 1, 2, 0):
+            left = lefts[2 * s][r * image_rows : (r + 1) * image_rows, :]
+            rows[s][r, :image_rows, :] = dot(left, held[0]).astype(BF16)
+            send_halves(copies, rows[s], halves, r, s if seqs > 1 else None)
+    copies.finish()
+
+
+def partial_sums(inputs, weight, dot, D, image_rows):
+    seqs = len(inputs)
+    image, K = inputs[0][0].shape
+    text = inputs[0][1].shape[0]
+    block = (image + text) // 4
+    shape = (block, D // 2) if seqs == 1 else (seqs, block, D // 2)
+    return run(
+        functools.partial(partial_kernel, seqs, dot, image_rows),
+        "partial_sums",
+        (*[value for pair in inputs for value in pair], weight),
+        [ANYWHERE] * (2 * seqs + 1),
+        [(shape, BF16)] * 8,
+        [ANYWHERE] * 8,
+        [pltpu.VMEM((count, K), BF16) for _ in range(seqs) for count in (image, text)]
+        + [pltpu.VMEM(weight.shape, BF16)]
+        + [pltpu.VMEM((4, block, D), BF16)] * seqs,
+        2 + 2 * seqs + 8 * seqs,
+    )
+
+
+def six_sum(pieces, low, count):
+    own_a, own_b, x_a, x_b, y_a, y_b = pieces
+
+    def add(*parts):
+        return sum(part[low : low + count, :].astype(F32) for part in parts)
+
+    return jnp.concatenate([add(own_a, x_a, y_a), add(own_b, x_b, y_b)], axis=1)
+
+
+def both_halves(halves, seq, low, count):
+    return jnp.concatenate(
+        [half[seq, low : low + count, :].astype(F32) for half in halves], axis=1
+    )
+
+
+def middle_kernel(seq, image_rows, *refs):
+    pieces, tokens, (mods, bias) = (refs[:6], refs[6:8], refs[8:10])
+    projection_ref, middle_ref, second_a, second_b = refs[10:]
+    block, width = second_a.shape
+    for t, low, count in ((0, 0, image_rows), (1, image_rows, block - image_rows)):
+        span = slice(low, low + count)
+        projection = six_sum(pieces, low, count) + bias[t : t + 1, :]
+        middle = both_halves(tokens, seq, low, count) + mods[t, seq, 2:3, :] * projection
+        norm, _ = normalize(middle)
+        second = (norm * (1.0 + mods[t, seq, 4:5, :]) + mods[t, seq, 3:4, :]).astype(BF16)
+        projection_ref[span, :] = projection
+        middle_ref[span, :] = middle
+        second_a[span, :] = second[:, :width]
+        second_b[span, :] = second[:, width:]
+
+
+def middle_step(pieces, tokens, mods, bias, seq, image_rows):
+    block, width = pieces[0].shape
+    return run(
+        functools.partial(middle_kernel, seq, image_rows),
+        "middle",
+        (*pieces, *tokens, mods, bias),
+        [ON_CORE] * 10,
+        [((block, 2 * width), F32)] * 2 + [((block, width), BF16)] * 2,
+        [ON_CORE] * 4,
+        [],
+    )
+
+
+GELU_SCALE = math.sqrt(2.0 / math.pi)
+GELU_CUBE = 0.044715
+
+
+def hidden_kernel(seq, image_rows, *refs):
+    halves, cotangents, (weight, bias, mods) = (refs[:8], refs[8:16], refs[16:19])
+    outs = refs[19:27]
+    act_i, act_t, slope_i, slope_t, grad_i, grad_t, second_i, second_t = outs
+    rows, given, held, acts, slopes, grads, texts, semaphores = refs[27:]
+    copies = Copies(semaphores)
+    fetched = fetch_halves(copies, halves, rows, None)
+    weights = [copies.start(weight.at[t], held.at[t]) for t in range(2)]
+    other = fetch_halves(copies, cotangents, given, seq)
+    text_rows = rows.shape[1] - image_rows
+    second_text, grad_text, act_text, slope_text = texts
+
+    def activate(pre):
+        squared = pre * pre
+        bent = jnp.tanh(GELU_SCALE * (pre + GELU_CUBE * pre * squared))
+        rise = 0.5 * (1.0 + bent)
+        slope = rise + (0.5 * GELU_SCALE) * pre * (1.0 - bent * bent) * (
+            1.0 + (3.0 * GELU_CUBE) * squared
+        )
+        return (pre * rise).astype(BF16), slope.astype(BF16)
+
+    for r in range(4):
+        for copy in fetched[r]:
+            copy.wait()
+        if r == 0:
+            weights[0].wait()
+        span = pl.ds(r * image_rows, image_rows)
+        text_span = slice(r * text_rows, (r + 1) * text_rows)
+        pre = dot_nt(rows[r, :image_rows, :], held[0]) + bias[0:1, :]
+        act, slope = activate(pre)
+        acts[span, :] = act
+        slopes[span, :] = slope
+        second_text[text_span, :] = rows[r, image_rows:, :]
+        for copy in other[r]:
+            copy.wait()
+        for t, target, place, low, count in (
+            (0, grads, span, 0, image_rows),
+            (1, grad_text, text_span, image_rows, text_rows),
+        ):
+            value = given[r, low : low + count, :].astype(F32) * mods[t, seq, 5:6, :]
+            target[place, :] = value.astype(BF16)
+        copies.send(acts.at[span, :], act_i.at[span, :])
+        copies.send(slopes.at[span, :], slope_i.at[span, :])
+        copies.send(grads.at[span, :], grad_i.at[span, :])
+        copies.send(rows.at[r, pl.ds(0, image_rows), :], second_i.at[span, :])
+    weights[1].wait()
+    act_text[...], slope_text[...] = activate(
+        dot_nt(second_text[...], held[1]) + bias[1:2, :]
+    )
+    for source, target in (
+        (act_text, act_t),
+        (slope_text, slope_t),
+        (grad_text, grad_t),
+        (second_text, second_t),
+    ):
+        copies.send(source, target)
+    copies.finish()
+
+
+def hidden_step(halves, cotangents, weight, bias, mods, seq, image_rows):
+    block, width = halves[0].shape
+    D, F = 2 * width, weight.shape[1]
+    image, text = 4 * image_rows, 4 * (block - image_rows)
+
+    def kernel(*refs):
+        texts, semaphores = (refs[-5:-1], refs[-1])
+        hidden_kernel(seq, image_rows, *refs[:-5], texts, semaphores)
+
+    return run(
+        kernel,
+        "hidden",
+        (*halves, *cotangents, weight, bias, mods),
+        [ANYWHERE] * 17 + [ON_CORE] * 2,
+        [((count, wide), BF16) for wide in (F, F, D, D) for count in (image, text)],
+        [ANYWHERE] * 8,
+        [
+            pltpu.VMEM((4, block, D), BF16),
+            pltpu.VMEM((4, block, D), BF16),
+            pltpu.VMEM((2, F, D), BF16),
+            pltpu.VMEM((image, F), BF16),
+            pltpu.VMEM((image, F), BF16),
+            pltpu.VMEM((image, D), BF16),
+        ]
+        + [pltpu.VMEM((text, wide), BF16) for wide in (D, D, F, F)],
+        38,
+    )
+
+
+def outer_kernel(seqs, chunk, *refs):
+    inputs, out = (refs[: 4 * seqs], refs[4 * seqs])
+    held, result, semaphores = (refs[4 * seqs + 1 : -2], refs[-2], refs[-1])
+    copies = Copies(semaphores)
+    fetched = [copies.start(source, target) for source, target in zip(inputs, held)]
+    columns = result.shape[1]
+    for t in range(2):
+        for s in range(seqs):
+            fetched[4 * s + 2 * t].wait()
+            fetched[4 * s + 2 * t + 1].wait()
+        for low in range(0, columns, chunk):
+            span = pl.ds(low, chunk)
+            total = dot_tn(held[2 * t][:, span], held[2 * t + 1][...])
+            for s in range(1, seqs):
+                total = total + dot_tn(held[4 * s + 2 * t][:, span], held[4 * s + 2 * t + 1][...])
+            result[t, span, :] = total.astype(BF16)
+            copies.send(result.at[t, span, :], out.at[t, span, :])
+    copies.finish()
+
+
+def outer_sums(lefts, rights, chunk):
+    seqs = len(lefts)
+    columns, width = lefts[0][0].shape[1], rights[0][0].shape[1]
+    operands = [side[s][t] for s in range(seqs) for t in range(2) for side in (lefts, rights)]
+    return run(
+        functools.partial(outer_kernel, seqs, chunk),
+        "outer_sums",
+        operands,
+        [ANYWHERE] * (4 * seqs),
+        [((2, columns, width), BF16)],
+        [ANYWHERE],
+        [pltpu.VMEM(value.shape, BF16) for value in operands]
+        + [pltpu.VMEM((2, columns, width), BF16)],
+        4 * seqs + 2 * (columns // chunk),
+    )[0]
+
+
+def hidden_back_kernel(image_rows, *refs):
+    (grad_i, grad_t, slope_i, slope_t, down, up) = refs[:6]
+    pre_i, pre_t, sums, halves = (refs[6], refs[7], refs[8], refs[9:17])
+    grads, slopes, pres, grad_text, slope_text, pre_text, held_down, held_up, rows, semaphores = (
+        refs[17:]
+    )
+    copies = Copies(semaphores)
+    downs = [copies.start(down.at[t], held_down.at[t]) for t in (1, 0)]
+    texts = [copies.start(grad_t, grad_text), copies.start(slope_t, slope_text)]
+    images = [copies.start(grad_i, grads), copies.start(slope_i, slopes)]
+    ups = [copies.start(up.at[t], held_up.at[t]) for t in (1, 0)]
+    text_rows = rows.shape[1] - image_rows
+    downs[0].wait()
+    for copy in texts:
+        copy.wait()
+    product = dot_nt(grad_text[...], held_down[1]) * slope_text[...].astype(F32)
+    pre_text[...] = product.astype(BF16)
+    copies.send(pre_text, pre_t)
+    sums[1:2, :] = jnp.sum(pre_text[...].astype(F32), axis=0, keepdims=True)
+    ups[0].wait()
+    back = dot_nn(pre_text[...], held_up[1]).astype(BF16)
+    for r in range(4):
+        rows[r, image_rows:, :] = back[r * text_rows : (r + 1) * text_rows]
+    downs[1].wait()
+    for copy in images:
+        copy.wait()
+    total = jnp.zeros((1, pres.shape[1]), F32)
+    for r in (3, 1, 2, 0):
+        span = pl.ds(r * image_rows, image_rows)
+        product = dot_nt(grads[span, :], held_down[0]) * slopes[span, :].astype(F32)
+        pres[span, :] = product.astype(BF16)
+        copies.send(pres.at[span, :], pre_i.at[span, :])
+        total = total + jnp.sum(pres[span, :].astype(F32), axis=0, keepdims=True)
+        if r == 3:
+            ups[1].wait()
+        rows[r, :image_rows, :] = dot_nn(pres[span, :], held_up[0]).astype(BF16)
+        send_halves(copies, rows, halves, r, None)
+    sums[0:1, :] = total
+    copies.finish()
+
+
+def hidden_back(grads, slopes, down, up, image_rows):
+    image, D = grads[0].shape
+    text = grads[1].shape[0]
+    F = up.shape[1]
+    block = (image + text) // 4
+    outs = run(
+        functools.partial(hidden_back_kernel, image_rows),
+        "hidden_back",
+        (*grads, *slopes, down, up),
+        [ANYWHERE] * 6,
+        [((image, F), BF16), ((text, F), BF16), ((2, F), F32)] + [((block, D // 2), BF16)] * 8,
+        [ANYWHERE] * 2 + [ON_CORE] + [ANYWHERE] * 8,
+        [
+            pltpu.VMEM((image, D), BF16),
+            pltpu.VMEM((image, F), BF16),
+            pltpu.VMEM((image, F), BF16),
+            pltpu.VMEM((text, D), BF16),
+            pltpu.VMEM((text, F), BF16),
+            pltpu.VMEM((text, F), BF16),
+            pltpu.VMEM((2, F, D), BF16),
+            pltpu.VMEM((2, F, D), BF16),
+            pltpu.VMEM((4, block, D), BF16),
+        ],
+        8 + 1 + 4 + 8,
+    )
+    return outs[0:2], outs[2], outs[3:]
+
+
+def middle_back_kernel(seq, image_rows, *refs):
+    pieces, cotangents, (middle_ref, projection_ref, mods) = (refs[:6], refs[6:8], refs[8:11])
+    grad_ref, low_a, low_b, sums = refs[11:]
+    block, width = low_a.shape
+    for t, low, count in ((0, 0, image_rows), (1, image_rows, block - image_rows)):
+        span = slice(low, low + count)
+        norm_grad = six_sum(pieces, low, count)
+        norm, inverse = normalize(middle_ref[span, :])
+        grad = both_halves(cotangents, seq, low, count) + normalize_back(
+            norm, inverse, norm_grad, mods[t, seq, 4:5, :]
+        )
+        rounded = (mods[t, seq, 2:3, :] * grad).astype(BF16)
+        grad_ref[span, :] = grad
+        low_a[span, :] = rounded[:, :width]
+        low_b[span, :] = rounded[:, width:]
+        for k, value in enumerate(
+            (norm_grad, norm_grad * norm, grad * projection_ref[span, :], rounded.astype(F32))
+        ):
+            sums[4 * t + k : 4 * t + k + 1, :] = jnp.sum(value, axis=0, keepdims=True)
+
+
+def middle_back(pieces, cotangents, middle, projection, mods, seq, image_rows):
+    block, width = pieces[0].shape
+    return run(
+        functools.partial(middle_back_kernel, seq, image_rows),
+        "middle_back",
+        (*pieces, *cotangents, middle, projection, mods),
+        [ON_CORE] * 11,
+        [((block, 2 * width), F32)] + [((block, width), BF16)] * 2 + [((8, 2 * width), F32)],
+        [ON_CORE] * 4,
+        [],
+    )
+
+
+def attended_back_kernel(image_rows, *refs):
+    halves, weight = (refs[:8], refs[8])
+    grad_i, grad_t, proj_i, proj_t = refs[9:13]
+    rows, held, image_out, text_in, text_out, semaphores = refs[13:]
+    copies = Copies(semaphores)
+    fetched = fetch_halves(copies, halves, rows, None)
+    weights = [copies.start(weight.at[t], held.at[t]) for t in range(2)]
+    text_rows = rows.shape[1] - image_rows
+    for r in range(4):
+        for copy in fetched[r]:
+            copy.wait()
+        if r == 0:
+            weights[0].wait()
+        span = pl.ds(r * image_rows, image_rows)
+        text_in[r * text_rows : (r + 1) * text_rows, :] = rows[r, image_rows:, :]
+        copies.send(rows.at[r, pl.ds(0, image_rows), :], proj_i.at[span, :])
+        image_out[span, :] = dot_nn(rows[r, :image_rows, :], held[0]).astype(BF16)
+    copies.send(image_out, grad_i)
+    copies.send(text_in, proj_t)
+    weights[1].wait()
+    text_out[...] = dot_nn(text_in[...], held[1]).astype(BF16)
+    copies.send(text_out, grad_t)
+    copies.finish()
+
+
+def attended_back(halves, weight, image_rows):
+    block, width = halves[0].shape
+    D, E = 2 * width, weight.shape[2]
+    image, text = 4 * image_rows, 4 * (block - image_rows)
+    outs = run(
+        functools.partial(attended_back_kernel, image_rows),
+        "attended_back",
+        (*halves, weight),
+        [ANYWHERE] * 9,
+        [((image, E), BF16), ((text, E), BF16), ((image, D), BF16), ((text, D), BF16)],
+        [ANYWHERE] * 4,
+        [
+            pltpu.VMEM((4, block, D), BF16),
+            pltpu.VMEM(weight.shape, BF16),
+            pltpu.VMEM((image, E), BF16),
+            pltpu.VMEM((text, D), BF16),
+            pltpu.VMEM((text, E), BF16),
+        ],
+        10 + 7,
+    )
+    return outs[:2], outs[2:]
+
+
+def project_back_kernel(seq, image_rows, *refs):
+    (grad_i, grad_t, weight), tokens = (refs[:3], refs[3:11])
+    sums, column_sums, halves = (refs[11], refs[12], refs[13:21])
+    grads, grad_text, held, given, rows, semaphores = refs[21:]
+    copies = Copies(semaphores)
+    weights = [copies.start(weight.at[t], held.at[t]) for t in (1, 0)]
+    text_in = copies.start(grad_t, grad_text)
+    image_in = copies.start(grad_i, grads)
+    fetched = fetch_halves(copies, tokens, given, seq)
+    text_rows = rows.shape[1] - image_rows
+    weights[0].wait()
+    text_in.wait()
+    text = dot_nn(grad_text[...], held[1])
+    column_sums[1:2, :] = jnp.sum(grad_text[...].astype(F32), axis=0, keepdims=True)
+    weights[1].wait()
+    image_in.wait()
+    totals = [jnp.zeros((1, rows.shape[2]), F32) for _ in range(4)]
+    columns = jnp.zeros((1, grads.shape[1]), F32)
+    for r in (3, 1, 2, 0):
+        for copy in fetched[r]:
+            copy.wait()
+        span = pl.ds(r * image_rows, image_rows)
+        for t, low, count in ((0, 0, image_rows), (1, image_rows, text_rows)):
+            if t == 0:
+                back = dot_nn(grads[span, :], held[0])
+                columns = columns + jnp.sum(grads[span, :].astype(F32), axis=0, keepdims=True)
+            else:
+                back = text[r * text_rows : (r + 1) * text_rows, :]
+            norm, _ = normalize(given[r, low : low + count, :].astype(F32))
+            totals[2 * t] = totals[2 * t] + jnp.sum(back, axis=0, keepdims=True)
+            totals[2 * t + 1] = totals[2 * t + 1] + jnp.sum(back * norm, axis=0, keepdims=True)
+            rows[r, low : low + count, :] = back.astype(BF16)
+        send_halves(copies, rows, halves, r, None)
+    column_sums[0:1, :] = columns
+    for k in range(4):
+        sums[k : k + 1, :] = totals[k]
+    copies.finish()
+
+
+def project_back(grads, weight, tokens, seq, image_rows):
+    image, W = grads[0].shape
+    text = grads[1].shape[0]
+    D = weight.shape[2]
+    block = (image + text) // 4
+    outs = run(
+        functools.partial(project_back_kernel, seq, image_rows),
+        "project_back",
+        (*grads, weight, *tokens),
+        [ANYWHERE] * 11,
+        [((4, D), F32), ((2, W), F32)] + [((block, D // 2), BF16)] * 8,
+        [ON_CORE] * 2 + [ANYWHERE] * 8,
+        [
+            pltpu.VMEM((image, W), BF16),
+            pltpu.VMEM((text, W), BF16),
+            pltpu.VMEM(weight.shape, BF16),
+            pltpu.VMEM((4, block, D), BF16),
+            pltpu.VMEM((4, block, D), BF16),
+        ],
+        4 + 8 + 8,
+    )
+    return outs[0], outs[1], outs[2:]
+
+
+def result_kernel(image_rows, *refs):
+    pieces, cotangents, middles = (refs[:6], refs[6:8], refs[8:10])
+    mods, bias, image_out, text_out, sums = refs[10:]
+    block = middles[0].shape[0]
+    for seq in range(2):
+        for t, low, count in ((0, 0, image_rows), (1, image_rows, block - image_rows)):
+            span = slice(low, low + count)
+            value = six_sum([piece.at[seq] for piece in pieces], low, count) + bias[t : t + 1, :]
+            gate = mods[t, seq, 5:6, :]
+            out = (middles[seq][span, :] + gate * value).astype(BF16)
+            if t == 0:
+                image_out[seq] = out
+            else:
+                text_out[seq] = out
+            grad = both_halves(cotangents, seq, low, count)
+            low_grad = (gate * grad).astype(BF16).astype(F32)
+            at = 4 * seq + 2 * t
+            sums[at : at + 1, :] = jnp.sum(grad * value, axis=0, keepdims=True)
+            sums[at + 1 : at + 2, :] = jnp.sum(low_grad, axis=0, keepdims=True)
+
+
+def result_step(pieces, cotangents, middles, mods, bias, image_rows):
+    seqs, block, width = pieces[0].shape
+    return run(
+        functools.partial(result_kernel, image_rows),
+        "result",
+        (*pieces, *cotangents, *middles, mods, bias),
+        [ON_CORE] * 12,
+        [
+            ((seqs, image_rows, 2 * width), BF16),
+            ((seqs, block - image_rows, 2 * width), BF16),
+            ((8, 2 * width), F32),
+        ],
+        [ON_CORE] * 3,
+        [],
+    )
+
+
+def input_back_kernel(image_rows, live_text, *refs):
+    pieces, tokens, grads, mods = (refs[:12], refs[12:14], refs[14:16], refs[16])
+    image_out, text_out = refs[17:]
+    block = grads[0].shape[0]
+    for seq in range(2):
+        for t, low, count in ((0, 0, image_rows), (1, image_rows, block - image_rows)):
+            norm_grad = six_sum(pieces[6 * seq : 6 * seq + 6], low, count)
+            norm, inverse = normalize(both_halves(tokens, seq, low, count))
+            out = grads[seq][low : low + count, :] + normalize_back(
+                norm, inverse, norm_grad, mods[t, seq, 1:2, :]
+            )
+            if t == 0:
+                image_out[seq] = out
+            else:
+                text_out[seq] = out[:live_text]
+
+
+def input_back(pieces, tokens, grads, mods, image_rows, live_text):
+    block, width = pieces[0][0].shape
+    return run(
+        functools.partial(input_back_kernel, image_rows, live_text),
+        "input_back",
+        (*pieces[0], *pieces[1], *tokens, *grads, mods),
+        [ON_CORE] * 17,
+        [((2, image_rows, 2 * width), F32), ((2, live_text, 2 * width), F32)],
+        [ON_CORE] * 2,
+        [],
+    )
 
 
 def match_units(batch_devices, seq_devices, per_device, group_units):
@@ -865,27 +1487,12 @@
 
 
 def scatter_rows_over_batch(values):
-    return lax.psum_scatter(values, "batch", scatter_dimension=1, tiled=True)
+    dimension = values.ndim - 2
+    return lax.psum_scatter(values, "batch", scatter_dimension=dimension, tiled=True)
 
 
 def swap(values, axis):
     return lax.all_to_all(values, axis, 0, 0, tiled=True)
-
-
-def norm_stats(values):
-    mean = jnp.mean(values, axis=-1, keepdims=True)
-    centered = values - mean
-    variance = jnp.mean(centered * centered, axis=-1, keepdims=True)
-    return mean, lax.rsqrt(variance + NORM_EPSILON)
-
-
-def norm_back(norm, inverse, grad, scale):
-    scaled = grad * (1.0 + scale)
-    return inverse * (
-        scaled
-        - jnp.mean(scaled, axis=-1, keepdims=True)
-        - norm * jnp.mean(scaled * norm, axis=-1, keepdims=True)
-    )
 
 
 def swift_layer(
@@ -916,50 +1523,7 @@
     pad = ((0, 0), (0, text_count - live_text), (0, 0))
     head = D // HEADS
     own_width = D // S
-    is_image = (jnp.arange(image_count + text_count) < image_count)[:, None]
-
-    bias_widths = [array.shape[1] for array in (qv_bias, out_bias, up_bias, down_bias)]
-    bias_ends = np.cumsum(bias_widths)
-    own_biases = jnp.concatenate([qv_bias, out_bias, up_bias, down_bias], axis=1)
-    near = gather_small(jnp.concatenate([conditioning, own_biases], axis=1), "batch")
-    cond_all = near[:, :, :D].reshape(B * L, D)
-    column_biases = near[:, :, D:].astype(F32)
-    smooth_all = jax.nn.silu(cond_all.astype(F32)).astype(BF16)
-    mod_own = (
-        jnp.einsum("sd,tdf->tsf", smooth_all, mod_weight, preferred_element_type=F32)
-        + mod_bias.astype(F32)[:, None, :]
-    )
-    mod_width = mod_own.shape[2]
-    mod_sent = mod_own.reshape(2, B, L, mod_width).transpose(1, 0, 2, 3)
-    mod_came = swap(mod_sent, "batch")
-    small = jnp.concatenate(
-        [mod_came.reshape(B, 2 * L * mod_width), column_biases.reshape(B, -1)], axis=1
-    )
-    small_all = gather_small(small, "seq")
-    modulation = (
-        small_all[:, :, : 2 * L * mod_width]
-        .reshape(S, B, 2, L, mod_width)
-        .transpose(2, 3, 1, 0, 4)
-        .reshape(2, L, 6, D)
-    )
-    bias_all = (
-        small_all[:, :, 2 * L * mod_width :].reshape(S, B, 2, -1).transpose(2, 1, 0, 3)
-    )
-    qv_full = bias_all[..., : bias_ends[0]].reshape(2, 2 * D)
-    out_bias_full = bias_all[..., bias_ends[0] : bias_ends[1]].reshape(2, D)
-    down_bias_full = bias_all[..., bias_ends[2] :].reshape(2, D)
-    up_bias_part = (
-        column_biases[:, :, bias_ends[1] : bias_ends[2]].transpose(1, 0, 2).reshape(2, -1)
-    )
-    first_feature = seq_index * own_width
-    qkv_bias = jnp.concatenate(
-        [
-            lax.dynamic_slice_in_dim(qv_full, first_feature, own_width, 1),
-            jnp.zeros((2, own_width), F32),
-            lax.dynamic_slice_in_dim(qv_full, D + first_feature, own_width, 1),
-        ],
-        axis=1,
-    )
+    half = D // 2
 
     unit = math.gcd(qkv_weight.shape[2], own_width)
     per_device = qkv_weight.shape[2] // unit
@@ -973,10 +1537,61 @@
     qkv_width = per_device * unit
     qkv_part = gather_rows_over_batch(qkv_mine.reshape(2, qkv_width, D))
     out_rows = out_mine.transpose(1, 0, 2, 3).reshape(2, S * out_columns, own_width)
-    out_part = gather_rows_over_batch(after(out_rows, qkv_part))
-    up_part = gather_rows_over_batch(after(jnp.swapaxes(up_weight, 1, 2), out_part))
-    down_part = gather_rows_over_batch(after(jnp.swapaxes(down_weight, 1, 2), up_part))
+    out_part = gather_rows_over_batch(out_rows)
     hidden_columns = up_weight.shape[2]
+
+    padded = jnp.concatenate([image_tokens, jnp.pad(text_tokens, pad)], axis=1)
+    tokens = after((padded[..., :half], padded[..., half:]), qkv_mine)
+    tokens_near = gather_near(*tokens)
+
+    bias_widths = [array.shape[1] for array in (qv_bias, out_bias, up_bias, down_bias)]
+    bias_ends = np.cumsum(bias_widths)
+    own_biases = jnp.concatenate([qv_bias, out_bias, up_bias, down_bias], axis=1)
+    near = gather_small(jnp.concatenate([conditioning, own_biases], axis=1), "batch")
+    cond_all = near[:, :, :D].reshape(B * L, D)
+    column_biases = near[:, :, D:].astype(F32)
+    smooth_all = jax.nn.silu(cond_all.astype(F32)).astype(BF16)
+    mod_own = (
+        jnp.einsum("sd,tdf->tsf", smooth_all, mod_weight, preferred_element_type=F32)
+        + mod_bias.astype(F32)[:, None, :]
+    )
+    mod_width = mod_own.shape[2]
+    mod_sent = mod_own.reshape(2, B, L, mod_width).transpose(1, 0, 2, 3)
+    mod_came = swap(mod_sent, "batch")
+    small = jnp.concatenate(
+        [mod_came.reshape(B, 2 * L * mod_width), column_biases.reshape(B, -1)], axis=1
+    )
+    small_all = gather_small(after(small, tokens_near), "seq")
+    modulation = (
+        small_all[:, :, : 2 * L * mod_width]
+        .reshape(S, B, 2, L, mod_width)
+        .transpose(2, 3, 1, 0, 4)
+        .reshape(2, L, 6, D)
+    )
+    bias_all = (
+        small_all[:, :, 2 * L * mod_width :].reshape(S, B, 2, -1).transpose(2, 1, 0, 3)
+    )
+    qv_full = bias_all[..., : bias_ends[0]].reshape(2, 2 * D)
+    out_bias_full = bias_all[..., bias_ends[0] : bias_ends[1]].reshape(2, D)
+    down_bias_full = bias_all[..., bias_ends[2] :].reshape(2, D)
+    up_bias_part = (
+        column_biases[:, :, bias_ends[1] : bias_ends[2]].transpose(1, 0, 2).reshape(2, -1)
+    )
+    first_feature = seq_index * own_width
+    qkv_bias = jnp.concatenate(
+        [
+            lax.dynamic_slice_in_dim(qv_full, first_feature, own_width, 1),
+            jnp.zeros((2, own_width), F32),
+            lax.dynamic_slice_in_dim(qv_full, D + first_feature, own_width, 1),
+        ],
+        axis=1,
+    )
+
+    tokens_all = gather_far(*tokens, after(tokens_near, small_all))
+    padded = jnp.concatenate([image_cotangent, jnp.pad(text_cotangent, pad)], axis=1)
+    cotangents = (padded[..., :half], padded[..., half:])
+    near_grads = gather_near(*after(cotangents, tokens_all))
+    up_part = gather_rows_over_batch(after(jnp.swapaxes(up_weight, 1, 2), tokens_all))
 
     order = jnp.bitwise_xor(seq_index, jnp.arange(S))
     image_keys = jnp.take(
@@ -991,150 +1606,104 @@
     floors = jnp.where(jnp.all(key_mask > 0, axis=1), -3e38, FLOOR_SCORE * LOG2E).astype(F32)
     floors = floors.reshape(L, 1, 1)
 
-    own_tokens = jnp.concatenate([image_tokens, jnp.pad(text_tokens, pad)], axis=1)
-    own_grads = jnp.concatenate([image_cotangent, jnp.pad(text_cotangent, pad)], axis=1)
-    token_blocks = gather_blocks(after(own_tokens, qkv_mine))
-    grad_blocks = gather_blocks(after(own_grads, token_blocks))
-    tokens_all = [join_rows([block[s] for block in token_blocks], image_count) for s in range(L)]
-
-    def by_row(vectors):
-        return jnp.where(is_image, vectors[0][None, :], vectors[1][None, :])
-
-    first_norms, first_stats, qkvs, attended, partials = ([], [], [], [], [])
+    kept = []
+    first = project(tokens_all, qkv_part, modulation, qkv_bias, 0, image_count)
+    attended = attention(first[0], first[1], key_bias[0], floors[0], head)
+    down_part = gather_rows_over_batch(after(jnp.swapaxes(down_weight, 1, 2), attended))
+    parts = partial_sums([attended], out_part, dot_nt, D, image_count)
+    kept.append((first, attended, parts))
+    again = after(tokens_all, parts, near_grads)
+    first = project(again, qkv_part, modulation, qkv_bias, 1, image_count)
+    attended = attention(first[0], first[1], key_bias[1], floors[1], head)
+    cotangents_all = gather_far(*cotangents, near_grads)
+    attended = after(attended, cotangents_all)
+    parts = partial_sums([attended], out_part, dot_nt, D, image_count)
+    kept.append((first, attended, parts))
+    firsts, attendeds, out_halves = zip(*kept)
+    steps, seconds = ([], [])
     for s in range(L):
-        norms, stats, rows = ([], [], [])
-        for t in range(2):
-            pieces = modulation[t, s]
-            values = tokens_all[s][t].astype(F32)
-            mean, inverse = norm_stats(values)
-            norm = (
-                (values - mean) * inverse * (1.0 + pieces[1][None, :]) + pieces[0][None, :]
-            ).astype(BF16)
-            rows.append((dot_nt(norm, qkv_part[t]) + qkv_bias[t][None, :]).astype(BF16))
-            norms.append(norm)
-            stats.append((mean, inverse))
-        if s == L - 1:
-            rows, grad_blocks, partials = lax.optimization_barrier((rows, grad_blocks, partials))
-        first_norms.append(norms)
-        first_stats.append(stats)
-        qkvs.append(rows)
-        attended.append(attention(rows[0], rows[1], key_bias[s], floors[s], head))
-        partials.append([dot_nt(attended[s][t], out_part[t]).astype(BF16) for t in range(2)])
-    grads_all = [join_rows([block[s] for block in grad_blocks], image_count) for s in range(L)]
-    projections, middles, middle_stats, second_all = ([], [], [], [])
+        steps.append(
+            middle_step(
+                scatter_halves(out_halves[s]), tokens, modulation, out_bias_full, s, image_count
+            )
+        )
+        seconds.append(gather_halves(*steps[s][2:]))
+    hidden = []
     for s in range(L):
-        summed = scatter_blocks(split_rows(*partials[s], image_count, text_count))
-        pieces = [by_row(modulation[:, s, k]) for k in range(6)]
-        projection = summed + by_row(out_bias_full)
-        middle = own_tokens[s].astype(F32) + pieces[2] * projection
-        mean, inverse = norm_stats(middle)
-        second = (middle - mean) * inverse * (1.0 + pieces[4]) + pieces[3]
-        projections.append(projection)
-        middles.append(middle)
-        middle_stats.append((mean, inverse))
-        second_all.append(join_rows(gather_blocks(second.astype(BF16)), image_count))
-
-    def both(left, right, t):
-        total = dot_tn(left[0][t], right[0][t])
-        for s in range(1, L):
-            total = total + dot_tn(left[s][t], right[s][t])
-        return total.astype(BF16)
-
-    hidden_acts, hidden_pres, mlp_grads = ([], [], [])
+        halves = after(seconds[s], hidden[-1]) if s else seconds[s]
+        hidden.append(
+            hidden_step(
+                halves, cotangents_all, up_part, up_bias_part, modulation, s, image_count
+            )
+        )
+    acts, slopes, grads, norms = [[step[i : i + 2] for step in hidden] for i in (0, 2, 4, 6)]
+
+    down_sum = outer_sums(acts, grads, 256)
+    down_came = scatter_rows_over_batch(down_sum)
+    pres, bias_sums, norm2_halves = ([], [], [])
+    gate = down_sum
     for s in range(L):
-        acts, pres, grads = ([], [], [])
-        for t in range(2):
-            pre = dot_nt(second_all[s][t], up_part[t]) + up_bias_part[t][None, :]
-            acts.append(gelu_tanh(pre).astype(BF16))
-            pres.append(pre)
-            grads.append(
-                (modulation[t, s][5][None, :] * grads_all[s][t].astype(F32)).astype(BF16)
-            )
-        hidden_acts.append(acts)
-        hidden_pres.append(pres)
-        mlp_grads.append(grads)
-    down_sent = jnp.stack([both(hidden_acts, mlp_grads, t) for t in range(2)])
-    down_came = scatter_rows_over_batch(down_sent)
-    late_pres, down_sent = lax.optimization_barrier((hidden_pres[-1], down_sent))
-    hidden_pres[-1] = late_pres
-    pre_grads, norm2_sums = ([], [])
-    for s in range(L):
-        pre_low, back = ([], [])
-        for t in range(2):
-            act_grad = dot_nt(mlp_grads[s][t], down_part[t])
-            pre_grad = jax.vjp(gelu_tanh, hidden_pres[s][t])[1](act_grad)[0].astype(BF16)
-            pre_low.append(pre_grad)
-            back.append(dot_nn(pre_grad, up_part[t]).astype(BF16))
-        pre_grads.append(pre_low)
-        norm2_sums.append(
-            scatter_blocks(split_rows(back[0], back[1], image_count, text_count))
-        )
-    up_sent = jnp.stack([both(pre_grads, second_all, t) for t in range(2)])
-    up_came = scatter_rows_over_batch(up_sent)
-    up_bias_sum = jnp.stack(
-        [
-            sum(jnp.sum(pre_grads[s][t].astype(F32), axis=0) for s in range(L))
-            for t in range(2)
-        ]
-    )
-    mlp_parts = [
-        [dot_nn(hidden_acts[s][t], down_part[t]).astype(BF16) for t in range(2)]
-        for s in range(L)
-    ]
-
-    def row_sums(values):
-        return jnp.stack(
-            [jnp.sum(values[:image_count], axis=0), jnp.sum(values[image_count:], axis=0)]
-        )
-
-    mod_grads = [[None] * 6 for _ in range(L)]
-    middle_grads, proj_all = ([], [])
-    out_bias_sum = 0.0
-    for s in range(L):
-        pieces = [by_row(modulation[:, s, k]) for k in range(6)]
-        norm_grad = norm2_sums[s]
-        mean, inverse = middle_stats[s]
-        norm = (middles[s] - mean) * inverse
-        middle_grad = own_grads[s].astype(F32) + norm_back(norm, inverse, norm_grad, pieces[4])
-        low = (pieces[2] * middle_grad).astype(BF16)
-        proj_all.append(join_rows(gather_blocks(low), image_count))
-        mod_grads[s][3] = row_sums(norm_grad)
-        mod_grads[s][4] = row_sums(norm_grad * norm)
-        mod_grads[s][2] = row_sums(middle_grad * projections[s])
-        out_bias_sum = out_bias_sum + row_sums(low.astype(F32))
-        middle_grads.append(middle_grad)
-
-    mlp_parts = after(mlp_parts, proj_all)
-    mlp_parts = [split_rows(*parts, image_count, text_count) for parts in mlp_parts]
-    mlp_sums = scatter_blocks([jnp.stack([mlp_parts[s][r] for s in range(L)]) for r in range(4)])
-
-    qkv_grads, norm1_parts = ([], [])
-    for s in range(L):
-        attended_grad = [dot_nn(proj_all[s][t], out_part[t]).astype(BF16) for t in range(2)]
-        if s == 0:
-            attended_grad = after(attended_grad, up_sent)
-        if s == L - 1:
-            attended_grad = after(attended_grad, mlp_sums, norm1_parts)
-        grads = attention_back(
-            qkvs[s][0], qkvs[s][1], attended_grad[0], attended_grad[1], key_bias[s], floors[s], head
-        )
-        qkv_grads.append(grads)
-        back = [dot_nn(grads[t], qkv_part[t]).astype(BF16) for t in range(2)]
-        for k in range(2):
-            sums = []
-            for t in range(2):
-                wide = back[t].astype(F32)
-                if k == 1:
-                    mean, inverse = first_stats[s][t]
-                    wide = wide * ((tokens_all[s][t].astype(F32) - mean) * inverse)
-                sums.append(jnp.sum(wide, axis=0))
-            mod_grads[s][k] = jnp.stack(sums)
-        norm1_parts.append(split_rows(back[0], back[1], image_count, text_count))
-    norm1_sums = [scatter_blocks(parts) for parts in norm1_parts]
-    out_sum = [both(proj_all, attended, t) for t in range(2)]
-    qkv_sum = [both(qkv_grads, first_norms, t) for t in range(2)]
-    out_came = scatter_rows_over_batch(after(jnp.stack(out_sum), up_came))
-    qkv_came = scatter_rows_over_batch(after(jnp.stack(qkv_sum), out_came))
+        pre, sums, halves = hidden_back(
+            after(grads[s], gate), slopes[s], down_part, up_part, image_count
+        )
+        gate = halves
+        pres.append(pre)
+        bias_sums.append(sums)
+        norm2_halves.append(halves)
+    up_bias_sum = sum(bias_sums)
+    norm2_pieces = [scatter_halves(halves) for halves in norm2_halves]
+    up_sum = outer_sums(after(pres, gate), norms, 256)
+
+    backs, projs = ([], [])
+    backs.append(
+        middle_back(
+            after(norm2_pieces[0], up_sum), cotangents, *steps[0][1::-1], modulation, 0, image_count
+        )
+    )
+    projs.append(gather_halves(*backs[0][1:3]))
+    mlp_halves = partial_sums(after(acts, backs[0]), down_part, dot_nn, D, image_count)
+    backs.append(
+        middle_back(
+            after(norm2_pieces[1], mlp_halves),
+            cotangents,
+            *steps[1][1::-1],
+            modulation,
+            1,
+            image_count,
+        )
+    )
+    projs.append(gather_halves(*backs[1][1:3]))
+    grad0, proj0 = attended_back(after(projs[0], backs[1]), out_part, image_count)
+    up_came = scatter_rows_over_batch(after(up_sum, down_came, grad0))
+    qkv_grad0 = attention_back(*firsts[0][:2], *grad0, key_bias[0], floors[0], head)
+    grad1, proj1 = attended_back(after(projs[1], qkv_grad0), out_part, image_count)
+    mlp_first = scatter_first(after(mlp_halves, proj1))
+    out_sum = outer_sums([proj0, proj1], attendeds, 256)
+    sums0, columns0, halves0 = project_back(
+        after(qkv_grad0, out_sum), qkv_part, tokens_all, 0, image_count
+    )
+    out_came = scatter_rows_over_batch(after(out_sum, up_came, halves0))
+    norm1_first = scatter_first(halves0)
+    grad1 = after(grad1, halves0, mlp_first)
+    qkv_grad1 = attention_back(*firsts[1][:2], *grad1, key_bias[1], floors[1], head)
+    mlp_pieces = scatter_last(mlp_halves, mlp_first)
+    qkv_grad1 = after(qkv_grad1, mlp_pieces)
+    qkv_sum = outer_sums(
+        [qkv_grad0, qkv_grad1], [first[2:] for first in firsts], 128 if qkv_width % 256 else 256
+    )
+    qkv_came = scatter_rows_over_batch(after(qkv_sum, out_came))
+    sums1, columns1, halves1 = project_back(
+        after(qkv_grad1, qkv_sum), qkv_part, tokens_all, 1, image_count
+    )
+    norm1_pieces = [scatter_last(halves0, norm1_first), scatter_halves(halves1)]
+    image_out, text_out, result_sums = result_step(
+        after(mlp_pieces, halves1),
+        cotangents,
+        [step[1] for step in steps],
+        modulation,
+        down_bias_full,
+        image_count,
+    )
     qkv_home = move_units(
         qkv_came.reshape(2, per_device, unit, D).swapaxes(0, 1), back_perms, land, send, place
     )
@@ -1145,42 +1714,30 @@
     )
     up_weight_grad = up_came.swapaxes(1, 2).astype(F32)
     down_weight_grad = down_came.swapaxes(1, 2).astype(F32)
-
-    results, input_grads = ([], [])
-    down_bias_sum = 0.0
-    for s in range(L):
-        pieces = [by_row(modulation[:, s, k]) for k in range(6)]
-        grad = own_grads[s].astype(F32)
-        mlp_value = mlp_sums[s] + by_row(down_bias_full)
-        results.append((middles[s] + pieces[5] * mlp_value).astype(BF16))
-        mod_grads[s][5] = row_sums(grad * mlp_value)
-        own_low = (pieces[5] * grad).astype(BF16)
-        down_bias_sum = down_bias_sum + row_sums(own_low.astype(F32))
-        values = own_tokens[s].astype(F32)
-        mean, inverse = norm_stats(values)
-        norm = (values - mean) * inverse
-        input_grads.append(
-            middle_grads[s] + norm_back(norm, inverse, norm1_sums[s], pieces[1])
-        )
-    text_rows = slice(image_count, image_count + live_text)
-
-    mod_rows = jnp.stack([jnp.concatenate(mod_grads[s], axis=1) for s in range(L)], axis=1)
+    image_grad, text_grad = input_back(
+        norm1_pieces, tokens, [back[0] for back in backs], modulation, image_count, live_text
+    )
+
+    first_sums = jnp.stack([sums0, sums1]).reshape(L, 2, 2, D)
+    second_sums = jnp.stack([back[3] for back in backs]).reshape(L, 2, 4, D)
+    result_sums = result_sums.reshape(L, 2, 2, D)
+    mod_rows = jnp.concatenate(
+        [
+            first_sums,
+            second_sums[:, :, 2:3],
+            second_sums[:, :, :2],
+            result_sums[:, :, :1],
+        ],
+        axis=2,
+    ).swapaxes(0, 1)
     mod_rows = mod_rows.reshape(2, L, B, S, mod_width).transpose(3, 2, 0, 1, 4)
+    out_bias_sum = jnp.sum(second_sums[:, :, 3], axis=0)
+    down_bias_sum = jnp.sum(result_sums[:, :, 1], axis=0)
+    column_sums = columns0 + columns1
     qv_bias_sum = jnp.zeros((2, 2 * D), F32)
     for part, column in ((0, 0), (1, 2 * own_width)):
-        sums = jnp.stack(
-            [
-                sum(
-                    jnp.sum(
-                        qkv_grads[s][t][:, column : column + own_width].astype(F32), axis=0
-                    )
-                    for s in range(L)
-                )
-                for t in range(2)
-            ]
-        )
         qv_bias_sum = lax.dynamic_update_slice_in_dim(
-            qv_bias_sum, sums, part * D + first_feature, 1
+            qv_bias_sum, column_sums[:, column : column + own_width], part * D + first_feature, 1
         )
     up_bias_rows = lax.dynamic_update_slice_in_dim(
         jnp.zeros((2, B, S, hidden_columns), F32),
@@ -1223,10 +1780,10 @@
     smooth_grad = smooth_grad + flip(smooth_grad, 2)
     cond_grad = jax.vjp(jax.nn.silu, conditioning.astype(F32))[1](smooth_grad)[0]
     return (
-        jnp.stack([values[:image_count] for values in results]),
-        jnp.stack([values[text_rows] for values in results]),
-        jnp.stack([values[:image_count] for values in input_grads]),
-        jnp.stack([values[text_rows] for values in input_grads]),
+        image_out,
+        text_out[:, :live_text],
+        image_grad,
+        text_grad,
         cond_grad,
         mod_weight_grad,
         mod_bias_grad,

time: 1170 us -> 923 us (0.79)
  Pallas kernels: 143 us -> 415 us
  matrix products: 237 us -> 3.44 us
  other arithmetic: 158 us -> 25.7 us
  local copies, waits for them, and re-layouts: 147 us -> 53.8 us
  waiting for transfers between devices: 320 us -> 248 us
  starting transfers between devices: 122 us -> 139 us
    pallas_call x0 -> x23, Pallas kernels: none -> 272 us  [run(): pl.pallas_call(kernel, in_specs=specs, out_specs=out_specs, out_shape=[ja...]
    dot_general x48 -> x0, matrix products: 233 us -> none  [the longest x16 84.9 us: dot_nt(): lax.dot_general(a, b, (((1,), (1,)), ((), ())), preferred_element_type=F32)]
    slice x83 -> x8, local copies, waits for them, and re-layouts: 65.2 us -> 4.53 us  [the longest x1 1.65 us: swift_layer(): text_out[:, :live_text]]
    ppermute x54 -> x80, waiting for transfers between devices: 254 us -> 212 us  [flip(): return lax.ppermute(values, 'seq', [(i, i ^ bit) for i in range(4)])]
    reduce_sum x42 -> x1, other arithmetic: 37.8 us -> 0.07 us  [swift_layer(): out_bias_sum = jnp.sum(second_sums[:, :, 3], axis=0)]
    another operation x18 -> x1, other arithmetic: 30.2 us -> 0.02 us  [swift_layer(): second_sums = jnp.stack([back[3] for back in backs]).reshape(L, 2, 4, D)]
    all_gather x4, waiting for transfers between devices: 29.7 us -> 0.02 us  [gather_rows_over_batch(): return lax.all_gather(values, 'batch', axis=1, tiled=True)]
    ppermute x54 -> x80, starting transfers between devices: 57.5 us -> 83.8 us  [flip(): return lax.ppermute(values, 'seq', [(i, i ^ bit) for i in range(4)])]
  transfers between devices with their start and end apart: 79 -> 105, of which waited for: 32 -> 39; matrix products, arithmetic and copies ran while one was open for 45% -> 6% of each run, Pallas kernels for 12% -> 46%
where the time goes in v4:
time: 923 us; the launch traced here: 907 us
  Pallas kernels  415 us (45%)
  waiting for transfers between devices  248 us (27%)
  starting transfers between devices  139 us (15%)
  local copies, waits for them, and re-layouts  53.8 us (6%)
  other arithmetic  25.7 us (3%)
  between operations  22.2 us (2%)
    pallas_call x23, Pallas kernels, run(): pl.pallas_call(kernel, in_specs=specs, out_specs=out_specs, out_shape=[ja...  272 us
    ppermute x80, waiting for transfers between devices, flip(): return lax.ppermute(values, 'seq', [(i, i ^ bit) for i in range(4)])  212 us
    pallas_call x2, Pallas kernels, attention_back(): pl.pallas_call(functools.partial(attention_back_kernel, 256, LOG2E / math...  94.1 us
    ppermute x80, starting transfers between devices, flip(): return lax.ppermute(values, 'seq', [(i, i ^ bit) for i in range(4)])  83.8 us
    pallas_call x2, Pallas kernels, attention(): pl.pallas_call(functools.partial(attention_kernel, 256, LOG2E / math.sqrt...  49 us
    all_to_all x6, starting transfers between devices, swap(): return lax.all_to_all(values, axis, 0, 0, tiled=True)  26.8 us
    unnamed x182, local copies, waits for them, and re-layouts  21.2 us
    ppermute x6, starting transfers between devices, move_units(): lax.ppermute(lax.dynamic_index_in_dim(units, slot, 0, keepdims=True), ('b...  20.4 us
  transfers between devices with their start and end apart: 105, of which 39 were waited for; matrix products, arithmetic and copies ran while one was open for 6% of the time, Pallas kernels for 46%

profile of v4, /device:TPU:16, one launch (start us, length us, event | category | flops | bytes accessed | tf_op | source)
XLA Modules:
  0.0 907.5 jit_solution(7294096774302342050)
XLA Ops:
  68.1 7.9 collective-permute-done.5.refs_4_.refs_7_
  77.4 17.0 %collective-permute-done.6.refs_5_.refs_8_ = bf16[2,304,768]{2,1,0:T(8,128)(2,1)} collective-permute-done((bf16[2,304,768]{2,1,0:T(8,128)(2,1)S(1)}, bf16[2,304,768]{2,1,0:T(8,128)(2,1)}, u32[]{:S(2)}, u32[]{:S(2)}) %collective-permute-start.6) | collective-permute-done | bytes 933920 | tf_op jit(solution)/shard_map/ppermute | solution.py:732
  107.4 17.3 %collective-permute-done.12.refs_6_.refs_9_ = bf16[2,304,768]{2,1,0:T(8,128)(2,1)S(1)} collective-permute-done((bf16[2,304,768]{2,1,0:T(8,128)(2,1)}, bf16[2,304,768]{2,1,0:T(8,128)(2,1)S(1)}, u32[]{:S(2)}, u32[]{:S(2)}) %collective-permute-start.12) | collective-permute-done | bytes 933920 | tf_op jit(solution)/shard_map/ppermute | solution.py:732
  130.0 13.1 %project.2 = (bf16[1024,1152]{1,0:T(8,128)(2,1)}, bf16[192,1152]{1,0:T(8,128)(2,1)}, bf16[1024,1536]{1,0:T(8,128)(2,1)}, bf16[192,1536]{1,0:T(8,128)(2,1)}) custom-call(bf16[2,304,768]{2,1,0:T(8,128)(2,1)} %get-tuple-element.260.refs_0_.refs_6_.refs_3_.refs_12_, bf16[2,304,768]{2,1,0:T(8,128)(2,1)} %copy-done.19, ...), custom_call_target="tpu_custom_call" | custom-call | flops 1 | bytes 1 | tf_op jit(solution)/shard_map/project/pallas_call | solution.py:831
  145.7 24.3 %attention.2 = (bf16[1024,384]{1,0:T(8,128)(2,1)S(1)}, bf16[192,384]{1,0:T(8,128)(2,1)S(1)}) custom-call(f32[1,1216]{1,0:T(1,128)S(1)} %get-tuple-element.470.bias_ref, f32[1,1]{1,0:T(1,128)} %bitcast.5.floor_ref, bf16[1024,1152]{1,0:T(8,128)(2,1)S(1)} %copy-done.2, bf16[192,1152]{1,0:T(8,128)(2,1)S(1)} %copy-done.5, bf16[1024,1152]{1,0:T(8,128)(2,1)S(1)} %copy-done.2, ...), custom_call_target="tpu_custom_call" | custom-call | flops 1 | bytes 1 | tf_op jit(solution)/shard_map/attention/pallas_call | solution.py:605
  178.7 19.9 %collective-permute-done.26.refs_10_ = bf16[2,304,768]{2,1,0:T(8,128)(2,1)} collective-permute-done((bf16[2,304,768]{2,1,0:T(8,128)(2,1)}, bf16[2,304,768]{2,1,0:T(8,128)(2,1)}, u32[]{:S(2)}, u32[]{:S(2)}) %collective-permute-start.26) | collective-permute-done | bytes 933920 | tf_op jit(solution)/shard_map/ppermute | solution.py:732
  207.0 12.6 %collective-permute-done.28.refs_12_ = bf16[2,304,768]{2,1,0:T(8,128)(2,1)} collective-permute-done((bf16[2,304,768]{2,1,0:T(8,128)(2,1)}, bf16[2,304,768]{2,1,0:T(8,128)(2,1)}, u32[]{:S(2)}, u32[]{:S(2)}) %collective-permute-start.28) | collective-permute-done | bytes 933920 | tf_op jit(solution)/shard_map/ppermute | solution.py:732
  221.9 13.2 %project.3 = (bf16[1024,1152]{1,0:T(8,128)(2,1)}, bf16[192,1152]{1,0:T(8,128)(2,1)}, bf16[1024,1536]{1,0:T(8,128)(2,1)}, bf16[192,1536]{1,0:T(8,128)(2,1)}) custom-call(bf16[2,304,768]{2,1,0:T(8,128)(2,1)} %get-tuple-element.260.refs_0_.refs_6_.refs_3_.refs_12_, bf16[2,304,768]{2,1,0:T(8,128)(2,1)} %copy-done.19, ...), custom_call_target="tpu_custom_call" | custom-call | flops 1 | bytes 1 | tf_op jit(solution)/shard_map/project/pallas_call | solution.py:831
  237.7 24.7 %attention.3 = (bf16[1024,384]{1,0:T(8,128)(2,1)S(1)}, bf16[192,384]{1,0:T(8,128)(2,1)S(1)}) custom-call(f32[1,1216]{1,0:T(1,128)S(1)} %get-tuple-element.469.bias_ref, f32[1,1]{1,0:T(1,128)} %bitcast.32.floor_ref, bf16[1024,1152]{1,0:T(8,128)(2,1)S(1)} %copy-done.1, bf16[192,1152]{1,0:T(8,128)(2,1)S(1)} %copy-done.3, bf16[1024,1152]{1,0:T(8,128)(2,1)S(1)} %copy-done.1, ...), custom_call_target="tpu_custom_call" | custom-call | flops 1 | bytes 1 | tf_op jit(solution)/shard_map/attention/pallas_call | solution.py:605
  274.5 11.4 %collective-permute-done.33 = bf16[304,768]{1,0:T(8,128)(2,1)S(1)} collective-permute-done((bf16[304,768]{1,0:T(8,128)(2,1)}, bf16[304,768]{1,0:T(8,128)(2,1)S(1)}, u32[]{:S(2)}, u32[]{:S(2)}) %collective-permute-start.33) | collective-permute-done | bytes 466976 | tf_op jit(solution)/shard_map/ppermute | solution.py:732
  291.8 12.5 %collective-permute-done.16.refs_3_ = bf16[304,768]{1,0:T(8,128)(2,1)} collective-permute-done((bf16[304,768]{1,0:T(8,128)(2,1)S(1)}, bf16[304,768]{1,0:T(8,128)(2,1)}, u32[]{:S(2)}, u32[]{:S(2)}) %collective-permute-start.16) | collective-permute-done | bytes 466976 | tf_op jit(solution)/shard_map/ppermute | solution.py:732
  332.0 8.1 collective-permute-done.23.refs_5_
  359.3 17.7 %hidden.2 = (bf16[1024,1536]{1,0:T(8,128)(2,1)}, bf16[192,1536]{1,0:T(8,128)(2,1)}, bf16[1024,1536]{1,0:T(8,128)(2,1)}, bf16[192,1536]{1,0:T(8,128)(2,1)}, bf16[...) custom-call(bf16[304,768]{1,0:T(8,128)(2,1)} %get-tuple-element.253.r, ...), custom_call_target="tpu_custom_call" | custom-call | flops 1 | bytes 1 | tf_op jit(solution)/shard_map/hidden/pallas_call | solution.py:831
  377.0 17.8 %hidden.3 = (bf16[1024,1536]{1,0:T(8,128)(2,1)}, bf16[192,1536]{1,0:T(8,128)(2,1)}, bf16[1024,1536]{1,0:T(8,128)(2,1)}, bf16[192,1536]{1,0:T(8,128)(2,1)}, bf16[...) custom-call(bf16[304,768]{1,0:T(8,128)(2,1)} %get-tuple-element.290.r, ...), custom_call_target="tpu_custom_call" | custom-call | flops 1 | bytes 1 | tf_op jit(solution)/shard_map/hidden/pallas_call | solution.py:831
  394.8 18.6 %outer_sums.4 = bf16[2,1536,1536]{2,1,0:T(8,128)(2,1)} custom-call(bf16[1024,1536]{1,0:T(8,128)(2,1)} %get-tuple-element.347.refs_0_, bf16[1024,1536]{1,0:T(8,128)(2,1)} %get-tuple-element.302.refs_1_.refs_0_, bf16[192,1536]{1,0:T(8,128)(2,1)} %get-tuple-element.348.refs_2_.refs_1_, bf16[192,1536]{1,0:T(8,128)(2,1)} %get-tuple-element.303.refs_3_.refs_1_, ...), custom_call_target="tpu_custom_call" | custom-call | flops 1 | bytes 1 | tf_op jit(solution)/shard_map/outer_sums/pallas_call | solution.py:831
  413.7 21.4 %hidden_back.2 = (bf16[1024,1536]{1,0:T(8,128)(2,1)}, bf16[192,1536]{1,0:T(8,128)(2,1)}, f32[2,1536]{1,0:T(2,128)}, bf16[304,768]{1,0:T(8,128)(2,1)}, bf16[304,7...) custom-call(bf16[1024,1536]{1,0:T(8,128)(2,1)} %get-tuple-element.30, ...), custom_call_target="tpu_custom_call" | custom-call | flops 1 | bytes 1 | tf_op jit(solution)/shard_map/hidden_back/pallas_call | solution.py:831
  439.2 21.3 %hidden_back.3 = (bf16[1024,1536]{1,0:T(8,128)(2,1)}, bf16[192,1536]{1,0:T(8,128)(2,1)}, f32[2,1536]{1,0:T(2,128)}, bf16[304,768]{1,0:T(8,128)(2,1)}, bf16[304,7...) custom-call(bf16[1024,1536]{1,0:T(8,128)(2,1)} %get-tuple-element.31, ...), custom_call_target="tpu_custom_call" | custom-call | flops 1 | bytes 1 | tf_op jit(solution)/shard_map/hidden_back/pallas_call | solution.py:831
  470.2 19.0 %outer_sums.5 = bf16[2,1536,1536]{2,1,0:T(8,128)(2,1)} custom-call(bf16[1024,1536]{1,0:T(8,128)(2,1)} %get-tuple-element.329.refs_0_, bf16[1024,1536]{1,0:T(8,128)(2,1)} %get-tuple-element.288.refs_1_, bf16[192,1536]{1,0:T(8,128)(2,1)} %get-tuple-element.330.refs_2_, bf16[192,1536]{1,0:T(8,128)(2,1)} %get-tuple-element.289.refs_3_, ...), custom_call_target="tpu_custom_call" | custom-call | flops 1 | bytes 1 | tf_op jit(solution)/shard_map/outer_sums/pallas_call | solution.py:831
  493.9 7.3 middle_back.2
  519.5 17.2 %partial_sums.5 = (bf16[2,304,768]{2,1,0:T(8,128)(2,1)}, bf16[2,304,768]{2,1,0:T(8,128)(2,1)}, bf16[2,304,768]{2,1,0:T(8,128)(2,1)}, bf16[2,304,768]{2,1,0:T(8,1...) custom-call(bf16[1024,1536]{1,0:T(8,128)(2,1)} %get-tuple-element.34, ...), custom_call_target="tpu_custom_call" | custom-call | flops 1 | bytes 1 | tf_op jit(solution)/shard_map/partial_sums/pallas_call | solution.py:831
  563.2 47.1 %attention_back.2 = (bf16[1024,1152]{1,0:T(8,128)(2,1)S(1)}, bf16[192,1152]{1,0:T(8,128)(2,1)S(1)}) custom-call(f32[1216,128]{1,0:T(8,128)S(1)} %broadcast_in_dim.108.bias_ref, f32[1,1]{1,0:T(1,128)} %bitcast.5.floor_ref, bf16[1024,1152]{1,0:T(8,128)(2,1)} %get-tuple-element.240.qi.ki.vi, bf16[192,1152]{1,0:T(8,128)(2,1)S(1)} %copy-done.6, ...), custom_call_target="tpu_custom_call" | custom-call | flops 1 | bytes 1 | tf_op jit(solution)/shard_map/attention_back/pallas_call | solution.py:690
  619.9 8.9 outer_sums.6
  628.8 12.3 %project_back.2 = (f32[4,1536]{1,0:T(4,128)}, f32[2,1152]{1,0:T(2,128)}, bf16[304,768]{1,0:T(8,128)(2,1)}, bf16[304,768]{1,0:T(8,128)(2,1)}, bf16[304,768]{1,0:T...) custom-call(bf16[1024,1152]{1,0:T(8,128)(2,1)} %copy-done.7, ...), custom_call_target="tpu_custom_call" | custom-call | flops 1 | bytes 1 | tf_op jit(solution)/shard_map/project_back/pallas_call | solution.py:831
  641.1 7.6 reduce-scatter.7.cloned.1.call-done
  653.0 19.7 %collective-permute-done.69 = bf16[2,304,768]{2,1,0:T(8,128)(2,1)S(1)} collective-permute-done((bf16[2,304,768]{2,1,0:T(8,128)(2,1)}, bf16[2,304,768]{2,1,0:T(8,128)(2,1)S(1)}, u32[]{:S(2)}, u32[]{:S(2)}) %collective-permute-start.69) | collective-permute-done | bytes 933920 | tf_op jit(solution)/shard_map/ppermute | solution.py:732
  676.2 17.8 %collective-permute-done.68.refs_2_ = bf16[2,304,768]{2,1,0:T(8,128)(2,1)S(1)} collective-permute-done((bf16[2,304,768]{2,1,0:T(8,128)(2,1)}, bf16[2,304,768]{2,1,0:T(8,128)(2,1)S(1)}, u32[]{:S(2)}, u32[]{:S(2)}) %collective-permute-start.68) | collective-permute-done | bytes 933920 | tf_op jit(solution)/shard_map/ppermute | solution.py:732
  695.3 47.0 %attention_back.3 = (bf16[1024,1152]{1,0:T(8,128)(2,1)S(1)}, bf16[192,1152]{1,0:T(8,128)(2,1)S(1)}) custom-call(f32[1216,128]{1,0:T(8,128)S(1)} %broadcast_in_dim.110.bias_ref, f32[1,1]{1,0:T(1,128)} %bitcast.32.floor_ref, bf16[1024,1152]{1,0:T(8,128)(2,1)} %get-tuple-element.268.qi.ki.vi, bf16[192,1152]{1,0:T(8,128)(2,1)S(1)} %copy-done.4, ...), custom_call_target="tpu_custom_call" | custom-call | flops 1 | bytes 1 | tf_op jit(solution)/shard_map/attention_back/pallas_call | solution.py:690
  746.5 15.0 %outer_sums.7 = bf16[2,1152,1536]{2,1,0:T(8,128)(2,1)} custom-call(bf16[1024,1152]{1,0:T(8,128)(2,1)} %copy-done.7, bf16[1024,1536]{1,0:T(8,128)(2,1)} %get-tuple-element.417.refs_1_, bf16[192,1152]{1,0:T(8,128)(2,1)} %copy-done.11, bf16[192,1536]{1,0:T(8,128)(2,1)} %get-tuple-element.418.refs_3_, bf16[1024,1152]{1,0:T(8,128)(2,1)} %copy-done.8, ...), custom_call_target="tpu_custom_call" | custom-call | flops 1 | bytes 1 | tf_op jit(solution)/shard_map/outer_sums/pallas_call | solution.py:831
  766.9 12.9 %project_back.3 = (f32[4,1536]{1,0:T(4,128)}, f32[2,1152]{1,0:T(2,128)}, bf16[304,768]{1,0:T(8,128)(2,1)}, bf16[304,768]{1,0:T(8,128)(2,1)}, bf16[304,768]{1,0:T...) custom-call(bf16[1024,1152]{1,0:T(8,128)(2,1)} %copy-done.8, ...), custom_call_target="tpu_custom_call" | custom-call | flops 1 | bytes 1 | tf_op jit(solution)/shard_map/project_back/pallas_call | solution.py:831
  779.8 7.4 result.1
  840.1 10.0 %collective-permute-done.80.refs_8_ = bf16[304,768]{1,0:T(8,128)(2,1)S(1)} collective-permute-done((bf16[304,768]{1,0:T(8,128)(2,1)}, bf16[304,768]{1,0:T(8,128)(2,1)S(1)}, u32[]{:S(2)}, u32[]{:S(2)}) %collective-permute-start.80) | collective-permute-done | bytes 466976 | tf_op jit(solution)/shard_map/ppermute | solution.py:732
  859.3 8.9 input_back.1
  (548 shorter events, 348.2 us)
Async XLA Ops:
  7.2 122.8 %all-gather.5.cloned.1.call-start = ((), (), s32[]{:S(2)}) async-start(), calls=%async_computation.10 | async-start | bytes 7962624 | tf_op jit(solution)/shard_map/all_gather | solution.py:1471
  44.1 156.3 %all-gather.7.cloned.1.call-start = ((), (), s32[]{:S(2)}) async-start(), calls=%async_computation.11 | async-start | bytes 2654208 | tf_op jit(solution)/shard_map/all_gather | solution.py:1471
  54.0 40.4 %collective-permute-start.6 = (bf16[2,304,768]{2,1,0:T(8,128)(2,1)S(1)}, bf16[2,304,768]{2,1,0:T(8,128)(2,1)}, u32[]{:S(2)}, u32[]{:S(2)}) collective-permute-start(bf16[2,304,768]{2,1,0:T(8,128)(2,1)S(1)} %get-tuple-element.261.refs_1_.refs_7_.refs_4_.refs_13_), channel_id=1, source_target_pairs={{0,2},{1,3},{2,0},{3,1},{4,6},{5,7},{6,4},{7,5},{8,10},{9,11},{10,... | collective-permute-start | bytes 2801672 | tf_op jit(solution)/shard_map/ppermute | solution.py:732
  55.4 40.1 %collective-permute-start.4 = (bf16[2,304,768]{2,1,0:T(8,128)(2,1)S(1)}, bf16[2,304,768]{2,1,0:T(8,128)(2,1)}, u32[]{:S(2)}, u32[]{:S(2)}) collective-permute-start(bf16[2,304,768]{2,1,0:T(8,128)(2,1)S(1)} %get-tuple-element.261.refs_1_.refs_7_.refs_4_.refs_13_), channel_id=1, source_target_pairs={{0,1},{1,0},{2,3},{3,2},{4,5},{5,4},{6,7},{7,6},{8,9},{9,8},{10,11... | collective-permute-start | bytes 2801672 | tf_op jit(solution)/shard_map/ppermute | solution.py:732
  63.2 296.0 %all-gather.9.cloned.1.call-start = ((), (), s32[]{:S(2)}) async-start(), calls=%async_computation.12 | async-start | bytes 10616832 | tf_op jit(solution)/shard_map/all_gather | solution.py:1471
  125.5 288.2 %all-gather.11.cloned.1.call-start = ((), (), s32[]{:S(2)}) async-start(), calls=%async_computation.13 | async-start | bytes 10616832 | tf_op jit(solution)/shard_map/all_gather | solution.py:1471
  171.6 380.4 %reduce-scatter.5.cloned.1.call-start = ((), (), s32[]{:S(2)}) async-start(), calls=%async_computation.14 | async-start | bytes 10616832 | tf_op jit(solution)/shard_map/reduce_scatter | solution.py:1491
  176.4 43.2 %collective-permute-start.28 = (bf16[2,304,768]{2,1,0:T(8,128)(2,1)}, bf16[2,304,768]{2,1,0:T(8,128)(2,1)}, u32[]{:S(2)}, u32[]{:S(2)}) collective-permute-start(bf16[2,304,768]{2,1,0:T(8,128)(2,1)} %get-tuple-element.255.refs_8_.refs_6_), channel_id=1, source_target_pairs={{0,2},{1,3},{2,0},{3,1},{4,6},{5,7},{6,4},{7,5},{8,10},{9,11},{10,... | collective-permute-start | bytes 2801672 | tf_op jit(solution)/shard_map/ppermute | solution.py:732
  177.9 42.6 %collective-permute-start.27 = (bf16[2,304,768]{2,1,0:T(8,128)(2,1)S(1)}, bf16[2,304,768]{2,1,0:T(8,128)(2,1)}, u32[]{:S(2)}, u32[]{:S(2)}) collective-permute-start(bf16[2,304,768]{2,1,0:T(8,128)(2,1)S(1)} %get-tuple-element.256.refs_9_.refs_7_), channel_id=1, source_target_pairs={{0,1},{1,0},{2,3},{3,2},{4,5},{5,4},{6,7},{7,6},{8,9},{9,8},{10,11... | collective-permute-start | bytes 2801672 | tf_op jit(solution)/shard_map/ppermute | solution.py:732
  198.6 65.5 %collective-permute-start.30 = (bf16[2,304,768]{2,1,0:T(8,128)(2,1)}, bf16[2,304,768]{2,1,0:T(8,128)(2,1)}, u32[]{:S(2)}, u32[]{:S(2)}) collective-permute-start(bf16[2,304,768]{2,1,0:T(8,128)(2,1)} %collective-permute-done.26.refs_10_), channel_id=1, source_target_pairs={{0,2},{1,3},{2,0},{3,1},{4,6},{5,7},{6,4},{7,5},{8,10},{9,11},{10,... | collective-permute-start | bytes 2801672 | tf_op jit(solution)/shard_map/ppermute | solution.py:732
  199.6 65.0 %collective-permute-start.31 = (bf16[2,304,768]{2,1,0:T(8,128)(2,1)}, bf16[2,304,768]{2,1,0:T(8,128)(2,1)}, u32[]{:S(2)}, u32[]{:S(2)}) collective-permute-start(bf16[2,304,768]{2,1,0:T(8,128)(2,1)} %collective-permute-done.29.refs_13_), channel_id=1, source_target_pairs={{0,1},{1,0},{2,3},{3,2},{4,5},{5,4},{6,7},{7,6},{8,9},{9,8},{10,11... | collective-permute-start | bytes 2801672 | tf_op jit(solution)/shard_map/ppermute | solution.py:732
  205.5 65.9 %collective-permute-start.15 = (bf16[304,768]{1,0:T(8,128)(2,1)}, bf16[304,768]{1,0:T(8,128)(2,1)S(1)}, u32[]{:S(2)}, u32[]{:S(2)}) collective-permute-start(bf16[304,768]{1,0:T(8,128)(2,1)} %get-tuple-element.249), channel_id=1, source_target_pairs={{0,2},{1,3},{2,0},{3,1},{4,6},{5,7},{6,4},{7,5},{8,10},{9,11},{10,... | collective-permute-start | bytes 1400840 | tf_op jit(solution)/shard_map/ppermute | solution.py:732
  219.6 52.5 %collective-permute-start.17 = (bf16[304,768]{1,0:T(8,128)(2,1)}, bf16[304,768]{1,0:T(8,128)(2,1)S(1)}, u32[]{:S(2)}, u32[]{:S(2)}) collective-permute-start(bf16[304,768]{1,0:T(8,128)(2,1)} %get-tuple-element.251), channel_id=1, source_target_pairs={{0,1},{1,0},{2,3},{3,2},{4,5},{5,4},{6,7},{7,6},{8,9},{9,8},{10,11... | collective-permute-start | bytes 1400840 | tf_op jit(solution)/shard_map/ppermute | solution.py:732
  220.5 68.6 %collective-permute-start.14 = (bf16[304,768]{1,0:T(8,128)(2,1)}, bf16[304,768]{1,0:T(8,128)(2,1)S(1)}, u32[]{:S(2)}, u32[]{:S(2)}) collective-permute-start(bf16[304,768]{1,0:T(8,128)(2,1)} %get-tuple-element.247), channel_id=1, source_target_pairs={{0,1},{1,0},{2,3},{3,2},{4,5},{5,4},{6,7},{7,6},{8,9},{9,8},{10,11... | collective-permute-start | bytes 1400840 | tf_op jit(solution)/shard_map/ppermute | solution.py:732
  272.2 40.1 %collective-permute-start.32 = (bf16[304,768]{1,0:T(8,128)(2,1)}, bf16[304,768]{1,0:T(8,128)(2,1)S(1)}, u32[]{:S(2)}, u32[]{:S(2)}) collective-permute-start(bf16[304,768]{1,0:T(8,128)(2,1)} %get-tuple-element.276), channel_id=1, source_target_pairs={{0,1},{1,0},{2,3},{3,2},{4,5},{5,4},{6,7},{7,6},{8,9},{9,8},{10,11... | collective-permute-start | bytes 1400840 | tf_op jit(solution)/shard_map/ppermute | solution.py:732
  413.4 235.3 %reduce-scatter.7.cloned.1.call-start = ((), (), s32[]{:S(2)}) async-start(), calls=%async_computation.15 | async-start | bytes 10616832 | tf_op jit(solution)/shard_map/reduce_scatter | solution.py:1491
  436.5 52.8 %collective-permute-start.44 = (bf16[304,768]{1,0:T(8,128)(2,1)}, bf16[304,768]{1,0:T(8,128)(2,1)S(1)}, u32[]{:S(2)}, u32[]{:S(2)}) collective-permute-start(bf16[304,768]{1,0:T(8,128)(2,1)} %get-tuple-element.307), channel_id=1, source_target_pairs={{0,1},{1,0},{2,3},{3,2},{4,5},{5,4},{6,7},{7,6},{8,9},{9,8},{10,11... | collective-permute-start | bytes 1400840 | tf_op jit(solution)/shard_map/ppermute | solution.py:732
  437.7 54.1 %collective-permute-start.49 = (bf16[304,768]{1,0:T(8,128)(2,1)}, bf16[304,768]{1,0:T(8,128)(2,1)S(1)}, u32[]{:S(2)}, u32[]{:S(2)}) collective-permute-start(bf16[304,768]{1,0:T(8,128)(2,1)} %get-tuple-element.312), channel_id=1, source_target_pairs={{0,2},{1,3},{2,0},{3,1},{4,6},{5,7},{6,4},{7,5},{8,10},{9,11},{10,... | collective-permute-start | bytes 1400840 | tf_op jit(solution)/shard_map/ppermute | solution.py:732
  505.7 39.0 %collective-permute-start.64 = (bf16[304,768]{1,0:T(8,128)(2,1)}, bf16[304,768]{1,0:T(8,128)(2,1)S(1)}, u32[]{:S(2)}, u32[]{:S(2)}) collective-permute-start(bf16[304,768]{1,0:T(8,128)(2,1)} %get-tuple-element.371.refs_0_), channel_id=1, source_target_pairs={{0,2},{1,3},{2,0},{3,1},{4,6},{5,7},{6,4},{7,5},{8,10},{9,11},{10,... | collective-permute-start | bytes 1400840 | tf_op jit(solution)/shard_map/ppermute | solution.py:732
  552.1 209.5 %reduce-scatter.9.cloned.1.call-start = ((), (), s32[]{:S(2)}) async-start(), calls=%async_computation.16 | async-start | bytes 2654208 | tf_op jit(solution)/shard_map/reduce_scatter | solution.py:1491
  553.5 59.0 %collective-permute-start.58 = (bf16[304,768]{1,0:T(8,128)(2,1)}, bf16[304,768]{1,0:T(8,128)(2,1)S(1)}, u32[]{:S(2)}, u32[]{:S(2)}) collective-permute-start(bf16[304,768]{1,0:T(8,128)(2,1)} %get-tuple-element.383.refs_0_), channel_id=1, source_target_pairs={{0,2},{1,3},{2,0},{3,1},{4,6},{5,7},{6,4},{7,5},{8,10},{9,11},{10,... | collective-permute-start | bytes 1400840 | tf_op jit(solution)/shard_map/ppermute | solution.py:732
  555.0 57.5 %collective-permute-start.57 = (bf16[304,768]{1,0:T(8,128)(2,1)}, bf16[304,768]{1,0:T(8,128)(2,1)S(1)}, u32[]{:S(2)}, u32[]{:S(2)}) collective-permute-start(bf16[304,768]{1,0:T(8,128)(2,1)} %get-tuple-element.384.refs_1_), channel_id=1, source_target_pairs={{0,1},{1,0},{2,3},{3,2},{4,5},{5,4},{6,7},{7,6},{8,9},{9,8},{10,11... | collective-permute-start | bytes 1400840 | tf_op jit(solution)/shard_map/ppermute | solution.py:732
  560.9 51.5 %collective-permute-start.60 = (bf16[304,768]{1,0:T(8,128)(2,1)S(1)}, bf16[304,768]{1,0:T(8,128)(2,1)S(1)}, u32[]{:S(2)}, u32[]{:S(2)}) collective-permute-start(bf16[304,768]{1,0:T(8,128)(2,1)S(1)} %collective-permute-done.56.refs_2_), channel_id=1, source_target_pairs={{0,2},{1,3},{2,0},{3,1},{4,6},{5,7},{6,4},{7,5},{8,10},{9,11},{10,... | collective-permute-start | bytes 1400840 | tf_op jit(solution)/shard_map/ppermute | solution.py:732
  561.7 50.8 %collective-permute-start.61 = (bf16[304,768]{1,0:T(8,128)(2,1)S(1)}, bf16[304,768]{1,0:T(8,128)(2,1)S(1)}, u32[]{:S(2)}, u32[]{:S(2)}) collective-permute-start(bf16[304,768]{1,0:T(8,128)(2,1)S(1)} %collective-permute-done.59.refs_5_), channel_id=1, source_target_pairs={{0,1},{1,0},{2,3},{3,2},{4,5},{5,4},{6,7},{7,6},{8,9},{9,8},{10,11... | collective-permute-start | bytes 1400840 | tf_op jit(solution)/shard_map/ppermute | solution.py:732
  648.8 225.3 %reduce-scatter.11.cloned.1.call-start = ((), (), s32[]{:S(2)}) async-start(), calls=%async_computation.17 | async-start | bytes 7962624 | tf_op jit(solution)/shard_map/reduce_scatter | solution.py:1491
  651.8 42.2 %collective-permute-start.68 = (bf16[2,304,768]{2,1,0:T(8,128)(2,1)}, bf16[2,304,768]{2,1,0:T(8,128)(2,1)S(1)}, u32[]{:S(2)}, u32[]{:S(2)}) collective-permute-start(bf16[2,304,768]{2,1,0:T(8,128)(2,1)} %get-tuple-element.393), channel_id=1, source_target_pairs={{0,1},{1,0},{2,3},{3,2},{4,5},{5,4},{6,7},{7,6},{8,9},{9,8},{10,11... | collective-permute-start | bytes 2801672 | tf_op jit(solution)/shard_map/ppermute | solution.py:732
  652.4 41.7 %collective-permute-start.73 = (bf16[2,304,768]{2,1,0:T(8,128)(2,1)}, bf16[2,304,768]{2,1,0:T(8,128)(2,1)S(1)}, u32[]{:S(2)}, u32[]{:S(2)}) collective-permute-start(bf16[2,304,768]{2,1,0:T(8,128)(2,1)} %get-tuple-element.396), channel_id=1, source_target_pairs={{0,2},{1,3},{2,0},{3,1},{4,6},{5,7},{6,4},{7,5},{8,10},{9,11},{10,... | collective-permute-start | bytes 2801672 | tf_op jit(solution)/shard_map/ppermute | solution.py:732
  672.9 71.6 %collective-permute-start.70 = (bf16[2,304,768]{2,1,0:T(8,128)(2,1)S(1)}, bf16[2,304,768]{2,1,0:T(8,128)(2,1)S(1)}, u32[]{:S(2)}, u32[]{:S(2)}) collective-permute-start(bf16[2,304,768]{2,1,0:T(8,128)(2,1)S(1)} %add_convert_fusion.1), channel_id=1, source_target_pairs={{0,1},{1,0},{2,3},{3,2},{4,5},{5,4},{6,7},{7,6},{8,9},{9,8},{10,11... | collective-permute-start | bytes 2801672 | tf_op jit(solution)/shard_map/ppermute | solution.py:732
  674.7 70.8 %collective-permute-start.72 = (bf16[2,304,768]{2,1,0:T(8,128)(2,1)S(1)}, bf16[2,304,768]{2,1,0:T(8,128)(2,1)S(1)}, u32[]{:S(2)}, u32[]{:S(2)}) collective-permute-start(bf16[2,304,768]{2,1,0:T(8,128)(2,1)S(1)} %add_convert_fusion), channel_id=1, source_target_pairs={{0,2},{1,3},{2,0},{3,1},{4,6},{5,7},{6,4},{7,5},{8,10},{9,11},{10,... | collective-permute-start | bytes 2801672 | tf_op jit(solution)/shard_map/ppermute | solution.py:732
  762.7 66.9 %collective-permute-start.74 = (bf16[304,768]{1,0:T(8,128)(2,1)}, bf16[304,768]{1,0:T(8,128)(2,1)S(1)}, u32[]{:S(2)}, u32[]{:S(2)}) collective-permute-start(bf16[304,768]{1,0:T(8,128)(2,1)} %get-tuple-element.405), channel_id=1, source_target_pairs={{0,1},{1,0},{2,3},{3,2},{4,5},{5,4},{6,7},{7,6},{8,9},{9,8},{10,11... | collective-permute-start | bytes 1400840 | tf_op jit(solution)/shard_map/ppermute | solution.py:732
  764.3 66.9 %collective-permute-start.79 = (bf16[304,768]{1,0:T(8,128)(2,1)}, bf16[304,768]{1,0:T(8,128)(2,1)S(1)}, u32[]{:S(2)}, u32[]{:S(2)}) collective-permute-start(bf16[304,768]{1,0:T(8,128)(2,1)} %get-tuple-element.408), channel_id=1, source_target_pairs={{0,2},{1,3},{2,0},{3,1},{4,6},{5,7},{6,4},{7,5},{8,10},{9,11},{10,... | collective-permute-start | bytes 1400840 | tf_op jit(solution)/shard_map/ppermute | solution.py:732
  765.4 39.8 %collective-permute-start.75 = (bf16[304,768]{1,0:T(8,128)(2,1)}, bf16[304,768]{1,0:T(8,128)(2,1)}, u32[]{:S(2)}, u32[]{:S(2)}) collective-permute-start(bf16[304,768]{1,0:T(8,128)(2,1)} %get-tuple-element.410), channel_id=1, source_target_pairs={{0,2},{1,3},{2,0},{3,1},{4,6},{5,7},{6,4},{7,5},{8,10},{9,11},{10,... | collective-permute-start | bytes 1400840 | tf_op jit(solution)/shard_map/ppermute | solution.py:732
  (165 other events, 2807.2 us)
Sparse Core Ops, SparseCore 0:
  30.5 75.2 all-gather.4
  108.0 31.5 all-gather.6
  141.2 89.1 all-gather.8
  231.8 89.1 all-gather.10
  413.6 96.8 reduce-scatter.4
  552.2 96.5 reduce-scatter.6
  651.1 31.3 reduce-scatter.8
  761.7 78.2 reduce-scatter.10

commit v5 on v4

--- a/solution.py
+++ b/solution.py
@@ -562,29 +562,81 @@
     return lax.dot_general(a, b, (((0,), (0,)), ((), ())), preferred_element_type=F32)
 
 
+WEIGHT = {
+    "attention": 8.5,
+    "attention_back": 16,
+    "project": 6.5,
+    "partial_sums": 2.5,
+    "middle": 2.5,
+    "hidden": 9,
+    "outer_sums": 9,
+    "hidden_back": 10,
+    "middle_back": 3.5,
+    "attended_back": 3,
+    "project_back": 6,
+    "result": 3.5,
+    "input_back": 4.5,
+}
+
+
+def lanes_of(columns, rows, width):
+    lane = lax.broadcasted_iota(jnp.int32, (rows, width), 1)
+    out = jnp.zeros((rows, width), F32)
+    for k, column in enumerate(columns):
+        out = jnp.where(lane == k, column, out)
+    return out.astype(BF16)
+
+
+def three_parts(column):
+    high = column.astype(BF16).astype(F32)
+    rest = column - high
+    mid = rest.astype(BF16).astype(F32)
+    return [high, mid, rest - mid]
+
+
 def attention_kernel(
-    query_rows, scale, head, bias_ref, floor_ref, qi, qt, ki, kt, vi, vt, oi, ot, keys, values
+    query_rows, scale, head, bias_ref, floor_ref, qi, qt, ki, kt, vi, vt, oi, ot, li, lt, keys, values
 ):
     image_rows = qi.shape[0]
-    keys[:image_rows] = ki[...]
-    keys[image_rows:] = kt[...]
-    values[:image_rows] = vi[...]
-    values[image_rows:] = vt[...]
-    bias = bias_ref[...]
+    rows = keys.shape[1]
     floor = floor_ref[0, 0]
-    spans = [(qi, oi, start, query_rows) for start in range(0, image_rows, query_rows)]
-    spans.append((qt, ot, 0, qt.shape[0]))
-    for source, target, start, size in spans:
-        sides = []
-        for side in range(2):
-            lanes = slice(side * head, (side + 1) * head)
-            scores = dot_nt(source[start : start + size, lanes], keys[:, lanes]) * scale + bias
-            row_max = jnp.maximum(jnp.max(scores, axis=1, keepdims=True), floor)
-            exps = jnp.exp2(scores - row_max)
-            total = jnp.maximum(jnp.sum(exps, axis=1, keepdims=True), 1.0)
-            probs = (exps * (1.0 / total)).astype(BF16)
-            sides.append(dot_nn(probs, values[:, lanes]))
-        target[start : start + size, :] = jnp.concatenate(sides, axis=1).astype(BF16)
+    key_side = lanes_of([bias_ref[:, 0:1]], rows, head)
+    value_side = lanes_of([1.0], rows, head)
+    for side in range(2):
+        lanes = slice(side * head, (side + 1) * head)
+        for ref, extra, first, second in (
+            (keys, key_side, ki, kt),
+            (values, value_side, vi, vt),
+        ):
+            ref[side, :image_rows, :] = jnp.concatenate(
+                [first[:, lanes], extra[:image_rows]], axis=1
+            )
+            ref[side, image_rows:, :] = jnp.concatenate(
+                [second[:, lanes], extra[image_rows:]], axis=1
+            )
+    spans = [(qi, oi, li, start, query_rows) for start in range(0, image_rows, query_rows)]
+    spans.append((qt, ot, lt, 0, qt.shape[0]))
+    steps = [(*span, side) for span in spans for side in range(2)]
+
+    def score(step):
+        source, _, _, start, size, side = step
+        query = source[start : start + size, side * head : (side + 1) * head]
+        query = jnp.concatenate([query, lanes_of([1.0], size, head)], axis=1)
+        return dot_nt(query, keys[side])
+
+    ahead = score(steps[0])
+    for at, (_, target, logs, start, size, side) in enumerate(steps):
+        scores = ahead
+        if at + 1 < len(steps):
+            ahead = score(steps[at + 1])
+        top = jnp.maximum(jnp.max(scores, axis=1, keepdims=True) * scale, floor)
+        exps = jnp.exp2(scores * scale - top).astype(BF16)
+        product = dot_nn(exps, values[side])
+        total = jnp.maximum(product[:, head : head + 1], 1.0)
+        span = slice(start, start + size)
+        lanes = slice(side * head, (side + 1) * head)
+        target[span, lanes] = (product[:, :head] * (1.0 / total)).astype(BF16)
+        logs[span, lanes] = jnp.broadcast_to(top + jnp.log2(total), (size, head))
 
 
 def pair_block(rows, lanes, pairs, part):
@@ -606,77 +658,101 @@
         functools.partial(attention_kernel, 256, LOG2E / math.sqrt(head), head),
         grid=(pairs,),
         in_specs=[
-            pl.BlockSpec((1, rows), lambda pair: (0, 0)),
+            pl.BlockSpec((rows, 128), lambda pair: (0, 0)),
             pl.BlockSpec(memory_space=pltpu.SMEM),
             *columns,
         ],
-        out_specs=[columns[0], columns[1]],
+        out_specs=[columns[0], columns[1], columns[0], columns[1]],
         out_shape=[
-            jax.ShapeDtypeStruct((image_rows, width // 3), BF16),
-            jax.ShapeDtypeStruct((text_rows, width // 3), BF16),
+            jax.ShapeDtypeStruct((count, width // 3), dtype)
+            for dtype in (BF16, F32)
+            for count in (image_rows, text_rows)
         ],
-        scratch_shapes=[pltpu.VMEM((rows, lanes), BF16), pltpu.VMEM((rows, lanes), BF16)],
-        compiler_params=pltpu.CompilerParams(vmem_limit_bytes=48 << 20),
+        scratch_shapes=[pltpu.VMEM((2, rows, lanes), BF16)] * 2,
+        compiler_params=pltpu.CompilerParams(vmem_limit_bytes=56 << 20),
         cost_estimate=pl.CostEstimate(
-            flops=1,
-            bytes_accessed=1,
-            transcendentals=0,
+            flops=int(WEIGHT["attention"] * 1.15e9), bytes_accessed=1, transcendentals=0
         ),
         name="attention",
-    )(key_bias[None, :], floor, qkv_image, qkv_text, qkv_image, qkv_text, qkv_image, qkv_text)
-
-
-def attention_back_kernel(
-    query_rows, scale, factor, head, pairs,
-    bias_ref, floor_ref, qi, qt, ki, kt, vi, vt, gi, gt, oi, ot, keys, values, key_sum, value_sum,
-):
+    )(key_bias, floor, qkv_image, qkv_text, qkv_image, qkv_text, qkv_image, qkv_text)
+
+
+def attention_back_kernel(query_rows, scale, factor, head, pairs, *refs):
+    (bias_ref, qi, qt, ki, kt, vi, vt, ai, at, li, lt, gi, gt) = refs[:13]
+    oi, ot, keys, values, key_sum, value_sum = refs[13:]
     pair = pl.program_id(0)
     image_rows = qi.shape[0]
+    rows = keys.shape[1]
     width = 2 * head
-    keys[:image_rows] = ki[...]
-    keys[image_rows:] = kt[...]
-    values[:image_rows] = vi[...]
-    values[image_rows:] = vt[...]
+    key_side = lanes_of([bias_ref[:, 0:1], 1.0, 1.0, 1.0], rows, head)
+    value_side = lanes_of([1.0, 1.0, 1.0], rows, head)
+    for side in range(2):
+        lanes = slice(side * head, (side + 1) * head)
+        for ref, extra, first, second in (
+            (keys, key_side, ki, kt),
+            (values, value_side, vi, vt),
+        ):
+            ref[side, :image_rows, :] = jnp.concatenate(
+                [first[:, lanes], extra[:image_rows]], axis=1
+            )
+            ref[side, image_rows:, :] = jnp.concatenate(
+                [second[:, lanes], extra[image_rows:]], axis=1
+            )
     key_sum[...] = jnp.zeros_like(key_sum)
     value_sum[...] = jnp.zeros_like(value_sum)
-    bias = bias_ref[...]
-    floor = floor_ref[0, 0]
-    spans = [(qi, gi, oi, start, query_rows) for start in range(0, image_rows, query_rows)]
-    spans.append((qt, gt, ot, 0, qt.shape[0]))
+    spans = [(qi, ai, li, gi, oi, start, query_rows) for start in range(0, image_rows, query_rows)]
+    spans.append((qt, at, lt, gt, ot, 0, qt.shape[0]))
+    steps = [(*span, side) for span in spans for side in range(2)]
     query_lanes = pl.ds(pl.multiple_of(pair * width, width), width)
     key_lanes = pl.ds(pl.multiple_of((pairs + pair) * width, width), width)
     value_lanes = pl.ds(pl.multiple_of((2 * pairs + pair) * width, width), width)
-    for source, grads, target, start, size in spans:
-        wide_bias = jnp.concatenate([bias] * -(-size // 128), axis=1)[:, :size]
-        dq, dk, dv = ([], [], [])
-        for side in range(2):
-            lanes = slice(side * head, (side + 1) * head)
-            query = source[start : start + size, lanes]
-            grad = grads[start : start + size, lanes]
-            scores = dot_nt(keys[:, lanes], query) * scale + wide_bias
-            top = jnp.maximum(jnp.max(scores, axis=0, keepdims=True), floor)
-            exps = jnp.exp2(scores - top)
-            total = jnp.maximum(jnp.sum(exps, axis=0, keepdims=True), 1.0)
-            probs = exps * (1.0 / total)
-            prob_grad = dot_nt(values[:, lanes], grad)
-            weighted = probs * prob_grad
-            inner = jnp.sum(weighted, axis=0, keepdims=True)
-            score_grad = (weighted - probs * inner).astype(BF16)
-            dv.append(dot_nn(probs.astype(BF16), grad))
-            dk.append(dot_nn(score_grad, query))
-            dq.append(dot_tn(score_grad, keys[:, lanes]))
-        key_sum[...] += jnp.concatenate(dk, axis=1)
-        value_sum[...] += jnp.concatenate(dv, axis=1)
-        target[start : start + size, query_lanes] = (
-            jnp.concatenate(dq, axis=1) * factor
-        ).astype(BF16)
+
+    def products(step):
+        source, outs, logs, grads, _, start, size, side = step
+        span = slice(start, start + size)
+        lanes = slice(side * head, (side + 1) * head)
+        query, grad = (source[span, lanes], grads[span, lanes])
+        log = logs[span, side * head : side * head + 1] * (-1.0 / scale)
+        inner = -jnp.sum(
+            grad.astype(F32) * outs[span, lanes].astype(F32), axis=1, keepdims=True
+        )
+        query_wide = jnp.concatenate(
+            [query, lanes_of([1.0, *three_parts(log)], size, head)], axis=1
+        )
+        grad_wide = jnp.concatenate([grad, lanes_of(three_parts(inner), size, head)], axis=1)
+        return (
+            query,
+            grad,
+            dot_nt(keys[side], query_wide),
+            dot_nt(values[side], grad_wide),
+        )
+
+    ahead = products(steps[0])
+    dq = []
+    for at_step, (_, _, _, _, target, start, size, side) in enumerate(steps):
+        query, grad, scores, prob_grad = ahead
+        if at_step + 1 < len(steps):
+            ahead = products(steps[at_step + 1])
+        probs = jnp.exp2(scores * scale)
+        score_grad = (probs * prob_grad).astype(BF16)
+        lanes = slice(side * head, (side + 1) * head)
+        value_sum[:, lanes] += dot_nn(probs.astype(BF16), grad)
+        key_sum[:, lanes] += dot_nn(score_grad, query)
+        dq.append(dot_tn(score_grad, keys[side][:, :head]))
+        if side == 1:
+            target[start : start + size, query_lanes] = (
+                jnp.concatenate(dq, axis=1) * factor
+            ).astype(BF16)
+            dq = []
     oi[:, key_lanes] = (key_sum[:image_rows] * factor).astype(BF16)
     ot[:, key_lanes] = (key_sum[image_rows:] * factor).astype(BF16)
     oi[:, value_lanes] = value_sum[:image_rows].astype(BF16)
     ot[:, value_lanes] = value_sum[image_rows:].astype(BF16)
 
 
-def attention_back(qkv_image, qkv_text, grad_image, grad_text, key_bias, floor, head):
+def attention_back(
+    qkv_image, qkv_text, out_image, out_text, log_image, log_text, grad_image, grad_text, key_bias, head
+):
     image_rows, width = qkv_image.shape
     text_rows = qkv_text.shape[0]
     rows = image_rows + text_rows
@@ -689,15 +765,13 @@
     ]
     return pl.pallas_call(
         functools.partial(
-            attention_back_kernel, 256, LOG2E / math.sqrt(head), 1.0 / math.sqrt(head), head, pairs
+            attention_back_kernel, 512, LOG2E / math.sqrt(head), 1.0 / math.sqrt(head), head, pairs
         ),
         grid=(pairs,),
         in_specs=[
             pl.BlockSpec((rows, 128), lambda pair: (0, 0)),
-            pl.BlockSpec(memory_space=pltpu.SMEM),
             *columns,
-            columns[0],
-            columns[1],
+            *(columns[:2] * 3),
         ],
         out_specs=[
             pl.BlockSpec((image_rows, width), lambda pair: (0, 0)),
@@ -707,24 +781,17 @@
             jax.ShapeDtypeStruct((image_rows, width), BF16),
             jax.ShapeDtypeStruct((text_rows, width), BF16),
         ],
-        scratch_shapes=[
-            pltpu.VMEM((rows, lanes), BF16),
-            pltpu.VMEM((rows, lanes), BF16),
-            pltpu.VMEM((rows, lanes), F32),
-            pltpu.VMEM((rows, lanes), F32),
-        ],
-        compiler_params=pltpu.CompilerParams(vmem_limit_bytes=48 << 20),
+        scratch_shapes=[pltpu.VMEM((2, rows, lanes), BF16)] * 2
+        + [pltpu.VMEM((rows, lanes), F32)] * 2,
+        compiler_params=pltpu.CompilerParams(vmem_limit_bytes=56 << 20),
         cost_estimate=pl.CostEstimate(
-            flops=1,
-            bytes_accessed=1,
-            transcendentals=0,
+            flops=int(WEIGHT["attention_back"] * 1.15e9), bytes_accessed=1, transcendentals=0
         ),
         name="attention_back",
     )(
-        jnp.broadcast_to(key_bias[:, None], (rows, 128)),
-        floor,
-        qkv_image, qkv_text, qkv_image, qkv_text, qkv_image, qkv_text,
-        grad_image, grad_text,
+        key_bias,
+        *(qkv_image, qkv_text) * 3,
+        out_image, out_text, log_image, log_text, grad_image, grad_text,
     )
 
 
@@ -748,15 +815,16 @@
     return (a.astype(F32) + b.astype(F32)).astype(BF16)
 
 
-def scatter_first(halves):
-    return (flip(halves[6], 1), flip(halves[7], 2), flip(halves[2], 1), flip(halves[5], 2))
-
-
-def scatter_last(halves, first):
-    for_y, for_x, x_a, y_b = first
-    x_b = flip(add_low(halves[3], for_x), 1)
-    y_a = flip(add_low(halves[4], for_y), 2)
-    return (halves[0], halves[1], x_a, x_b, y_a, y_b)
+def scatter_first(sent):
+    return (flip(sent[1], 1), flip(sent[2], 2))
+
+
+def scatter_last(sent, first):
+    from_x, from_y = first
+    width = sent[3].shape[-1]
+    late_x = flip(add_low(sent[3], from_y[..., :width]), 1)
+    late_y = flip(add_low(sent[4], from_x[..., :width]), 2)
+    return (sent[0], from_x, from_y, late_x, late_y)
 
 
 def scatter_halves(halves):
@@ -800,12 +868,25 @@
     return fetched
 
 
-def send_halves(copies, rows, halves, r, seq):
+def send_block(copies, rows, sent, r, seq):
+    own, for_x, for_y, late_x, late_y = sent if seq is None else [ref.at[seq] for ref in sent]
     width = rows.shape[2] // 2
-    for side in range(2):
-        half = halves[2 * r + side]
-        half = half if seq is None else half.at[seq]
-        copies.send(rows.at[r, :, pl.ds(side * width, width)], half)
+    low, high = pl.ds(0, width), pl.ds(width, width)
+    if r == 0:
+        copies.send(rows.at[0], own)
+        return
+    first, second = {
+        1: (for_x.at[:, high], late_x),
+        2: (late_y, for_y.at[:, high]),
+        3: (for_x.at[:, low], for_y.at[:, low]),
+    }[r]
+    copies.send(rows.at[r, :, low], first)
+    copies.send(rows.at[r, :, high], second)
+
+
+def sent_shapes(block, D, seqs=1):
+    lead = () if seqs == 1 else (seqs,)
+    return [((*lead, block, width), BF16) for width in (D, D, D, D // 2, D // 2)]
 
 
 def normalize(values):
@@ -835,7 +916,9 @@
         out_shape=[jax.ShapeDtypeStruct(shape, dtype) for shape, dtype in outs],
         scratch_shapes=scratch,
         compiler_params=pltpu.CompilerParams(vmem_limit_bytes=56 << 20),
-        cost_estimate=pl.CostEstimate(flops=1, bytes_accessed=1, transcendentals=0),
+        cost_estimate=pl.CostEstimate(
+            flops=int(WEIGHT[name] * 1.15e9), bytes_accessed=1, transcendentals=0
+        ),
         name=name,
     )(*operands)
 
@@ -896,12 +979,12 @@
 
 
 def partial_kernel(seqs, dot, image_rows, *refs):
-    inputs, weight, halves = (refs[: 2 * seqs], refs[2 * seqs], refs[2 * seqs + 1 : 2 * seqs + 9])
+    inputs, weight, halves = (refs[: 2 * seqs], refs[2 * seqs], refs[2 * seqs + 1 : 2 * seqs + 6])
     lefts, held, rows, semaphores = (
-        refs[2 * seqs + 9 : 4 * seqs + 9],
-        refs[4 * seqs + 9],
-        refs[4 * seqs + 10 : 5 * seqs + 10],
-        refs[5 * seqs + 10],
+        refs[2 * seqs + 6 : 4 * seqs + 6],
+        refs[4 * seqs + 6],
+        refs[4 * seqs + 7 : 5 * seqs + 7],
+        refs[5 * seqs + 7],
     )
     copies = Copies(semaphores)
     weights = [copies.start(weight.at[t], held.at[t]) for t in (1, 0)]
@@ -922,7 +1005,7 @@
         for r in (3, 1, 2, 0):
             left = lefts[2 * s][r * image_rows : (r + 1) * image_rows, :]
             rows[s][r, :image_rows, :] = dot(left, held[0]).astype(BF16)
-            send_halves(copies, rows[s], halves, r, s if seqs > 1 else None)
+            send_block(copies, rows[s], halves, r, s if seqs > 1 else None)
     copies.finish()
 
 
@@ -931,28 +1014,35 @@
     image, K = inputs[0][0].shape
     text = inputs[0][1].shape[0]
     block = (image + text) // 4
-    shape = (block, D // 2) if seqs == 1 else (seqs, block, D // 2)
     return run(
         functools.partial(partial_kernel, seqs, dot, image_rows),
         "partial_sums",
         (*[value for pair in inputs for value in pair], weight),
         [ANYWHERE] * (2 * seqs + 1),
-        [(shape, BF16)] * 8,
-        [ANYWHERE] * 8,
+        sent_shapes(block, D, seqs),
+        [ANYWHERE] * 5,
         [pltpu.VMEM((count, K), BF16) for _ in range(seqs) for count in (image, text)]
         + [pltpu.VMEM(weight.shape, BF16)]
         + [pltpu.VMEM((4, block, D), BF16)] * seqs,
-        2 + 2 * seqs + 8 * seqs,
-    )
-
-
-def six_sum(pieces, low, count):
-    own_a, own_b, x_a, x_b, y_a, y_b = pieces
+        2 + 2 * seqs + 7 * seqs,
+    )
+
+
+def piece_sum(pieces, low, count):
+    own, from_x, from_y, late_x, late_y = pieces
+    width = late_x.shape[-1]
 
     def add(*parts):
-        return sum(part[low : low + count, :].astype(F32) for part in parts)
-
-    return jnp.concatenate([add(own_a, x_a, y_a), add(own_b, x_b, y_b)], axis=1)
+        return sum(part.astype(F32) for part in parts)
+
+    span = pl.ds(low, count)
+    return jnp.concatenate(
+        [
+            add(own[span, :width], from_x[span, width:], late_y[span, :]),
+            add(own[span, width:], late_x[span, :], from_y[span, width:]),
+        ],
+        axis=1,
+    )
 
 
 def both_halves(halves, seq, low, count):
@@ -962,12 +1052,12 @@
 
 
 def middle_kernel(seq, image_rows, *refs):
-    pieces, tokens, (mods, bias) = (refs[:6], refs[6:8], refs[8:10])
-    projection_ref, middle_ref, second_a, second_b = refs[10:]
+    pieces, tokens, (mods, bias) = (refs[:5], refs[5:7], refs[7:9])
+    projection_ref, middle_ref, second_a, second_b = refs[9:]
     block, width = second_a.shape
     for t, low, count in ((0, 0, image_rows), (1, image_rows, block - image_rows)):
         span = slice(low, low + count)
-        projection = six_sum(pieces, low, count) + bias[t : t + 1, :]
+        projection = piece_sum(pieces, low, count) + bias[t : t + 1, :]
         middle = both_halves(tokens, seq, low, count) + mods[t, seq, 2:3, :] * projection
         norm, _ = normalize(middle)
         second = (norm * (1.0 + mods[t, seq, 4:5, :]) + mods[t, seq, 3:4, :]).astype(BF16)
@@ -978,12 +1068,12 @@
 
 
 def middle_step(pieces, tokens, mods, bias, seq, image_rows):
-    block, width = pieces[0].shape
+    block, width = pieces[3].shape
     return run(
         functools.partial(middle_kernel, seq, image_rows),
         "middle",
         (*pieces, *tokens, mods, bias),
-        [ON_CORE] * 10,
+        [ON_CORE] * 9,
         [((block, 2 * width), F32)] * 2 + [((block, width), BF16)] * 2,
         [ON_CORE] * 4,
         [],
@@ -1008,12 +1098,13 @@
 
     def activate(pre):
         squared = pre * pre
-        bent = jnp.tanh(GELU_SCALE * (pre + GELU_CUBE * pre * squared))
-        rise = 0.5 * (1.0 + bent)
-        slope = rise + (0.5 * GELU_SCALE) * pre * (1.0 - bent * bent) * (
-            1.0 + (3.0 * GELU_CUBE) * squared
-        )
-        return (pre * rise).astype(BF16), slope.astype(BF16)
+        bent = jnp.tanh(pre * (GELU_SCALE + (GELU_SCALE * GELU_CUBE) * squared))
+        rise = 0.5 + 0.5 * bent
+        act = pre * rise
+        slope = rise + (act * (1.0 - rise)) * (
+            2.0 * GELU_SCALE + (6.0 * GELU_SCALE * GELU_CUBE) * squared
+        )
+        return act.astype(BF16), slope.astype(BF16)
 
     for r in range(4):
         for copy in fetched[r]:
@@ -1086,9 +1177,10 @@
     inputs, out = (refs[: 4 * seqs], refs[4 * seqs])
     held, result, semaphores = (refs[4 * seqs + 1 : -2], refs[-2], refs[-1])
     copies = Copies(semaphores)
-    fetched = [copies.start(source, target) for source, target in zip(inputs, held)]
+    order = [4 * s + 2 * t + side for t in (1, 0) for s in range(seqs) for side in range(2)]
+    fetched = {k: copies.start(inputs[k], held[k]) for k in order}
     columns = result.shape[1]
-    for t in range(2):
+    for t in (1, 0):
         for s in range(seqs):
             fetched[4 * s + 2 * t].wait()
             fetched[4 * s + 2 * t + 1].wait()
@@ -1121,41 +1213,55 @@
 
 def hidden_back_kernel(image_rows, *refs):
     (grad_i, grad_t, slope_i, slope_t, down, up) = refs[:6]
-    pre_i, pre_t, sums, halves = (refs[6], refs[7], refs[8], refs[9:17])
+    pre_i, pre_t, sums, sent = (refs[6], refs[7], refs[8], refs[9:14])
     grads, slopes, pres, grad_text, slope_text, pre_text, held_down, held_up, rows, semaphores = (
-        refs[17:]
+        refs[14:]
     )
     copies = Copies(semaphores)
-    downs = [copies.start(down.at[t], held_down.at[t]) for t in (1, 0)]
+    order = (3, 1, 2, 0)
+    spans = {r: pl.ds(r * image_rows, image_rows) for r in order}
+    images = {}
+    downs, ups = ([None, None], [None, None])
+    for k, r in enumerate(order):
+        images[r] = [copies.start(grad_i.at[spans[r], :], grads.at[spans[r], :])]
+        if k == 0:
+            downs[0] = copies.start(down.at[0], held_down.at[0])
+        images[r].append(copies.start(slope_i.at[spans[r], :], slopes.at[spans[r], :]))
+        if k == 0:
+            ups[0] = copies.start(up.at[0], held_up.at[0])
     texts = [copies.start(grad_t, grad_text), copies.start(slope_t, slope_text)]
-    images = [copies.start(grad_i, grads), copies.start(slope_i, slopes)]
-    ups = [copies.start(up.at[t], held_up.at[t]) for t in (1, 0)]
+    downs[1] = copies.start(down.at[1], held_down.at[1])
+    ups[1] = copies.start(up.at[1], held_up.at[1])
     text_rows = rows.shape[1] - image_rows
-    downs[0].wait()
-    for copy in texts:
-        copy.wait()
-    product = dot_nt(grad_text[...], held_down[1]) * slope_text[...].astype(F32)
-    pre_text[...] = product.astype(BF16)
-    copies.send(pre_text, pre_t)
-    sums[1:2, :] = jnp.sum(pre_text[...].astype(F32), axis=0, keepdims=True)
-    ups[0].wait()
-    back = dot_nn(pre_text[...], held_up[1]).astype(BF16)
-    for r in range(4):
-        rows[r, image_rows:, :] = back[r * text_rows : (r + 1) * text_rows]
-    downs[1].wait()
-    for copy in images:
-        copy.wait()
     total = jnp.zeros((1, pres.shape[1]), F32)
-    for r in (3, 1, 2, 0):
-        span = pl.ds(r * image_rows, image_rows)
-        product = dot_nt(grads[span, :], held_down[0]) * slopes[span, :].astype(F32)
-        pres[span, :] = product.astype(BF16)
-        copies.send(pres.at[span, :], pre_i.at[span, :])
-        total = total + jnp.sum(pres[span, :].astype(F32), axis=0, keepdims=True)
-        if r == 3:
+    for k, r in enumerate(order):
+        for copy in images[r]:
+            copy.wait()
+        if k == 0:
+            downs[0].wait()
+        product = dot_nt(grads[spans[r], :], held_down[0]) * slopes[spans[r], :].astype(F32)
+        low = product.astype(BF16)
+        pres[spans[r], :] = low
+        copies.send(pres.at[spans[r], :], pre_i.at[spans[r], :])
+        total = total + jnp.sum(low.astype(F32), axis=0, keepdims=True)
+        if k == 0:
+            ups[0].wait()
+        rows[r, :image_rows, :] = dot_nn(pres[spans[r], :], held_up[0]).astype(BF16)
+        if k == 1:
+            for copy in texts:
+                copy.wait()
+            downs[1].wait()
+            product = dot_nt(grad_text[...], held_down[1]) * slope_text[...].astype(F32)
+            pre_text[...] = product.astype(BF16)
+            copies.send(pre_text, pre_t)
+            sums[1:2, :] = jnp.sum(pre_text[...].astype(F32), axis=0, keepdims=True)
             ups[1].wait()
-        rows[r, :image_rows, :] = dot_nn(pres[span, :], held_up[0]).astype(BF16)
-        send_halves(copies, rows, halves, r, None)
+            back = dot_nn(pre_text[...], held_up[1]).astype(BF16)
+            for q in range(4):
+                rows[q, image_rows:, :] = back[q * text_rows : (q + 1) * text_rows]
+            send_block(copies, rows, sent, order[0], None)
+        if k >= 1:
+            send_block(copies, rows, sent, r, None)
     sums[0:1, :] = total
     copies.finish()
 
@@ -1170,8 +1276,8 @@
         "hidden_back",
         (*grads, *slopes, down, up),
         [ANYWHERE] * 6,
-        [((image, F), BF16), ((text, F), BF16), ((2, F), F32)] + [((block, D // 2), BF16)] * 8,
-        [ANYWHERE] * 2 + [ON_CORE] + [ANYWHERE] * 8,
+        [((image, F), BF16), ((text, F), BF16), ((2, F), F32)] + sent_shapes(block, D),
+        [ANYWHERE] * 2 + [ON_CORE] + [ANYWHERE] * 5,
         [
             pltpu.VMEM((image, D), BF16),
             pltpu.VMEM((image, F), BF16),
@@ -1183,18 +1289,18 @@
             pltpu.VMEM((2, F, D), BF16),
             pltpu.VMEM((4, block, D), BF16),
         ],
-        8 + 1 + 4 + 8,
+        8 + 2 + 4 + 1 + 4 + 7,
     )
     return outs[0:2], outs[2], outs[3:]
 
 
 def middle_back_kernel(seq, image_rows, *refs):
-    pieces, cotangents, (middle_ref, projection_ref, mods) = (refs[:6], refs[6:8], refs[8:11])
-    grad_ref, low_a, low_b, sums = refs[11:]
+    pieces, cotangents, (middle_ref, projection_ref, mods) = (refs[:5], refs[5:7], refs[7:10])
+    grad_ref, low_a, low_b, sums = refs[10:]
     block, width = low_a.shape
     for t, low, count in ((0, 0, image_rows), (1, image_rows, block - image_rows)):
         span = slice(low, low + count)
-        norm_grad = six_sum(pieces, low, count)
+        norm_grad = piece_sum(pieces, low, count)
         norm, inverse = normalize(middle_ref[span, :])
         grad = both_halves(cotangents, seq, low, count) + normalize_back(
             norm, inverse, norm_grad, mods[t, seq, 4:5, :]
@@ -1210,12 +1316,12 @@
 
 
 def middle_back(pieces, cotangents, middle, projection, mods, seq, image_rows):
-    block, width = pieces[0].shape
+    block, width = pieces[3].shape
     return run(
         functools.partial(middle_back_kernel, seq, image_rows),
         "middle_back",
         (*pieces, *cotangents, middle, projection, mods),
-        [ON_CORE] * 11,
+        [ON_CORE] * 10,
         [((block, 2 * width), F32)] + [((block, width), BF16)] * 2 + [((8, 2 * width), F32)],
         [ON_CORE] * 4,
         [],
@@ -1272,8 +1378,8 @@
 
 def project_back_kernel(seq, image_rows, *refs):
     (grad_i, grad_t, weight), tokens = (refs[:3], refs[3:11])
-    sums, column_sums, halves = (refs[11], refs[12], refs[13:21])
-    grads, grad_text, held, given, rows, semaphores = refs[21:]
+    sums, column_sums, sent = (refs[11], refs[12], refs[13:18])
+    grads, grad_text, held, given, rows, semaphores = refs[18:]
     copies = Copies(semaphores)
     weights = [copies.start(weight.at[t], held.at[t]) for t in (1, 0)]
     text_in = copies.start(grad_t, grad_text)
@@ -1302,7 +1408,7 @@
             totals[2 * t] = totals[2 * t] + jnp.sum(back, axis=0, keepdims=True)
             totals[2 * t + 1] = totals[2 * t + 1] + jnp.sum(back * norm, axis=0, keepdims=True)
             rows[r, low : low + count, :] = back.astype(BF16)
-        send_halves(copies, rows, halves, r, None)
+        send_block(copies, rows, sent, r, None)
     column_sums[0:1, :] = columns
     for k in range(4):
         sums[k : k + 1, :] = totals[k]
@@ -1319,8 +1425,8 @@
         "project_back",
         (*grads, weight, *tokens),
         [ANYWHERE] * 11,
-        [((4, D), F32), ((2, W), F32)] + [((block, D // 2), BF16)] * 8,
-        [ON_CORE] * 2 + [ANYWHERE] * 8,
+        [((4, D), F32), ((2, W), F32)] + sent_shapes(block, D),
+        [ON_CORE] * 2 + [ANYWHERE] * 5,
         [
             pltpu.VMEM((image, W), BF16),
             pltpu.VMEM((text, W), BF16),
@@ -1328,19 +1434,19 @@
             pltpu.VMEM((4, block, D), BF16),
             pltpu.VMEM((4, block, D), BF16),
         ],
-        4 + 8 + 8,
+        4 + 8 + 7,
     )
     return outs[0], outs[1], outs[2:]
 
 
 def result_kernel(image_rows, *refs):
-    pieces, cotangents, middles = (refs[:6], refs[6:8], refs[8:10])
-    mods, bias, image_out, text_out, sums = refs[10:]
+    pieces, cotangents, middles = (refs[:5], refs[5:7], refs[7:9])
+    mods, bias, image_out, text_out, sums = refs[9:]
     block = middles[0].shape[0]
     for seq in range(2):
         for t, low, count in ((0, 0, image_rows), (1, image_rows, block - image_rows)):
             span = slice(low, low + count)
-            value = six_sum([piece.at[seq] for piece in pieces], low, count) + bias[t : t + 1, :]
+            value = piece_sum([piece.at[seq] for piece in pieces], low, count) + bias[t : t + 1, :]
             gate = mods[t, seq, 5:6, :]
             out = (middles[seq][span, :] + gate * value).astype(BF16)
             if t == 0:
@@ -1355,12 +1461,12 @@
 
 
 def result_step(pieces, cotangents, middles, mods, bias, image_rows):
-    seqs, block, width = pieces[0].shape
+    seqs, block, width = pieces[3].shape
     return run(
         functools.partial(result_kernel, image_rows),
         "result",
         (*pieces, *cotangents, *middles, mods, bias),
-        [ON_CORE] * 12,
+        [ON_CORE] * 11,
         [
             ((seqs, image_rows, 2 * width), BF16),
             ((seqs, block - image_rows, 2 * width), BF16),
@@ -1372,12 +1478,12 @@
 
 
 def input_back_kernel(image_rows, live_text, *refs):
-    pieces, tokens, grads, mods = (refs[:12], refs[12:14], refs[14:16], refs[16])
-    image_out, text_out = refs[17:]
+    pieces, tokens, grads, mods = (refs[:10], refs[10:12], refs[12:14], refs[14])
+    image_out, text_out = refs[15:]
     block = grads[0].shape[0]
     for seq in range(2):
         for t, low, count in ((0, 0, image_rows), (1, image_rows, block - image_rows)):
-            norm_grad = six_sum(pieces[6 * seq : 6 * seq + 6], low, count)
+            norm_grad = piece_sum(pieces[5 * seq : 5 * seq + 5], low, count)
             norm, inverse = normalize(both_halves(tokens, seq, low, count))
             out = grads[seq][low : low + count, :] + normalize_back(
                 norm, inverse, norm_grad, mods[t, seq, 1:2, :]
@@ -1389,12 +1495,12 @@
 
 
 def input_back(pieces, tokens, grads, mods, image_rows, live_text):
-    block, width = pieces[0][0].shape
+    block, width = pieces[0][3].shape
     return run(
         functools.partial(input_back_kernel, image_rows, live_text),
         "input_back",
         (*pieces[0], *pieces[1], *tokens, *grads, mods),
-        [ON_CORE] * 17,
+        [ON_CORE] * 15,
         [((2, image_rows, 2 * width), F32), ((2, live_text, 2 * width), F32)],
         [ON_CORE] * 2,
         [],
@@ -1531,15 +1637,8 @@
     back_perms = [[(target, source) for source, target in pairs] for pairs in perms]
     qkv_units = jnp.swapaxes(qkv_weight, 1, 2).reshape(2, per_device, unit, D).swapaxes(0, 1)
     qkv_mine = move_units(qkv_units, perms, send, land, place).swapaxes(0, 1)
-    out_units = jnp.swapaxes(out_weight, 1, 2).reshape(2, -1, S, own_width).transpose(2, 0, 1, 3)
-    out_mine = swap(after(out_units, qkv_mine), "seq")
-    out_columns = out_mine.shape[2]
     qkv_width = per_device * unit
     qkv_part = gather_rows_over_batch(qkv_mine.reshape(2, qkv_width, D))
-    out_rows = out_mine.transpose(1, 0, 2, 3).reshape(2, S * out_columns, own_width)
-    out_part = gather_rows_over_batch(out_rows)
-    hidden_columns = up_weight.shape[2]
-
     padded = jnp.concatenate([image_tokens, jnp.pad(text_tokens, pad)], axis=1)
     tokens = after((padded[..., :half], padded[..., half:]), qkv_mine)
     tokens_near = gather_near(*tokens)
@@ -1557,11 +1656,17 @@
     )
     mod_width = mod_own.shape[2]
     mod_sent = mod_own.reshape(2, B, L, mod_width).transpose(1, 0, 2, 3)
-    mod_came = swap(mod_sent, "batch")
+    mod_came = swap(after(mod_sent, tokens_near), "batch")
+    out_units = jnp.swapaxes(out_weight, 1, 2).reshape(2, -1, S, own_width).transpose(2, 0, 1, 3)
+    out_mine = swap(after(out_units, mod_came), "seq")
+    out_columns = out_mine.shape[2]
+    out_rows = out_mine.transpose(1, 0, 2, 3).reshape(2, S * out_columns, own_width)
+    out_part = gather_rows_over_batch(out_rows)
+    hidden_columns = up_weight.shape[2]
     small = jnp.concatenate(
         [mod_came.reshape(B, 2 * L * mod_width), column_biases.reshape(B, -1)], axis=1
     )
-    small_all = gather_small(after(small, tokens_near), "seq")
+    small_all = gather_small(small, "seq")
     modulation = (
         small_all[:, :, : 2 * L * mod_width]
         .reshape(S, B, 2, L, mod_width)
@@ -1587,11 +1692,12 @@
         axis=1,
     )
 
-    tokens_all = gather_far(*tokens, after(tokens_near, small_all))
+    tokens_all = gather_far(*tokens, tokens_near)
     padded = jnp.concatenate([image_cotangent, jnp.pad(text_cotangent, pad)], axis=1)
     cotangents = (padded[..., :half], padded[..., half:])
-    near_grads = gather_near(*after(cotangents, tokens_all))
+    near_grads = gather_near(*after(cotangents, tokens_all, small_all))
     up_part = gather_rows_over_batch(after(jnp.swapaxes(up_weight, 1, 2), tokens_all))
+    down_part = gather_rows_over_batch(after(jnp.swapaxes(down_weight, 1, 2), tokens_all))
 
     order = jnp.bitwise_xor(seq_index, jnp.arange(S))
     image_keys = jnp.take(
@@ -1605,26 +1711,35 @@
     key_bias = jnp.where(live, 0.0, DEAD).astype(F32)
     floors = jnp.where(jnp.all(key_mask > 0, axis=1), -3e38, FLOOR_SCORE * LOG2E).astype(F32)
     floors = floors.reshape(L, 1, 1)
+    key_bias = jnp.broadcast_to(key_bias[:, :, None], (*key_bias.shape, 128))
 
     kept = []
     first = project(tokens_all, qkv_part, modulation, qkv_bias, 0, image_count)
     attended = attention(first[0], first[1], key_bias[0], floors[0], head)
-    down_part = gather_rows_over_batch(after(jnp.swapaxes(down_weight, 1, 2), attended))
+    attended, logs = (attended[:2], attended[2:])
+    attended = after(attended, near_grads)
     parts = partial_sums([attended], out_part, dot_nt, D, image_count)
-    kept.append((first, attended, parts))
-    again = after(tokens_all, parts, near_grads)
+    kept.append((first, attended, logs, parts))
+    again = after(tokens_all, parts)
     first = project(again, qkv_part, modulation, qkv_bias, 1, image_count)
     attended = attention(first[0], first[1], key_bias[1], floors[1], head)
-    cotangents_all = gather_far(*cotangents, near_grads)
-    attended = after(attended, cotangents_all)
+    attended, logs = (attended[:2], attended[2:])
+    cotangents_all = gather_far(*cotangents, after(near_grads, kept[0][0]))
+    out_first = scatter_first(kept[0][3])
+    attended = after(attended, cotangents_all, out_first)
     parts = partial_sums([attended], out_part, dot_nt, D, image_count)
-    kept.append((first, attended, parts))
-    firsts, attendeds, out_halves = zip(*kept)
+    kept.append((first, attended, logs, parts))
+    firsts, attendeds, logs, out_halves = zip(*kept)
     steps, seconds = ([], [])
     for s in range(L):
         steps.append(
             middle_step(
-                scatter_halves(out_halves[s]), tokens, modulation, out_bias_full, s, image_count
+                scatter_last(out_halves[s], out_first if s == 0 else scatter_first(out_halves[s])),
+                tokens,
+                modulation,
+                out_bias_full,
+                s,
+                image_count,
             )
         )
         seconds.append(gather_halves(*steps[s][2:]))
@@ -1651,8 +1766,12 @@
         bias_sums.append(sums)
         norm2_halves.append(halves)
     up_bias_sum = sum(bias_sums)
-    norm2_pieces = [scatter_halves(halves) for halves in norm2_halves]
-    up_sum = outer_sums(after(pres, gate), norms, 256)
+    norm2_first = [scatter_first(halves) for halves in norm2_halves]
+    norm2_pieces = [
+        scatter_last(halves, first) for halves, first in zip(norm2_halves, norm2_first)
+    ]
+    up_sum = outer_sums(after(pres, gate, norm2_first[0]), norms, 256)
+    up_came = scatter_rows_over_batch(up_sum)
 
     backs, projs = ([], [])
     backs.append(
@@ -1660,11 +1779,14 @@
             after(norm2_pieces[0], up_sum), cotangents, *steps[0][1::-1], modulation, 0, image_count
         )
     )
-    projs.append(gather_halves(*backs[0][1:3]))
-    mlp_halves = partial_sums(after(acts, backs[0]), down_part, dot_nn, D, image_count)
+    proj_near = gather_near(*backs[0][1:3])
+    projs.append(gather_far(*backs[0][1:3], proj_near))
+    mlp_halves = partial_sums(
+        after(acts, backs[0], norm2_first[1]), down_part, dot_nn, D, image_count
+    )
     backs.append(
         middle_back(
-            after(norm2_pieces[1], mlp_halves),
+            after(norm2_pieces[1], mlp_halves, proj_near),
             cotangents,
             *steps[1][1::-1],
             modulation,
@@ -1673,21 +1795,26 @@
         )
     )
     projs.append(gather_halves(*backs[1][1:3]))
-    grad0, proj0 = attended_back(after(projs[0], backs[1]), out_part, image_count)
-    up_came = scatter_rows_over_batch(after(up_sum, down_came, grad0))
-    qkv_grad0 = attention_back(*firsts[0][:2], *grad0, key_bias[0], floors[0], head)
+    grad0, proj0 = attended_back(
+        after(projs[0], backs[1], down_came), out_part, image_count
+    )
+    qkv_grad0 = attention_back(
+        *firsts[0][:2], *attendeds[0], *logs[0], *grad0, key_bias[0], head
+    )
     grad1, proj1 = attended_back(after(projs[1], qkv_grad0), out_part, image_count)
-    mlp_first = scatter_first(after(mlp_halves, proj1))
+    mlp_first = scatter_first(after(mlp_halves, projs[1]))
     out_sum = outer_sums([proj0, proj1], attendeds, 256)
     sums0, columns0, halves0 = project_back(
         after(qkv_grad0, out_sum), qkv_part, tokens_all, 0, image_count
     )
-    out_came = scatter_rows_over_batch(after(out_sum, up_came, halves0))
+    out_came = scatter_rows_over_batch(after(out_sum, halves0))
     norm1_first = scatter_first(halves0)
-    grad1 = after(grad1, halves0, mlp_first)
-    qkv_grad1 = attention_back(*firsts[1][:2], *grad1, key_bias[1], floors[1], head)
+    grad1 = after(grad1, halves0, up_came, mlp_first)
+    qkv_grad1 = attention_back(
+        *firsts[1][:2], *attendeds[1], *logs[1], *grad1, key_bias[1], head
+    )
     mlp_pieces = scatter_last(mlp_halves, mlp_first)
-    qkv_grad1 = after(qkv_grad1, mlp_pieces)
+    qkv_grad1 = after(qkv_grad1, norm1_first)
     qkv_sum = outer_sums(
         [qkv_grad0, qkv_grad1], [first[2:] for first in firsts], 128 if qkv_width % 256 else 256
     )

time: 923 us -> 809 us (0.88)
  Pallas kernels: 415 us -> 363 us
  waiting for transfers between devices: 248 us -> 205 us
  local copies, waits for them, and re-layouts: 53.8 us -> 41.5 us
  starting transfers between devices: 139 us -> 127 us
    ppermute x80 -> x66, waiting for transfers between devices: 212 us -> 180 us  [flip(): return lax.ppermute(values, 'seq', [(i, i ^ bit) for i in range(4)])]
    pallas_call x2, Pallas kernels: 94.1 us -> 63.9 us  [attention_back(): pl.pallas_call(functools.partial(attention_back_kernel, 512, LOG2E / math...]
    unnamed x182 -> x134, local copies, waits for them, and re-layouts: 21.2 us -> 5.25 us
    pallas_call x2, Pallas kernels: 49 us -> 34.4 us  [attention(): pl.pallas_call(functools.partial(attention_kernel, 256, LOG2E / math.sqrt...]
    ppermute x80 -> x66, starting transfers between devices: 83.8 us -> 71.5 us  [flip(): return lax.ppermute(values, 'seq', [(i, i ^ bit) for i in range(4)])]
    all_to_all x6 -> x5, starting transfers between devices: 26.8 us -> 28.4 us  [swap(): return lax.all_to_all(values, axis, 0, 0, tiled=True)]
  transfers between devices with their start and end apart: 105 -> 90, of which waited for: 39 -> 40; matrix products, arithmetic and copies ran while one was open for 6% -> 8% of each run, Pallas kernels for 46% -> 45%
where the time goes in v5:
time: 809 us; the launch traced here: 801 us
  Pallas kernels  363 us (45%)
  waiting for transfers between devices  205 us (25%)
  starting transfers between devices  127 us (16%)
  local copies, waits for them, and re-layouts  41.5 us (5%)
  other arithmetic  29.6 us (4%)
  between operations  21.7 us (3%)
  blocking collectives  9.1 us (1%)
    pallas_call x23, Pallas kernels, run(): pl.pallas_call(kernel, in_specs=specs, out_specs=out_specs, out_shape=[ja...  265 us
    ppermute x66, waiting for transfers between devices, flip(): return lax.ppermute(values, 'seq', [(i, i ^ bit) for i in range(4)])  180 us
    ppermute x66, starting transfers between devices, flip(): return lax.ppermute(values, 'seq', [(i, i ^ bit) for i in range(4)])  71.5 us
    pallas_call x2, Pallas kernels, attention_back(): pl.pallas_call(functools.partial(attention_back_kernel, 512, LOG2E / math...  63.9 us
    pallas_call x2, Pallas kernels, attention(): pl.pallas_call(functools.partial(attention_kernel, 256, LOG2E / math.sqrt...  34.4 us
    all_to_all x5, starting transfers between devices, swap(): return lax.all_to_all(values, axis, 0, 0, tiled=True)  28.4 us
    ppermute x6, starting transfers between devices, move_units(): lax.ppermute(lax.dynamic_index_in_dim(units, slot, 0, keepdims=True), ('b...  20.8 us
  transfers between devices with their start and end apart: 90, of which 40 were waited for; matrix products, arithmetic and copies ran while one was open for 8% of the time, Pallas kernels for 45%

profile of v5, /device:TPU:16, one launch (start us, length us, event | category | flops | bytes accessed | tf_op | source)
XLA Modules:
  0.0 800.9 jit_solution(9904530503841490556)
XLA Ops:
  61.9 12.9 %collective-permute-done.6.refs_5_.refs_8_ = bf16[2,304,768]{2,1,0:T(8,128)(2,1)} collective-permute-done((bf16[2,304,768]{2,1,0:T(8,128)(2,1)S(1)}, bf16[2,304,768]{2,1,0:T(8,128)(2,1)}, u32[]{:S(2)}, u32[]{:S(2)}) %collective-permute-start.6) | collective-permute-done | bytes 933920 | tf_op jit(solution)/shard_map/ppermute | solution.py:799
  88.5 9.1 %all_to_all.37 = bf16[4,2,48,384]{3,2,1,0:T(8,128)(2,1)S(1)} all-to-all(bf16[4,2,48,384]{3,2,1,0:T(8,128)(2,1)S(1)} %copy.193), channel_id=1, replica_groups=mesh['batch'=8,'seq'=4] {'seq'}, dimensions={0} | all-to-all | bytes 589824 | tf_op jit(solution)/shard_map/all_to_all | solution.py:1601
  99.7 20.3 %collective-permute-done.7.refs_6_.refs_9_ = bf16[2,304,768]{2,1,0:T(8,128)(2,1)} collective-permute-done((bf16[2,304,768]{2,1,0:T(8,128)(2,1)}, bf16[2,304,768]{2,1,0:T(8,128)(2,1)}, u32[]{:S(2)}, u32[]{:S(2)}) %collective-permute-start.7) | collective-permute-done | bytes 933920 | tf_op jit(solution)/shard_map/ppermute | solution.py:799
  141.4 13.0 %project.2 = (bf16[1024,1152]{1,0:T(8,128)(2,1)}, bf16[192,1152]{1,0:T(8,128)(2,1)}, bf16[1024,1536]{1,0:T(8,128)(2,1)}, bf16[192,1536]{1,0:T(8,128)(2,1)}) custom-call(bf16[2,304,768]{2,1,0:T(8,128)(2,1)} %get-tuple-element.240.refs_0_.refs_5_.refs_3_.refs_10_, bf16[2,304,768]{2,1,0:T(8,128)(2,1)} %copy-done.5, ...), custom_call_target="tpu_custom_call" | custom-call | flops 7474999808 | bytes 1 | tf_op jit(solution)/shard_map/project/pallas_call | solution.py:912
  162.1 15.4 %collective-permute-done.17.refs_13_ = bf16[2,304,768]{2,1,0:T(8,128)(2,1)} collective-permute-done((bf16[2,304,768]{2,1,0:T(8,128)(2,1)S(1)}, bf16[2,304,768]{2,1,0:T(8,128)(2,1)}, u32[]{:S(2)}, u32[]{:S(2)}) %collective-permute-start.17) | collective-permute-done | bytes 933920 | tf_op jit(solution)/shard_map/ppermute | solution.py:799
  180.4 17.3 %attention.2 = (bf16[1024,384]{1,0:T(8,128)(2,1)}, bf16[192,384]{1,0:T(8,128)(2,1)}, f32[1024,384]{1,0:T(8,128)}, f32[192,384]{1,0:T(8,128)}) custom-call(f32[1216,128]{1,0:T(8,128)} %broadcast_in_dim.97.bias_ref.refs_0_, f32[1,1]{1,0:T(1,128)} %bitcast.6.floor_ref, bf16[1024,1152]{1,0:T(8,128)(2,1)} %get-tuple-element.215.qi.ki.vi.refs_1_.refs_3_.refs_5_, ...), custom_call_target="tpu_custom_call" | custom-call | flops 9774999552 | bytes 1 | tf_op jit(solution)/shard_map/attention/pallas_call | solution.py:657
  205.6 13.0 %project.3 = (bf16[1024,1152]{1,0:T(8,128)(2,1)}, bf16[192,1152]{1,0:T(8,128)(2,1)}, bf16[1024,1536]{1,0:T(8,128)(2,1)}, bf16[192,1536]{1,0:T(8,128)(2,1)}) custom-call(bf16[2,304,768]{2,1,0:T(8,128)(2,1)} %get-tuple-element.240.refs_0_.refs_5_.refs_3_.refs_10_, bf16[2,304,768]{2,1,0:T(8,128)(2,1)} %copy-done.5, ...), custom_call_target="tpu_custom_call" | custom-call | flops 7474999808 | bytes 1 | tf_op jit(solution)/shard_map/project/pallas_call | solution.py:912
  219.7 17.1 %attention.3 = (bf16[1024,384]{1,0:T(8,128)(2,1)}, bf16[192,384]{1,0:T(8,128)(2,1)}, f32[1024,384]{1,0:T(8,128)}, f32[192,384]{1,0:T(8,128)}) custom-call(f32[1216,128]{1,0:T(8,128)} %broadcast_in_dim.108.bias_ref.refs_0_, f32[1,1]{1,0:T(1,128)} %bitcast.33.floor_ref, bf16[1024,1152]{1,0:T(8,128)(2,1)} %get-tuple-element.248.qi.ki.vi.refs_1_.refs_3_.refs_5_, ...), custom_call_target="tpu_custom_call" | custom-call | flops 9774999552 | bytes 1 | tf_op jit(solution)/shard_map/attention/pallas_call | solution.py:657
  250.6 18.6 %collective-permute-done.20.refs_3_ = bf16[304,768]{1,0:T(8,128)(2,1)} collective-permute-done((bf16[304,768]{1,0:T(8,128)(2,1)S(1)}, bf16[304,768]{1,0:T(8,128)(2,1)}, u32[]{:S(2)}, u32[]{:S(2)}) %collective-permute-start.20) | collective-permute-done | bytes 466976 | tf_op jit(solution)/shard_map/ppermute | solution.py:799
  291.2 7.5 collective-permute-done.32.refs_3_
  329.9 17.0 %hidden.2 = (bf16[1024,1536]{1,0:T(8,128)(2,1)}, bf16[192,1536]{1,0:T(8,128)(2,1)}, bf16[1024,1536]{1,0:T(8,128)(2,1)}, bf16[192,1536]{1,0:T(8,128)(2,1)}, bf16[...) custom-call(bf16[304,768]{1,0:T(8,128)(2,1)} %get-tuple-element.229.r, ...), custom_call_target="tpu_custom_call" | custom-call | flops 10350000128 | bytes 1 | tf_op jit(solution)/shard_map/hidden/pallas_call | solution.py:912
  347.9 16.7 %hidden.3 = (bf16[1024,1536]{1,0:T(8,128)(2,1)}, bf16[192,1536]{1,0:T(8,128)(2,1)}, bf16[1024,1536]{1,0:T(8,128)(2,1)}, bf16[192,1536]{1,0:T(8,128)(2,1)}, bf16[...) custom-call(bf16[304,768]{1,0:T(8,128)(2,1)} %get-tuple-element.267.r, ...), custom_call_target="tpu_custom_call" | custom-call | flops 10350000128 | bytes 1 | tf_op jit(solution)/shard_map/hidden/pallas_call | solution.py:912
  364.6 18.1 %outer_sums.4 = bf16[2,1536,1536]{2,1,0:T(8,128)(2,1)} custom-call(bf16[1024,1536]{1,0:T(8,128)(2,1)} %get-tuple-element.317.refs_0_, bf16[1024,1536]{1,0:T(8,128)(2,1)} %get-tuple-element.279.refs_1_.refs_0_, bf16[192,1536]{1,0:T(8,128)(2,1)} %get-tuple-element.318.refs_2_.refs_1_, bf16[192,1536]{1,0:T(8,128)(2,1)} %get-tuple-element.280.refs_3_.refs_1_, ...), custom_call_target="tpu_custom_call" | custom-call | flops 10350000128 | bytes 1 | tf_op jit(solution)/shard_map/outer_sums/pallas_call | solution.py:912
  383.0 18.1 %hidden_back.2 = (bf16[1024,1536]{1,0:T(8,128)(2,1)}, bf16[192,1536]{1,0:T(8,128)(2,1)}, f32[2,1536]{1,0:T(2,128)}, bf16[304,1536]{1,0:T(8,128)(2,1)}, bf16[304,...) custom-call(bf16[1024,1536]{1,0:T(8,128)(2,1)} %get-tuple-element.279.refs_1_, ...), custom_call_target="tpu_custom_call" | custom-call | flops 11500000256 | bytes 1 | tf_op jit(solution)/shard_map/hidden_back/pallas_call | solution.py:912
  402.1 18.7 %hidden_back.3 = (bf16[1024,1536]{1,0:T(8,128)(2,1)}, bf16[192,1536]{1,0:T(8,128)(2,1)}, f32[2,1536]{1,0:T(2,128)}, bf16[304,1536]{1,0:T(8,128)(2,1)}, bf16[304,...) custom-call(bf16[1024,1536]{1,0:T(8,128)(2,1)} %get-tuple-element.289.refs_5_, ...), custom_call_target="tpu_custom_call" | custom-call | flops 11500000256 | bytes 1 | tf_op jit(solution)/shard_map/hidden_back/pallas_call | solution.py:912
  420.8 18.4 %outer_sums.5 = bf16[2,1536,1536]{2,1,0:T(8,128)(2,1)} custom-call(bf16[1024,1536]{1,0:T(8,128)(2,1)} %get-tuple-element.300.refs_0_, bf16[1024,1536]{1,0:T(8,128)(2,1)} %get-tuple-element.265.refs_1_, bf16[192,1536]{1,0:T(8,128)(2,1)} %get-tuple-element.301.refs_2_, bf16[192,1536]{1,0:T(8,128)(2,1)} %get-tuple-element.266.refs_3_, ...), custom_call_target="tpu_custom_call" | custom-call | flops 10350000128 | bytes 1 | tf_op jit(solution)/shard_map/outer_sums/pallas_call | solution.py:912
  445.9 10.2 %collective-permute-done.44.refs_1_ = bf16[304,1536]{1,0:T(8,128)(2,1)S(1)} collective-permute-done((bf16[304,1536]{1,0:T(8,128)(2,1)}, bf16[304,1536]{1,0:T(8,128)(2,1)S(1)}, u32[]{:S(2)}, u32[]{:S(2)}) %collective-permute-start.44) | collective-permute-done | bytes 933920 | tf_op jit(solution)/shard_map/ppermute | solution.py:799
  461.2 8.6 %collective-permute-done.43.refs_4_ = bf16[304,768]{1,0:T(8,128)(2,1)S(1)} collective-permute-done((bf16[304,768]{1,0:T(8,128)(2,1)S(1)}, bf16[304,768]{1,0:T(8,128)(2,1)S(1)}, u32[]{:S(2)}, u32[]{:S(2)}) %collective-permute-start.43) | collective-permute-done | bytes 466976 | tf_op jit(solution)/shard_map/ppermute | solution.py:799
  470.7 7.5 middle_back.2
  482.3 17.2 %partial_sums.5 = (bf16[2,304,1536]{2,1,0:T(8,128)(2,1)}, bf16[2,304,1536]{2,1,0:T(8,128)(2,1)}, bf16[2,304,1536]{2,1,0:T(8,128)(2,1)}, bf16[2,304,768]{2,1,0:T(8,128)(2,1)}, bf16[2,304,768]{2,1,0:T(8,128)(2,1)}) custom-call(bf16[1024,1536]{1,0:T(8,128)(2,1)} %get-tuple-element.317.refs_0_, bf16[192,1536]{1,0:T(8,128)(2,1)} %get-tuple-element.318.refs_2_.refs_1_, ...), custom_call_target="tpu_custom_call" | custom-call | flops 2875000064 | bytes 1 | tf_op jit(solution)/shard_map/partial_sums/pallas_call | solution.py:912
  503.6 7.9 middle_back.3
  532.0 31.9 %attention_back.2 = (bf16[1024,1152]{1,0:T(8,128)(2,1)}, bf16[192,1152]{1,0:T(8,128)(2,1)}) custom-call(f32[1216,128]{1,0:T(8,128)} %broadcast_in_dim.97.bias_ref.refs_0_, bf16[1024,1152]{1,0:T(8,128)(2,1)} %get-tuple-element.215.qi.ki.vi.refs_1_.refs_3_.refs_5_, bf16[192,1152]{1,0:T(8,128)(2,1)} %get-tuple-element.216.qt.kt.vt.refs_2_.refs_4_.refs_6_, ...), custom_call_target="tpu_custom_call" | custom-call | flops 18400000000 | bytes 1 | tf_op jit(solution)/shard_map/attention_back/pallas_call | solution.py:766
  570.8 8.5 %outer_sums.6 = bf16[2,1536,384]{2,1,0:T(8,128)(2,1)} custom-call(bf16[1024,1536]{1,0:T(8,128)(2,1)} %get-tuple-element.365.refs_0_, bf16[1024,384]{1,0:T(8,128)(2,1)} %get-tuple-element.221.refs_0_.refs_7_.refs_1_, bf16[192,1536]{1,0:T(8,128)(2,1)} %get-tuple-element.366.refs_2_, bf16[192,384]{1,0:T(8,128)(2,1)} %get-tuple-element.222.refs_1_.refs_8_.refs_3_, ...), custom_call_target="tpu_custom_call" | custom-call | flops 10350000128 | bytes 1 | tf_op jit(solution)/shard_map/outer_sums/pallas_call | solution.py:912
  579.3 12.4 %project_back.2 = (f32[4,1536]{1,0:T(4,128)}, f32[2,1152]{1,0:T(2,128)}, bf16[304,1536]{1,0:T(8,128)(2,1)}, bf16[304,1536]{1,0:T(8,128)(2,1)}, bf16[304,1536]{1,...) custom-call(bf16[1024,1152]{1,0:T(8,128)(2,1)} %get-tuple-element.369.refs_0_, ...), custom_call_target="tpu_custom_call" | custom-call | flops 6899999744 | bytes 1 | tf_op jit(solution)/shard_map/project_back/pallas_call | solution.py:912
  595.9 24.6 %collective-permute-done.58.refs_1_ = bf16[2,304,1536]{2,1,0:T(8,128)(2,1)} collective-permute-done((bf16[2,304,1536]{2,1,0:T(8,128)(2,1)}, bf16[2,304,1536]{2,1,0:T(8,128)(2,1)}, u32[]{:S(2)}, u32[]{:S(2)}) %collective-permute-start.58) | collective-permute-done | bytes 1867808 | tf_op jit(solution)/shard_map/ppermute | solution.py:799
  621.4 32.0 %attention_back.3 = (bf16[1024,1152]{1,0:T(8,128)(2,1)}, bf16[192,1152]{1,0:T(8,128)(2,1)}) custom-call(f32[1216,128]{1,0:T(8,128)} %broadcast_in_dim.108.bias_ref.refs_0_, bf16[1024,1152]{1,0:T(8,128)(2,1)} %get-tuple-element.248.qi.ki.vi.refs_1_.refs_3_.refs_5_, bf16[192,1152]{1,0:T(8,128)(2,1)} %get-tuple-element.249.qt.kt.vt.refs_2_.refs_4_.refs_6_, ...), custom_call_target="tpu_custom_call" | custom-call | flops 18400000000 | bytes 1 | tf_op jit(solution)/shard_map/attention_back/pallas_call | solution.py:766
  653.5 14.9 %outer_sums.7 = bf16[2,1152,1536]{2,1,0:T(8,128)(2,1)} custom-call(bf16[1024,1152]{1,0:T(8,128)(2,1)} %get-tuple-element.369.refs_0_, bf16[1024,1536]{1,0:T(8,128)(2,1)} %get-tuple-element.231.refs_1_, bf16[192,1152]{1,0:T(8,128)(2,1)} %get-tuple-element.370.refs_1_.refs_2_, bf16[192,1536]{1,0:T(8,128)(2,1)} %get-tuple-element.232.refs_3_, ...), custom_call_target="tpu_custom_call" | custom-call | flops 10350000128 | bytes 1 | tf_op jit(solution)/shard_map/outer_sums/pallas_call | solution.py:912
  683.3 12.4 %project_back.3 = (f32[4,1536]{1,0:T(4,128)}, f32[2,1152]{1,0:T(2,128)}, bf16[304,1536]{1,0:T(8,128)(2,1)}, bf16[304,1536]{1,0:T(8,128)(2,1)}, bf16[304,1536]{1,...) custom-call(bf16[1024,1152]{1,0:T(8,128)(2,1)} %get-tuple-element.384.refs_4_.refs_0_, ...), custom_call_target="tpu_custom_call" | custom-call | flops 6899999744 | bytes 1 | tf_op jit(solution)/shard_map/project_back/pallas_call | solution.py:912
  699.5 8.0 result.1
  720.4 10.6 %all-to-all-start.3 = ((f32[8,1,1920]{2,1,0:T(1,128)}), f32[8,1,1920]{2,1,0:T(1,128)S(1)}, u32[]{:S(2)}, u32[]{:S(2)}) async-start(f32[8,1,1920]{2,1,0:T(1,128)} %all_to_all.26), calls=%async_computation.5 | async-start | bytes 122880 | tf_op jit(solution)/shard_map/all_to_all | solution.py:1601
  766.6 7.3 collective-permute-start.74
  773.9 9.5 %input_back.1 = (f32[2,256,1536]{2,1,0:T(8,128)}, f32[2,40,1536]{2,1,0:T(8,128)}) custom-call(bf16[304,1536]{1,0:T(8,128)(2,1)} %get-tuple-element.371.refs_0_, bf16[304,1536]{1,0:T(8,128)(2,1)} %copy-done.24, bf16[304,1536]{1,0:T(8,128)(2,1)} %collective-permute-done.65.refs_2_, bf16[304,768]{1,0:T(8,128)(2,1)} %collective-permute-done.66.refs_3_, ...), custom_call_target="tpu_custom_call" | custom-call | flops 5175000064 | bytes 1 | tf_op jit(solution)/shard_map/input_back/pallas_call | solution.py:912
  (471 shorter events, 304.6 us)
Async XLA Ops:
  7.2 134.2 %all-gather.5.cloned.1.call-start = ((), (), s32[]{:S(2)}) async-start(), calls=%async_computation.10 | async-start | bytes 7962624 | tf_op jit(solution)/shard_map/all_gather | solution.py:1577
  40.0 34.9 %collective-permute-start.6 = (bf16[2,304,768]{2,1,0:T(8,128)(2,1)S(1)}, bf16[2,304,768]{2,1,0:T(8,128)(2,1)}, u32[]{:S(2)}, u32[]{:S(2)}) collective-permute-start(bf16[2,304,768]{2,1,0:T(8,128)(2,1)S(1)} %get-tuple-element.241.refs_1_.refs_6_.refs_4_.refs_11_), channel_id=1, source_target_pairs={{0,2},{1,3},{2,0},{3,1},{4,6},{5,7},{6,4},{7,5},{8,10},{9,11},{10,... | collective-permute-start | bytes 2801672 | tf_op jit(solution)/shard_map/ppermute | solution.py:799
  40.0 39.5 %collective-permute-start.4 = (bf16[2,304,768]{2,1,0:T(8,128)(2,1)S(1)}, bf16[2,304,768]{2,1,0:T(8,128)(2,1)}, u32[]{:S(2)}, u32[]{:S(2)}) collective-permute-start(bf16[2,304,768]{2,1,0:T(8,128)(2,1)S(1)} %get-tuple-element.241.refs_1_.refs_6_.refs_4_.refs_11_), channel_id=1, source_target_pairs={{0,1},{1,0},{2,3},{3,2},{4,5},{5,4},{6,7},{7,6},{8,9},{9,8},{10,11... | collective-permute-start | bytes 2801672 | tf_op jit(solution)/shard_map/ppermute | solution.py:799
  84.5 113.3 %all-gather.7.cloned.1.call-start = ((), (), s32[]{:S(2)}) async-start(), calls=%async_computation.11 | async-start | bytes 2654208 | tf_op jit(solution)/shard_map/all_gather | solution.py:1577
  98.4 231.5 %all-gather.9.cloned.1.call-start = ((), (), s32[]{:S(2)}) async-start(), calls=%async_computation.12 | async-start | bytes 10616832 | tf_op jit(solution)/shard_map/all_gather | solution.py:1577
  120.5 262.5 %all-gather.11.cloned.1.call-start = ((), (), s32[]{:S(2)}) async-start(), calls=%async_computation.13 | async-start | bytes 10616832 | tf_op jit(solution)/shard_map/all_gather | solution.py:1577
  121.0 404.9 %reduce-scatter.5.cloned.1.call-start = ((), (), s32[]{:S(2)}) async-start(), calls=%async_computation.14 | async-start | bytes 10616832 | tf_op jit(solution)/shard_map/reduce_scatter | solution.py:1597
  138.8 38.7 %collective-permute-start.17 = (bf16[2,304,768]{2,1,0:T(8,128)(2,1)S(1)}, bf16[2,304,768]{2,1,0:T(8,128)(2,1)}, u32[]{:S(2)}, u32[]{:S(2)}) collective-permute-start(bf16[2,304,768]{2,1,0:T(8,128)(2,1)S(1)} %get-tuple-element.220.refs_9_.refs_6_), channel_id=1, source_target_pairs={{0,2},{1,3},{2,0},{3,1},{4,6},{5,7},{6,4},{7,5},{8,10},{9,11},{10,... | collective-permute-start | bytes 2801672 | tf_op jit(solution)/shard_map/ppermute | solution.py:799
  139.3 38.6 %collective-permute-start.15 = (bf16[2,304,768]{2,1,0:T(8,128)(2,1)S(1)}, bf16[2,304,768]{2,1,0:T(8,128)(2,1)}, u32[]{:S(2)}, u32[]{:S(2)}) collective-permute-start(bf16[2,304,768]{2,1,0:T(8,128)(2,1)S(1)} %get-tuple-element.220.refs_9_.refs_6_), channel_id=1, source_target_pairs={{0,1},{1,0},{2,3},{3,2},{4,5},{5,4},{6,7},{7,6},{8,9},{9,8},{10,11... | collective-permute-start | bytes 2801672 | tf_op jit(solution)/shard_map/ppermute | solution.py:799
  178.0 60.2 %collective-permute-start.28 = (bf16[2,304,768]{2,1,0:T(8,128)(2,1)}, bf16[2,304,768]{2,1,0:T(8,128)(2,1)}, u32[]{:S(2)}, u32[]{:S(2)}) collective-permute-start(bf16[2,304,768]{2,1,0:T(8,128)(2,1)} %collective-permute-done.14.refs_10_), channel_id=1, source_target_pairs={{0,2},{1,3},{2,0},{3,1},{4,6},{5,7},{6,4},{7,5},{8,10},{9,11},{10,... | collective-permute-start | bytes 2801672 | tf_op jit(solution)/shard_map/ppermute | solution.py:799
  179.2 58.9 %collective-permute-start.29 = (bf16[2,304,768]{2,1,0:T(8,128)(2,1)}, bf16[2,304,768]{2,1,0:T(8,128)(2,1)}, u32[]{:S(2)}, u32[]{:S(2)}) collective-permute-start(bf16[2,304,768]{2,1,0:T(8,128)(2,1)} %collective-permute-done.17.refs_13_), channel_id=1, source_target_pairs={{0,1},{1,0},{2,3},{3,2},{4,5},{5,4},{6,7},{7,6},{8,9},{9,8},{10,11... | collective-permute-start | bytes 2801672 | tf_op jit(solution)/shard_map/ppermute | solution.py:799
  202.8 33.9 %collective-permute-start.18 = (bf16[304,1536]{1,0:T(8,128)(2,1)}, bf16[304,1536]{1,0:T(8,128)(2,1)S(1)}, u32[]{:S(2)}, u32[]{:S(2)}) collective-permute-start(bf16[304,1536]{1,0:T(8,128)(2,1)} %get-tuple-element.225), channel_id=1, source_target_pairs={{0,1},{1,0},{2,3},{3,2},{4,5},{5,4},{6,7},{7,6},{8,9},{9,8},{10,11... | collective-permute-start | bytes 2801672 | tf_op jit(solution)/shard_map/ppermute | solution.py:799
  204.8 33.4 %collective-permute-start.19 = (bf16[304,1536]{1,0:T(8,128)(2,1)}, bf16[304,1536]{1,0:T(8,128)(2,1)S(1)}, u32[]{:S(2)}, u32[]{:S(2)}) collective-permute-start(bf16[304,1536]{1,0:T(8,128)(2,1)} %get-tuple-element.226), channel_id=1, source_target_pairs={{0,2},{1,3},{2,0},{3,1},{4,6},{5,7},{6,4},{7,5},{8,10},{9,11},{10,... | collective-permute-start | bytes 2801672 | tf_op jit(solution)/shard_map/ppermute | solution.py:799
  243.8 31.1 %collective-permute-start.30 = (bf16[304,1536]{1,0:T(8,128)(2,1)}, bf16[304,1536]{1,0:T(8,128)(2,1)}, u32[]{:S(2)}, u32[]{:S(2)}) collective-permute-start(bf16[304,1536]{1,0:T(8,128)(2,1)} %get-tuple-element.255), channel_id=1, source_target_pairs={{0,1},{1,0},{2,3},{3,2},{4,5},{5,4},{6,7},{7,6},{8,9},{9,8},{10,11... | collective-permute-start | bytes 2801672 | tf_op jit(solution)/shard_map/ppermute | solution.py:799
  246.1 31.5 %collective-permute-start.31 = (bf16[304,1536]{1,0:T(8,128)(2,1)}, bf16[304,1536]{1,0:T(8,128)(2,1)}, u32[]{:S(2)}, u32[]{:S(2)}) collective-permute-start(bf16[304,1536]{1,0:T(8,128)(2,1)} %get-tuple-element.256), channel_id=1, source_target_pairs={{0,2},{1,3},{2,0},{3,1},{4,6},{5,7},{6,4},{7,5},{8,10},{9,11},{10,... | collective-permute-start | bytes 2801672 | tf_op jit(solution)/shard_map/ppermute | solution.py:799
  289.8 30.1 %collective-permute-start.26 = (bf16[304,768]{1,0:T(8,128)(2,1)S(1)}, bf16[304,768]{1,0:T(8,128)(2,1)}, u32[]{:S(2)}, u32[]{:S(2)}) collective-permute-start(bf16[304,768]{1,0:T(8,128)(2,1)S(1)} %collective-permute-done.22.refs_2_), channel_id=1, source_target_pairs={{0,2},{1,3},{2,0},{3,1},{4,6},{5,7},{6,4},{7,5},{8,10},{9,11},{10,... | collective-permute-start | bytes 1400840 | tf_op jit(solution)/shard_map/ppermute | solution.py:799
  312.7 34.3 %collective-permute-start.36 = (bf16[304,768]{1,0:T(8,128)(2,1)}, bf16[304,768]{1,0:T(8,128)(2,1)S(1)}, u32[]{:S(2)}, u32[]{:S(2)}) collective-permute-start(bf16[304,768]{1,0:T(8,128)(2,1)} %get-tuple-element.267.refs_0_), channel_id=1, source_target_pairs={{0,2},{1,3},{2,0},{3,1},{4,6},{5,7},{6,4},{7,5},{8,10},{9,11},{10,... | collective-permute-start | bytes 1400840 | tf_op jit(solution)/shard_map/ppermute | solution.py:799
  382.7 238.7 %reduce-scatter.7.cloned.1.call-start = ((), (), s32[]{:S(2)}) async-start(), calls=%async_computation.15 | async-start | bytes 10616832 | tf_op jit(solution)/shard_map/reduce_scatter | solution.py:1597
  439.3 229.2 %reduce-scatter.9.cloned.1.call-start = ((), (), s32[]{:S(2)}) async-start(), calls=%async_computation.16 | async-start | bytes 2654208 | tf_op jit(solution)/shard_map/reduce_scatter | solution.py:1597
  460.3 39.2 %collective-permute-start.46 = (bf16[304,768]{1,0:T(8,128)(2,1)S(1)}, bf16[304,768]{1,0:T(8,128)(2,1)S(1)}, u32[]{:S(2)}, u32[]{:S(2)}) collective-permute-start(bf16[304,768]{1,0:T(8,128)(2,1)S(1)} %add_convert_fusion.7), channel_id=1, source_target_pairs={{0,1},{1,0},{2,3},{3,2},{4,5},{5,4},{6,7},{7,6},{8,9},{9,8},{10,11... | collective-permute-start | bytes 1400840 | tf_op jit(solution)/shard_map/ppermute | solution.py:799
  515.6 48.3 %collective-permute-start.54 = (bf16[304,768]{1,0:T(8,128)(2,1)}, bf16[304,768]{1,0:T(8,128)(2,1)}, u32[]{:S(2)}, u32[]{:S(2)}) collective-permute-start(bf16[304,768]{1,0:T(8,128)(2,1)} %get-tuple-element.355.refs_0_), channel_id=1, source_target_pairs={{0,2},{1,3},{2,0},{3,1},{4,6},{5,7},{6,4},{7,5},{8,10},{9,11},{10,... | collective-permute-start | bytes 1400840 | tf_op jit(solution)/shard_map/ppermute | solution.py:799
  520.2 43.8 %collective-permute-start.53 = (bf16[304,768]{1,0:T(8,128)(2,1)}, bf16[304,768]{1,0:T(8,128)(2,1)S(1)}, u32[]{:S(2)}, u32[]{:S(2)}) collective-permute-start(bf16[304,768]{1,0:T(8,128)(2,1)} %get-tuple-element.356.refs_1_), channel_id=1, source_target_pairs={{0,1},{1,0},{2,3},{3,2},{4,5},{5,4},{6,7},{7,6},{8,9},{9,8},{10,11... | collective-permute-start | bytes 1400840 | tf_op jit(solution)/shard_map/ppermute | solution.py:799
  520.9 43.0 %collective-permute-start.56 = (bf16[304,768]{1,0:T(8,128)(2,1)S(1)}, bf16[304,768]{1,0:T(8,128)(2,1)}, u32[]{:S(2)}, u32[]{:S(2)}) collective-permute-start(bf16[304,768]{1,0:T(8,128)(2,1)S(1)} %collective-permute-done.52.refs_2_), channel_id=1, source_target_pairs={{0,2},{1,3},{2,0},{3,1},{4,6},{5,7},{6,4},{7,5},{8,10},{9,11},{10,... | collective-permute-start | bytes 1400840 | tf_op jit(solution)/shard_map/ppermute | solution.py:799
  525.3 38.7 %collective-permute-start.57 = (bf16[304,768]{1,0:T(8,128)(2,1)}, bf16[304,768]{1,0:T(8,128)(2,1)}, u32[]{:S(2)}, u32[]{:S(2)}) collective-permute-start(bf16[304,768]{1,0:T(8,128)(2,1)} %collective-permute-done.55.refs_5_), channel_id=1, source_target_pairs={{0,1},{1,0},{2,3},{3,2},{4,5},{5,4},{6,7},{7,6},{8,9},{9,8},{10,11... | collective-permute-start | bytes 1400840 | tf_op jit(solution)/shard_map/ppermute | solution.py:799
  591.7 170.7 %reduce-scatter.11.cloned.1.call-start = ((), (), s32[]{:S(2)}) async-start(), calls=%async_computation.17 | async-start | bytes 7962624 | tf_op jit(solution)/shard_map/reduce_scatter | solution.py:1597
  591.8 28.7 %collective-permute-start.58 = (bf16[2,304,1536]{2,1,0:T(8,128)(2,1)}, bf16[2,304,1536]{2,1,0:T(8,128)(2,1)}, u32[]{:S(2)}, u32[]{:S(2)}) collective-permute-start(bf16[2,304,1536]{2,1,0:T(8,128)(2,1)} %get-tuple-element.335), channel_id=1, source_target_pairs={{0,1},{1,0},{2,3},{3,2},{4,5},{5,4},{6,7},{7,6},{8,9},{9,8},{10,11... | collective-permute-start | bytes 5603336 | tf_op jit(solution)/shard_map/ppermute | solution.py:799
  594.1 59.4 %collective-permute-start.64 = (bf16[304,1536]{1,0:T(8,128)(2,1)}, bf16[304,1536]{1,0:T(8,128)(2,1)S(1)}, u32[]{:S(2)}, u32[]{:S(2)}) collective-permute-start(bf16[304,1536]{1,0:T(8,128)(2,1)} %get-tuple-element.372), channel_id=1, source_target_pairs={{0,1},{1,0},{2,3},{3,2},{4,5},{5,4},{6,7},{7,6},{8,9},{9,8},{10,11... | collective-permute-start | bytes 2801672 | tf_op jit(solution)/shard_map/ppermute | solution.py:799
  595.4 58.1 %collective-permute-start.65 = (bf16[304,1536]{1,0:T(8,128)(2,1)}, bf16[304,1536]{1,0:T(8,128)(2,1)}, u32[]{:S(2)}, u32[]{:S(2)}) collective-permute-start(bf16[304,1536]{1,0:T(8,128)(2,1)} %get-tuple-element.373), channel_id=1, source_target_pairs={{0,2},{1,3},{2,0},{3,1},{4,6},{5,7},{6,4},{7,5},{8,10},{9,11},{10,... | collective-permute-start | bytes 2801672 | tf_op jit(solution)/shard_map/ppermute | solution.py:799
  696.4 56.0 %collective-permute-start.68 = (bf16[304,1536]{1,0:T(8,128)(2,1)}, bf16[304,1536]{1,0:T(8,128)(2,1)}, u32[]{:S(2)}, u32[]{:S(2)}) collective-permute-start(bf16[304,1536]{1,0:T(8,128)(2,1)} %get-tuple-element.387), channel_id=1, source_target_pairs={{0,1},{1,0},{2,3},{3,2},{4,5},{5,4},{6,7},{7,6},{8,9},{9,8},{10,11... | collective-permute-start | bytes 2801672 | tf_op jit(solution)/shard_map/ppermute | solution.py:799
  697.4 57.7 %collective-permute-start.69 = (bf16[304,1536]{1,0:T(8,128)(2,1)}, bf16[304,1536]{1,0:T(8,128)(2,1)}, u32[]{:S(2)}, u32[]{:S(2)}) collective-permute-start(bf16[304,1536]{1,0:T(8,128)(2,1)} %get-tuple-element.388), channel_id=1, source_target_pairs={{0,2},{1,3},{2,0},{3,1},{4,6},{5,7},{6,4},{7,5},{8,10},{9,11},{10,... | collective-permute-start | bytes 2801672 | tf_op jit(solution)/shard_map/ppermute | solution.py:799
  716.3 50.3 %collective-permute-start.67 = (bf16[304,768]{1,0:T(8,128)(2,1)}, bf16[304,768]{1,0:T(8,128)(2,1)}, u32[]{:S(2)}, u32[]{:S(2)}) collective-permute-start(bf16[304,768]{1,0:T(8,128)(2,1)} %add_convert_fusion.4), channel_id=1, source_target_pairs={{0,2},{1,3},{2,0},{3,1},{4,6},{5,7},{6,4},{7,5},{8,10},{9,11},{10,... | collective-permute-start | bytes 1400840 | tf_op jit(solution)/shard_map/ppermute | solution.py:799
  733.8 40.1 %collective-permute-start.66 = (bf16[304,768]{1,0:T(8,128)(2,1)S(1)}, bf16[304,768]{1,0:T(8,128)(2,1)}, u32[]{:S(2)}, u32[]{:S(2)}) collective-permute-start(bf16[304,768]{1,0:T(8,128)(2,1)S(1)} %add_convert_fusion.5), channel_id=1, source_target_pairs={{0,1},{1,0},{2,3},{3,2},{4,5},{5,4},{6,7},{7,6},{8,9},{9,8},{10,11... | collective-permute-start | bytes 1400840 | tf_op jit(solution)/shard_map/ppermute | solution.py:799
  (126 other events, 1931.5 us)
Sparse Core Ops, SparseCore 0:
  30.4 75.5 all-gather.4
  108.1 31.4 all-gather.6
  141.2 89.1 all-gather.8
  231.8 89.1 all-gather.10
  382.8 98.9 reduce-scatter.4
  483.9 97.8 reduce-scatter.6
  591.9 32.3 reduce-scatter.8
  668.6 82.5 reduce-scatter.10

commit v6 on v5

--- a/solution.py
+++ b/solution.py
@@ -563,19 +563,19 @@
 
 
 WEIGHT = {
-    "attention": 8.5,
-    "attention_back": 16,
-    "project": 6.5,
-    "partial_sums": 2.5,
-    "middle": 2.5,
-    "hidden": 9,
-    "outer_sums": 9,
-    "hidden_back": 10,
-    "middle_back": 3.5,
-    "attended_back": 3,
-    "project_back": 6,
-    "result": 3.5,
-    "input_back": 4.5,
+    "attention": 0.17,
+    "attention_back": 0.32,
+    "project": 0.13,
+    "partial_sums": 0.05,
+    "middle": 0.05,
+    "hidden": 0.18,
+    "outer_sums": 0.18,
+    "hidden_back": 0.2,
+    "middle_back": 0.07,
+    "attended_back": 0.06,
+    "project_back": 0.12,
+    "result": 0.07,
+    "input_back": 0.09,
 }
 
 
@@ -819,12 +819,20 @@
     return (flip(sent[1], 1), flip(sent[2], 2))
 
 
+def scatter_added(sent, first):
+    width = sent[3].shape[-1]
+    return (
+        add_low(sent[3], first[1][..., :width]),
+        add_low(sent[4], first[0][..., :width]),
+    )
+
+
+def scatter_sent(sent, first, added):
+    return (sent[0], *first, flip(added[0], 1), flip(added[1], 2))
+
+
 def scatter_last(sent, first):
-    from_x, from_y = first
-    width = sent[3].shape[-1]
-    late_x = flip(add_low(sent[3], from_y[..., :width]), 1)
-    late_y = flip(add_low(sent[4], from_x[..., :width]), 2)
-    return (sent[0], from_x, from_y, late_x, late_y)
+    return scatter_sent(sent, first, scatter_added(sent, first))
 
 
 def scatter_halves(halves):
@@ -868,8 +876,8 @@
     return fetched
 
 
-def send_block(copies, rows, sent, r, seq):
-    own, for_x, for_y, late_x, late_y = sent if seq is None else [ref.at[seq] for ref in sent]
+def send_block(copies, rows, sent, r):
+    own, for_x, for_y, late_x, late_y = sent
     width = rows.shape[2] // 2
     low, high = pl.ds(0, width), pl.ds(width, width)
     if r == 0:
@@ -884,9 +892,8 @@
     copies.send(rows.at[r, :, high], second)
 
 
-def sent_shapes(block, D, seqs=1):
-    lead = () if seqs == 1 else (seqs,)
-    return [((*lead, block, width), BF16) for width in (D, D, D, D // 2, D // 2)]
+def sent_shapes(block, D):
+    return [((block, width), BF16) for width in (D, D, D, D // 2, D // 2)]
 
 
 def normalize(values):
@@ -979,12 +986,12 @@
 
 
 def partial_kernel(seqs, dot, image_rows, *refs):
-    inputs, weight, halves = (refs[: 2 * seqs], refs[2 * seqs], refs[2 * seqs + 1 : 2 * seqs + 6])
+    inputs, weight, halves = (refs[: 2 * seqs], refs[2 * seqs], refs[2 * seqs + 1 : 7 * seqs + 1])
     lefts, held, rows, semaphores = (
-        refs[2 * seqs + 6 : 4 * seqs + 6],
-        refs[4 * seqs + 6],
-        refs[4 * seqs + 7 : 5 * seqs + 7],
-        refs[5 * seqs + 7],
+        refs[7 * seqs + 1 : 9 * seqs + 1],
+        refs[9 * seqs + 1],
+        refs[9 * seqs + 2 : 10 * seqs + 2],
+        refs[10 * seqs + 2],
     )
     copies = Copies(semaphores)
     weights = [copies.start(weight.at[t], held.at[t]) for t in (1, 0)]
@@ -1005,7 +1012,7 @@
         for r in (3, 1, 2, 0):
             left = lefts[2 * s][r * image_rows : (r + 1) * image_rows, :]
             rows[s][r, :image_rows, :] = dot(left, held[0]).astype(BF16)
-            send_block(copies, rows[s], halves, r, s if seqs > 1 else None)
+            send_block(copies, rows[s], halves[5 * s : 5 * s + 5], r)
     copies.finish()
 
 
@@ -1019,8 +1026,8 @@
         "partial_sums",
         (*[value for pair in inputs for value in pair], weight),
         [ANYWHERE] * (2 * seqs + 1),
-        sent_shapes(block, D, seqs),
-        [ANYWHERE] * 5,
+        sent_shapes(block, D) * seqs,
+        [ANYWHERE] * (5 * seqs),
         [pltpu.VMEM((count, K), BF16) for _ in range(seqs) for count in (image, text)]
         + [pltpu.VMEM(weight.shape, BF16)]
         + [pltpu.VMEM((4, block, D), BF16)] * seqs,
@@ -1259,9 +1266,9 @@
             back = dot_nn(pre_text[...], held_up[1]).astype(BF16)
             for q in range(4):
                 rows[q, image_rows:, :] = back[q * text_rows : (q + 1) * text_rows]
-            send_block(copies, rows, sent, order[0], None)
+            send_block(copies, rows, sent, order[0])
         if k >= 1:
-            send_block(copies, rows, sent, r, None)
+            send_block(copies, rows, sent, r)
     sums[0:1, :] = total
     copies.finish()
 
@@ -1408,7 +1415,7 @@
             totals[2 * t] = totals[2 * t] + jnp.sum(back, axis=0, keepdims=True)
             totals[2 * t + 1] = totals[2 * t + 1] + jnp.sum(back * norm, axis=0, keepdims=True)
             rows[r, low : low + count, :] = back.astype(BF16)
-        send_block(copies, rows, sent, r, None)
+        send_block(copies, rows, sent, r)
     column_sums[0:1, :] = columns
     for k in range(4):
         sums[k : k + 1, :] = totals[k]
@@ -1440,13 +1447,13 @@
 
 
 def result_kernel(image_rows, *refs):
-    pieces, cotangents, middles = (refs[:5], refs[5:7], refs[7:9])
-    mods, bias, image_out, text_out, sums = refs[9:]
+    pieces, cotangents, middles = (refs[:10], refs[10:12], refs[12:14])
+    mods, bias, image_out, text_out, sums = refs[14:]
     block = middles[0].shape[0]
     for seq in range(2):
         for t, low, count in ((0, 0, image_rows), (1, image_rows, block - image_rows)):
             span = slice(low, low + count)
-            value = piece_sum([piece.at[seq] for piece in pieces], low, count) + bias[t : t + 1, :]
+            value = piece_sum(pieces[5 * seq : 5 * seq + 5], low, count) + bias[t : t + 1, :]
             gate = mods[t, seq, 5:6, :]
             out = (middles[seq][span, :] + gate * value).astype(BF16)
             if t == 0:
@@ -1461,12 +1468,12 @@
 
 
 def result_step(pieces, cotangents, middles, mods, bias, image_rows):
-    seqs, block, width = pieces[3].shape
+    seqs, (block, width) = (len(middles), pieces[3].shape)
     return run(
         functools.partial(result_kernel, image_rows),
         "result",
         (*pieces, *cotangents, *middles, mods, bias),
-        [ON_CORE] * 11,
+        [ON_CORE] * 16,
         [
             ((seqs, image_rows, 2 * width), BF16),
             ((seqs, block - image_rows, 2 * width), BF16),
@@ -1577,19 +1584,21 @@
     return lax.all_gather(values, "batch", axis=1, tiled=True)
 
 
-def gather_small(values, axis):
+def after(values, *others):
+    return lax.optimization_barrier((values, others))[0]
+
+
+def gather_small(values, axis, last=()):
     count = lax.axis_size(axis)
     held = values[None]
     bit = 1
     while bit < count:
         pairs = [(i, i ^ bit) for i in range(count)]
+        if 2 * bit == count:
+            held = after(held, last)
         held = jnp.concatenate([held, lax.ppermute(held, axis, pairs)])
         bit *= 2
     return jnp.take(held, jnp.bitwise_xor(lax.axis_index(axis), jnp.arange(count)), axis=0)
-
-
-def after(values, *others):
-    return lax.optimization_barrier((values, others))[0]
 
 
 def scatter_rows_over_batch(values):
@@ -1646,7 +1655,11 @@
     bias_widths = [array.shape[1] for array in (qv_bias, out_bias, up_bias, down_bias)]
     bias_ends = np.cumsum(bias_widths)
     own_biases = jnp.concatenate([qv_bias, out_bias, up_bias, down_bias], axis=1)
-    near = gather_small(jnp.concatenate([conditioning, own_biases], axis=1), "batch")
+    near = gather_small(
+        jnp.concatenate([conditioning, own_biases], axis=1),
+        "batch",
+        (tokens_near[0], tokens_near[3]),
+    )
     cond_all = near[:, :, :D].reshape(B * L, D)
     column_biases = near[:, :, D:].astype(F32)
     smooth_all = jax.nn.silu(cond_all.astype(F32)).astype(BF16)
@@ -1655,18 +1668,13 @@
         + mod_bias.astype(F32)[:, None, :]
     )
     mod_width = mod_own.shape[2]
-    mod_sent = mod_own.reshape(2, B, L, mod_width).transpose(1, 0, 2, 3)
-    mod_came = swap(after(mod_sent, tokens_near), "batch")
-    out_units = jnp.swapaxes(out_weight, 1, 2).reshape(2, -1, S, own_width).transpose(2, 0, 1, 3)
-    out_mine = swap(after(out_units, mod_came), "seq")
-    out_columns = out_mine.shape[2]
-    out_rows = out_mine.transpose(1, 0, 2, 3).reshape(2, S * out_columns, own_width)
-    out_part = gather_rows_over_batch(out_rows)
-    hidden_columns = up_weight.shape[2]
+    mod_all = gather_small(mod_own, "batch", (tokens_near[1], tokens_near[2]))
+    mod_came = lax.dynamic_slice_in_dim(mod_all, lax.axis_index("batch") * L, L, 2)
     small = jnp.concatenate(
         [mod_came.reshape(B, 2 * L * mod_width), column_biases.reshape(B, -1)], axis=1
     )
-    small_all = gather_small(small, "seq")
+    tokens_all = gather_far(*tokens, tokens_near)
+    small_all = gather_small(small, "seq", tokens_all[6:])
     modulation = (
         small_all[:, :, : 2 * L * mod_width]
         .reshape(S, B, 2, L, mod_width)
@@ -1692,14 +1700,21 @@
         axis=1,
     )
 
-    tokens_all = gather_far(*tokens, tokens_near)
+    out_units = jnp.swapaxes(out_weight, 1, 2).reshape(2, -1, S, own_width).transpose(2, 0, 1, 3)
+    order = jnp.bitwise_xor(seq_index, jnp.arange(S))
+    out_units = jnp.take(after(out_units, mod_own), order, axis=0)
+    out_mine = jnp.stack([out_units[0], *(flip(out_units[r], r) for r in range(1, S))])
+    out_mine = jnp.take(out_mine, order, axis=0)
+    out_columns = out_mine.shape[2]
+    out_rows = out_mine.transpose(1, 0, 2, 3).reshape(2, S * out_columns, own_width)
+    out_part = gather_rows_over_batch(out_rows)
+    hidden_columns = up_weight.shape[2]
     padded = jnp.concatenate([image_cotangent, jnp.pad(text_cotangent, pad)], axis=1)
     cotangents = (padded[..., :half], padded[..., half:])
     near_grads = gather_near(*after(cotangents, tokens_all, small_all))
-    up_part = gather_rows_over_batch(after(jnp.swapaxes(up_weight, 1, 2), tokens_all))
-    down_part = gather_rows_over_batch(after(jnp.swapaxes(down_weight, 1, 2), tokens_all))
-
-    order = jnp.bitwise_xor(seq_index, jnp.arange(S))
+    up_part = gather_rows_over_batch(after(jnp.swapaxes(up_weight, 1, 2), out_mine, mod_own))
+    down_part = gather_rows_over_batch(after(jnp.swapaxes(down_weight, 1, 2), out_mine, mod_own))
+
     image_keys = jnp.take(
         key_mask[:, : S * image_count].reshape(L, S, image_count), order, axis=1
     )
@@ -1724,17 +1739,20 @@
     first = project(again, qkv_part, modulation, qkv_bias, 1, image_count)
     attended = attention(first[0], first[1], key_bias[1], floors[1], head)
     attended, logs = (attended[:2], attended[2:])
-    cotangents_all = gather_far(*cotangents, after(near_grads, kept[0][0]))
+    cotangents_all = gather_far(*cotangents, after(near_grads, kept[0][1]))
     out_first = scatter_first(kept[0][3])
-    attended = after(attended, cotangents_all, out_first)
+    out_added = scatter_added(kept[0][3], after(out_first, attended))
+    attended = after(attended, cotangents_all, out_added)
     parts = partial_sums([attended], out_part, dot_nt, D, image_count)
     kept.append((first, attended, logs, parts))
     firsts, attendeds, logs, out_halves = zip(*kept)
-    steps, seconds = ([], [])
+    out_pieces = [scatter_sent(out_halves[0], out_first, out_added)]
+    out_pieces.append(scatter_halves(after(out_halves[1], out_pieces[0])))
+    steps = []
     for s in range(L):
         steps.append(
             middle_step(
-                scatter_last(out_halves[s], out_first if s == 0 else scatter_first(out_halves[s])),
+                out_pieces[s],
                 tokens,
                 modulation,
                 out_bias_full,
@@ -1742,10 +1760,11 @@
                 image_count,
             )
         )
-        seconds.append(gather_halves(*steps[s][2:]))
+    second_near = [gather_near(*step[2:]) for step in steps]
     hidden = []
     for s in range(L):
-        halves = after(seconds[s], hidden[-1]) if s else seconds[s]
+        near = after(second_near[s], hidden[-1]) if s else second_near[s]
+        halves = gather_far(*steps[s][2:], near)
         hidden.append(
             hidden_step(
                 halves, cotangents_all, up_part, up_bias_part, modulation, s, image_count
@@ -1766,27 +1785,29 @@
         bias_sums.append(sums)
         norm2_halves.append(halves)
     up_bias_sum = sum(bias_sums)
-    norm2_first = [scatter_first(halves) for halves in norm2_halves]
-    norm2_pieces = [
-        scatter_last(halves, first) for halves, first in zip(norm2_halves, norm2_first)
+    norm2_first = scatter_first(norm2_halves[0])
+    norm2_added = scatter_added(norm2_halves[0], after(norm2_first, gate))
+    norm2_pieces = scatter_sent(norm2_halves[0], norm2_first, norm2_added)
+    norm2_first1 = scatter_first(after(norm2_halves[1], norm2_pieces[3:]))
+    backs = [
+        middle_back(
+            after(norm2_pieces, gate),
+            cotangents,
+            *steps[0][1::-1],
+            modulation,
+            0,
+            image_count,
+        )
     ]
-    up_sum = outer_sums(after(pres, gate, norm2_first[0]), norms, 256)
-    up_came = scatter_rows_over_batch(up_sum)
-
-    backs, projs = ([], [])
+    proj_near0 = gather_near(*backs[0][1:3])
+    mlp_halves = partial_sums(after(acts, backs[0]), down_part, dot_nn, D, image_count)
+    up_sum = outer_sums(after(pres, mlp_halves), norms, 256)
+    norm2_added = scatter_added(norm2_halves[1], after(norm2_first1, mlp_halves))
+    norm2_pieces = scatter_sent(norm2_halves[1], norm2_first1, norm2_added)
+    projs = [gather_far(*backs[0][1:3], after(proj_near0, up_sum))]
     backs.append(
         middle_back(
-            after(norm2_pieces[0], up_sum), cotangents, *steps[0][1::-1], modulation, 0, image_count
-        )
-    )
-    proj_near = gather_near(*backs[0][1:3])
-    projs.append(gather_far(*backs[0][1:3], proj_near))
-    mlp_halves = partial_sums(
-        after(acts, backs[0], norm2_first[1]), down_part, dot_nn, D, image_count
-    )
-    backs.append(
-        middle_back(
-            after(norm2_pieces[1], mlp_halves, proj_near),
+            after(norm2_pieces, up_sum, proj_near0),
             cotangents,
             *steps[1][1::-1],
             modulation,
@@ -1794,33 +1815,46 @@
             image_count,
         )
     )
-    projs.append(gather_halves(*backs[1][1:3]))
+    proj_near1 = gather_near(*backs[1][1:3])
     grad0, proj0 = attended_back(
         after(projs[0], backs[1], down_came), out_part, image_count
     )
+    up_came = scatter_rows_over_batch(after(up_sum, backs[1]))
     qkv_grad0 = attention_back(
         *firsts[0][:2], *attendeds[0], *logs[0], *grad0, key_bias[0], head
     )
-    grad1, proj1 = attended_back(after(projs[1], qkv_grad0), out_part, image_count)
-    mlp_first = scatter_first(after(mlp_halves, projs[1]))
+    projs.append(gather_far(*backs[1][1:3], after(proj_near1, qkv_grad0)))
+    sums0, columns0, halves0 = project_back(
+        qkv_grad0, qkv_part, tokens_all, 0, image_count
+    )
+    grad1, proj1 = attended_back(after(projs[1], halves0), out_part, image_count)
+    mlp_halves = (mlp_halves[:5], mlp_halves[5:])
+    mlp_first = [scatter_first(after(halves, projs[1])) for halves in mlp_halves]
     out_sum = outer_sums([proj0, proj1], attendeds, 256)
-    sums0, columns0, halves0 = project_back(
-        after(qkv_grad0, out_sum), qkv_part, tokens_all, 0, image_count
-    )
-    out_came = scatter_rows_over_batch(after(out_sum, halves0))
-    norm1_first = scatter_first(halves0)
-    grad1 = after(grad1, halves0, up_came, mlp_first)
+    out_came = scatter_rows_over_batch(out_sum)
+    grad1 = after(grad1, out_sum)
     qkv_grad1 = attention_back(
         *firsts[1][:2], *attendeds[1], *logs[1], *grad1, key_bias[1], head
     )
-    mlp_pieces = scatter_last(mlp_halves, mlp_first)
-    qkv_grad1 = after(qkv_grad1, norm1_first)
+    mlp_added = [
+        scatter_added(halves, after(first, qkv_grad1))
+        for halves, first in zip(mlp_halves, mlp_first)
+    ]
+    mlp_pieces = [
+        piece
+        for halves, first, added in zip(mlp_halves, mlp_first, mlp_added)
+        for piece in scatter_sent(halves, first, added)
+    ]
+    norm1_first = scatter_first(after(halves0, mlp_pieces))
     qkv_sum = outer_sums(
-        [qkv_grad0, qkv_grad1], [first[2:] for first in firsts], 128 if qkv_width % 256 else 256
+        [qkv_grad0, after(qkv_grad1, mlp_added, up_came)],
+        [first[2:] for first in firsts],
+        128 if qkv_width % 256 else 256,
     )
     qkv_came = scatter_rows_over_batch(after(qkv_sum, out_came))
+    out_home = swap(out_came.reshape(2, S, out_columns, own_width).swapaxes(0, 1), "seq")
     sums1, columns1, halves1 = project_back(
-        after(qkv_grad1, qkv_sum), qkv_part, tokens_all, 1, image_count
+        after(qkv_grad1, qkv_sum, mlp_pieces, out_home), qkv_part, tokens_all, 1, image_count
     )
     norm1_pieces = [scatter_last(halves0, norm1_first), scatter_halves(halves1)]
     image_out, text_out, result_sums = result_step(
@@ -1831,19 +1865,20 @@
         down_bias_full,
         image_count,
     )
+    image_grad, text_grad = input_back(
+        norm1_pieces, tokens, [back[0] for back in backs], modulation, image_count, live_text
+    )
     qkv_home = move_units(
-        qkv_came.reshape(2, per_device, unit, D).swapaxes(0, 1), back_perms, land, send, place
-    )
-    out_home = swap(out_came.reshape(2, S, out_columns, own_width).swapaxes(0, 1), "seq")
+        after(qkv_came, image_grad).reshape(2, per_device, unit, D).swapaxes(0, 1),
+        back_perms, land, send, place
+    )
     qkv_weight_grad = qkv_home.swapaxes(0, 1).reshape(2, -1, D).swapaxes(1, 2).astype(F32)
     out_weight_grad = (
         out_home.transpose(1, 2, 0, 3).reshape(2, out_columns, D).swapaxes(1, 2).astype(F32)
     )
     up_weight_grad = up_came.swapaxes(1, 2).astype(F32)
     down_weight_grad = down_came.swapaxes(1, 2).astype(F32)
-    image_grad, text_grad = input_back(
-        norm1_pieces, tokens, [back[0] for back in backs], modulation, image_count, live_text
-    )
+
 
     first_sums = jnp.stack([sums0, sums1]).reshape(L, 2, 2, D)
     second_sums = jnp.stack([back[3] for back in backs]).reshape(L, 2, 4, D)
@@ -1902,7 +1937,8 @@
     )
     mod_bias_grad = jnp.sum(mod_mine.astype(F32), axis=1)
     smooth_part = jnp.einsum("tsf,tdf->sd", mod_mine, mod_weight, preferred_element_type=F32)
-    smooth_grad = jnp.sum(swap(smooth_part.reshape(B, L, D), "batch"), axis=0)
+    smooth_grad = jnp.sum(swap(after(smooth_part, norm1_pieces[1]).reshape(B, L, D), "batch"), axis=0)
+    smooth_grad = after(smooth_grad, qkv_home)
     smooth_grad = smooth_grad + flip(smooth_grad, 1)
     smooth_grad = smooth_grad + flip(smooth_grad, 2)
     cond_grad = jax.vjp(jax.nn.silu, conditioning.astype(F32))[1](smooth_grad)[0]

time: 809 us -> 788 us (0.974)
  waiting for transfers between devices: 205 us -> 189 us
  blocking collectives: 9.1 us -> 0 us
    ppermute x66 -> x73, waiting for transfers between devices: 180 us -> 134 us  [flip(): return lax.ppermute(values, 'seq', [(i, i ^ bit) for i in range(4)])]
    ppermute x5 -> x8, waiting for transfers between devices: 14.3 us -> 33 us  [gather_small(): held = jnp.concatenate([held, lax.ppermute(held, axis, pairs)])]
    all_to_all x5 -> x4, starting transfers between devices: 28.4 us -> 18.7 us  [swap(): return lax.all_to_all(values, axis, 0, 0, tiled=True)]
    all_to_all x1 -> x0, blocking collectives: 9.1 us -> none  [swap(): return lax.all_to_all(values, axis, 0, 0, tiled=True)]
    ppermute x66 -> x73, starting transfers between devices: 71.5 us -> 80 us  [flip(): return lax.ppermute(values, 'seq', [(i, i ^ bit) for i in range(4)])]
  transfers between devices with their start and end apart: 90 -> 99, of which waited for: 40 -> 38; matrix products, arithmetic and copies ran while one was open for 8% -> 9% of each run, Pallas kernels for 45% -> 47%
where the time goes in v6:
time: 788 us; the launch traced here: 782 us
  Pallas kernels  364 us (46%)
  waiting for transfers between devices  189 us (24%)
  starting transfers between devices  126 us (16%)
  local copies, waits for them, and re-layouts  41.8 us (5%)
  other arithmetic  34.4 us (4%)
  between operations  22 us (3%)
    pallas_call x23, Pallas kernels, run(): pl.pallas_call(kernel, in_specs=specs, out_specs=out_specs, out_shape=[ja...  265 us
    ppermute x73, waiting for transfers between devices, flip(): return lax.ppermute(values, 'seq', [(i, i ^ bit) for i in range(4)])  134 us
    ppermute x73, starting transfers between devices, flip(): return lax.ppermute(values, 'seq', [(i, i ^ bit) for i in range(4)])  80 us
    pallas_call x2, Pallas kernels, attention_back(): pl.pallas_call(functools.partial(attention_back_kernel, 512, LOG2E / math...  64.3 us
    pallas_call x2, Pallas kernels, attention(): pl.pallas_call(functools.partial(attention_kernel, 256, LOG2E / math.sqrt...  35 us
    ppermute x8, waiting for transfers between devices, gather_small(): held = jnp.concatenate([held, lax.ppermute(held, axis, pairs)])  33 us
    all_to_all x4, starting transfers between devices, swap(): return lax.all_to_all(values, axis, 0, 0, tiled=True)  18.7 us
    ppermute x6, starting transfers between devices, move_units(): lax.ppermute(lax.dynamic_index_in_dim(units, slot, 0, keepdims=True), ('b...  18.3 us
  transfers between devices with their start and end apart: 99, of which 38 were waited for; matrix products, arithmetic and copies ran while one was open for 9% of the time, Pallas kernels for 47%

profile of v6, /device:TPU:16, one launch (start us, length us, event | category | flops | bytes accessed | tf_op | source)
XLA Modules:
  0.0 781.7 jit_solution(17969901173850603267)
XLA Ops:
  44.0 14.8 %collective-permute-done.3.refs_2_.refs_5_ = bf16[2,304,768]{2,1,0:T(8,128)(2,1)S(1)} collective-permute-done((bf16[2,304,768]{2,1,0:T(8,128)(2,1)S(1)}, bf16[2,304,768]{2,1,0:T(8,128)(2,1)S(1)}, u32[]{:S(2)}, u32[]{:S(2)}) %collective-permute-start.3) | collective-permute-done | bytes 933920 | tf_op jit(solution)/shard_map/ppermute | solution.py:799
  91.7 8.5 %collective-permute-done.13 = f32[2,2,16,288]{3,2,1,0:T(8,128)S(1)} collective-permute-done((f32[2,2,16,288]{3,2,1,0:T(8,128)S(1)}, f32[2,2,16,288]{3,2,1,0:T(8,128)S(1)}, u32[]{:S(2)}, u32[]{:S(2)}) %collective-permute-start.13) | collective-permute-done | bytes 73760 | tf_op jit(solution)/shard_map/ppermute | solution.py:1599
  136.5 13.0 %project.2 = (bf16[1024,1152]{1,0:T(8,128)(2,1)}, bf16[192,1152]{1,0:T(8,128)(2,1)}, bf16[1024,1536]{1,0:T(8,128)(2,1)}, bf16[192,1536]{1,0:T(8,128)(2,1)}) custom-call(bf16[2,304,768]{2,1,0:T(8,128)(2,1)} %copy-done.2, bf16[2,304,768]{2,1,0:T(8,128)(2,1)} %copy-done.1, bf16[2,304,768]{2,1,0:T(8,128)(2,1)} %copy-done.4, ...), custom_call_target="tpu_custom_call" | custom-call | flops 149500000 | bytes 1 | tf_op jit(solution)/shard_map/project/pallas_call | solution.py:919
  150.6 17.9 %attention.2 = (bf16[1024,384]{1,0:T(8,128)(2,1)}, bf16[192,384]{1,0:T(8,128)(2,1)}, f32[1024,384]{1,0:T(8,128)}, f32[192,384]{1,0:T(8,128)}) custom-call(f32[1216,128]{1,0:T(8,128)} %broadcast_in_dim.119.bias_ref.refs_0_, f32[1,1]{1,0:T(1,128)} %bitcast.6.floor_ref, bf16[1024,1152]{1,0:T(8,128)(2,1)} %get-tuple-element.256.qi.ki.vi.refs_1_.refs_3_.refs_5_, ...), custom_call_target="tpu_custom_call" | custom-call | flops 195500000 | bytes 1 | tf_op jit(solution)/shard_map/attention/pallas_call | solution.py:657
  177.8 13.1 %project.3 = (bf16[1024,1152]{1,0:T(8,128)(2,1)}, bf16[192,1152]{1,0:T(8,128)(2,1)}, bf16[1024,1536]{1,0:T(8,128)(2,1)}, bf16[192,1536]{1,0:T(8,128)(2,1)}) custom-call(bf16[2,304,768]{2,1,0:T(8,128)(2,1)} %copy-done.2, bf16[2,304,768]{2,1,0:T(8,128)(2,1)} %copy-done.1, bf16[2,304,768]{2,1,0:T(8,128)(2,1)} %copy-done.4, ...), custom_call_target="tpu_custom_call" | custom-call | flops 149500000 | bytes 1 | tf_op jit(solution)/shard_map/project/pallas_call | solution.py:919
  192.0 17.1 %attention.3 = (bf16[1024,384]{1,0:T(8,128)(2,1)}, bf16[192,384]{1,0:T(8,128)(2,1)}, f32[1024,384]{1,0:T(8,128)}, f32[192,384]{1,0:T(8,128)}) custom-call(f32[1216,128]{1,0:T(8,128)} %broadcast_in_dim.133.bias_ref.refs_0_, f32[1,1]{1,0:T(1,128)} %bitcast.38.floor_ref, bf16[1024,1152]{1,0:T(8,128)(2,1)} %get-tuple-element.278.qi.ki.vi.refs_1_.refs_3_.refs_5_, ...), custom_call_target="tpu_custom_call" | custom-call | flops 195500000 | bytes 1 | tf_op jit(solution)/shard_map/attention/pallas_call | solution.py:657
  234.3 13.4 %collective-permute-done.36.refs_1_ = bf16[304,1536]{1,0:T(8,128)(2,1)} collective-permute-done((bf16[304,1536]{1,0:T(8,128)(2,1)}, bf16[304,1536]{1,0:T(8,128)(2,1)}, u32[]{:S(2)}, u32[]{:S(2)}) %collective-permute-start.36) | collective-permute-done | bytes 933920 | tf_op jit(solution)/shard_map/ppermute | solution.py:799
  260.9 8.0 %collective-permute-done.39.refs_4_ = bf16[304,768]{1,0:T(8,128)(2,1)S(1)} collective-permute-done((bf16[304,768]{1,0:T(8,128)(2,1)S(1)}, bf16[304,768]{1,0:T(8,128)(2,1)S(1)}, u32[]{:S(2)}, u32[]{:S(2)}) %collective-permute-start.39) | collective-permute-done | bytes 466976 | tf_op jit(solution)/shard_map/ppermute | solution.py:799
  281.3 7.6 collective-permute-done.32.refs_6_
  290.5 17.1 %hidden.2 = (bf16[1024,1536]{1,0:T(8,128)(2,1)}, bf16[192,1536]{1,0:T(8,128)(2,1)}, bf16[1024,1536]{1,0:T(8,128)(2,1)}, bf16[192,1536]{1,0:T(8,128)(2,1)}, bf16[...) custom-call(bf16[304,768]{1,0:T(8,128)(2,1)} %get-tuple-element.284.r, ...), custom_call_target="tpu_custom_call" | custom-call | flops 207000000 | bytes 1 | tf_op jit(solution)/shard_map/hidden/pallas_call | solution.py:919
  319.3 16.6 %hidden.3 = (bf16[1024,1536]{1,0:T(8,128)(2,1)}, bf16[192,1536]{1,0:T(8,128)(2,1)}, bf16[1024,1536]{1,0:T(8,128)(2,1)}, bf16[192,1536]{1,0:T(8,128)(2,1)}, bf16[...) custom-call(bf16[304,768]{1,0:T(8,128)(2,1)} %get-tuple-element.305.r, ...), custom_call_target="tpu_custom_call" | custom-call | flops 207000000 | bytes 1 | tf_op jit(solution)/shard_map/hidden/pallas_call | solution.py:919
  335.9 18.0 %outer_sums.4 = bf16[2,1536,1536]{2,1,0:T(8,128)(2,1)} custom-call(bf16[1024,1536]{1,0:T(8,128)(2,1)} %get-tuple-element.351.refs_0_, bf16[1024,1536]{1,0:T(8,128)(2,1)} %get-tuple-element.321.refs_1_.refs_0_, bf16[192,1536]{1,0:T(8,128)(2,1)} %get-tuple-element.352.refs_2_.refs_1_, bf16[192,1536]{1,0:T(8,128)(2,1)} %get-tuple-element.322.refs_3_.refs_1_, ...), custom_call_target="tpu_custom_call" | custom-call | flops 207000000 | bytes 1 | tf_op jit(solution)/shard_map/outer_sums/pallas_call | solution.py:919
  354.3 18.2 %hidden_back.2 = (bf16[1024,1536]{1,0:T(8,128)(2,1)}, bf16[192,1536]{1,0:T(8,128)(2,1)}, f32[2,1536]{1,0:T(2,128)}, bf16[304,1536]{1,0:T(8,128)(2,1)}, bf16[304,...) custom-call(bf16[1024,1536]{1,0:T(8,128)(2,1)} %get-tuple-element.321.refs_1_, ...), custom_call_target="tpu_custom_call" | custom-call | flops 230000000 | bytes 1 | tf_op jit(solution)/shard_map/hidden_back/pallas_call | solution.py:919
  374.4 18.7 %hidden_back.3 = (bf16[1024,1536]{1,0:T(8,128)(2,1)}, bf16[192,1536]{1,0:T(8,128)(2,1)}, f32[2,1536]{1,0:T(2,128)}, bf16[304,1536]{1,0:T(8,128)(2,1)}, bf16[304,...) custom-call(bf16[1024,1536]{1,0:T(8,128)(2,1)} %get-tuple-element.329.refs_5_, ...), custom_call_target="tpu_custom_call" | custom-call | flops 230000000 | bytes 1 | tf_op jit(solution)/shard_map/hidden_back/pallas_call | solution.py:919
  395.6 11.4 %collective-permute-done.49.refs_4_ = bf16[304,768]{1,0:T(8,128)(2,1)S(1)} collective-permute-done((bf16[304,768]{1,0:T(8,128)(2,1)S(1)}, bf16[304,768]{1,0:T(8,128)(2,1)S(1)}, u32[]{:S(2)}, u32[]{:S(2)}) %collective-permute-start.49) | collective-permute-done | bytes 466976 | tf_op jit(solution)/shard_map/ppermute | solution.py:799
  409.9 7.4 middle_back.2
  420.6 17.7 %partial_sums.5 = (bf16[304,1536]{1,0:T(8,128)(2,1)}, bf16[304,1536]{1,0:T(8,128)(2,1)}, bf16[304,1536]{1,0:T(8,128)(2,1)}, bf16[304,768]{1,0:T(8,128)(2,1)}, bf...) custom-call(bf16[1024,1536]{1,0:T(8,128)(2,1)} %get-tuple-element.35, ...), custom_call_target="tpu_custom_call" | custom-call | flops 57500000 | bytes 1 | tf_op jit(solution)/shard_map/partial_sums/pallas_call | solution.py:919
  444.6 18.4 %outer_sums.5 = bf16[2,1536,1536]{2,1,0:T(8,128)(2,1)} custom-call(bf16[1024,1536]{1,0:T(8,128)(2,1)} %get-tuple-element.373.refs_0_, bf16[1024,1536]{1,0:T(8,128)(2,1)} %get-tuple-element.311.refs_1_, bf16[192,1536]{1,0:T(8,128)(2,1)} %get-tuple-element.374.refs_2_, bf16[192,1536]{1,0:T(8,128)(2,1)} %get-tuple-element.312.refs_3_, ...), custom_call_target="tpu_custom_call" | custom-call | flops 207000000 | bytes 1 | tf_op jit(solution)/shard_map/outer_sums/pallas_call | solution.py:919
  463.1 7.4 middle_back.3
  480.2 6.8 attended_back.2
  487.0 32.2 %attention_back.2 = (bf16[1024,1152]{1,0:T(8,128)(2,1)}, bf16[192,1152]{1,0:T(8,128)(2,1)}) custom-call(f32[1216,128]{1,0:T(8,128)} %broadcast_in_dim.119.bias_ref.refs_0_, bf16[1024,1152]{1,0:T(8,128)(2,1)} %get-tuple-element.256.qi.ki.vi.refs_1_.refs_3_.refs_5_, bf16[192,1152]{1,0:T(8,128)(2,1)} %get-tuple-element.257.qt.kt.vt.refs_2_.refs_4_.refs_6_, ...), custom_call_target="tpu_custom_call" | custom-call | flops 368000000 | bytes 1 | tf_op jit(solution)/shard_map/attention_back/pallas_call | solution.py:766
  520.9 12.2 %project_back.2 = (f32[4,1536]{1,0:T(4,128)}, f32[2,1152]{1,0:T(2,128)}, bf16[304,1536]{1,0:T(8,128)(2,1)}, bf16[304,1536]{1,0:T(8,128)(2,1)}, bf16[304,1536]{1,...) custom-call(bf16[1024,1152]{1,0:T(8,128)(2,1)} %get-tuple-element.406.refs_0_, ...), custom_call_target="tpu_custom_call" | custom-call | flops 138000000 | bytes 1 | tf_op jit(solution)/shard_map/project_back/pallas_call | solution.py:919
  540.1 8.7 %outer_sums.6 = bf16[2,1536,384]{2,1,0:T(8,128)(2,1)} custom-call(bf16[1024,1536]{1,0:T(8,128)(2,1)} %get-tuple-element.431.refs_0_, bf16[1024,384]{1,0:T(8,128)(2,1)} %get-tuple-element.262.refs_0_.refs_7_.refs_1_, bf16[192,1536]{1,0:T(8,128)(2,1)} %get-tuple-element.432.refs_2_, bf16[192,384]{1,0:T(8,128)(2,1)} %get-tuple-element.263.refs_1_.refs_8_.refs_3_, ...), custom_call_target="tpu_custom_call" | custom-call | flops 207000000 | bytes 1 | tf_op jit(solution)/shard_map/outer_sums/pallas_call | solution.py:919
  553.0 32.1 %attention_back.3 = (bf16[1024,1152]{1,0:T(8,128)(2,1)}, bf16[192,1152]{1,0:T(8,128)(2,1)}) custom-call(f32[1216,128]{1,0:T(8,128)} %broadcast_in_dim.133.bias_ref.refs_0_, bf16[1024,1152]{1,0:T(8,128)(2,1)} %get-tuple-element.278.qi.ki.vi.refs_1_.refs_3_.refs_5_, bf16[192,1152]{1,0:T(8,128)(2,1)} %get-tuple-element.279.qt.kt.vt.refs_2_.refs_4_.refs_6_, ...), custom_call_target="tpu_custom_call" | custom-call | flops 368000000 | bytes 1 | tf_op jit(solution)/shard_map/attention_back/pallas_call | solution.py:766
  588.3 14.7 %outer_sums.7 = bf16[2,1152,1536]{2,1,0:T(8,128)(2,1)} custom-call(bf16[1024,1152]{1,0:T(8,128)(2,1)} %get-tuple-element.406.refs_0_, bf16[1024,1536]{1,0:T(8,128)(2,1)} %get-tuple-element.445.refs_1_, bf16[192,1152]{1,0:T(8,128)(2,1)} %get-tuple-element.407.refs_1_.refs_2_, bf16[192,1536]{1,0:T(8,128)(2,1)} %get-tuple-element.446.refs_3_, ...), custom_call_target="tpu_custom_call" | custom-call | flops 207000000 | bytes 1 | tf_op jit(solution)/shard_map/outer_sums/pallas_call | solution.py:919
  610.8 9.1 %collective-permute-done.69.refs_4_ = bf16[304,768]{1,0:T(8,128)(2,1)S(1)} collective-permute-done((bf16[304,768]{1,0:T(8,128)(2,1)}, bf16[304,768]{1,0:T(8,128)(2,1)S(1)}, u32[]{:S(2)}, u32[]{:S(2)}) %collective-permute-start.69) | collective-permute-done | bytes 466976 | tf_op jit(solution)/shard_map/ppermute | solution.py:799
  621.9 8.1 %collective-permute-done.73.refs_9_ = bf16[304,768]{1,0:T(8,128)(2,1)S(1)} collective-permute-done((bf16[304,768]{1,0:T(8,128)(2,1)S(1)}, bf16[304,768]{1,0:T(8,128)(2,1)S(1)}, u32[]{:S(2)}, u32[]{:S(2)}) %collective-permute-start.73) | collective-permute-done | bytes 466976 | tf_op jit(solution)/shard_map/ppermute | solution.py:799
  640.3 15.7 %collective-permute-done.74.refs_1_ = bf16[304,1536]{1,0:T(8,128)(2,1)S(1)} collective-permute-done((bf16[304,1536]{1,0:T(8,128)(2,1)}, bf16[304,1536]{1,0:T(8,128)(2,1)S(1)}, u32[]{:S(2)}, u32[]{:S(2)}) %collective-permute-start.74) | collective-permute-done | bytes 933920 | tf_op jit(solution)/shard_map/ppermute | solution.py:799
  673.0 12.1 %project_back.3 = (f32[4,1536]{1,0:T(4,128)}, f32[2,1152]{1,0:T(2,128)}, bf16[304,1536]{1,0:T(8,128)(2,1)}, bf16[304,1536]{1,0:T(8,128)(2,1)}, bf16[304,1536]{1,...) custom-call(bf16[1024,1152]{1,0:T(8,128)(2,1)} %get-tuple-element.452.refs_4_.refs_0_, ...), custom_call_target="tpu_custom_call" | custom-call | flops 138000000 | bytes 1 | tf_op jit(solution)/shard_map/project_back/pallas_call | solution.py:919
  689.7 7.8 result.1
  718.1 7.5 all-to-all-start.2
  729.6 9.5 %input_back.1 = (f32[2,256,1536]{2,1,0:T(8,128)}, f32[2,40,1536]{2,1,0:T(8,128)}) custom-call(bf16[304,1536]{1,0:T(8,128)(2,1)} %get-tuple-element.416.refs_0_, bf16[304,1536]{1,0:T(8,128)(2,1)} %copy-done.8, bf16[304,1536]{1,0:T(8,128)(2,1)} %collective-permute-done.75.refs_2_, bf16[304,768]{1,0:T(8,128)(2,1)} %collective-permute-done.76.refs_3_, ...), custom_call_target="tpu_custom_call" | custom-call | flops 103500000 | bytes 1 | tf_op jit(solution)/shard_map/input_back/pallas_call | solution.py:919
  (535 shorter events, 319.0 us)
Async XLA Ops:
  7.2 129.3 %all-gather.5.cloned.1.call-start = ((), (), s32[]{:S(2)}) async-start(), calls=%async_computation.8 | async-start | bytes 7962624 | tf_op jit(solution)/shard_map/all_gather | solution.py:1584
  30.3 138.3 %all-gather.7.cloned.1.call-start = ((), (), s32[]{:S(2)}) async-start(), calls=%async_computation.9 | async-start | bytes 2654208 | tf_op jit(solution)/shard_map/all_gather | solution.py:1584
  77.3 213.1 %all-gather.9.cloned.1.call-start = ((), (), s32[]{:S(2)}) async-start(), calls=%async_computation.10 | async-start | bytes 10616832 | tf_op jit(solution)/shard_map/all_gather | solution.py:1584
  78.1 276.2 %all-gather.11.cloned.1.call-start = ((), (), s32[]{:S(2)}) async-start(), calls=%async_computation.11 | async-start | bytes 10616832 | tf_op jit(solution)/shard_map/all_gather | solution.py:1584
  78.6 401.6 %reduce-scatter.5.cloned.1.call-start = ((), (), s32[]{:S(2)}) async-start(), calls=%async_computation.12 | async-start | bytes 10616832 | tf_op jit(solution)/shard_map/reduce_scatter | solution.py:1606
  89.5 32.9 %collective-permute-start.7 = (bf16[2,304,768]{2,1,0:T(8,128)(2,1)}, bf16[2,304,768]{2,1,0:T(8,128)(2,1)}, u32[]{:S(2)}, u32[]{:S(2)}) collective-permute-start(bf16[2,304,768]{2,1,0:T(8,128)(2,1)} %copy-done.4), channel_id=1, source_target_pairs={{0,2},{1,3},{2,0},{3,1},{4,6},{5,7},{6,4},{7,5},{8,10},{9,11},{10,... | collective-permute-start | bytes 2801672 | tf_op jit(solution)/shard_map/ppermute | solution.py:799
  90.2 32.2 %collective-permute-start.8 = (bf16[2,304,768]{2,1,0:T(8,128)(2,1)}, bf16[2,304,768]{2,1,0:T(8,128)(2,1)}, u32[]{:S(2)}, u32[]{:S(2)}) collective-permute-start(bf16[2,304,768]{2,1,0:T(8,128)(2,1)} %copy-done.5), channel_id=1, source_target_pairs={{0,1},{1,0},{2,3},{3,2},{4,5},{5,4},{6,7},{7,6},{8,9},{9,8},{10,11... | collective-permute-start | bytes 2801672 | tf_op jit(solution)/shard_map/ppermute | solution.py:799
  128.8 39.6 %collective-permute-start.19 = (bf16[2,304,768]{2,1,0:T(8,128)(2,1)}, bf16[2,304,768]{2,1,0:T(8,128)(2,1)}, u32[]{:S(2)}, u32[]{:S(2)}) collective-permute-start(bf16[2,304,768]{2,1,0:T(8,128)(2,1)} %get-tuple-element.260.refs_8_.refs_5_.refs_10_), channel_id=1, source_target_pairs={{0,2},{1,3},{2,0},{3,1},{4,6},{5,7},{6,4},{7,5},{8,10},{9,11},{10,... | collective-permute-start | bytes 2801672 | tf_op jit(solution)/shard_map/ppermute | solution.py:799
  129.3 39.2 %collective-permute-start.17 = (bf16[2,304,768]{2,1,0:T(8,128)(2,1)}, bf16[2,304,768]{2,1,0:T(8,128)(2,1)}, u32[]{:S(2)}, u32[]{:S(2)}) collective-permute-start(bf16[2,304,768]{2,1,0:T(8,128)(2,1)} %get-tuple-element.260.refs_8_.refs_5_.refs_10_), channel_id=1, source_target_pairs={{0,1},{1,0},{2,3},{3,2},{4,5},{5,4},{6,7},{7,6},{8,9},{9,8},{10,11... | collective-permute-start | bytes 2801672 | tf_op jit(solution)/shard_map/ppermute | solution.py:799
  130.8 37.6 %collective-permute-start.20 = (bf16[2,304,768]{2,1,0:T(8,128)(2,1)S(1)}, bf16[2,304,768]{2,1,0:T(8,128)(2,1)}, u32[]{:S(2)}, u32[]{:S(2)}) collective-permute-start(bf16[2,304,768]{2,1,0:T(8,128)(2,1)S(1)} %copy-done.3), channel_id=1, source_target_pairs={{0,2},{1,3},{2,0},{3,1},{4,6},{5,7},{6,4},{7,5},{8,10},{9,11},{10,... | collective-permute-start | bytes 2801672 | tf_op jit(solution)/shard_map/ppermute | solution.py:799
  132.1 36.3 %collective-permute-start.18 = (bf16[2,304,768]{2,1,0:T(8,128)(2,1)S(1)}, bf16[2,304,768]{2,1,0:T(8,128)(2,1)}, u32[]{:S(2)}, u32[]{:S(2)}) collective-permute-start(bf16[2,304,768]{2,1,0:T(8,128)(2,1)S(1)} %copy-done.3), channel_id=1, source_target_pairs={{0,1},{1,0},{2,3},{3,2},{4,5},{5,4},{6,7},{7,6},{8,9},{9,8},{10,11... | collective-permute-start | bytes 2801672 | tf_op jit(solution)/shard_map/ppermute | solution.py:799
  173.7 35.4 %collective-permute-start.24 = (bf16[304,1536]{1,0:T(8,128)(2,1)}, bf16[304,1536]{1,0:T(8,128)(2,1)S(1)}, u32[]{:S(2)}, u32[]{:S(2)}) collective-permute-start(bf16[304,1536]{1,0:T(8,128)(2,1)} %get-tuple-element.266), channel_id=1, source_target_pairs={{0,1},{1,0},{2,3},{3,2},{4,5},{5,4},{6,7},{7,6},{8,9},{9,8},{10,11... | collective-permute-start | bytes 2801672 | tf_op jit(solution)/shard_map/ppermute | solution.py:799
  174.7 34.4 %collective-permute-start.25 = (bf16[304,1536]{1,0:T(8,128)(2,1)}, bf16[304,1536]{1,0:T(8,128)(2,1)S(1)}, u32[]{:S(2)}, u32[]{:S(2)}) collective-permute-start(bf16[304,1536]{1,0:T(8,128)(2,1)} %get-tuple-element.267), channel_id=1, source_target_pairs={{0,2},{1,3},{2,0},{3,1},{4,6},{5,7},{6,4},{7,5},{8,10},{9,11},{10,... | collective-permute-start | bytes 2801672 | tf_op jit(solution)/shard_map/ppermute | solution.py:799
  175.4 41.7 %collective-permute-start.34 = (bf16[2,304,768]{2,1,0:T(8,128)(2,1)}, bf16[2,304,768]{2,1,0:T(8,128)(2,1)S(1)}, u32[]{:S(2)}, u32[]{:S(2)}) collective-permute-start(bf16[2,304,768]{2,1,0:T(8,128)(2,1)} %collective-permute-done.17.refs_10_), channel_id=1, source_target_pairs={{0,2},{1,3},{2,0},{3,1},{4,6},{5,7},{6,4},{7,5},{8,10},{9,11},{10,... | collective-permute-start | bytes 2801672 | tf_op jit(solution)/shard_map/ppermute | solution.py:799
  176.7 40.4 %collective-permute-start.35 = (bf16[2,304,768]{2,1,0:T(8,128)(2,1)}, bf16[2,304,768]{2,1,0:T(8,128)(2,1)}, u32[]{:S(2)}, u32[]{:S(2)}) collective-permute-start(bf16[2,304,768]{2,1,0:T(8,128)(2,1)} %collective-permute-done.20.refs_13_), channel_id=1, source_target_pairs={{0,1},{1,0},{2,3},{3,2},{4,5},{5,4},{6,7},{7,6},{8,9},{9,8},{10,11... | collective-permute-start | bytes 2801672 | tf_op jit(solution)/shard_map/ppermute | solution.py:799
  258.9 30.0 %collective-permute-start.32 = (bf16[304,768]{1,0:T(8,128)(2,1)S(1)}, bf16[304,768]{1,0:T(8,128)(2,1)S(1)}, u32[]{:S(2)}, u32[]{:S(2)}) collective-permute-start(bf16[304,768]{1,0:T(8,128)(2,1)S(1)} %collective-permute-done.28.refs_2_), channel_id=1, source_target_pairs={{0,2},{1,3},{2,0},{3,1},{4,6},{5,7},{6,4},{7,5},{8,10},{9,11},{10,... | collective-permute-start | bytes 1400840 | tf_op jit(solution)/shard_map/ppermute | solution.py:799
  275.9 31.7 %collective-permute-start.42 = (bf16[304,768]{1,0:T(8,128)(2,1)}, bf16[304,768]{1,0:T(8,128)(2,1)}, u32[]{:S(2)}, u32[]{:S(2)}) collective-permute-start(bf16[304,768]{1,0:T(8,128)(2,1)} %get-tuple-element.305.refs_0_), channel_id=1, source_target_pairs={{0,2},{1,3},{2,0},{3,1},{4,6},{5,7},{6,4},{7,5},{8,10},{9,11},{10,... | collective-permute-start | bytes 1400840 | tf_op jit(solution)/shard_map/ppermute | solution.py:799
  354.0 234.4 %reduce-scatter.7.cloned.1.call-start = ((), (), s32[]{:S(2)}) async-start(), calls=%async_computation.13 | async-start | bytes 10616832 | tf_op jit(solution)/shard_map/reduce_scatter | solution.py:1606
  418.8 44.3 %collective-permute-start.54 = (bf16[304,768]{1,0:T(8,128)(2,1)}, bf16[304,768]{1,0:T(8,128)(2,1)}, u32[]{:S(2)}, u32[]{:S(2)}) collective-permute-start(bf16[304,768]{1,0:T(8,128)(2,1)} %get-tuple-element.396.refs_0_), channel_id=1, source_target_pairs={{0,1},{1,0},{2,3},{3,2},{4,5},{5,4},{6,7},{7,6},{8,9},{9,8},{10,11... | collective-permute-start | bytes 1400840 | tf_op jit(solution)/shard_map/ppermute | solution.py:799
  420.0 43.0 %collective-permute-start.57 = (bf16[304,768]{1,0:T(8,128)(2,1)}, bf16[304,768]{1,0:T(8,128)(2,1)}, u32[]{:S(2)}, u32[]{:S(2)}) collective-permute-start(bf16[304,768]{1,0:T(8,128)(2,1)} %get-tuple-element.397.refs_1_), channel_id=1, source_target_pairs={{0,2},{1,3},{2,0},{3,1},{4,6},{5,7},{6,4},{7,5},{8,10},{9,11},{10,... | collective-permute-start | bytes 1400840 | tf_op jit(solution)/shard_map/ppermute | solution.py:799
  470.5 136.2 %reduce-scatter.9.cloned.1.call-start = ((), (), s32[]{:S(2)}) async-start(), calls=%async_computation.14 | async-start | bytes 2654208 | tf_op jit(solution)/shard_map/reduce_scatter | solution.py:1606
  472.0 47.3 %collective-permute-start.60 = (bf16[304,768]{1,0:T(8,128)(2,1)S(1)}, bf16[304,768]{1,0:T(8,128)(2,1)S(1)}, u32[]{:S(2)}, u32[]{:S(2)}) collective-permute-start(bf16[304,768]{1,0:T(8,128)(2,1)S(1)} %copy-done.22), channel_id=1, source_target_pairs={{0,2},{1,3},{2,0},{3,1},{4,6},{5,7},{6,4},{7,5},{8,10},{9,11},{10,... | collective-permute-start | bytes 1400840 | tf_op jit(solution)/shard_map/ppermute | solution.py:799
  473.5 45.8 %collective-permute-start.58 = (bf16[304,768]{1,0:T(8,128)(2,1)S(1)}, bf16[304,768]{1,0:T(8,128)(2,1)}, u32[]{:S(2)}, u32[]{:S(2)}) collective-permute-start(bf16[304,768]{1,0:T(8,128)(2,1)S(1)} %copy-done.22), channel_id=1, source_target_pairs={{0,1},{1,0},{2,3},{3,2},{4,5},{5,4},{6,7},{7,6},{8,9},{9,8},{10,11... | collective-permute-start | bytes 1400840 | tf_op jit(solution)/shard_map/ppermute | solution.py:799
  474.7 44.6 %collective-permute-start.61 = (bf16[304,768]{1,0:T(8,128)(2,1)S(1)}, bf16[304,768]{1,0:T(8,128)(2,1)}, u32[]{:S(2)}, u32[]{:S(2)}) collective-permute-start(bf16[304,768]{1,0:T(8,128)(2,1)S(1)} %copy-done.23), channel_id=1, source_target_pairs={{0,2},{1,3},{2,0},{3,1},{4,6},{5,7},{6,4},{7,5},{8,10},{9,11},{10,... | collective-permute-start | bytes 1400840 | tf_op jit(solution)/shard_map/ppermute | solution.py:799
  479.4 39.9 %collective-permute-start.59 = (bf16[304,768]{1,0:T(8,128)(2,1)S(1)}, bf16[304,768]{1,0:T(8,128)(2,1)}, u32[]{:S(2)}, u32[]{:S(2)}) collective-permute-start(bf16[304,768]{1,0:T(8,128)(2,1)S(1)} %copy-done.23), channel_id=1, source_target_pairs={{0,1},{1,0},{2,3},{3,2},{4,5},{5,4},{6,7},{7,6},{8,9},{9,8},{10,11... | collective-permute-start | bytes 1400840 | tf_op jit(solution)/shard_map/ppermute | solution.py:799
  548.8 190.3 %reduce-scatter.11.cloned.1.call-start = ((), (), s32[]{:S(2)}) async-start(), calls=%async_computation.15 | async-start | bytes 7962624 | tf_op jit(solution)/shard_map/reduce_scatter | solution.py:1606
  548.9 36.2 %collective-permute-start.70 = (bf16[304,1536]{1,0:T(8,128)(2,1)}, bf16[304,1536]{1,0:T(8,128)(2,1)S(1)}, u32[]{:S(2)}, u32[]{:S(2)}) collective-permute-start(bf16[304,1536]{1,0:T(8,128)(2,1)} %get-tuple-element.441), channel_id=1, source_target_pairs={{0,1},{1,0},{2,3},{3,2},{4,5},{5,4},{6,7},{7,6},{8,9},{9,8},{10,11... | collective-permute-start | bytes 2801672 | tf_op jit(solution)/shard_map/ppermute | solution.py:799
  550.7 34.4 %collective-permute-start.71 = (bf16[304,1536]{1,0:T(8,128)(2,1)}, bf16[304,1536]{1,0:T(8,128)(2,1)S(1)}, u32[]{:S(2)}, u32[]{:S(2)}) collective-permute-start(bf16[304,1536]{1,0:T(8,128)(2,1)} %get-tuple-element.442), channel_id=1, source_target_pairs={{0,2},{1,3},{2,0},{3,1},{4,6},{5,7},{6,4},{7,5},{8,10},{9,11},{10,... | collective-permute-start | bytes 2801672 | tf_op jit(solution)/shard_map/ppermute | solution.py:799
  551.5 33.6 %collective-permute-start.66 = (bf16[304,1536]{1,0:T(8,128)(2,1)}, bf16[304,1536]{1,0:T(8,128)(2,1)S(1)}, u32[]{:S(2)}, u32[]{:S(2)}) collective-permute-start(bf16[304,1536]{1,0:T(8,128)(2,1)} %get-tuple-element.412), channel_id=1, source_target_pairs={{0,1},{1,0},{2,3},{3,2},{4,5},{5,4},{6,7},{7,6},{8,9},{9,8},{10,11... | collective-permute-start | bytes 2801672 | tf_op jit(solution)/shard_map/ppermute | solution.py:799
  552.5 32.6 %collective-permute-start.67 = (bf16[304,1536]{1,0:T(8,128)(2,1)}, bf16[304,1536]{1,0:T(8,128)(2,1)S(1)}, u32[]{:S(2)}, u32[]{:S(2)}) collective-permute-start(bf16[304,1536]{1,0:T(8,128)(2,1)} %get-tuple-element.413), channel_id=1, source_target_pairs={{0,2},{1,3},{2,0},{3,1},{4,6},{5,7},{6,4},{7,5},{8,10},{9,11},{10,... | collective-permute-start | bytes 2801672 | tf_op jit(solution)/shard_map/ppermute | solution.py:799
  657.1 72.5 %collective-permute-start.77 = (bf16[304,768]{1,0:T(8,128)(2,1)}, bf16[304,768]{1,0:T(8,128)(2,1)}, u32[]{:S(2)}, u32[]{:S(2)}) collective-permute-start(bf16[304,768]{1,0:T(8,128)(2,1)} %add_convert_fusion.2), channel_id=1, source_target_pairs={{0,2},{1,3},{2,0},{3,1},{4,6},{5,7},{6,4},{7,5},{8,10},{9,11},{10,... | collective-permute-start | bytes 1400840 | tf_op jit(solution)/shard_map/ppermute | solution.py:799
  664.3 65.3 %collective-permute-start.76 = (bf16[304,768]{1,0:T(8,128)(2,1)}, bf16[304,768]{1,0:T(8,128)(2,1)}, u32[]{:S(2)}, u32[]{:S(2)}) collective-permute-start(bf16[304,768]{1,0:T(8,128)(2,1)} %add_convert_fusion.3), channel_id=1, source_target_pairs={{0,1},{1,0},{2,3},{3,2},{4,5},{5,4},{6,7},{7,6},{8,9},{9,8},{10,11... | collective-permute-start | bytes 1400840 | tf_op jit(solution)/shard_map/ppermute | solution.py:799
  (152 other events, 2450.8 us)
Sparse Core Ops, SparseCore 0:
  30.4 77.3 all-gather.4
  109.9 30.8 all-gather.6
  142.4 89.1 all-gather.8
  233.1 89.1 all-gather.10
  354.1 101.4 reduce-scatter.4
  470.7 101.8 reduce-scatter.6
  575.5 31.1 reduce-scatter.8
  609.0 79.9 reduce-scatter.10

commit v7 on v6

--- a/solution.py
+++ b/solution.py
@@ -1824,12 +1824,13 @@
         *firsts[0][:2], *attendeds[0], *logs[0], *grad0, key_bias[0], head
     )
     projs.append(gather_far(*backs[1][1:3], after(proj_near1, qkv_grad0)))
+    mlp_halves = (mlp_halves[:5], mlp_halves[5:])
+    mlp_first = [scatter_first(after(mlp_halves[0], grad0))]
     sums0, columns0, halves0 = project_back(
-        qkv_grad0, qkv_part, tokens_all, 0, image_count
+        after(qkv_grad0, mlp_first), qkv_part, tokens_all, 0, image_count
     )
     grad1, proj1 = attended_back(after(projs[1], halves0), out_part, image_count)
-    mlp_halves = (mlp_halves[:5], mlp_halves[5:])
-    mlp_first = [scatter_first(after(halves, projs[1])) for halves in mlp_halves]
+    mlp_first.append(scatter_first(after(mlp_halves[1], projs[1])))
     out_sum = outer_sums([proj0, proj1], attendeds, 256)
     out_came = scatter_rows_over_batch(out_sum)
     grad1 = after(grad1, out_sum)
@@ -1845,18 +1846,19 @@
         for halves, first, added in zip(mlp_halves, mlp_first, mlp_added)
         for piece in scatter_sent(halves, first, added)
     ]
-    norm1_first = scatter_first(after(halves0, mlp_pieces))
     qkv_sum = outer_sums(
         [qkv_grad0, after(qkv_grad1, mlp_added, up_came)],
         [first[2:] for first in firsts],
         128 if qkv_width % 256 else 256,
     )
     qkv_came = scatter_rows_over_batch(after(qkv_sum, out_came))
-    out_home = swap(out_came.reshape(2, S, out_columns, own_width).swapaxes(0, 1), "seq")
     sums1, columns1, halves1 = project_back(
-        after(qkv_grad1, qkv_sum, mlp_pieces, out_home), qkv_part, tokens_all, 1, image_count
-    )
-    norm1_pieces = [scatter_last(halves0, norm1_first), scatter_halves(halves1)]
+        after(qkv_grad1, qkv_sum), qkv_part, tokens_all, 1, image_count
+    )
+    norm1_pieces = [
+        scatter_halves(after(halves0, qkv_sum)),
+        scatter_halves(after(halves1, mlp_pieces)),
+    ]
     image_out, text_out, result_sums = result_step(
         after(mlp_pieces, halves1),
         cotangents,
@@ -1866,10 +1868,18 @@
         image_count,
     )
     image_grad, text_grad = input_back(
-        norm1_pieces, tokens, [back[0] for back in backs], modulation, image_count, live_text
+        after(norm1_pieces, qkv_came),
+        tokens,
+        [back[0] for back in backs],
+        modulation,
+        image_count,
+        live_text,
+    )
+    out_home = swap(
+        after(out_came, image_grad).reshape(2, S, out_columns, own_width).swapaxes(0, 1), "seq"
     )
     qkv_home = move_units(
-        after(qkv_came, image_grad).reshape(2, per_device, unit, D).swapaxes(0, 1),
+        qkv_came.reshape(2, per_device, unit, D).swapaxes(0, 1),
         back_perms, land, send, place
     )
     qkv_weight_grad = qkv_home.swapaxes(0, 1).reshape(2, -1, D).swapaxes(1, 2).astype(F32)
@@ -1937,7 +1947,7 @@
     )
     mod_bias_grad = jnp.sum(mod_mine.astype(F32), axis=1)
     smooth_part = jnp.einsum("tsf,tdf->sd", mod_mine, mod_weight, preferred_element_type=F32)
-    smooth_grad = jnp.sum(swap(after(smooth_part, norm1_pieces[1]).reshape(B, L, D), "batch"), axis=0)
+    smooth_grad = jnp.sum(swap(smooth_part.reshape(B, L, D), "batch"), axis=0)
     smooth_grad = after(smooth_grad, qkv_home)
     smooth_grad = smooth_grad + flip(smooth_grad, 1)
     smooth_grad = smooth_grad + flip(smooth_grad, 2)

time: 788 us -> 775 us (0.984)
  waiting for transfers between devices: 189 us -> 160 us
  starting transfers between devices: 126 us -> 134 us
    all_to_all x4, waiting for transfers between devices: 11.6 us -> 0.01 us  [swap(): return lax.all_to_all(values, axis, 0, 0, tiled=True)]
    ppermute x73, waiting for transfers between devices: 134 us -> 126 us  [flip(): return lax.ppermute(values, 'seq', [(i, i ^ bit) for i in range(4)])]
  transfers between devices with their start and end apart: 99 -> 99, of which waited for: 38 -> 30; matrix products, arithmetic and copies ran while one was open for 9% -> 10% of each run, Pallas kernels for 47% -> 47%
where the time goes in v7:
time: 775 us; the launch traced here: 770 us
  Pallas kernels  365 us (47%)
  waiting for transfers between devices  160 us (21%)
  starting transfers between devices  134 us (17%)
  local copies, waits for them, and re-layouts  47.8 us (6%)
  other arithmetic  36.9 us (5%)
  between operations  22 us (3%)
    pallas_call x23, Pallas kernels, run(): pl.pallas_call(kernel, in_specs=specs, out_specs=out_specs, out_shape=[ja...  266 us
    ppermute x73, waiting for transfers between devices, flip(): return lax.ppermute(values, 'seq', [(i, i ^ bit) for i in range(4)])  126 us
    ppermute x73, starting transfers between devices, flip(): return lax.ppermute(values, 'seq', [(i, i ^ bit) for i in range(4)])  86.1 us
    pallas_call x2, Pallas kernels, attention_back(): pl.pallas_call(functools.partial(attention_back_kernel, 512, LOG2E / math...  64.5 us
    pallas_call x2, Pallas kernels, attention(): pl.pallas_call(functools.partial(attention_kernel, 256, LOG2E / math.sqrt...  35 us
    ppermute x8, waiting for transfers between devices, gather_small(): held = jnp.concatenate([held, lax.ppermute(held, axis, pairs)])  33 us
    all_to_all x4, starting transfers between devices, swap(): return lax.all_to_all(values, axis, 0, 0, tiled=True)  21.7 us
    ppermute x6, starting transfers between devices, move_units(): lax.ppermute(lax.dynamic_index_in_dim(units, slot, 0, keepdims=True), ('b...  16.7 us
  transfers between devices with their start and end apart: 99, of which 30 were waited for; matrix products, arithmetic and copies ran while one was open for 10% of the time, Pallas kernels for 47%

profile of v7, /device:TPU:16, one launch (start us, length us, event | category | flops | bytes accessed | tf_op | source)
XLA Modules:
  0.0 769.5 jit_solution(4010928104905543945)
XLA Ops:
  44.0 14.8 %collective-permute-done.3.refs_2_.refs_5_ = bf16[2,304,768]{2,1,0:T(8,128)(2,1)S(1)} collective-permute-done((bf16[2,304,768]{2,1,0:T(8,128)(2,1)S(1)}, bf16[2,304,768]{2,1,0:T(8,128)(2,1)S(1)}, u32[]{:S(2)}, u32[]{:S(2)}) %collective-permute-start.3) | collective-permute-done | bytes 933920 | tf_op jit(solution)/shard_map/ppermute | solution.py:799
  91.7 8.5 %collective-permute-done.13 = f32[2,2,16,288]{3,2,1,0:T(8,128)S(1)} collective-permute-done((f32[2,2,16,288]{3,2,1,0:T(8,128)S(1)}, f32[2,2,16,288]{3,2,1,0:T(8,128)S(1)}, u32[]{:S(2)}, u32[]{:S(2)}) %collective-permute-start.13) | collective-permute-done | bytes 73760 | tf_op jit(solution)/shard_map/ppermute | solution.py:1599
  115.7 6.7 collective-permute-done.15
  136.5 13.0 %project.2 = (bf16[1024,1152]{1,0:T(8,128)(2,1)}, bf16[192,1152]{1,0:T(8,128)(2,1)}, bf16[1024,1536]{1,0:T(8,128)(2,1)}, bf16[192,1536]{1,0:T(8,128)(2,1)}) custom-call(bf16[2,304,768]{2,1,0:T(8,128)(2,1)} %copy-done.2, bf16[2,304,768]{2,1,0:T(8,128)(2,1)} %copy-done.1, bf16[2,304,768]{2,1,0:T(8,128)(2,1)} %copy-done.4, ...), custom_call_target="tpu_custom_call" | custom-call | flops 149500000 | bytes 1 | tf_op jit(solution)/shard_map/project/pallas_call | solution.py:919
  150.6 17.9 %attention.2 = (bf16[1024,384]{1,0:T(8,128)(2,1)}, bf16[192,384]{1,0:T(8,128)(2,1)}, f32[1024,384]{1,0:T(8,128)}, f32[192,384]{1,0:T(8,128)}) custom-call(f32[1216,128]{1,0:T(8,128)} %broadcast_in_dim.119.bias_ref.refs_0_, f32[1,1]{1,0:T(1,128)} %bitcast.6.floor_ref, bf16[1024,1152]{1,0:T(8,128)(2,1)} %get-tuple-element.275.qi.ki.vi.refs_1_.refs_3_.refs_5_, ...), custom_call_target="tpu_custom_call" | custom-call | flops 195500000 | bytes 1 | tf_op jit(solution)/shard_map/attention/pallas_call | solution.py:657
  177.8 13.1 %project.3 = (bf16[1024,1152]{1,0:T(8,128)(2,1)}, bf16[192,1152]{1,0:T(8,128)(2,1)}, bf16[1024,1536]{1,0:T(8,128)(2,1)}, bf16[192,1536]{1,0:T(8,128)(2,1)}) custom-call(bf16[2,304,768]{2,1,0:T(8,128)(2,1)} %copy-done.2, bf16[2,304,768]{2,1,0:T(8,128)(2,1)} %copy-done.1, bf16[2,304,768]{2,1,0:T(8,128)(2,1)} %copy-done.4, ...), custom_call_target="tpu_custom_call" | custom-call | flops 149500000 | bytes 1 | tf_op jit(solution)/shard_map/project/pallas_call | solution.py:919
  192.0 17.1 %attention.3 = (bf16[1024,384]{1,0:T(8,128)(2,1)}, bf16[192,384]{1,0:T(8,128)(2,1)}, f32[1024,384]{1,0:T(8,128)}, f32[192,384]{1,0:T(8,128)}) custom-call(f32[1216,128]{1,0:T(8,128)} %broadcast_in_dim.133.bias_ref.refs_0_, f32[1,1]{1,0:T(1,128)} %bitcast.38.floor_ref, bf16[1024,1152]{1,0:T(8,128)(2,1)} %get-tuple-element.297.qi.ki.vi.refs_1_.refs_3_.refs_5_, ...), custom_call_target="tpu_custom_call" | custom-call | flops 195500000 | bytes 1 | tf_op jit(solution)/shard_map/attention/pallas_call | solution.py:657
  234.8 12.8 %collective-permute-done.36.refs_1_ = bf16[304,1536]{1,0:T(8,128)(2,1)} collective-permute-done((bf16[304,1536]{1,0:T(8,128)(2,1)}, bf16[304,1536]{1,0:T(8,128)(2,1)}, u32[]{:S(2)}, u32[]{:S(2)}) %collective-permute-start.36) | collective-permute-done | bytes 933920 | tf_op jit(solution)/shard_map/ppermute | solution.py:799
  260.9 8.0 %collective-permute-done.39.refs_4_ = bf16[304,768]{1,0:T(8,128)(2,1)S(1)} collective-permute-done((bf16[304,768]{1,0:T(8,128)(2,1)S(1)}, bf16[304,768]{1,0:T(8,128)(2,1)S(1)}, u32[]{:S(2)}, u32[]{:S(2)}) %collective-permute-start.39) | collective-permute-done | bytes 466976 | tf_op jit(solution)/shard_map/ppermute | solution.py:799
  281.2 7.6 collective-permute-done.32.refs_6_
  290.4 17.2 %hidden.2 = (bf16[1024,1536]{1,0:T(8,128)(2,1)}, bf16[192,1536]{1,0:T(8,128)(2,1)}, bf16[1024,1536]{1,0:T(8,128)(2,1)}, bf16[192,1536]{1,0:T(8,128)(2,1)}, bf16[...) custom-call(bf16[304,768]{1,0:T(8,128)(2,1)} %get-tuple-element.303.r, ...), custom_call_target="tpu_custom_call" | custom-call | flops 207000000 | bytes 1 | tf_op jit(solution)/shard_map/hidden/pallas_call | solution.py:919
  319.3 16.7 %hidden.3 = (bf16[1024,1536]{1,0:T(8,128)(2,1)}, bf16[192,1536]{1,0:T(8,128)(2,1)}, bf16[1024,1536]{1,0:T(8,128)(2,1)}, bf16[192,1536]{1,0:T(8,128)(2,1)}, bf16[...) custom-call(bf16[304,768]{1,0:T(8,128)(2,1)} %get-tuple-element.324.r, ...), custom_call_target="tpu_custom_call" | custom-call | flops 207000000 | bytes 1 | tf_op jit(solution)/shard_map/hidden/pallas_call | solution.py:919
  335.9 18.0 %outer_sums.4 = bf16[2,1536,1536]{2,1,0:T(8,128)(2,1)} custom-call(bf16[1024,1536]{1,0:T(8,128)(2,1)} %get-tuple-element.370.refs_0_, bf16[1024,1536]{1,0:T(8,128)(2,1)} %get-tuple-element.340.refs_1_.refs_0_, bf16[192,1536]{1,0:T(8,128)(2,1)} %get-tuple-element.371.refs_2_.refs_1_, bf16[192,1536]{1,0:T(8,128)(2,1)} %get-tuple-element.341.refs_3_.refs_1_, ...), custom_call_target="tpu_custom_call" | custom-call | flops 207000000 | bytes 1 | tf_op jit(solution)/shard_map/outer_sums/pallas_call | solution.py:919
  354.3 18.1 %hidden_back.2 = (bf16[1024,1536]{1,0:T(8,128)(2,1)}, bf16[192,1536]{1,0:T(8,128)(2,1)}, f32[2,1536]{1,0:T(2,128)}, bf16[304,1536]{1,0:T(8,128)(2,1)}, bf16[304,...) custom-call(bf16[1024,1536]{1,0:T(8,128)(2,1)} %get-tuple-element.340.refs_1_, ...), custom_call_target="tpu_custom_call" | custom-call | flops 230000000 | bytes 1 | tf_op jit(solution)/shard_map/hidden_back/pallas_call | solution.py:919
  374.3 18.7 %hidden_back.3 = (bf16[1024,1536]{1,0:T(8,128)(2,1)}, bf16[192,1536]{1,0:T(8,128)(2,1)}, f32[2,1536]{1,0:T(2,128)}, bf16[304,1536]{1,0:T(8,128)(2,1)}, bf16[304,...) custom-call(bf16[1024,1536]{1,0:T(8,128)(2,1)} %get-tuple-element.348.refs_5_, ...), custom_call_target="tpu_custom_call" | custom-call | flops 230000000 | bytes 1 | tf_op jit(solution)/shard_map/hidden_back/pallas_call | solution.py:919
  395.6 11.4 %collective-permute-done.49.refs_4_ = bf16[304,768]{1,0:T(8,128)(2,1)S(1)} collective-permute-done((bf16[304,768]{1,0:T(8,128)(2,1)S(1)}, bf16[304,768]{1,0:T(8,128)(2,1)S(1)}, u32[]{:S(2)}, u32[]{:S(2)}) %collective-permute-start.49) | collective-permute-done | bytes 466976 | tf_op jit(solution)/shard_map/ppermute | solution.py:799
  409.8 7.5 middle_back.2
  420.6 17.7 %partial_sums.5 = (bf16[304,1536]{1,0:T(8,128)(2,1)}, bf16[304,1536]{1,0:T(8,128)(2,1)}, bf16[304,1536]{1,0:T(8,128)(2,1)}, bf16[304,768]{1,0:T(8,128)(2,1)}, bf...) custom-call(bf16[1024,1536]{1,0:T(8,128)(2,1)} %get-tuple-element.37, ...), custom_call_target="tpu_custom_call" | custom-call | flops 57500000 | bytes 1 | tf_op jit(solution)/shard_map/partial_sums/pallas_call | solution.py:919
  444.6 18.4 %outer_sums.5 = bf16[2,1536,1536]{2,1,0:T(8,128)(2,1)} custom-call(bf16[1024,1536]{1,0:T(8,128)(2,1)} %get-tuple-element.388.refs_0_, bf16[1024,1536]{1,0:T(8,128)(2,1)} %get-tuple-element.330.refs_1_, bf16[192,1536]{1,0:T(8,128)(2,1)} %get-tuple-element.389.refs_2_, bf16[192,1536]{1,0:T(8,128)(2,1)} %get-tuple-element.331.refs_3_, ...), custom_call_target="tpu_custom_call" | custom-call | flops 207000000 | bytes 1 | tf_op jit(solution)/shard_map/outer_sums/pallas_call | solution.py:919
  463.1 7.4 middle_back.3
  473.5 11.0 %collective-permute-done.54.refs_6_ = bf16[304,768]{1,0:T(8,128)(2,1)S(1)} collective-permute-done((bf16[304,768]{1,0:T(8,128)(2,1)}, bf16[304,768]{1,0:T(8,128)(2,1)S(1)}, u32[]{:S(2)}, u32[]{:S(2)}) %collective-permute-start.54) | collective-permute-done | bytes 466976 | tf_op jit(solution)/shard_map/ppermute | solution.py:799
  485.9 6.3 attended_back.2
  496.9 32.3 %attention_back.2 = (bf16[1024,1152]{1,0:T(8,128)(2,1)}, bf16[192,1152]{1,0:T(8,128)(2,1)}) custom-call(f32[1216,128]{1,0:T(8,128)} %broadcast_in_dim.119.bias_ref.refs_0_, bf16[1024,1152]{1,0:T(8,128)(2,1)} %get-tuple-element.275.qi.ki.vi.refs_1_.refs_3_.refs_5_, bf16[192,1152]{1,0:T(8,128)(2,1)} %get-tuple-element.276.qt.kt.vt.refs_2_.refs_4_.refs_6_, ...), custom_call_target="tpu_custom_call" | custom-call | flops 368000000 | bytes 1 | tf_op jit(solution)/shard_map/attention_back/pallas_call | solution.py:766
  532.2 12.9 %project_back.2 = (f32[4,1536]{1,0:T(4,128)}, f32[2,1152]{1,0:T(2,128)}, bf16[304,1536]{1,0:T(8,128)(2,1)}, bf16[304,1536]{1,0:T(8,128)(2,1)}, bf16[304,1536]{1,...) custom-call(bf16[1024,1152]{1,0:T(8,128)(2,1)} %get-tuple-element.435.refs_0_, ...), custom_call_target="tpu_custom_call" | custom-call | flops 138000000 | bytes 1 | tf_op jit(solution)/shard_map/project_back/pallas_call | solution.py:919
  552.1 8.8 %outer_sums.6 = bf16[2,1536,384]{2,1,0:T(8,128)(2,1)} custom-call(bf16[1024,1536]{1,0:T(8,128)(2,1)} %get-tuple-element.452.refs_0_, bf16[1024,384]{1,0:T(8,128)(2,1)} %get-tuple-element.281.refs_0_.refs_7_.refs_1_, bf16[192,1536]{1,0:T(8,128)(2,1)} %get-tuple-element.453.refs_2_, bf16[192,384]{1,0:T(8,128)(2,1)} %get-tuple-element.282.refs_1_.refs_8_.refs_3_, ...), custom_call_target="tpu_custom_call" | custom-call | flops 207000000 | bytes 1 | tf_op jit(solution)/shard_map/outer_sums/pallas_call | solution.py:919
  562.3 32.2 %attention_back.3 = (bf16[1024,1152]{1,0:T(8,128)(2,1)}, bf16[192,1152]{1,0:T(8,128)(2,1)}) custom-call(f32[1216,128]{1,0:T(8,128)} %broadcast_in_dim.133.bias_ref.refs_0_, bf16[1024,1152]{1,0:T(8,128)(2,1)} %get-tuple-element.297.qi.ki.vi.refs_1_.refs_3_.refs_5_, bf16[192,1152]{1,0:T(8,128)(2,1)} %get-tuple-element.298.qt.kt.vt.refs_2_.refs_4_.refs_6_, ...), custom_call_target="tpu_custom_call" | custom-call | flops 368000000 | bytes 1 | tf_op jit(solution)/shard_map/attention_back/pallas_call | solution.py:766
  599.1 14.7 %outer_sums.7 = bf16[2,1152,1536]{2,1,0:T(8,128)(2,1)} custom-call(bf16[1024,1152]{1,0:T(8,128)(2,1)} %get-tuple-element.435.refs_0_, bf16[1024,1536]{1,0:T(8,128)(2,1)} %get-tuple-element.466.refs_1_, bf16[192,1152]{1,0:T(8,128)(2,1)} %get-tuple-element.436.refs_1_.refs_2_, bf16[192,1536]{1,0:T(8,128)(2,1)} %get-tuple-element.467.refs_3_, ...), custom_call_target="tpu_custom_call" | custom-call | flops 207000000 | bytes 1 | tf_op jit(solution)/shard_map/outer_sums/pallas_call | solution.py:919
  622.2 12.9 %project_back.3 = (f32[4,1536]{1,0:T(4,128)}, f32[2,1152]{1,0:T(2,128)}, bf16[304,1536]{1,0:T(8,128)(2,1)}, bf16[304,1536]{1,0:T(8,128)(2,1)}, bf16[304,1536]{1,...) custom-call(bf16[1024,1152]{1,0:T(8,128)(2,1)} %get-tuple-element.473.refs_4_.refs_0_, ...), custom_call_target="tpu_custom_call" | custom-call | flops 138000000 | bytes 1 | tf_op jit(solution)/shard_map/project_back/pallas_call | solution.py:919
  638.0 8.0 %result.1 = (bf16[2,256,1536]{2,1,0:T(8,128)(2,1)}, bf16[2,48,1536]{2,1,0:T(8,128)(2,1)}, f32[8,1536]{1,0:T(8,128)}) custom-call(bf16[304,1536]{1,0:T(8,128)(2,1)} %get-tuple-element.480.refs_0_, bf16[304,1536]{1,0:T(8,128)(2,1)} %copy-done.15, bf16[304,1536]{1,0:T(8,128)(2,1)} %copy-done.16, bf16[304,768]{1,0:T(8,128)(2,1)} %collective-permute-done.68.refs_3_, ...), custom_call_target="tpu_custom_call" | custom-call | flops 80500000 | bytes 1 | tf_op jit(solution)/shard_map/result/pallas_call | solution.py:919
  660.4 9.8 %all-to-all-start.1 = ((f32[8,1,1920]{2,1,0:T(1,128)}), f32[8,1,1920]{2,1,0:T(1,128)S(1)}, u32[]{:S(2)}, u32[]{:S(2)}) async-start(f32[8,1,1920]{2,1,0:T(1,128)} %all_to_all.18), calls=%async_computation.5 | async-start | bytes 122880 | tf_op jit(solution)/shard_map/all_to_all | solution.py:1610
  717.6 19.3 %collective-permute-done.77.refs_4_ = bf16[304,768]{1,0:T(8,128)(2,1)} collective-permute-done((bf16[304,768]{1,0:T(8,128)(2,1)}, bf16[304,768]{1,0:T(8,128)(2,1)}, u32[]{:S(2)}, u32[]{:S(2)}) %collective-permute-start.77) | collective-permute-done | bytes 466976 | tf_op jit(solution)/shard_map/ppermute | solution.py:799
  737.0 9.5 %input_back.1 = (f32[2,256,1536]{2,1,0:T(8,128)}, f32[2,40,1536]{2,1,0:T(8,128)}) custom-call(bf16[304,1536]{1,0:T(8,128)(2,1)} %get-tuple-element.503.refs_0_, bf16[304,1536]{1,0:T(8,128)(2,1)} %collective-permute-done.74.refs_1_, bf16[304,1536]{1,0:T(8,128)(2,1)} %collective-permute-done.75.refs_2_, bf16[304,768]{1,0:T(8,128)(2,1)} %collective-permute-done.76.refs_3_, ...), custom_call_target="tpu_custom_call" | custom-call | flops 103500000 | bytes 1 | tf_op jit(solution)/shard_map/input_back/pallas_call | solution.py:919
  (548 shorter events, 299.7 us)
Async XLA Ops:
  7.2 129.3 %all-gather.5.cloned.1.call-start = ((), (), s32[]{:S(2)}) async-start(), calls=%async_computation.8 | async-start | bytes 7962624 | tf_op jit(solution)/shard_map/all_gather | solution.py:1584
  30.3 138.2 %all-gather.7.cloned.1.call-start = ((), (), s32[]{:S(2)}) async-start(), calls=%async_computation.9 | async-start | bytes 2654208 | tf_op jit(solution)/shard_map/all_gather | solution.py:1584
  77.3 213.1 %all-gather.9.cloned.1.call-start = ((), (), s32[]{:S(2)}) async-start(), calls=%async_computation.10 | async-start | bytes 10616832 | tf_op jit(solution)/shard_map/all_gather | solution.py:1584
  78.1 276.2 %all-gather.11.cloned.1.call-start = ((), (), s32[]{:S(2)}) async-start(), calls=%async_computation.11 | async-start | bytes 10616832 | tf_op jit(solution)/shard_map/all_gather | solution.py:1584
  78.6 406.5 %reduce-scatter.5.cloned.1.call-start = ((), (), s32[]{:S(2)}) async-start(), calls=%async_computation.12 | async-start | bytes 10616832 | tf_op jit(solution)/shard_map/reduce_scatter | solution.py:1606
  89.5 32.9 %collective-permute-start.7 = (bf16[2,304,768]{2,1,0:T(8,128)(2,1)}, bf16[2,304,768]{2,1,0:T(8,128)(2,1)}, u32[]{:S(2)}, u32[]{:S(2)}) collective-permute-start(bf16[2,304,768]{2,1,0:T(8,128)(2,1)} %copy-done.4), channel_id=1, source_target_pairs={{0,2},{1,3},{2,0},{3,1},{4,6},{5,7},{6,4},{7,5},{8,10},{9,11},{10,... | collective-permute-start | bytes 2801672 | tf_op jit(solution)/shard_map/ppermute | solution.py:799
  128.8 39.6 %collective-permute-start.19 = (bf16[2,304,768]{2,1,0:T(8,128)(2,1)}, bf16[2,304,768]{2,1,0:T(8,128)(2,1)}, u32[]{:S(2)}, u32[]{:S(2)}) collective-permute-start(bf16[2,304,768]{2,1,0:T(8,128)(2,1)} %get-tuple-element.279.refs_8_.refs_5_.refs_10_), channel_id=1, source_target_pairs={{0,2},{1,3},{2,0},{3,1},{4,6},{5,7},{6,4},{7,5},{8,10},{9,11},{10,... | collective-permute-start | bytes 2801672 | tf_op jit(solution)/shard_map/ppermute | solution.py:799
  129.3 39.2 %collective-permute-start.17 = (bf16[2,304,768]{2,1,0:T(8,128)(2,1)}, bf16[2,304,768]{2,1,0:T(8,128)(2,1)}, u32[]{:S(2)}, u32[]{:S(2)}) collective-permute-start(bf16[2,304,768]{2,1,0:T(8,128)(2,1)} %get-tuple-element.279.refs_8_.refs_5_.refs_10_), channel_id=1, source_target_pairs={{0,1},{1,0},{2,3},{3,2},{4,5},{5,4},{6,7},{7,6},{8,9},{9,8},{10,11... | collective-permute-start | bytes 2801672 | tf_op jit(solution)/shard_map/ppermute | solution.py:799
  130.8 37.6 %collective-permute-start.20 = (bf16[2,304,768]{2,1,0:T(8,128)(2,1)S(1)}, bf16[2,304,768]{2,1,0:T(8,128)(2,1)}, u32[]{:S(2)}, u32[]{:S(2)}) collective-permute-start(bf16[2,304,768]{2,1,0:T(8,128)(2,1)S(1)} %copy-done.3), channel_id=1, source_target_pairs={{0,2},{1,3},{2,0},{3,1},{4,6},{5,7},{6,4},{7,5},{8,10},{9,11},{10,... | collective-permute-start | bytes 2801672 | tf_op jit(solution)/shard_map/ppermute | solution.py:799
  132.2 36.3 %collective-permute-start.18 = (bf16[2,304,768]{2,1,0:T(8,128)(2,1)S(1)}, bf16[2,304,768]{2,1,0:T(8,128)(2,1)}, u32[]{:S(2)}, u32[]{:S(2)}) collective-permute-start(bf16[2,304,768]{2,1,0:T(8,128)(2,1)S(1)} %copy-done.3), channel_id=1, source_target_pairs={{0,1},{1,0},{2,3},{3,2},{4,5},{5,4},{6,7},{7,6},{8,9},{9,8},{10,11... | collective-permute-start | bytes 2801672 | tf_op jit(solution)/shard_map/ppermute | solution.py:799
  173.6 35.5 %collective-permute-start.24 = (bf16[304,1536]{1,0:T(8,128)(2,1)}, bf16[304,1536]{1,0:T(8,128)(2,1)S(1)}, u32[]{:S(2)}, u32[]{:S(2)}) collective-permute-start(bf16[304,1536]{1,0:T(8,128)(2,1)} %get-tuple-element.285), channel_id=1, source_target_pairs={{0,1},{1,0},{2,3},{3,2},{4,5},{5,4},{6,7},{7,6},{8,9},{9,8},{10,11... | collective-permute-start | bytes 2801672 | tf_op jit(solution)/shard_map/ppermute | solution.py:799
  174.7 34.4 %collective-permute-start.25 = (bf16[304,1536]{1,0:T(8,128)(2,1)}, bf16[304,1536]{1,0:T(8,128)(2,1)S(1)}, u32[]{:S(2)}, u32[]{:S(2)}) collective-permute-start(bf16[304,1536]{1,0:T(8,128)(2,1)} %get-tuple-element.286), channel_id=1, source_target_pairs={{0,2},{1,3},{2,0},{3,1},{4,6},{5,7},{6,4},{7,5},{8,10},{9,11},{10,... | collective-permute-start | bytes 2801672 | tf_op jit(solution)/shard_map/ppermute | solution.py:799
  175.4 41.6 %collective-permute-start.34 = (bf16[2,304,768]{2,1,0:T(8,128)(2,1)}, bf16[2,304,768]{2,1,0:T(8,128)(2,1)S(1)}, u32[]{:S(2)}, u32[]{:S(2)}) collective-permute-start(bf16[2,304,768]{2,1,0:T(8,128)(2,1)} %collective-permute-done.17.refs_10_), channel_id=1, source_target_pairs={{0,2},{1,3},{2,0},{3,1},{4,6},{5,7},{6,4},{7,5},{8,10},{9,11},{10,... | collective-permute-start | bytes 2801672 | tf_op jit(solution)/shard_map/ppermute | solution.py:799
  176.7 40.4 %collective-permute-start.35 = (bf16[2,304,768]{2,1,0:T(8,128)(2,1)}, bf16[2,304,768]{2,1,0:T(8,128)(2,1)}, u32[]{:S(2)}, u32[]{:S(2)}) collective-permute-start(bf16[2,304,768]{2,1,0:T(8,128)(2,1)} %collective-permute-done.20.refs_13_), channel_id=1, source_target_pairs={{0,1},{1,0},{2,3},{3,2},{4,5},{5,4},{6,7},{7,6},{8,9},{9,8},{10,11... | collective-permute-start | bytes 2801672 | tf_op jit(solution)/shard_map/ppermute | solution.py:799
  354.0 245.1 %reduce-scatter.7.cloned.1.call-start = ((), (), s32[]{:S(2)}) async-start(), calls=%async_computation.13 | async-start | bytes 10616832 | tf_op jit(solution)/shard_map/reduce_scatter | solution.py:1606
  418.7 44.3 %collective-permute-start.50 = (bf16[304,768]{1,0:T(8,128)(2,1)}, bf16[304,768]{1,0:T(8,128)(2,1)}, u32[]{:S(2)}, u32[]{:S(2)}) collective-permute-start(bf16[304,768]{1,0:T(8,128)(2,1)} %get-tuple-element.413.refs_0_), channel_id=1, source_target_pairs={{0,1},{1,0},{2,3},{3,2},{4,5},{5,4},{6,7},{7,6},{8,9},{9,8},{10,11... | collective-permute-start | bytes 1400840 | tf_op jit(solution)/shard_map/ppermute | solution.py:799
  420.0 43.0 %collective-permute-start.53 = (bf16[304,768]{1,0:T(8,128)(2,1)}, bf16[304,768]{1,0:T(8,128)(2,1)}, u32[]{:S(2)}, u32[]{:S(2)}) collective-permute-start(bf16[304,768]{1,0:T(8,128)(2,1)} %get-tuple-element.414.refs_1_), channel_id=1, source_target_pairs={{0,2},{1,3},{2,0},{3,1},{4,6},{5,7},{6,4},{7,5},{8,10},{9,11},{10,... | collective-permute-start | bytes 1400840 | tf_op jit(solution)/shard_map/ppermute | solution.py:799
  470.5 143.4 %reduce-scatter.9.cloned.1.call-start = ((), (), s32[]{:S(2)}) async-start(), calls=%async_computation.14 | async-start | bytes 2654208 | tf_op jit(solution)/shard_map/reduce_scatter | solution.py:1606
  492.2 39.9 %collective-permute-start.60 = (bf16[304,1536]{1,0:T(8,128)(2,1)S(1)}, bf16[304,1536]{1,0:T(8,128)(2,1)S(1)}, u32[]{:S(2)}, u32[]{:S(2)}) collective-permute-start(bf16[304,1536]{1,0:T(8,128)(2,1)S(1)} %copy-done.88), channel_id=1, source_target_pairs={{0,1},{1,0},{2,3},{3,2},{4,5},{5,4},{6,7},{7,6},{8,9},{9,8},{10,11... | collective-permute-start | bytes 2801672 | tf_op jit(solution)/shard_map/ppermute | solution.py:799
  492.9 39.3 %collective-permute-start.61 = (bf16[304,1536]{1,0:T(8,128)(2,1)S(1)}, bf16[304,1536]{1,0:T(8,128)(2,1)S(1)}, u32[]{:S(2)}, u32[]{:S(2)}) collective-permute-start(bf16[304,1536]{1,0:T(8,128)(2,1)S(1)} %copy-done.87), channel_id=1, source_target_pairs={{0,2},{1,3},{2,0},{3,1},{4,6},{5,7},{6,4},{7,5},{8,10},{9,11},{10,... | collective-permute-start | bytes 2801672 | tf_op jit(solution)/shard_map/ppermute | solution.py:799
  494.4 34.8 %collective-permute-start.62 = (bf16[304,768]{1,0:T(8,128)(2,1)S(1)}, bf16[304,768]{1,0:T(8,128)(2,1)S(1)}, u32[]{:S(2)}, u32[]{:S(2)}) collective-permute-start(bf16[304,768]{1,0:T(8,128)(2,1)S(1)} %copy-done.22), channel_id=1, source_target_pairs={{0,1},{1,0},{2,3},{3,2},{4,5},{5,4},{6,7},{7,6},{8,9},{9,8},{10,11... | collective-permute-start | bytes 1400840 | tf_op jit(solution)/shard_map/ppermute | solution.py:799
  495.7 33.6 %collective-permute-start.65 = (bf16[304,768]{1,0:T(8,128)(2,1)}, bf16[304,768]{1,0:T(8,128)(2,1)S(1)}, u32[]{:S(2)}, u32[]{:S(2)}) collective-permute-start(bf16[304,768]{1,0:T(8,128)(2,1)} %get-tuple-element.443.refs_1_), channel_id=1, source_target_pairs={{0,2},{1,3},{2,0},{3,1},{4,6},{5,7},{6,4},{7,5},{8,10},{9,11},{10,... | collective-permute-start | bytes 1400840 | tf_op jit(solution)/shard_map/ppermute | solution.py:799
  496.3 33.0 %collective-permute-start.63 = (bf16[304,768]{1,0:T(8,128)(2,1)}, bf16[304,768]{1,0:T(8,128)(2,1)S(1)}, u32[]{:S(2)}, u32[]{:S(2)}) collective-permute-start(bf16[304,768]{1,0:T(8,128)(2,1)} %get-tuple-element.443.refs_1_), channel_id=1, source_target_pairs={{0,1},{1,0},{2,3},{3,2},{4,5},{5,4},{6,7},{7,6},{8,9},{9,8},{10,11... | collective-permute-start | bytes 1400840 | tf_op jit(solution)/shard_map/ppermute | solution.py:799
  560.9 141.5 %reduce-scatter.11.cloned.1.call-start = ((), (), s32[]{:S(2)}) async-start(), calls=%async_computation.15 | async-start | bytes 7962624 | tf_op jit(solution)/shard_map/reduce_scatter | solution.py:1606
  560.9 35.5 %collective-permute-start.70 = (bf16[304,1536]{1,0:T(8,128)(2,1)}, bf16[304,1536]{1,0:T(8,128)(2,1)S(1)}, u32[]{:S(2)}, u32[]{:S(2)}) collective-permute-start(bf16[304,1536]{1,0:T(8,128)(2,1)} %get-tuple-element.462), channel_id=1, source_target_pairs={{0,1},{1,0},{2,3},{3,2},{4,5},{5,4},{6,7},{7,6},{8,9},{9,8},{10,11... | collective-permute-start | bytes 2801672 | tf_op jit(solution)/shard_map/ppermute | solution.py:799
  561.9 34.5 %collective-permute-start.71 = (bf16[304,1536]{1,0:T(8,128)(2,1)}, bf16[304,1536]{1,0:T(8,128)(2,1)S(1)}, u32[]{:S(2)}, u32[]{:S(2)}) collective-permute-start(bf16[304,1536]{1,0:T(8,128)(2,1)} %get-tuple-element.463), channel_id=1, source_target_pairs={{0,2},{1,3},{2,0},{3,1},{4,6},{5,7},{6,4},{7,5},{8,10},{9,11},{10,... | collective-permute-start | bytes 2801672 | tf_op jit(solution)/shard_map/ppermute | solution.py:799
  677.1 40.5 %all-to-all-start.2 = ((f32[8,2,1536]{2,1,0:T(2,128)}), f32[8,2,1536]{2,1,0:T(2,128)S(1)}, u32[]{:S(2)}, u32[]{:S(2)}) async-start(f32[8,2,1536]{2,1,0:T(2,128)} %copy.207), calls=%async_computation.6 | async-start | bytes 196608 | tf_op jit(solution)/shard_map/all_to_all | solution.py:1610
  692.9 44.0 %collective-permute-start.77 = (bf16[304,768]{1,0:T(8,128)(2,1)}, bf16[304,768]{1,0:T(8,128)(2,1)}, u32[]{:S(2)}, u32[]{:S(2)}) collective-permute-start(bf16[304,768]{1,0:T(8,128)(2,1)} %add_convert_fusion.2), channel_id=1, source_target_pairs={{0,2},{1,3},{2,0},{3,1},{4,6},{5,7},{6,4},{7,5},{8,10},{9,11},{10,... | collective-permute-start | bytes 1400840 | tf_op jit(solution)/shard_map/ppermute | solution.py:799
  700.8 36.1 %collective-permute-start.76 = (bf16[304,768]{1,0:T(8,128)(2,1)}, bf16[304,768]{1,0:T(8,128)(2,1)}, u32[]{:S(2)}, u32[]{:S(2)}) collective-permute-start(bf16[304,768]{1,0:T(8,128)(2,1)} %add_convert_fusion.3), channel_id=1, source_target_pairs={{0,1},{1,0},{2,3},{3,2},{4,5},{5,4},{6,7},{7,6},{8,9},{9,8},{10,11... | collective-permute-start | bytes 1400840 | tf_op jit(solution)/shard_map/ppermute | solution.py:799
  704.3 47.3 %collective-permute-start.83 = (bf16[1,2,48,1536]{3,2,0,1:T(8,128)(2,1)}, bf16[1,2,48,1536]{3,2,0,1:T(8,128)(2,1)}, u32[]{:S(2)}, u32[]{:S(2)}) collective-permute-start(bf16[1,2,48,1536]{3,2,0,1:T(8,128)(2,1)} %get-tuple-element.531), channel_id=1, source_target_pairs={{0,0},{4,1},{8,2},{1,3},{5,4},{2,5},{6,6},{10,7},{3,8},{7,9},{11,1... | collective-permute-start | bytes 884744 | tf_op jit(solution)/shard_map/ppermute | solution.py:1576
  708.7 41.9 %collective-permute-start.82 = (bf16[1,2,48,1536]{3,2,0,1:T(8,128)(2,1)S(1)}, bf16[1,2,48,1536]{3,2,0,1:T(8,128)(2,1)}, u32[]{:S(2)}, u32[]{:S(2)}) collective-permute-start(bf16[1,2,48,1536]{3,2,0,1:T(8,128)(2,1)S(1)} %get-tuple-element.532), channel_id=1, source_target_pairs={{0,0},{4,1},{8,2},{1,3},{5,4},{9,5},{2,6},{6,7},{3,8},{7,9},{11,10... | collective-permute-start | bytes 884744 | tf_op jit(solution)/shard_map/ppermute | solution.py:1576
  711.2 41.4 %collective-permute-start.84 = (bf16[1,2,48,1536]{3,2,0,1:T(8,128)(2,1)}, bf16[1,2,48,1536]{3,2,0,1:T(8,128)(2,1)}, u32[]{:S(2)}, u32[]{:S(2)}) collective-permute-start(bf16[1,2,48,1536]{3,2,0,1:T(8,128)(2,1)} %get-tuple-element.530), channel_id=1, source_target_pairs={{0,0},{4,1},{1,2},{5,3},{9,4},{2,5},{6,6},{10,7},{3,8},{7,9},{8,10... | collective-permute-start | bytes 884744 | tf_op jit(solution)/shard_map/ppermute | solution.py:1576
  (159 other events, 2532.4 us)
Sparse Core Ops, SparseCore 0:
  30.4 77.3 all-gather.4
  109.9 30.8 all-gather.6
  142.4 89.1 all-gather.8
  233.1 89.1 all-gather.10
  354.1 101.5 reduce-scatter.4
  470.6 101.9 reduce-scatter.6
  574.9 31.4 reduce-scatter.8
  614.1 83.7 reduce-scatter.10

commit v8 on v7

--- a/solution.py
+++ b/solution.py
@@ -669,7 +669,7 @@
             for count in (image_rows, text_rows)
         ],
         scratch_shapes=[pltpu.VMEM((2, rows, lanes), BF16)] * 2,
-        compiler_params=pltpu.CompilerParams(vmem_limit_bytes=56 << 20),
+        compiler_params=pltpu.CompilerParams(vmem_limit_bytes=24 << 20),
         cost_estimate=pl.CostEstimate(
             flops=int(WEIGHT["attention"] * 1.15e9), bytes_accessed=1, transcendentals=0
         ),
@@ -783,7 +783,7 @@
         ],
         scratch_shapes=[pltpu.VMEM((2, rows, lanes), BF16)] * 2
         + [pltpu.VMEM((rows, lanes), F32)] * 2,
-        compiler_params=pltpu.CompilerParams(vmem_limit_bytes=56 << 20),
+        compiler_params=pltpu.CompilerParams(vmem_limit_bytes=24 << 20),
         cost_estimate=pl.CostEstimate(
             flops=int(WEIGHT["attention_back"] * 1.15e9), bytes_accessed=1, transcendentals=0
         ),
@@ -841,6 +841,7 @@
 
 ANYWHERE = pl.BlockSpec(memory_space=pl.ANY)
 ON_CORE = pl.BlockSpec(memory_space=pltpu.VMEM)
+ROOM = 10 << 20
 
 
 class Copies:
@@ -914,6 +915,12 @@
 
 
 def run(kernel, name, operands, specs, outs, out_specs, scratch, copies=0):
+    held = sum(math.prod(ref.shape) * np.dtype(ref.dtype).itemsize for ref in scratch)
+    for spec, (shape, dtype) in zip(
+        [*specs, *out_specs],
+        [*((value.shape, value.dtype) for value in operands), *outs],
+    ):
+        held += math.prod(shape) * np.dtype(dtype).itemsize if spec is ON_CORE else 0
     if copies:
         scratch = [*scratch, pltpu.SemaphoreType.DMA((copies,))]
     return pl.pallas_call(
@@ -922,7 +929,7 @@
         out_specs=out_specs,
         out_shape=[jax.ShapeDtypeStruct(shape, dtype) for shape, dtype in outs],
         scratch_shapes=scratch,
-        compiler_params=pltpu.CompilerParams(vmem_limit_bytes=56 << 20),
+        compiler_params=pltpu.CompilerParams(vmem_limit_bytes=min(held + ROOM, 56 << 20)),
         cost_estimate=pl.CostEstimate(
             flops=int(WEIGHT[name] * 1.15e9), bytes_accessed=1, transcendentals=0
         ),

time: 775 us -> 872 us (1.13)
  local copies, waits for them, and re-layouts: 47.8 us -> 196 us
  Pallas kernels: 365 us -> 313 us
    unnamed x182 -> x498, local copies, waits for them, and re-layouts: 7.77 us -> 161 us
    pallas_call x23, Pallas kernels: 266 us -> 225 us  [run(): pl.pallas_call(kernel, in_specs=specs, out_specs=out_specs, out_shape=[ja...]
  transfers between devices with their start and end apart: 99 -> 99, of which waited for: 30 -> 30; matrix products, arithmetic and copies ran while one was open for 10% -> 8% of each run, Pallas kernels for 47% -> 36%
where the time goes in v8:
time: 872 us; the launch traced here: 862 us
  Pallas kernels  313 us (36%)
  local copies, waits for them, and re-layouts  196 us (22%)
  waiting for transfers between devices  154 us (18%)
  starting transfers between devices  137 us (16%)
  other arithmetic  35.6 us (4%)
  between operations  22.7 us (3%)
    pallas_call x23, Pallas kernels, run(): pl.pallas_call(kernel, in_specs=specs, out_specs=out_specs, out_shape=[ja...  225 us
    unnamed x498, local copies, waits for them, and re-layouts  161 us
    ppermute x73, waiting for transfers between devices, flip(): return lax.ppermute(values, 'seq', [(i, i ^ bit) for i in range(4)])  118 us
    ppermute x73, starting transfers between devices, flip(): return lax.ppermute(values, 'seq', [(i, i ^ bit) for i in range(4)])  87.7 us
    pallas_call x2, Pallas kernels, attention_back(): pl.pallas_call(functools.partial(attention_back_kernel, 512, LOG2E / math...  58 us
    ppermute x8, waiting for transfers between devices, gather_small(): held = jnp.concatenate([held, lax.ppermute(held, axis, pairs)])  35 us
    pallas_call x2, Pallas kernels, attention(): pl.pallas_call(functools.partial(attention_kernel, 256, LOG2E / math.sqrt...  30.5 us
    all_to_all x4, starting transfers between devices, swap(): return lax.all_to_all(values, axis, 0, 0, tiled=True)  22.2 us
  transfers between devices with their start and end apart: 99, of which 30 were waited for; matrix products, arithmetic and copies ran while one was open for 8% of the time, Pallas kernels for 36%

profile of v8, /device:TPU:16, one launch (start us, length us, event | category | flops | bytes accessed | tf_op | source)
XLA Modules:
  0.0 862.3 jit_solution(13770714900671574500)
XLA Ops:
  44.3 14.7 %collective-permute-done.3.refs_2_.refs_5_ = bf16[2,304,768]{2,1,0:T(8,128)(2,1)S(1)} collective-permute-done((bf16[2,304,768]{2,1,0:T(8,128)(2,1)S(1)}, bf16[2,304,768]{2,1,0:T(8,128)(2,1)S(1)}, u32[]{:S(2)}, u32[]{:S(2)}) %collective-permute-start.3) | collective-permute-done | bytes 933920 | tf_op jit(solution)/shard_map/ppermute | solution.py:799
  92.1 8.1 collective-permute-done.13
  105.5 6.4 collective-permute-done.14
  114.4 7.0 collective-permute-done.15
  140.9 10.9 %project.2 = (bf16[1024,1152]{1,0:T(8,128)(2,1)S(1)}, bf16[192,1152]{1,0:T(8,128)(2,1)S(1)}, bf16[1024,1536]{1,0:T(8,128)(2,1)S(1)}, bf16[192,1536]{1,0:T(8,128)(2,1)S(1)}) custom-call(bf16[2,304,768]{2,1,0:T(8,128)(2,1)S(1)} %copy-done.9, bf16[2,304,768]{2,1,0:T(8,128)(2,1)S(1)} %get-tuple-element.290.refs_1_.refs_6_.refs_4_.refs_11_, ...), custom_call_target="tpu_custom_call" | custom-call | flops 149500000 | bytes 1 | tf_op jit(solution)/shard_map/project/pallas_call | solution.py:926
  152.1 15.1 %attention.2 = (bf16[1024,384]{1,0:T(8,128)(2,1)S(1)}, bf16[192,384]{1,0:T(8,128)(2,1)S(1)}, f32[1024,384]{1,0:T(8,128)S(1)}, f32[192,384]{1,0:T(8,128)S(1)}) custom-call(f32[1216,128]{1,0:T(8,128)S(1)} %broadcast_in_dim.119.bias_ref.refs_0_, f32[1,1]{1,0:T(1,128)} %bitcast.6.floor_ref, ...), custom_call_target="tpu_custom_call" | custom-call | flops 195500000 | bytes 1 | tf_op jit(solution)/shard_map/attention/pallas_call | solution.py:657
  185.5 10.7 %project.3 = (bf16[1024,1152]{1,0:T(8,128)(2,1)S(1)}, bf16[192,1152]{1,0:T(8,128)(2,1)S(1)}, bf16[1024,1536]{1,0:T(8,128)(2,1)S(1)}, bf16[192,1536]{1,0:T(8,128)(2,1)S(1)}) custom-call(bf16[2,304,768]{2,1,0:T(8,128)(2,1)S(1)} %copy-done.10, bf16[2,304,768]{2,1,0:T(8,128)(2,1)S(1)} %get-tuple-element.290.refs_1_.refs_6_.refs_4_.refs_11_, ...), custom_call_target="tpu_custom_call" | custom-call | flops 149500000 | bytes 1 | tf_op jit(solution)/shard_map/project/pallas_call | solution.py:926
  196.5 15.4 %attention.3 = (bf16[1024,384]{1,0:T(8,128)(2,1)S(1)}, bf16[192,384]{1,0:T(8,128)(2,1)S(1)}, f32[1024,384]{1,0:T(8,128)S(1)}, f32[192,384]{1,0:T(8,128)S(1)}) custom-call(f32[1216,128]{1,0:T(8,128)S(1)} %broadcast_in_dim.133.bias_ref.refs_0_, f32[1,1]{1,0:T(1,128)} %bitcast.38.floor_ref, ...), custom_call_target="tpu_custom_call" | custom-call | flops 195500000 | bytes 1 | tf_op jit(solution)/shard_map/attention/pallas_call | solution.py:657
  215.0 6.0 collective-permute-done.34.refs_14_
  245.8 6.0 collective-permute-done.36.refs_1_
  265.9 7.4 collective-permute-done.39.refs_4_
  287.4 5.9 collective-permute-done.32.refs_6_
  305.4 14.7 %hidden.2 = (bf16[1024,1536]{1,0:T(8,128)(2,1)S(1)}, bf16[192,1536]{1,0:T(8,128)(2,1)S(1)}, bf16[1024,1536]{1,0:T(8,128)(2,1)}, bf16[192,1536]{1,0:T(8,128)(2,1)...) custom-call(bf16[304,768]{1,0:T(8,128)(2,1)S(1)} %copy-done.186, ...), custom_call_target="tpu_custom_call" | custom-call | flops 207000000 | bytes 1 | tf_op jit(solution)/shard_map/hidden/pallas_call | solution.py:926
  333.1 15.2 %hidden.3 = (bf16[1024,1536]{1,0:T(8,128)(2,1)S(1)}, bf16[192,1536]{1,0:T(8,128)(2,1)S(1)}, bf16[1024,1536]{1,0:T(8,128)(2,1)}, bf16[192,1536]{1,0:T(8,128)(2,1)...) custom-call(bf16[304,768]{1,0:T(8,128)(2,1)} %get-tuple-element.324., ...), custom_call_target="tpu_custom_call" | custom-call | flops 207000000 | bytes 1 | tf_op jit(solution)/shard_map/hidden/pallas_call | solution.py:926
  353.7 14.9 %outer_sums.4 = bf16[2,1536,1536]{2,1,0:T(8,128)(2,1)} custom-call(bf16[1024,1536]{1,0:T(8,128)(2,1)S(1)} %get-tuple-element.370.refs_0_, bf16[1024,1536]{1,0:T(8,128)(2,1)S(1)} %copy-done.44, bf16[192,1536]{1,0:T(8,128)(2,1)S(1)} %get-tuple-element.371.refs_2_.refs_1_, bf16[192,1536]{1,0:T(8,128)(2,1)S(1)} %get-tuple-element.341.refs_3_.refs_1_, ...), custom_call_target="tpu_custom_call" | custom-call | flops 207000000 | bytes 1 | tf_op jit(solution)/shard_map/outer_sums/pallas_call | solution.py:926
  376.3 18.2 %hidden_back.2 = (bf16[1024,1536]{1,0:T(8,128)(2,1)S(1)}, bf16[192,1536]{1,0:T(8,128)(2,1)S(1)}, f32[2,1536]{1,0:T(2,128)S(1)}, bf16[304,1536]{1,0:T(8,128)(2,1)...) custom-call(bf16[1024,1536]{1,0:T(8,128)(2,1)S(1)} %copy-done.45, ...), custom_call_target="tpu_custom_call" | custom-call | flops 230000000 | bytes 1 | tf_op jit(solution)/shard_map/hidden_back/pallas_call | solution.py:926
  400.0 18.3 %hidden_back.3 = (bf16[1024,1536]{1,0:T(8,128)(2,1)S(1)}, bf16[192,1536]{1,0:T(8,128)(2,1)S(1)}, f32[2,1536]{1,0:T(2,128)S(1)}, bf16[304,1536]{1,0:T(8,128)(2,1)...) custom-call(bf16[1024,1536]{1,0:T(8,128)(2,1)S(1)} %copy-done.47, ...), custom_call_target="tpu_custom_call" | custom-call | flops 230000000 | bytes 1 | tf_op jit(solution)/shard_map/hidden_back/pallas_call | solution.py:926
  427.1 11.4 %collective-permute-done.49.refs_4_ = bf16[304,768]{1,0:T(8,128)(2,1)S(1)} collective-permute-done((bf16[304,768]{1,0:T(8,128)(2,1)S(1)}, bf16[304,768]{1,0:T(8,128)(2,1)S(1)}, u32[]{:S(2)}, u32[]{:S(2)}) %collective-permute-start.49) | collective-permute-done | bytes 466976 | tf_op jit(solution)/shard_map/ppermute | solution.py:799
  453.1 17.2 %partial_sums.5 = (bf16[304,1536]{1,0:T(8,128)(2,1)S(1)}, bf16[304,1536]{1,0:T(8,128)(2,1)S(1)}, bf16[304,1536]{1,0:T(8,128)(2,1)S(1)}, bf16[304,768]{1,0:T(8,12...) custom-call(bf16[1024,1536]{1,0:T(8,128)(2,1)S(1)} %copy-done.41, ...), custom_call_target="tpu_custom_call" | custom-call | flops 57500000 | bytes 1 | tf_op jit(solution)/shard_map/partial_sums/pallas_call | solution.py:926
  487.1 15.1 %outer_sums.5 = bf16[2,1536,1536]{2,1,0:T(8,128)(2,1)} custom-call(bf16[1024,1536]{1,0:T(8,128)(2,1)S(1)} %get-tuple-element.388.refs_0_, bf16[1024,1536]{1,0:T(8,128)(2,1)S(1)} %copy-done.78, bf16[192,1536]{1,0:T(8,128)(2,1)S(1)} %copy-done.151, bf16[192,1536]{1,0:T(8,128)(2,1)S(1)} %copy-done.147, bf16[1024,1536]{1,0:T(8,128)(2,1)S(1)} %copy-done.81, ...), custom_call_target="tpu_custom_call" | custom-call | flops 207000000 | bytes 1 | tf_op jit(solution)/shard_map/outer_sums/pallas_call | solution.py:926
  520.1 11.8 %collective-permute-done.54.refs_6_ = bf16[304,768]{1,0:T(8,128)(2,1)S(1)} collective-permute-done((bf16[304,768]{1,0:T(8,128)(2,1)}, bf16[304,768]{1,0:T(8,128)(2,1)S(1)}, u32[]{:S(2)}, u32[]{:S(2)}) %collective-permute-start.54) | collective-permute-done | bytes 466976 | tf_op jit(solution)/shard_map/ppermute | solution.py:799
  547.5 29.0 %attention_back.2 = (bf16[1024,1152]{1,0:T(8,128)(2,1)S(1)}, bf16[192,1152]{1,0:T(8,128)(2,1)S(1)}) custom-call(f32[1216,128]{1,0:T(8,128)S(1)} %copy-done.69, bf16[1024,1152]{1,0:T(8,128)(2,1)S(1)} %copy-done.7, bf16[192,1152]{1,0:T(8,128)(2,1)S(1)} %copy-done.29, bf16[1024,1152]{1,0:T(8,128)(2,1)S(1)} %copy-done.7, bf16[192,1152]{1,0:T(8,128)(2,1)S(1)} %copy-done.29, ...), custom_call_target="tpu_custom_call" | custom-call | flops 368000000 | bytes 1 | tf_op jit(solution)/shard_map/attention_back/pallas_call | solution.py:766
  579.9 8.8 %project_back.2 = (f32[4,1536]{1,0:T(4,128)S(1)}, f32[2,1152]{1,0:T(2,128)S(1)}, bf16[304,1536]{1,0:T(8,128)(2,1)S(1)}, bf16[304,1536]{1,0:T(8,128)(2,1)}, bf16[...) custom-call(bf16[1024,1152]{1,0:T(8,128)(2,1)S(1)} %get-tuple-element.435.refs_0_, ...), custom_call_target="tpu_custom_call" | custom-call | flops 138000000 | bytes 1 | tf_op jit(solution)/shard_map/project_back/pallas_call | solution.py:926
  597.5 11.2 %outer_sums.6 = bf16[2,1536,384]{2,1,0:T(8,128)(2,1)S(1)} custom-call(bf16[1024,1536]{1,0:T(8,128)(2,1)S(1)} %get-tuple-element.452.refs_0_, bf16[1024,384]{1,0:T(8,128)(2,1)S(1)} %copy-done.62, bf16[192,1536]{1,0:T(8,128)(2,1)S(1)} %get-tuple-element.453.refs_2_, bf16[192,384]{1,0:T(8,128)(2,1)S(1)} %get-tuple-element.282.refs_1_.refs_8_.refs_3_, ...), custom_call_target="tpu_custom_call" | custom-call | flops 207000000 | bytes 1 | tf_op jit(solution)/shard_map/outer_sums/pallas_call | solution.py:926
  621.4 29.0 %attention_back.3 = (bf16[1024,1152]{1,0:T(8,128)(2,1)S(1)}, bf16[192,1152]{1,0:T(8,128)(2,1)S(1)}) custom-call(f32[1216,128]{1,0:T(8,128)S(1)} %copy-done.67, bf16[1024,1152]{1,0:T(8,128)(2,1)S(1)} %copy-done.5, bf16[192,1152]{1,0:T(8,128)(2,1)S(1)} %get-tuple-element.298.qt.kt.vt.refs_2_.refs_4_.refs_6_, bf16[1024,1152]{1,0:T(8,128)(2,1)S(1)} %copy-done.5, ...), custom_call_target="tpu_custom_call" | custom-call | flops 368000000 | bytes 1 | tf_op jit(solution)/shard_map/attention_back/pallas_call | solution.py:766
  669.1 17.7 %outer_sums.7 = bf16[2,1152,1536]{2,1,0:T(8,128)(2,1)S(1)} custom-call(bf16[1024,1152]{1,0:T(8,128)(2,1)S(1)} %copy-done.49, bf16[1024,1536]{1,0:T(8,128)(2,1)S(1)} %copy-done.75, bf16[192,1152]{1,0:T(8,128)(2,1)S(1)} %copy-done.113, bf16[192,1536]{1,0:T(8,128)(2,1)S(1)} %copy-done.143, bf16[1024,1152]{1,0:T(8,128)(2,1)S(1)} %copy-done.51, ...), custom_call_target="tpu_custom_call" | custom-call | flops 207000000 | bytes 1 | tf_op jit(solution)/shard_map/outer_sums/pallas_call | solution.py:926
  706.1 9.1 %project_back.3 = (f32[4,1536]{1,0:T(4,128)S(1)}, f32[2,1152]{1,0:T(2,128)S(1)}, bf16[304,1536]{1,0:T(8,128)(2,1)S(1)}, bf16[304,1536]{1,0:T(8,128)(2,1)S(1)}, b...) custom-call(bf16[1024,1152]{1,0:T(8,128)(2,1)S(1)} %copy-done.52, ...), custom_call_target="tpu_custom_call" | custom-call | flops 138000000 | bytes 1 | tf_op jit(solution)/shard_map/project_back/pallas_call | solution.py:926
  748.7 10.0 %all-to-all-start.1 = ((f32[8,1,1920]{2,1,0:T(1,128)}), f32[8,1,1920]{2,1,0:T(1,128)S(1)}, u32[]{:S(2)}, u32[]{:S(2)}) async-start(f32[8,1,1920]{2,1,0:T(1,128)} %all_to_all.18), calls=%async_computation.5 | async-start | bytes 122880 | tf_op jit(solution)/shard_map/all_to_all | solution.py:1617
  764.7 5.4 all-to-all-start.2
  779.7 7.5 collective-permute-done.75.refs_2_
  806.1 19.3 %collective-permute-done.77.refs_4_ = bf16[304,768]{1,0:T(8,128)(2,1)} collective-permute-done((bf16[304,768]{1,0:T(8,128)(2,1)}, bf16[304,768]{1,0:T(8,128)(2,1)}, u32[]{:S(2)}, u32[]{:S(2)}) %collective-permute-start.77) | collective-permute-done | bytes 466976 | tf_op jit(solution)/shard_map/ppermute | solution.py:799
  832.0 7.1 input_back.1
  (865 shorter events, 434.9 us)
Async XLA Ops:
  7.2 127.1 %all-gather.5.cloned.1.call-start = ((), (), s32[]{:S(2)}) async-start(), calls=%async_computation.8 | async-start | bytes 7962624 | tf_op jit(solution)/shard_map/all_gather | solution.py:1591
  31.3 138.8 %all-gather.7.cloned.1.call-start = ((), (), s32[]{:S(2)}) async-start(), calls=%async_computation.9 | async-start | bytes 2654208 | tf_op jit(solution)/shard_map/all_gather | solution.py:1591
  77.3 217.1 %all-gather.9.cloned.1.call-start = ((), (), s32[]{:S(2)}) async-start(), calls=%async_computation.10 | async-start | bytes 10616832 | tf_op jit(solution)/shard_map/all_gather | solution.py:1591
  78.1 294.2 %all-gather.11.cloned.1.call-start = ((), (), s32[]{:S(2)}) async-start(), calls=%async_computation.11 | async-start | bytes 10616832 | tf_op jit(solution)/shard_map/all_gather | solution.py:1591
  78.6 454.9 %reduce-scatter.5.cloned.1.call-start = ((), (), s32[]{:S(2)}) async-start(), calls=%async_computation.12 | async-start | bytes 10616832 | tf_op jit(solution)/shard_map/reduce_scatter | solution.py:1613
  128.0 42.0 %collective-permute-start.19 = (bf16[2,304,768]{2,1,0:T(8,128)(2,1)}, bf16[2,304,768]{2,1,0:T(8,128)(2,1)}, u32[]{:S(2)}, u32[]{:S(2)}) collective-permute-start(bf16[2,304,768]{2,1,0:T(8,128)(2,1)} %get-tuple-element.279.refs_8_.refs_5_.refs_10_), channel_id=1, source_target_pairs={{0,2},{1,3},{2,0},{3,1},{4,6},{5,7},{6,4},{7,5},{8,10},{9,11},{10,... | collective-permute-start | bytes 2801672 | tf_op jit(solution)/shard_map/ppermute | solution.py:799
  128.9 41.1 %collective-permute-start.17 = (bf16[2,304,768]{2,1,0:T(8,128)(2,1)}, bf16[2,304,768]{2,1,0:T(8,128)(2,1)}, u32[]{:S(2)}, u32[]{:S(2)}) collective-permute-start(bf16[2,304,768]{2,1,0:T(8,128)(2,1)} %get-tuple-element.279.refs_8_.refs_5_.refs_10_), channel_id=1, source_target_pairs={{0,1},{1,0},{2,3},{3,2},{4,5},{5,4},{6,7},{7,6},{8,9},{9,8},{10,11... | collective-permute-start | bytes 2801672 | tf_op jit(solution)/shard_map/ppermute | solution.py:799
  129.9 40.1 %collective-permute-start.20 = (bf16[2,304,768]{2,1,0:T(8,128)(2,1)}, bf16[2,304,768]{2,1,0:T(8,128)(2,1)}, u32[]{:S(2)}, u32[]{:S(2)}) collective-permute-start(bf16[2,304,768]{2,1,0:T(8,128)(2,1)} %get-tuple-element.280.refs_9_.refs_6_.refs_11_), channel_id=1, source_target_pairs={{0,2},{1,3},{2,0},{3,1},{4,6},{5,7},{6,4},{7,5},{8,10},{9,11},{10,... | collective-permute-start | bytes 2801672 | tf_op jit(solution)/shard_map/ppermute | solution.py:799
  131.8 38.2 %collective-permute-start.18 = (bf16[2,304,768]{2,1,0:T(8,128)(2,1)}, bf16[2,304,768]{2,1,0:T(8,128)(2,1)}, u32[]{:S(2)}, u32[]{:S(2)}) collective-permute-start(bf16[2,304,768]{2,1,0:T(8,128)(2,1)} %get-tuple-element.280.refs_9_.refs_6_.refs_11_), channel_id=1, source_target_pairs={{0,1},{1,0},{2,3},{3,2},{4,5},{5,4},{6,7},{7,6},{8,9},{9,8},{10,11... | collective-permute-start | bytes 2801672 | tf_op jit(solution)/shard_map/ppermute | solution.py:799
  178.3 34.4 %collective-permute-start.24 = (bf16[304,1536]{1,0:T(8,128)(2,1)S(1)}, bf16[304,1536]{1,0:T(8,128)(2,1)S(1)}, u32[]{:S(2)}, u32[]{:S(2)}) collective-permute-start(bf16[304,1536]{1,0:T(8,128)(2,1)S(1)} %get-tuple-element.285), channel_id=1, source_target_pairs={{0,1},{1,0},{2,3},{3,2},{4,5},{5,4},{6,7},{7,6},{8,9},{9,8},{10,11... | collective-permute-start | bytes 2801672 | tf_op jit(solution)/shard_map/ppermute | solution.py:799
  180.2 40.7 %collective-permute-start.34 = (bf16[2,304,768]{2,1,0:T(8,128)(2,1)}, bf16[2,304,768]{2,1,0:T(8,128)(2,1)S(1)}, u32[]{:S(2)}, u32[]{:S(2)}) collective-permute-start(bf16[2,304,768]{2,1,0:T(8,128)(2,1)} %collective-permute-done.17.refs_10_), channel_id=1, source_target_pairs={{0,2},{1,3},{2,0},{3,1},{4,6},{5,7},{6,4},{7,5},{8,10},{9,11},{10,... | collective-permute-start | bytes 2801672 | tf_op jit(solution)/shard_map/ppermute | solution.py:799
  182.0 38.9 %collective-permute-start.35 = (bf16[2,304,768]{2,1,0:T(8,128)(2,1)}, bf16[2,304,768]{2,1,0:T(8,128)(2,1)S(1)}, u32[]{:S(2)}, u32[]{:S(2)}) collective-permute-start(bf16[2,304,768]{2,1,0:T(8,128)(2,1)} %collective-permute-done.20.refs_13_), channel_id=1, source_target_pairs={{0,1},{1,0},{2,3},{3,2},{4,5},{5,4},{6,7},{7,6},{8,9},{9,8},{10,11... | collective-permute-start | bytes 2801672 | tf_op jit(solution)/shard_map/ppermute | solution.py:799
  279.6 42.1 %collective-permute-start.42 = (bf16[304,768]{1,0:T(8,128)(2,1)}, bf16[304,768]{1,0:T(8,128)(2,1)}, u32[]{:S(2)}, u32[]{:S(2)}) collective-permute-start(bf16[304,768]{1,0:T(8,128)(2,1)} %get-tuple-element.324.refs_0_), channel_id=1, source_target_pairs={{0,2},{1,3},{2,0},{3,1},{4,6},{5,7},{6,4},{7,5},{8,10},{9,11},{10,... | collective-permute-start | bytes 1400840 | tf_op jit(solution)/shard_map/ppermute | solution.py:799
  284.1 37.7 %collective-permute-start.40 = (bf16[304,768]{1,0:T(8,128)(2,1)}, bf16[304,768]{1,0:T(8,128)(2,1)}, u32[]{:S(2)}, u32[]{:S(2)}) collective-permute-start(bf16[304,768]{1,0:T(8,128)(2,1)} %get-tuple-element.324.refs_0_), channel_id=1, source_target_pairs={{0,1},{1,0},{2,3},{3,2},{4,5},{5,4},{6,7},{7,6},{8,9},{9,8},{10,11... | collective-permute-start | bytes 1400840 | tf_op jit(solution)/shard_map/ppermute | solution.py:799
  285.6 36.2 %collective-permute-start.43 = (bf16[304,768]{1,0:T(8,128)(2,1)}, bf16[304,768]{1,0:T(8,128)(2,1)}, u32[]{:S(2)}, u32[]{:S(2)}) collective-permute-start(bf16[304,768]{1,0:T(8,128)(2,1)} %get-tuple-element.325.refs_1_), channel_id=1, source_target_pairs={{0,2},{1,3},{2,0},{3,1},{4,6},{5,7},{6,4},{7,5},{8,10},{9,11},{10,... | collective-permute-start | bytes 1400840 | tf_op jit(solution)/shard_map/ppermute | solution.py:799
  372.1 286.7 %reduce-scatter.7.cloned.1.call-start = ((), (), s32[]{:S(2)}) async-start(), calls=%async_computation.13 | async-start | bytes 10616832 | tf_op jit(solution)/shard_map/reduce_scatter | solution.py:1613
  440.6 37.6 %collective-permute-start.56 = (bf16[304,1536]{1,0:T(8,128)(2,1)}, bf16[304,1536]{1,0:T(8,128)(2,1)S(1)}, u32[]{:S(2)}, u32[]{:S(2)}) collective-permute-start(bf16[304,1536]{1,0:T(8,128)(2,1)} %get-tuple-element.398), channel_id=1, source_target_pairs={{0,1},{1,0},{2,3},{3,2},{4,5},{5,4},{6,7},{7,6},{8,9},{9,8},{10,11... | collective-permute-start | bytes 2801672 | tf_op jit(solution)/shard_map/ppermute | solution.py:799
  440.6 38.0 %collective-permute-start.57 = (bf16[304,1536]{1,0:T(8,128)(2,1)}, bf16[304,1536]{1,0:T(8,128)(2,1)S(1)}, u32[]{:S(2)}, u32[]{:S(2)}) collective-permute-start(bf16[304,1536]{1,0:T(8,128)(2,1)} %get-tuple-element.399), channel_id=1, source_target_pairs={{0,2},{1,3},{2,0},{3,1},{4,6},{5,7},{6,4},{7,5},{8,10},{9,11},{10,... | collective-permute-start | bytes 2801672 | tf_op jit(solution)/shard_map/ppermute | solution.py:799
  451.0 51.3 %collective-permute-start.50 = (bf16[304,768]{1,0:T(8,128)(2,1)}, bf16[304,768]{1,0:T(8,128)(2,1)}, u32[]{:S(2)}, u32[]{:S(2)}) collective-permute-start(bf16[304,768]{1,0:T(8,128)(2,1)} %get-tuple-element.413.refs_0_), channel_id=1, source_target_pairs={{0,1},{1,0},{2,3},{3,2},{4,5},{5,4},{6,7},{7,6},{8,9},{9,8},{10,11... | collective-permute-start | bytes 1400840 | tf_op jit(solution)/shard_map/ppermute | solution.py:799
  453.0 49.2 %collective-permute-start.53 = (bf16[304,768]{1,0:T(8,128)(2,1)}, bf16[304,768]{1,0:T(8,128)(2,1)}, u32[]{:S(2)}, u32[]{:S(2)}) collective-permute-start(bf16[304,768]{1,0:T(8,128)(2,1)} %get-tuple-element.414.refs_1_), channel_id=1, source_target_pairs={{0,2},{1,3},{2,0},{3,1},{4,6},{5,7},{6,4},{7,5},{8,10},{9,11},{10,... | collective-permute-start | bytes 1400840 | tf_op jit(solution)/shard_map/ppermute | solution.py:799
  518.0 171.8 %reduce-scatter.9.cloned.1.call-start = ((), (), s32[]{:S(2)}) async-start(), calls=%async_computation.14 | async-start | bytes 2654208 | tf_op jit(solution)/shard_map/reduce_scatter | solution.py:1613
  543.2 36.7 %collective-permute-start.60 = (bf16[304,1536]{1,0:T(8,128)(2,1)}, bf16[304,1536]{1,0:T(8,128)(2,1)}, u32[]{:S(2)}, u32[]{:S(2)}) collective-permute-start(bf16[304,1536]{1,0:T(8,128)(2,1)} %copy-done.225), channel_id=1, source_target_pairs={{0,1},{1,0},{2,3},{3,2},{4,5},{5,4},{6,7},{7,6},{8,9},{9,8},{10,11... | collective-permute-start | bytes 2801672 | tf_op jit(solution)/shard_map/ppermute | solution.py:799
  543.3 36.6 %collective-permute-start.61 = (bf16[304,1536]{1,0:T(8,128)(2,1)}, bf16[304,1536]{1,0:T(8,128)(2,1)}, u32[]{:S(2)}, u32[]{:S(2)}) collective-permute-start(bf16[304,1536]{1,0:T(8,128)(2,1)} %copy-done.224), channel_id=1, source_target_pairs={{0,2},{1,3},{2,0},{3,1},{4,6},{5,7},{6,4},{7,5},{8,10},{9,11},{10,... | collective-permute-start | bytes 2801672 | tf_op jit(solution)/shard_map/ppermute | solution.py:799
  610.2 180.5 %reduce-scatter.11.cloned.1.call-start = ((), (), s32[]{:S(2)}) async-start(), calls=%async_computation.15 | async-start | bytes 7962624 | tf_op jit(solution)/shard_map/reduce_scatter | solution.py:1613
  610.2 45.7 %collective-permute-start.70 = (bf16[304,1536]{1,0:T(8,128)(2,1)}, bf16[304,1536]{1,0:T(8,128)(2,1)S(1)}, u32[]{:S(2)}, u32[]{:S(2)}) collective-permute-start(bf16[304,1536]{1,0:T(8,128)(2,1)} %copy-done.223), channel_id=1, source_target_pairs={{0,1},{1,0},{2,3},{3,2},{4,5},{5,4},{6,7},{7,6},{8,9},{9,8},{10,11... | collective-permute-start | bytes 2801672 | tf_op jit(solution)/shard_map/ppermute | solution.py:799
  612.2 43.7 %collective-permute-start.71 = (bf16[304,1536]{1,0:T(8,128)(2,1)}, bf16[304,1536]{1,0:T(8,128)(2,1)S(1)}, u32[]{:S(2)}, u32[]{:S(2)}) collective-permute-start(bf16[304,1536]{1,0:T(8,128)(2,1)} %copy-done.222), channel_id=1, source_target_pairs={{0,2},{1,3},{2,0},{3,1},{4,6},{5,7},{6,4},{7,5},{8,10},{9,11},{10,... | collective-permute-start | bytes 2801672 | tf_op jit(solution)/shard_map/ppermute | solution.py:799
  764.7 41.4 %all-to-all-start.2 = ((f32[8,2,1536]{2,1,0:T(2,128)}), f32[8,2,1536]{2,1,0:T(2,128)S(1)}, u32[]{:S(2)}, u32[]{:S(2)}) async-start(f32[8,2,1536]{2,1,0:T(2,128)} %copy.207), calls=%async_computation.6 | async-start | bytes 196608 | tf_op jit(solution)/shard_map/all_to_all | solution.py:1617
  779.2 46.2 %collective-permute-start.77 = (bf16[304,768]{1,0:T(8,128)(2,1)}, bf16[304,768]{1,0:T(8,128)(2,1)}, u32[]{:S(2)}, u32[]{:S(2)}) collective-permute-start(bf16[304,768]{1,0:T(8,128)(2,1)} %add_convert_fusion.2), channel_id=1, source_target_pairs={{0,2},{1,3},{2,0},{3,1},{4,6},{5,7},{6,4},{7,5},{8,10},{9,11},{10,... | collective-permute-start | bytes 1400840 | tf_op jit(solution)/shard_map/ppermute | solution.py:799
  789.3 36.1 %collective-permute-start.76 = (bf16[304,768]{1,0:T(8,128)(2,1)}, bf16[304,768]{1,0:T(8,128)(2,1)}, u32[]{:S(2)}, u32[]{:S(2)}) collective-permute-start(bf16[304,768]{1,0:T(8,128)(2,1)} %add_convert_fusion.3), channel_id=1, source_target_pairs={{0,1},{1,0},{2,3},{3,2},{4,5},{5,4},{6,7},{7,6},{8,9},{9,8},{10,11... | collective-permute-start | bytes 1400840 | tf_op jit(solution)/shard_map/ppermute | solution.py:799
  792.8 51.6 %collective-permute-start.83 = (bf16[1,2,48,1536]{3,2,0,1:T(8,128)(2,1)}, bf16[1,2,48,1536]{3,2,0,1:T(8,128)(2,1)}, u32[]{:S(2)}, u32[]{:S(2)}) collective-permute-start(bf16[1,2,48,1536]{3,2,0,1:T(8,128)(2,1)} %get-tuple-element.531), channel_id=1, source_target_pairs={{0,0},{4,1},{8,2},{1,3},{5,4},{2,5},{6,6},{10,7},{3,8},{7,9},{11,1... | collective-permute-start | bytes 884744 | tf_op jit(solution)/shard_map/ppermute | solution.py:1583
  797.1 46.2 %collective-permute-start.82 = (bf16[1,2,48,1536]{3,2,0,1:T(8,128)(2,1)}, bf16[1,2,48,1536]{3,2,0,1:T(8,128)(2,1)}, u32[]{:S(2)}, u32[]{:S(2)}) collective-permute-start(bf16[1,2,48,1536]{3,2,0,1:T(8,128)(2,1)} %get-tuple-element.532), channel_id=1, source_target_pairs={{0,0},{4,1},{8,2},{1,3},{5,4},{9,5},{2,6},{6,7},{3,8},{7,9},{11,10... | collective-permute-start | bytes 884744 | tf_op jit(solution)/shard_map/ppermute | solution.py:1583
  799.7 45.7 %collective-permute-start.84 = (bf16[1,2,48,1536]{3,2,0,1:T(8,128)(2,1)}, bf16[1,2,48,1536]{3,2,0,1:T(8,128)(2,1)}, u32[]{:S(2)}, u32[]{:S(2)}) collective-permute-start(bf16[1,2,48,1536]{3,2,0,1:T(8,128)(2,1)} %get-tuple-element.530), channel_id=1, source_target_pairs={{0,0},{4,1},{1,2},{5,3},{9,4},{2,5},{6,6},{10,7},{3,8},{7,9},{8,10... | collective-permute-start | bytes 884744 | tf_op jit(solution)/shard_map/ppermute | solution.py:1583
  (317 other events, 3210.5 us)
Sparse Core Ops, SparseCore 0:
  31.4 78.0 all-gather.4
  111.7 31.1 all-gather.6
  144.5 89.1 all-gather.8
  235.2 89.1 all-gather.10
  372.3 101.4 reduce-scatter.4
  518.1 101.9 reduce-scatter.6
  623.0 31.1 reduce-scatter.8
  689.9 81.5 reduce-scatter.10

commit v9 on v7

--- a/solution.py
+++ b/solution.py
@@ -563,19 +563,19 @@
 
 
 WEIGHT = {
-    "attention": 0.17,
-    "attention_back": 0.32,
-    "project": 0.13,
-    "partial_sums": 0.05,
-    "middle": 0.05,
-    "hidden": 0.18,
-    "outer_sums": 0.18,
-    "hidden_back": 0.2,
-    "middle_back": 0.07,
-    "attended_back": 0.06,
-    "project_back": 0.12,
-    "result": 0.07,
-    "input_back": 0.09,
+    "attention": 6.8,
+    "attention_back": 12.8,
+    "project": 5.2,
+    "partial_sums": 2,
+    "middle": 2,
+    "hidden": 7.2,
+    "outer_sums": 7.2,
+    "hidden_back": 8,
+    "middle_back": 2.8,
+    "attended_back": 2.4,
+    "project_back": 4.8,
+    "result": 2.8,
+    "input_back": 3.6,
 }
 
 

time: 775 us -> 762 us (0.983)
  other arithmetic: 36.9 us -> 27.7 us
  transfers between devices with their start and end apart: 99 -> 99, of which waited for: 30 -> 34; matrix products, arithmetic and copies ran while one was open for 10% -> 9% of each run, Pallas kernels for 47% -> 48%
where the time goes in v9:
time: 762 us; the launch traced here: 757 us
  Pallas kernels  365 us (48%)
  waiting for transfers between devices  164 us (22%)
  starting transfers between devices  130 us (17%)
  local copies, waits for them, and re-layouts  45.1 us (6%)
  other arithmetic  27.7 us (4%)
  between operations  21.9 us (3%)
    pallas_call x23, Pallas kernels, run(): pl.pallas_call(kernel, in_specs=specs, out_specs=out_specs, out_shape=[ja...  266 us
    ppermute x73, waiting for transfers between devices, flip(): return lax.ppermute(values, 'seq', [(i, i ^ bit) for i in range(4)])  129 us
    ppermute x73, starting transfers between devices, flip(): return lax.ppermute(values, 'seq', [(i, i ^ bit) for i in range(4)])  80.6 us
    pallas_call x2, Pallas kernels, attention_back(): pl.pallas_call(functools.partial(attention_back_kernel, 512, LOG2E / math...  64.5 us
    pallas_call x2, Pallas kernels, attention(): pl.pallas_call(functools.partial(attention_kernel, 256, LOG2E / math.sqrt...  34.3 us
    ppermute x8, waiting for transfers between devices, gather_small(): held = jnp.concatenate([held, lax.ppermute(held, axis, pairs)])  33.1 us
    all_to_all x4, starting transfers between devices, swap(): return lax.all_to_all(values, axis, 0, 0, tiled=True)  20.8 us
    ppermute x6, starting transfers between devices, move_units(): lax.ppermute(lax.dynamic_index_in_dim(units, slot, 0, keepdims=True), ('b...  19.1 us
  transfers between devices with their start and end apart: 99, of which 34 were waited for; matrix products, arithmetic and copies ran while one was open for 9% of the time, Pallas kernels for 48%

profile of v9, /device:TPU:16, one launch (start us, length us, event | category | flops | bytes accessed | tf_op | source)
XLA Modules:
  0.0 757.1 jit_solution(3181610650177214592)
XLA Ops:
  44.0 14.8 %collective-permute-done.3.refs_2_.refs_5_ = bf16[2,304,768]{2,1,0:T(8,128)(2,1)S(1)} collective-permute-done((bf16[2,304,768]{2,1,0:T(8,128)(2,1)S(1)}, bf16[2,304,768]{2,1,0:T(8,128)(2,1)S(1)}, u32[]{:S(2)}, u32[]{:S(2)}) %collective-permute-start.3) | collective-permute-done | bytes 933920 | tf_op jit(solution)/shard_map/ppermute | solution.py:799
  116.8 8.9 %collective-permute-done.15 = f32[1,8,1920]{2,1,0:T(8,128)S(1)} collective-permute-done((f32[1,8,1920]{2,1,0:T(8,128)S(1)}, f32[1,8,1920]{2,1,0:T(8,128)S(1)}, u32[]{:S(2)}, u32[]{:S(2)}) %collective-permute-start.15) | collective-permute-done | bytes 61472 | tf_op jit(solution)/shard_map/ppermute | solution.py:1599
  137.6 13.0 %project.2 = (bf16[1024,1152]{1,0:T(8,128)(2,1)}, bf16[192,1152]{1,0:T(8,128)(2,1)}, bf16[1024,1536]{1,0:T(8,128)(2,1)}, bf16[192,1536]{1,0:T(8,128)(2,1)}) custom-call(bf16[2,304,768]{2,1,0:T(8,128)(2,1)} %copy-done.11, bf16[2,304,768]{2,1,0:T(8,128)(2,1)} %copy-done.10, bf16[2,304,768]{2,1,0:T(8,128)(2,1)} %copy-done.52, ...), custom_call_target="tpu_custom_call" | custom-call | flops 5980000256 | bytes 1 | tf_op jit(solution)/shard_map/project/pallas_call | solution.py:919
  151.7 17.3 %attention.2 = (bf16[1024,384]{1,0:T(8,128)(2,1)}, bf16[192,384]{1,0:T(8,128)(2,1)}, f32[1024,384]{1,0:T(8,128)}, f32[192,384]{1,0:T(8,128)}) custom-call(f32[1216,128]{1,0:T(8,128)} %broadcast_in_dim.119.bias_ref.refs_0_, f32[1,1]{1,0:T(1,128)} %bitcast.6.floor_ref, bf16[1024,1152]{1,0:T(8,128)(2,1)} %get-tuple-element.275.qi.ki.vi.refs_1_.refs_3_.refs_5_, ...), custom_call_target="tpu_custom_call" | custom-call | flops 7820000256 | bytes 1 | tf_op jit(solution)/shard_map/attention/pallas_call | solution.py:657
  181.6 13.0 %project.3 = (bf16[1024,1152]{1,0:T(8,128)(2,1)}, bf16[192,1152]{1,0:T(8,128)(2,1)}, bf16[1024,1536]{1,0:T(8,128)(2,1)}, bf16[192,1536]{1,0:T(8,128)(2,1)}) custom-call(bf16[2,304,768]{2,1,0:T(8,128)(2,1)} %copy-done.11, bf16[2,304,768]{2,1,0:T(8,128)(2,1)} %copy-done.10, bf16[2,304,768]{2,1,0:T(8,128)(2,1)} %copy-done.52, ...), custom_call_target="tpu_custom_call" | custom-call | flops 5980000256 | bytes 1 | tf_op jit(solution)/shard_map/project/pallas_call | solution.py:919
  195.7 17.1 %attention.3 = (bf16[1024,384]{1,0:T(8,128)(2,1)}, bf16[192,384]{1,0:T(8,128)(2,1)}, f32[1024,384]{1,0:T(8,128)}, f32[192,384]{1,0:T(8,128)}) custom-call(f32[1216,128]{1,0:T(8,128)} %broadcast_in_dim.133.bias_ref.refs_0_, f32[1,1]{1,0:T(1,128)} %bitcast.38.floor_ref, bf16[1024,1152]{1,0:T(8,128)(2,1)} %get-tuple-element.297.qi.ki.vi.refs_1_.refs_3_.refs_5_, ...), custom_call_target="tpu_custom_call" | custom-call | flops 7820000256 | bytes 1 | tf_op jit(solution)/shard_map/attention/pallas_call | solution.py:657
  238.6 13.5 %collective-permute-done.36.refs_1_ = bf16[304,1536]{1,0:T(8,128)(2,1)S(1)} collective-permute-done((bf16[304,1536]{1,0:T(8,128)(2,1)}, bf16[304,1536]{1,0:T(8,128)(2,1)S(1)}, u32[]{:S(2)}, u32[]{:S(2)}) %collective-permute-start.36) | collective-permute-done | bytes 933920 | tf_op jit(solution)/shard_map/ppermute | solution.py:799
  264.1 7.9 %collective-permute-done.39.refs_4_ = bf16[304,768]{1,0:T(8,128)(2,1)S(1)} collective-permute-done((bf16[304,768]{1,0:T(8,128)(2,1)S(1)}, bf16[304,768]{1,0:T(8,128)(2,1)S(1)}, u32[]{:S(2)}, u32[]{:S(2)}) %collective-permute-start.39) | collective-permute-done | bytes 466976 | tf_op jit(solution)/shard_map/ppermute | solution.py:799
  284.1 7.8 %collective-permute-done.32.refs_6_ = bf16[304,768]{1,0:T(8,128)(2,1)} collective-permute-done((bf16[304,768]{1,0:T(8,128)(2,1)}, bf16[304,768]{1,0:T(8,128)(2,1)}, u32[]{:S(2)}, u32[]{:S(2)}) %collective-permute-start.32) | collective-permute-done | bytes 466976 | tf_op jit(solution)/shard_map/ppermute | solution.py:799
  293.6 17.2 %hidden.2 = (bf16[1024,1536]{1,0:T(8,128)(2,1)}, bf16[192,1536]{1,0:T(8,128)(2,1)}, bf16[1024,1536]{1,0:T(8,128)(2,1)}, bf16[192,1536]{1,0:T(8,128)(2,1)}, bf16[...) custom-call(bf16[304,768]{1,0:T(8,128)(2,1)} %get-tuple-element.303.r, ...), custom_call_target="tpu_custom_call" | custom-call | flops 8280000000 | bytes 1 | tf_op jit(solution)/shard_map/hidden/pallas_call | solution.py:919
  313.0 6.6 collective-permute-done.44.refs_6_
  321.1 16.6 %hidden.3 = (bf16[1024,1536]{1,0:T(8,128)(2,1)}, bf16[192,1536]{1,0:T(8,128)(2,1)}, bf16[1024,1536]{1,0:T(8,128)(2,1)}, bf16[192,1536]{1,0:T(8,128)(2,1)}, bf16[...) custom-call(bf16[304,768]{1,0:T(8,128)(2,1)} %get-tuple-element.324.r, ...), custom_call_target="tpu_custom_call" | custom-call | flops 8280000000 | bytes 1 | tf_op jit(solution)/shard_map/hidden/pallas_call | solution.py:919
  337.7 18.0 %outer_sums.4 = bf16[2,1536,1536]{2,1,0:T(8,128)(2,1)} custom-call(bf16[1024,1536]{1,0:T(8,128)(2,1)} %get-tuple-element.370.refs_0_, bf16[1024,1536]{1,0:T(8,128)(2,1)} %get-tuple-element.340.refs_1_.refs_0_, bf16[192,1536]{1,0:T(8,128)(2,1)} %get-tuple-element.371.refs_2_.refs_1_, bf16[192,1536]{1,0:T(8,128)(2,1)} %get-tuple-element.341.refs_3_.refs_1_, ...), custom_call_target="tpu_custom_call" | custom-call | flops 8280000000 | bytes 1 | tf_op jit(solution)/shard_map/outer_sums/pallas_call | solution.py:919
  356.1 18.1 %hidden_back.2 = (bf16[1024,1536]{1,0:T(8,128)(2,1)}, bf16[192,1536]{1,0:T(8,128)(2,1)}, f32[2,1536]{1,0:T(2,128)}, bf16[304,1536]{1,0:T(8,128)(2,1)}, bf16[304,...) custom-call(bf16[1024,1536]{1,0:T(8,128)(2,1)} %get-tuple-element.340.refs_1_, ...), custom_call_target="tpu_custom_call" | custom-call | flops 9200000000 | bytes 1 | tf_op jit(solution)/shard_map/hidden_back/pallas_call | solution.py:919
  376.3 18.6 %hidden_back.3 = (bf16[1024,1536]{1,0:T(8,128)(2,1)}, bf16[192,1536]{1,0:T(8,128)(2,1)}, f32[2,1536]{1,0:T(2,128)}, bf16[304,1536]{1,0:T(8,128)(2,1)}, bf16[304,...) custom-call(bf16[1024,1536]{1,0:T(8,128)(2,1)} %get-tuple-element.348.refs_5_, ...), custom_call_target="tpu_custom_call" | custom-call | flops 9200000000 | bytes 1 | tf_op jit(solution)/shard_map/hidden_back/pallas_call | solution.py:919
  397.3 11.6 %collective-permute-done.49.refs_4_ = bf16[304,768]{1,0:T(8,128)(2,1)S(1)} collective-permute-done((bf16[304,768]{1,0:T(8,128)(2,1)S(1)}, bf16[304,768]{1,0:T(8,128)(2,1)S(1)}, u32[]{:S(2)}, u32[]{:S(2)}) %collective-permute-start.49) | collective-permute-done | bytes 466976 | tf_op jit(solution)/shard_map/ppermute | solution.py:799
  412.4 7.5 middle_back.2
  422.5 17.7 %partial_sums.5 = (bf16[304,1536]{1,0:T(8,128)(2,1)}, bf16[304,1536]{1,0:T(8,128)(2,1)}, bf16[304,1536]{1,0:T(8,128)(2,1)}, bf16[304,768]{1,0:T(8,128)(2,1)}, bf...) custom-call(bf16[1024,1536]{1,0:T(8,128)(2,1)} %get-tuple-element.37, ...), custom_call_target="tpu_custom_call" | custom-call | flops 2300000000 | bytes 1 | tf_op jit(solution)/shard_map/partial_sums/pallas_call | solution.py:919
  444.1 18.4 %outer_sums.5 = bf16[2,1536,1536]{2,1,0:T(8,128)(2,1)} custom-call(bf16[1024,1536]{1,0:T(8,128)(2,1)} %get-tuple-element.388.refs_0_, bf16[1024,1536]{1,0:T(8,128)(2,1)} %get-tuple-element.330.refs_1_, bf16[192,1536]{1,0:T(8,128)(2,1)} %get-tuple-element.389.refs_2_, bf16[192,1536]{1,0:T(8,128)(2,1)} %get-tuple-element.331.refs_3_, ...), custom_call_target="tpu_custom_call" | custom-call | flops 8280000000 | bytes 1 | tf_op jit(solution)/shard_map/outer_sums/pallas_call | solution.py:919
  462.6 7.4 middle_back.3
  474.9 9.0 %collective-permute-done.54.refs_6_ = bf16[304,768]{1,0:T(8,128)(2,1)S(1)} collective-permute-done((bf16[304,768]{1,0:T(8,128)(2,1)}, bf16[304,768]{1,0:T(8,128)(2,1)S(1)}, u32[]{:S(2)}, u32[]{:S(2)}) %collective-permute-start.54) | collective-permute-done | bytes 466976 | tf_op jit(solution)/shard_map/ppermute | solution.py:799
  493.6 32.3 %attention_back.2 = (bf16[1024,1152]{1,0:T(8,128)(2,1)}, bf16[192,1152]{1,0:T(8,128)(2,1)}) custom-call(f32[1216,128]{1,0:T(8,128)} %broadcast_in_dim.119.bias_ref.refs_0_, bf16[1024,1152]{1,0:T(8,128)(2,1)} %get-tuple-element.275.qi.ki.vi.refs_1_.refs_3_.refs_5_, bf16[192,1152]{1,0:T(8,128)(2,1)} %get-tuple-element.276.qt.kt.vt.refs_2_.refs_4_.refs_6_, ...), custom_call_target="tpu_custom_call" | custom-call | flops 14720000000 | bytes 1 | tf_op jit(solution)/shard_map/attention_back/pallas_call | solution.py:766
  528.1 12.9 %project_back.2 = (f32[4,1536]{1,0:T(4,128)}, f32[2,1152]{1,0:T(2,128)}, bf16[304,1536]{1,0:T(8,128)(2,1)}, bf16[304,1536]{1,0:T(8,128)(2,1)}, bf16[304,1536]{1,...) custom-call(bf16[1024,1152]{1,0:T(8,128)(2,1)} %get-tuple-element.435.refs_0_, ...), custom_call_target="tpu_custom_call" | custom-call | flops 5520000000 | bytes 1 | tf_op jit(solution)/shard_map/project_back/pallas_call | solution.py:919
  548.0 8.8 %outer_sums.6 = bf16[2,1536,384]{2,1,0:T(8,128)(2,1)} custom-call(bf16[1024,1536]{1,0:T(8,128)(2,1)} %get-tuple-element.452.refs_0_, bf16[1024,384]{1,0:T(8,128)(2,1)} %get-tuple-element.281.refs_0_.refs_7_.refs_1_, bf16[192,1536]{1,0:T(8,128)(2,1)} %get-tuple-element.453.refs_2_, bf16[192,384]{1,0:T(8,128)(2,1)} %get-tuple-element.282.refs_1_.refs_8_.refs_3_, ...), custom_call_target="tpu_custom_call" | custom-call | flops 8280000000 | bytes 1 | tf_op jit(solution)/shard_map/outer_sums/pallas_call | solution.py:919
  558.9 32.2 %attention_back.3 = (bf16[1024,1152]{1,0:T(8,128)(2,1)}, bf16[192,1152]{1,0:T(8,128)(2,1)}) custom-call(f32[1216,128]{1,0:T(8,128)} %broadcast_in_dim.133.bias_ref.refs_0_, bf16[1024,1152]{1,0:T(8,128)(2,1)} %get-tuple-element.297.qi.ki.vi.refs_1_.refs_3_.refs_5_, bf16[192,1152]{1,0:T(8,128)(2,1)} %get-tuple-element.298.qt.kt.vt.refs_2_.refs_4_.refs_6_, ...), custom_call_target="tpu_custom_call" | custom-call | flops 14720000000 | bytes 1 | tf_op jit(solution)/shard_map/attention_back/pallas_call | solution.py:766
  595.1 14.7 %outer_sums.7 = bf16[2,1152,1536]{2,1,0:T(8,128)(2,1)} custom-call(bf16[1024,1152]{1,0:T(8,128)(2,1)} %get-tuple-element.435.refs_0_, bf16[1024,1536]{1,0:T(8,128)(2,1)} %get-tuple-element.466.refs_1_, bf16[192,1152]{1,0:T(8,128)(2,1)} %get-tuple-element.436.refs_1_.refs_2_, bf16[192,1536]{1,0:T(8,128)(2,1)} %get-tuple-element.467.refs_3_, ...), custom_call_target="tpu_custom_call" | custom-call | flops 8280000000 | bytes 1 | tf_op jit(solution)/shard_map/outer_sums/pallas_call | solution.py:919
  615.3 12.9 %project_back.3 = (f32[4,1536]{1,0:T(4,128)}, f32[2,1152]{1,0:T(2,128)}, bf16[304,1536]{1,0:T(8,128)(2,1)}, bf16[304,1536]{1,0:T(8,128)(2,1)}, bf16[304,1536]{1,...) custom-call(bf16[1024,1152]{1,0:T(8,128)(2,1)} %get-tuple-element.473.refs_4_.refs_0_, ...), custom_call_target="tpu_custom_call" | custom-call | flops 5520000000 | bytes 1 | tf_op jit(solution)/shard_map/project_back/pallas_call | solution.py:919
  629.9 8.0 %result.1 = (bf16[2,256,1536]{2,1,0:T(8,128)(2,1)}, bf16[2,48,1536]{2,1,0:T(8,128)(2,1)}, f32[8,1536]{1,0:T(8,128)}) custom-call(bf16[304,1536]{1,0:T(8,128)(2,1)} %get-tuple-element.480.refs_0_, bf16[304,1536]{1,0:T(8,128)(2,1)} %copy-done.3, bf16[304,1536]{1,0:T(8,128)(2,1)} %copy-done.4, bf16[304,768]{1,0:T(8,128)(2,1)} %collective-permute-done.68.refs_3_, ...), custom_call_target="tpu_custom_call" | custom-call | flops 3220000000 | bytes 1 | tf_op jit(solution)/shard_map/result/pallas_call | solution.py:919
  651.0 8.0 %all-to-all-start.1 = ((f32[8,1,1920]{2,1,0:T(1,128)}), f32[8,1,1920]{2,1,0:T(1,128)S(1)}, u32[]{:S(2)}, u32[]{:S(2)}) async-start(f32[8,1,1920]{2,1,0:T(1,128)} %all_to_all.18), calls=%async_computation.5 | async-start | bytes 122880 | tf_op jit(solution)/shard_map/all_to_all | solution.py:1610
  677.2 11.3 %collective-permute-done.74.refs_1_ = bf16[304,1536]{1,0:T(8,128)(2,1)} collective-permute-done((bf16[304,1536]{1,0:T(8,128)(2,1)}, bf16[304,1536]{1,0:T(8,128)(2,1)}, u32[]{:S(2)}, u32[]{:S(2)}) %collective-permute-start.74) | collective-permute-done | bytes 933920 | tf_op jit(solution)/shard_map/ppermute | solution.py:799
  708.8 15.7 %collective-permute-done.77.refs_4_ = bf16[304,768]{1,0:T(8,128)(2,1)} collective-permute-done((bf16[304,768]{1,0:T(8,128)(2,1)S(1)}, bf16[304,768]{1,0:T(8,128)(2,1)}, u32[]{:S(2)}, u32[]{:S(2)}) %collective-permute-start.77) | collective-permute-done | bytes 466976 | tf_op jit(solution)/shard_map/ppermute | solution.py:799
  724.5 9.4 %input_back.1 = (f32[2,256,1536]{2,1,0:T(8,128)}, f32[2,40,1536]{2,1,0:T(8,128)}) custom-call(bf16[304,1536]{1,0:T(8,128)(2,1)} %get-tuple-element.503.refs_0_, bf16[304,1536]{1,0:T(8,128)(2,1)} %collective-permute-done.74.refs_1_, bf16[304,1536]{1,0:T(8,128)(2,1)} %collective-permute-done.75.refs_2_, bf16[304,768]{1,0:T(8,128)(2,1)} %collective-permute-done.76.refs_3_, ...), custom_call_target="tpu_custom_call" | custom-call | flops 4140000000 | bytes 1 | tf_op jit(solution)/shard_map/input_back/pallas_call | solution.py:919
  (516 shorter events, 289.2 us)
Async XLA Ops:
  7.2 130.4 %all-gather.5.cloned.1.call-start = ((), (), s32[]{:S(2)}) async-start(), calls=%async_computation.8 | async-start | bytes 7962624 | tf_op jit(solution)/shard_map/all_gather | solution.py:1584
  30.3 144.1 %all-gather.7.cloned.1.call-start = ((), (), s32[]{:S(2)}) async-start(), calls=%async_computation.9 | async-start | bytes 2654208 | tf_op jit(solution)/shard_map/all_gather | solution.py:1584
  80.5 213.2 %all-gather.9.cloned.1.call-start = ((), (), s32[]{:S(2)}) async-start(), calls=%async_computation.10 | async-start | bytes 10616832 | tf_op jit(solution)/shard_map/all_gather | solution.py:1584
  81.2 274.9 %all-gather.11.cloned.1.call-start = ((), (), s32[]{:S(2)}) async-start(), calls=%async_computation.11 | async-start | bytes 10616832 | tf_op jit(solution)/shard_map/all_gather | solution.py:1584
  81.8 403.0 %reduce-scatter.5.cloned.1.call-start = ((), (), s32[]{:S(2)}) async-start(), calls=%async_computation.12 | async-start | bytes 10616832 | tf_op jit(solution)/shard_map/reduce_scatter | solution.py:1606
  131.4 37.5 %collective-permute-start.19 = (bf16[2,304,768]{2,1,0:T(8,128)(2,1)}, bf16[2,304,768]{2,1,0:T(8,128)(2,1)}, u32[]{:S(2)}, u32[]{:S(2)}) collective-permute-start(bf16[2,304,768]{2,1,0:T(8,128)(2,1)} %get-tuple-element.279.refs_8_.refs_5_.refs_10_), channel_id=1, source_target_pairs={{0,2},{1,3},{2,0},{3,1},{4,6},{5,7},{6,4},{7,5},{8,10},{9,11},{10,... | collective-permute-start | bytes 2801672 | tf_op jit(solution)/shard_map/ppermute | solution.py:799
  131.9 37.0 %collective-permute-start.17 = (bf16[2,304,768]{2,1,0:T(8,128)(2,1)}, bf16[2,304,768]{2,1,0:T(8,128)(2,1)}, u32[]{:S(2)}, u32[]{:S(2)}) collective-permute-start(bf16[2,304,768]{2,1,0:T(8,128)(2,1)} %get-tuple-element.279.refs_8_.refs_5_.refs_10_), channel_id=1, source_target_pairs={{0,1},{1,0},{2,3},{3,2},{4,5},{5,4},{6,7},{7,6},{8,9},{9,8},{10,11... | collective-permute-start | bytes 2801672 | tf_op jit(solution)/shard_map/ppermute | solution.py:799
  133.4 38.9 %collective-permute-start.20 = (bf16[2,304,768]{2,1,0:T(8,128)(2,1)S(1)}, bf16[2,304,768]{2,1,0:T(8,128)(2,1)}, u32[]{:S(2)}, u32[]{:S(2)}) collective-permute-start(bf16[2,304,768]{2,1,0:T(8,128)(2,1)S(1)} %get-tuple-element.280.refs_9_.refs_6_.refs_11_), channel_id=1, source_target_pairs={{0,2},{1,3},{2,0},{3,1},{4,6},{5,7},{6,4},{7,5},{8,10},{9,11},{10,... | collective-permute-start | bytes 2801672 | tf_op jit(solution)/shard_map/ppermute | solution.py:799
  135.2 37.1 %collective-permute-start.18 = (bf16[2,304,768]{2,1,0:T(8,128)(2,1)S(1)}, bf16[2,304,768]{2,1,0:T(8,128)(2,1)}, u32[]{:S(2)}, u32[]{:S(2)}) collective-permute-start(bf16[2,304,768]{2,1,0:T(8,128)(2,1)S(1)} %get-tuple-element.280.refs_9_.refs_6_.refs_11_), channel_id=1, source_target_pairs={{0,1},{1,0},{2,3},{3,2},{4,5},{5,4},{6,7},{7,6},{8,9},{9,8},{10,11... | collective-permute-start | bytes 2801672 | tf_op jit(solution)/shard_map/ppermute | solution.py:799
  172.4 42.8 %collective-permute-start.34 = (bf16[2,304,768]{2,1,0:T(8,128)(2,1)}, bf16[2,304,768]{2,1,0:T(8,128)(2,1)S(1)}, u32[]{:S(2)}, u32[]{:S(2)}) collective-permute-start(bf16[2,304,768]{2,1,0:T(8,128)(2,1)} %collective-permute-done.17.refs_10_), channel_id=1, source_target_pairs={{0,2},{1,3},{2,0},{3,1},{4,6},{5,7},{6,4},{7,5},{8,10},{9,11},{10,... | collective-permute-start | bytes 2801672 | tf_op jit(solution)/shard_map/ppermute | solution.py:799
  174.1 41.1 %collective-permute-start.35 = (bf16[2,304,768]{2,1,0:T(8,128)(2,1)}, bf16[2,304,768]{2,1,0:T(8,128)(2,1)}, u32[]{:S(2)}, u32[]{:S(2)}) collective-permute-start(bf16[2,304,768]{2,1,0:T(8,128)(2,1)} %collective-permute-done.20.refs_13_), channel_id=1, source_target_pairs={{0,1},{1,0},{2,3},{3,2},{4,5},{5,4},{6,7},{7,6},{8,9},{9,8},{10,11... | collective-permute-start | bytes 2801672 | tf_op jit(solution)/shard_map/ppermute | solution.py:799
  179.4 33.4 %collective-permute-start.24 = (bf16[304,1536]{1,0:T(8,128)(2,1)}, bf16[304,1536]{1,0:T(8,128)(2,1)S(1)}, u32[]{:S(2)}, u32[]{:S(2)}) collective-permute-start(bf16[304,1536]{1,0:T(8,128)(2,1)} %get-tuple-element.285), channel_id=1, source_target_pairs={{0,1},{1,0},{2,3},{3,2},{4,5},{5,4},{6,7},{7,6},{8,9},{9,8},{10,11... | collective-permute-start | bytes 2801672 | tf_op jit(solution)/shard_map/ppermute | solution.py:799
  355.8 239.3 %reduce-scatter.7.cloned.1.call-start = ((), (), s32[]{:S(2)}) async-start(), calls=%async_computation.13 | async-start | bytes 10616832 | tf_op jit(solution)/shard_map/reduce_scatter | solution.py:1606
  420.4 42.1 %collective-permute-start.50 = (bf16[304,768]{1,0:T(8,128)(2,1)}, bf16[304,768]{1,0:T(8,128)(2,1)}, u32[]{:S(2)}, u32[]{:S(2)}) collective-permute-start(bf16[304,768]{1,0:T(8,128)(2,1)} %get-tuple-element.413.refs_0_), channel_id=1, source_target_pairs={{0,1},{1,0},{2,3},{3,2},{4,5},{5,4},{6,7},{7,6},{8,9},{9,8},{10,11... | collective-permute-start | bytes 1400840 | tf_op jit(solution)/shard_map/ppermute | solution.py:799
  421.9 40.6 %collective-permute-start.53 = (bf16[304,768]{1,0:T(8,128)(2,1)}, bf16[304,768]{1,0:T(8,128)(2,1)}, u32[]{:S(2)}, u32[]{:S(2)}) collective-permute-start(bf16[304,768]{1,0:T(8,128)(2,1)} %get-tuple-element.414.refs_1_), channel_id=1, source_target_pairs={{0,2},{1,3},{2,0},{3,1},{4,6},{5,7},{6,4},{7,5},{8,10},{9,11},{10,... | collective-permute-start | bytes 1400840 | tf_op jit(solution)/shard_map/ppermute | solution.py:799
  470.0 139.9 %reduce-scatter.9.cloned.1.call-start = ((), (), s32[]{:S(2)}) async-start(), calls=%async_computation.14 | async-start | bytes 2654208 | tf_op jit(solution)/shard_map/reduce_scatter | solution.py:1606
  472.9 53.1 %collective-permute-start.62 = (bf16[304,768]{1,0:T(8,128)(2,1)S(1)}, bf16[304,768]{1,0:T(8,128)(2,1)}, u32[]{:S(2)}, u32[]{:S(2)}) collective-permute-start(bf16[304,768]{1,0:T(8,128)(2,1)S(1)} %copy-done.58), channel_id=1, source_target_pairs={{0,1},{1,0},{2,3},{3,2},{4,5},{5,4},{6,7},{7,6},{8,9},{9,8},{10,11... | collective-permute-start | bytes 1400840 | tf_op jit(solution)/shard_map/ppermute | solution.py:799
  474.2 51.8 %collective-permute-start.65 = (bf16[304,768]{1,0:T(8,128)(2,1)}, bf16[304,768]{1,0:T(8,128)(2,1)}, u32[]{:S(2)}, u32[]{:S(2)}) collective-permute-start(bf16[304,768]{1,0:T(8,128)(2,1)} %get-tuple-element.443.refs_1_), channel_id=1, source_target_pairs={{0,2},{1,3},{2,0},{3,1},{4,6},{5,7},{6,4},{7,5},{8,10},{9,11},{10,... | collective-permute-start | bytes 1400840 | tf_op jit(solution)/shard_map/ppermute | solution.py:799
  483.9 42.0 %collective-permute-start.63 = (bf16[304,768]{1,0:T(8,128)(2,1)}, bf16[304,768]{1,0:T(8,128)(2,1)}, u32[]{:S(2)}, u32[]{:S(2)}) collective-permute-start(bf16[304,768]{1,0:T(8,128)(2,1)} %get-tuple-element.443.refs_1_), channel_id=1, source_target_pairs={{0,1},{1,0},{2,3},{3,2},{4,5},{5,4},{6,7},{7,6},{8,9},{9,8},{10,11... | collective-permute-start | bytes 1400840 | tf_op jit(solution)/shard_map/ppermute | solution.py:799
  491.6 36.5 %collective-permute-start.60 = (bf16[304,1536]{1,0:T(8,128)(2,1)}, bf16[304,1536]{1,0:T(8,128)(2,1)S(1)}, u32[]{:S(2)}, u32[]{:S(2)}) collective-permute-start(bf16[304,1536]{1,0:T(8,128)(2,1)} %get-tuple-element.423), channel_id=1, source_target_pairs={{0,1},{1,0},{2,3},{3,2},{4,5},{5,4},{6,7},{7,6},{8,9},{9,8},{10,11... | collective-permute-start | bytes 2801672 | tf_op jit(solution)/shard_map/ppermute | solution.py:799
  493.0 35.1 %collective-permute-start.61 = (bf16[304,1536]{1,0:T(8,128)(2,1)}, bf16[304,1536]{1,0:T(8,128)(2,1)S(1)}, u32[]{:S(2)}, u32[]{:S(2)}) collective-permute-start(bf16[304,1536]{1,0:T(8,128)(2,1)} %get-tuple-element.424), channel_id=1, source_target_pairs={{0,2},{1,3},{2,0},{3,1},{4,6},{5,7},{6,4},{7,5},{8,10},{9,11},{10,... | collective-permute-start | bytes 2801672 | tf_op jit(solution)/shard_map/ppermute | solution.py:799
  556.8 139.4 %reduce-scatter.11.cloned.1.call-start = ((), (), s32[]{:S(2)}) async-start(), calls=%async_computation.15 | async-start | bytes 7962624 | tf_op jit(solution)/shard_map/reduce_scatter | solution.py:1606
  556.9 36.1 %collective-permute-start.70 = (bf16[304,1536]{1,0:T(8,128)(2,1)}, bf16[304,1536]{1,0:T(8,128)(2,1)S(1)}, u32[]{:S(2)}, u32[]{:S(2)}) collective-permute-start(bf16[304,1536]{1,0:T(8,128)(2,1)} %get-tuple-element.462), channel_id=1, source_target_pairs={{0,1},{1,0},{2,3},{3,2},{4,5},{5,4},{6,7},{7,6},{8,9},{9,8},{10,11... | collective-permute-start | bytes 2801672 | tf_op jit(solution)/shard_map/ppermute | solution.py:799
  558.3 34.7 %collective-permute-start.71 = (bf16[304,1536]{1,0:T(8,128)(2,1)}, bf16[304,1536]{1,0:T(8,128)(2,1)S(1)}, u32[]{:S(2)}, u32[]{:S(2)}) collective-permute-start(bf16[304,1536]{1,0:T(8,128)(2,1)} %get-tuple-element.463), channel_id=1, source_target_pairs={{0,2},{1,3},{2,0},{3,1},{4,6},{5,7},{6,4},{7,5},{8,10},{9,11},{10,... | collective-permute-start | bytes 2801672 | tf_op jit(solution)/shard_map/ppermute | solution.py:799
  649.1 39.4 %collective-permute-start.74 = (bf16[304,1536]{1,0:T(8,128)(2,1)}, bf16[304,1536]{1,0:T(8,128)(2,1)}, u32[]{:S(2)}, u32[]{:S(2)}) collective-permute-start(bf16[304,1536]{1,0:T(8,128)(2,1)} %get-tuple-element.493), channel_id=1, source_target_pairs={{0,1},{1,0},{2,3},{3,2},{4,5},{5,4},{6,7},{7,6},{8,9},{9,8},{10,11... | collective-permute-start | bytes 2801672 | tf_op jit(solution)/shard_map/ppermute | solution.py:799
  649.6 41.9 %collective-permute-start.75 = (bf16[304,1536]{1,0:T(8,128)(2,1)}, bf16[304,1536]{1,0:T(8,128)(2,1)}, u32[]{:S(2)}, u32[]{:S(2)}) collective-permute-start(bf16[304,1536]{1,0:T(8,128)(2,1)} %get-tuple-element.494), channel_id=1, source_target_pairs={{0,2},{1,3},{2,0},{3,1},{4,6},{5,7},{6,4},{7,5},{8,10},{9,11},{10,... | collective-permute-start | bytes 2801672 | tf_op jit(solution)/shard_map/ppermute | solution.py:799
  664.4 31.7 %all-to-all-start.2 = ((f32[8,2,1536]{2,1,0:T(2,128)}), f32[8,2,1536]{2,1,0:T(2,128)S(1)}, u32[]{:S(2)}, u32[]{:S(2)}) async-start(f32[8,2,1536]{2,1,0:T(2,128)} %copy.207), calls=%async_computation.6 | async-start | bytes 196608 | tf_op jit(solution)/shard_map/all_to_all | solution.py:1610
  689.6 34.9 %collective-permute-start.77 = (bf16[304,768]{1,0:T(8,128)(2,1)S(1)}, bf16[304,768]{1,0:T(8,128)(2,1)}, u32[]{:S(2)}, u32[]{:S(2)}) collective-permute-start(bf16[304,768]{1,0:T(8,128)(2,1)S(1)} %add_convert_fusion.2), channel_id=1, source_target_pairs={{0,2},{1,3},{2,0},{3,1},{4,6},{5,7},{6,4},{7,5},{8,10},{9,11},{10,... | collective-permute-start | bytes 1400840 | tf_op jit(solution)/shard_map/ppermute | solution.py:799
  692.7 31.8 %collective-permute-start.76 = (bf16[304,768]{1,0:T(8,128)(2,1)S(1)}, bf16[304,768]{1,0:T(8,128)(2,1)}, u32[]{:S(2)}, u32[]{:S(2)}) collective-permute-start(bf16[304,768]{1,0:T(8,128)(2,1)S(1)} %add_convert_fusion.3), channel_id=1, source_target_pairs={{0,1},{1,0},{2,3},{3,2},{4,5},{5,4},{6,7},{7,6},{8,9},{9,8},{10,11... | collective-permute-start | bytes 1400840 | tf_op jit(solution)/shard_map/ppermute | solution.py:799
  698.2 42.0 %collective-permute-start.84 = (bf16[1,2,48,1536]{3,2,0,1:T(8,128)(2,1)}, bf16[1,2,48,1536]{3,2,0,1:T(8,128)(2,1)}, u32[]{:S(2)}, u32[]{:S(2)}) collective-permute-start(bf16[1,2,48,1536]{3,2,0,1:T(8,128)(2,1)} %get-tuple-element.530), channel_id=1, source_target_pairs={{0,0},{4,1},{1,2},{5,3},{9,4},{2,5},{6,6},{10,7},{3,8},{7,9},{8,10... | collective-permute-start | bytes 884744 | tf_op jit(solution)/shard_map/ppermute | solution.py:1576
  700.5 38.7 %collective-permute-start.83 = (bf16[1,2,48,1536]{3,2,0,1:T(8,128)(2,1)}, bf16[1,2,48,1536]{3,2,0,1:T(8,128)(2,1)}, u32[]{:S(2)}, u32[]{:S(2)}) collective-permute-start(bf16[1,2,48,1536]{3,2,0,1:T(8,128)(2,1)} %get-tuple-element.531), channel_id=1, source_target_pairs={{0,0},{4,1},{8,2},{1,3},{5,4},{2,5},{6,6},{10,7},{3,8},{7,9},{11,1... | collective-permute-start | bytes 884744 | tf_op jit(solution)/shard_map/ppermute | solution.py:1576
  705.0 33.2 %collective-permute-start.82 = (bf16[1,2,48,1536]{3,2,0,1:T(8,128)(2,1)S(1)}, bf16[1,2,48,1536]{3,2,0,1:T(8,128)(2,1)}, u32[]{:S(2)}, u32[]{:S(2)}) collective-permute-start(bf16[1,2,48,1536]{3,2,0,1:T(8,128)(2,1)S(1)} %get-tuple-element.532), channel_id=1, source_target_pairs={{0,0},{4,1},{8,2},{1,3},{5,4},{9,5},{2,6},{6,7},{3,8},{7,9},{11,10... | collective-permute-start | bytes 884744 | tf_op jit(solution)/shard_map/ppermute | solution.py:1576
  (143 other events, 2232.9 us)
Sparse Core Ops, SparseCore 0:
  30.4 76.4 all-gather.4
  109.1 30.7 all-gather.6
  141.5 89.1 all-gather.8
  232.2 89.1 all-gather.10
  355.9 98.8 reduce-scatter.4
  470.1 99.2 reduce-scatter.6
  571.7 31.2 reduce-scatter.8
  610.1 80.1 reduce-scatter.10
